TPU v7x, 32 devices: a whole 2x2x4 slice. The times are simulated.
32 devices in a mesh: group: 2 (over y), gx: 4 (over z), gy: 4 (over x, core).
Axes of the slice: x: 2, y: 2, z: 4, core: 2. Of those that a mesh axis runs over, the one named last changes fastest.
Arguments:
- tokens: bfloat16 [512, 8192], P(('group', 'gx'), 'gy'), parts along dimension 0, may hold values from -6 to 6
- gate_weight: bfloat16 [8192, 26624], P('gy', 'gx'), may hold values from -0.0625 to 0.0625
- up_weight: bfloat16 [8192, 26624], P('gy', 'gx'), may hold values from -0.0625 to 0.0625
- down_weight: bfloat16 [26624, 8192], P('gx', 'gy'), may hold values from -0.0390625 to 0.0390625
- lengths: int32 [8], P('group'), parts along dimension 0, may hold values from 1 to 64, 192 in all
Outputs:
- scored: bfloat16 [512, 8192], P(('group', 'gx'), 'gy'), parts along dimension 0
There are 2 independent parts, one for each index of `group`. A program takes and returns all parts, laid end to end along the dimension named above; an argument that names none is the same for every part. Nothing has to cross between parts.
Inputs may be any that keep to these rules, and one draw needn't show every extreme that they name: The live tokens of row group g are its first lengths[g] slots; the lengths of one part sum to exactly 192, and the longest is exactly 64.
All inputs are finite; a program needn't handle non-finite values.
Results may differ from a plain program's by a relative error of at most 0.019.
Values may be sent and summed in bfloat16 or wider, within the bound.
No kernel may reach another device: no remote copies, remote signals or barrier semaphores. Data moves between devices by JAX's collectives and lax.ppermute only.
A program may use at most 192 MiB of HBM per device.

v0:
```python
import jax
import jax.numpy as jnp
from jax import lax
from jax.sharding import PartitionSpec as P


def local(tokens, gate_weight, up_weight, down_weight, lengths):
    tok_dev = tokens.shape[0]
    all_rows = tok_dev * lax.axis_size("gx")
    gy_count = lax.axis_size("gy")
    ffn_cols = gate_weight.shape[1]
    positions = jnp.arange(tok_dev, dtype=jnp.int32)
    live_mask = (positions[None, :] < lengths[:, None]).reshape(all_rows)
    gathered = lax.all_gather(tokens, "gx", axis=0, tiled=True)
    live_total = 3 * all_rows // 4
    chosen = jnp.nonzero(live_mask, size=live_total)[0].astype(jnp.int32)
    compact = jnp.take(gathered, chosen, axis=0)
    row_block = lax.dynamic_slice_in_dim(
        compact, jnp.int32(0), live_total // gy_count * lax.axis_size("gy"), 0
    )
    gate_part = jnp.dot(row_block, gate_weight, preferred_element_type=jnp.float32)
    up_part = jnp.dot(row_block, up_weight, preferred_element_type=jnp.float32)
    paired = lax.psum_scatter(
        jnp.concatenate([gate_part, up_part], axis=1).astype(jnp.bfloat16),
        "gy",
        scatter_dimension=0,
        tiled=True,
    ).astype(jnp.float32)
    hidden = (jax.nn.silu(paired[:, :ffn_cols]) * paired[:, ffn_cols:]).astype(jnp.bfloat16)
    partial_out = jnp.dot(
        lax.all_gather(hidden, "gy", axis=0, tiled=True),
        down_weight,
        preferred_element_type=jnp.float32,
    )
    spread = jnp.zeros((all_rows, down_weight.shape[1]), jnp.float32).at[chosen].set(partial_out)
    mixed_out = lax.psum_scatter(spread.astype(jnp.bfloat16), "gx", scatter_dimension=0, tiled=True)
    return mixed_out


def solution(mesh):
    placed = (P(("group", "gx"), "gy"), P("gy", "gx"), P("gy", "gx"), P("gx", "gy"), P("group"))
    return jax.shard_map(
        local, mesh=mesh, in_specs=placed, out_specs=P(("group", "gx"), "gy"), check_vma=False
    )
```

profile of v0, /device:TPU:0, one launch (start us, length us, event | category | flops | bytes accessed | tf_op | source)
XLA Modules:
  0.0 198.6 jit_solution(6024100935172844724)
XLA Ops:
  6.5 0.7 all-gather.3.cloned.1.call-update
  7.3 0.7 lt.62
  8.1 0.1 lt.64
  8.3 0.3 reduce-window.16
  8.7 0.1 slice_reduce_fusion.1
  8.9 2.3 %scatter_custom_fusion = s32[192]{0:T(256)S(1)} fusion(s32[256]{0:T(256)S(1)} %bitcast.12, s32[256]{0:T(256)S(1)} %broadcast.49, s32[]{:T(128)} %constant.51.clone.1), kind=kCustom, calls=%fused_computation.28 | custom fusion | flops 256 | bytes 772 | tf_op jit(solution)/shard_map/scatter-add | solution.py:16
  11.2 0.3 reduce-window.24
  11.7 0.1 slice_reduce_fusion
  11.8 1.4 convert_reduce_fusion
  13.2 0.7 compare_and_fusion
  13.9 25.7 %all-gather.3.cloned.1.call-done = bf16[256,2048]{1,0:T(8,128)(2,1)} async-done(((bf16[64,2048]{1,0:T(8,128)(2,1)}), bf16[256,2048]{1,0:T(8,128)(2,1)}) %all-gather.3.cloned.1.call-update) | async-done | bytes 1048592 | tf_op jit(solution)/shard_map/all_gather | solution.py:14
  39.6 3.3 %gather_fusion = bf16[192,2048]{1,0:T(8,128)(2,1)S(1)} fusion(bf16[256,2048]{1,0:T(8,128)(2,1)} %all-gather.3.cloned.1.call-done, s32[1024]{0:T(1024)S(1)} %pad_clamp_fusion), kind=kCustom, calls=%fused_computation | custom fusion | bytes 1573632 | tf_op jit(solution)/shard_map/jit(_take)/gather | solution.py:17
  42.9 11.7 %convolution_convert_fusion = bf16[192,6656]{1,0:T(8,128)(2,1)S(1)} fusion(bf16[2048,6656]{1,0:T(8,128)(2,1)} %param.7, bf16[192,2048]{1,0:T(8,128)(2,1)S(1)} %gather_fusion, pred[192]{0:T(512)(128)(4,1)S(1)} %get-tuple-element.5), kind=kOutput, calls=%fused_computation.3 | convolution fusion | flops 5236162560 | bytes 30605504 | tf_op jit(solution)/shard_map/dot_general | solution.py:22
  54.5 11.7 %convolution_convert_fusion.1 = bf16[192,6656]{1,0:T(8,128)(2,1)S(1)} fusion(bf16[2048,6656]{1,0:T(8,128)(2,1)} %param.6, bf16[192,2048]{1,0:T(8,128)(2,1)S(1)} %gather_fusion, pred[192]{0:T(512)(128)(4,1)S(1)} %get-tuple-element.5), kind=kOutput, calls=%fused_computation.4 | convolution fusion | flops 5236162560 | bytes 30605504 | tf_op jit(solution)/shard_map/dot_general | solution.py:21
  66.2 2.9 %pad_maximum_fusion = bf16[192,13312]{1,0:T(8,128)(2,1)} fusion(bf16[192,6656]{1,0:T(8,128)(2,1)S(1)} %convolution_convert_fusion, bf16[192,6656]{1,0:T(8,128)(2,1)S(1)} %convolution_convert_fusion.1), kind=kLoop, calls=%fused_computation.5 | loop fusion | flops 10223616 | bytes 10223616 | tf_op jit(solution)/shard_map/concatenate | solution.py:24
  69.2 50.1 %reduce-scatter.3.cloned.1.call-done = bf16[48,13312]{1,0:T(8,128)(2,1)} async-done(((bf16[192,13312]{1,0:T(8,128)(2,1)}), bf16[48,13312]{1,0:T(8,128)(2,1)}) %reduce-scatter.3.cloned.1.call-update) | async-done | bytes 1277968 | tf_op jit(solution)/shard_map/reduce_scatter | solution.py:23
  119.3 1.5 convert_element_type.21
  120.7 1.2 fusion
  121.9 0.2 reduce-scatter.5.cloned.1.call-start
  122.2 25.1 %all-gather.5.cloned.1.call-done = bf16[192,6656]{1,0:T(8,128)(2,1)} async-done(((bf16[48,6656]{1,0:T(8,128)(2,1)}), bf16[192,6656]{1,0:T(8,128)(2,1)}) %all-gather.5.cloned.1.call-update) | async-done | bytes 2555920 | tf_op jit(solution)/shard_map/all_gather | solution.py:31
  147.3 13.3 %fusion.8 = f32[192,2048]{1,0:T(8,128)} fusion(bf16[192,6656]{1,0:T(8,128)(2,1)} %all-gather.5.cloned.1.call-done, bf16[6656,2048]{1,0:T(8,128)(2,1)} %param.8), kind=kOutput, calls=%fused_computation.32 | convolution fusion | flops 5234491392 | bytes 31391744 | tf_op jit(solution)/shard_map/dot_general | solution.py:30
  160.6 2.9 %scatter_custom_fusion.1 = f32[256,2048]{1,0:T(8,128)S(1)} fusion(s32[192]{0:T(256)S(1)} %get-tuple-element.6, f32[192,2048]{1,0:T(8,128)} %fusion.8, f32[]{:T(128)} %constant.50.clone.1), kind=kCustom, calls=%fused_computation.8 | custom fusion | bytes 2097664 | tf_op jit(solution)/shard_map/scatter | solution.py:35
  163.5 1.1 convert_element_type.23
  164.7 27.3 %reduce-scatter.5.cloned.1.call-done = bf16[64,2048]{1,0:T(8,128)(2,1)} async-done(((bf16[256,2048]{1,0:T(8,128)(2,1)}), bf16[64,2048]{1,0:T(8,128)(2,1)}) %reduce-scatter.5.cloned.1.call-update) | async-done | bytes 262160 | tf_op jit(solution)/shard_map/reduce_scatter | solution.py:36
  (20 shorter events, 0.7 us)
Async XLA Ops:
  6.5 33.1 %all-gather.3.cloned.1.call-start = ((), (), s32[]{:S(2)}) async-start(), calls=%async_computation.2 | async-start | bytes 1310720 | tf_op jit(solution)/shard_map/all_gather | solution.py:14
  7.3 112.0 %reduce-scatter.3.cloned.1.call-start = ((), (), s32[]{:S(2)}) async-start(), calls=%async_computation.3 | async-start | bytes 6389760 | tf_op jit(solution)/shard_map/reduce_scatter | solution.py:23
  69.1 78.2 %all-gather.5.cloned.1.call-start = ((), (), s32[]{:S(2)}) async-start(), calls=%async_computation.4 | async-start | bytes 3194880 | tf_op jit(solution)/shard_map/all_gather | solution.py:31
  121.9 70.1 %reduce-scatter.5.cloned.1.call-start = ((), (), s32[]{:S(2)}) async-start(), calls=%async_computation.5 | async-start | bytes 1310720 | tf_op jit(solution)/shard_map/reduce_scatter | solution.py:36
Sparse Core Ops, SparseCore 0:
  8.9 30.6 all-gather.2
  69.2 49.9 reduce-scatter.2
  122.1 25.2 all-gather.4
  164.8 27.1 reduce-scatter.4
where the time goes:
time: 199 us
  waiting for transfers between devices  129 us (65%)
  matrix products  36.7 us (18%)
  between operations  13.2 us (7%)
  other arithmetic  11.9 us (6%)
  local copies, waits for them, and re-layouts  7.54 us (4%)
    reduce_scatter x1, waiting for transfers between devices, local(): lax.psum_scatter(jnp.concatenate([gate_part, up_part], axis=1).astype(jnp...  50.1 us
    reduce_scatter x1, waiting for transfers between devices, local(): lax.psum_scatter(spread.astype(jnp.bfloat16), 'gx', scatter_dimension=0,...  27.3 us
    all_gather x1, waiting for transfers between devices, local(): gathered = lax.all_gather(tokens, 'gx', axis=0, tiled=True)  25.7 us
    all_gather x1, waiting for transfers between devices, local(): lax.all_gather(hidden, 'gy', axis=0, tiled=True)  25.1 us
    dot_general x1, matrix products, local(): jnp.dot(lax.all_gather(hidden, 'gy', axis=0, tiled=True), down_weight, pr...  13.3 us
    dot_general x1, matrix products, local(): jnp.dot(row_block, gate_weight, preferred_element_type=jnp.float32)  11.7 us
    dot_general x1, matrix products, local(): up_part = jnp.dot(row_block, up_weight, preferred_element_type=jnp.float32)  11.7 us
  transfers between devices with their start and end apart: 4, of which 4 were waited for; matrix products, arithmetic and copies ran while one was open for 3% of the time, Pallas kernels for 0%

commit v1 on v0

v1 whole, which is shorter than its diff:
```python
import functools

import jax
import jax.numpy as jnp
from jax import lax
from jax.experimental import pallas as pl
from jax.experimental.pallas import tpu as pltpu
from jax.sharding import PartitionSpec as P

MIB = 1 << 20
BF16, F32 = jnp.bfloat16, jnp.float32


def row_sources(lengths_ref, rows, n_gx, tok_dev):
    start = jnp.int32(0)
    slot = rows
    for g in range(n_gx):
        slot = jnp.where(rows >= start, rows - start + g * tok_dev, slot)
        start = start + lengths_ref[g]
    return slot


def local_rows(shape, dim, quarter, nx):
    gy = lax.axis_index("gy")
    x, core = gy // 2, gy % 2
    j = lax.broadcasted_iota(jnp.int32, shape, dim)
    rows = jnp.zeros(shape, jnp.int32)
    for kc in range(2):
        for kx in range(nx):
            first = (kc * nx + kx) * quarter
            owner = lax.rem(x + kx, nx) * 2 + (1 - core if kc else core)
            rows = jnp.where(j >= first, owner * quarter + j - first, rows)
    return rows


def compact_kernel(n_gx, nx, lengths_ref, *refs):
    blocks, out_ref = refs[:-1], refs[-1]
    live, tok_dev = out_ref.shape[0], blocks[0].shape[0]
    z = lax.axis_index("gx")
    slot = row_sources(lengths_ref, local_rows((live, tok_dev), 0, live // (2 * nx), nx), n_gx, tok_dev)
    column = lax.broadcasted_iota(jnp.int32, (live, tok_dev), 1)
    total = jnp.zeros(out_ref.shape, F32)
    for k in range(n_gx):
        pick = (slot == column + (z ^ k) * tok_dev).astype(F32).astype(BF16)
        total += jnp.dot(pick, blocks[k][...], preferred_element_type=F32)
    out_ref[...] = total.astype(BF16)


def compact(lengths, blocks, live, nx):
    n_gx = len(blocks)
    rows, width = blocks[0].shape
    tile = min(width, 512)
    return pl.pallas_call(
        functools.partial(compact_kernel, n_gx, nx),
        out_shape=jax.ShapeDtypeStruct((live, width), BF16),
        grid_spec=pltpu.PrefetchScalarGridSpec(
            num_scalar_prefetch=1,
            grid=(width // tile,),
            in_specs=[pl.BlockSpec((rows, tile), lambda j, s: (0, j))] * n_gx,
            out_specs=pl.BlockSpec((live, tile), lambda j, s: (0, j)),
        ),
        name="compact",
    )(lengths, *blocks)


def gate_up_kernel(tok_ref, gate_ref, up_ref, send_ref, keep_ref):
    half = keep_ref.shape[1]
    rows = tok_ref[...]
    for i, w_ref in enumerate((gate_ref, up_ref)):
        part = jnp.dot(rows, w_ref[...], preferred_element_type=F32)
        keep_ref[i] = part[:half]
        send_ref[i] = part[half:].astype(BF16)


def gate_up(tok, gate_weight, up_weight, start, width, tile):
    live, depth = tok.shape
    half = live // 2
    weight = pl.BlockSpec((depth, tile), lambda j: (0, start // tile + j))
    out = pl.BlockSpec((2, half, tile), lambda j: (0, 0, j))
    return pl.pallas_call(
        gate_up_kernel,
        out_shape=[jax.ShapeDtypeStruct((2, half, width), BF16), jax.ShapeDtypeStruct((2, half, width), F32)],
        grid=(width // tile,),
        in_specs=[pl.BlockSpec((live, depth), lambda j: (0, 0)), weight, weight],
        out_specs=[out, out],
        compiler_params=pltpu.CompilerParams(vmem_limit_bytes=32 * MIB),
        cost_estimate=pl.CostEstimate(
            flops=4 * live * depth * width, bytes_accessed=4 * depth * width, transcendentals=0
        ),
        name="gate_up",
    )(tok, gate_weight, up_weight)


def down_kernel(n_h, n_gx, nx, first, last, lengths_ref, *refs):
    h_refs, w_ref, refs = refs[:n_h], refs[n_h], refs[n_h + 1:]
    h = jnp.concatenate([r[...] for r in h_refs], axis=0)
    total = jnp.dot(h, w_ref[...], preferred_element_type=F32)
    if not first:
        total += refs[0][...]
        refs = refs[1:]
    if not last:
        refs[0][...] = total
        return
    live, tok_dev = total.shape[0], refs[0].shape[0]
    z = lax.axis_index("gx")
    slot = row_sources(lengths_ref, local_rows((tok_dev, live), 1, live // (2 * nx), nx), n_gx, tok_dev)
    row = lax.broadcasted_iota(jnp.int32, (tok_dev, live), 0)
    total = total.astype(BF16)
    for k in range(n_gx):
        pick = (slot == row + (z ^ k) * tok_dev).astype(F32).astype(BF16)
        refs[k][...] = jnp.dot(pick, total, preferred_element_type=F32).astype(BF16)


def down(lengths, hidden, down_weight, total, start, width, n_gx, nx, tok_dev, last):
    live = sum(h.shape[0] for h in hidden)
    out_width = down_weight.shape[1]
    tile = min(out_width, 512)
    rows = pl.BlockSpec((live, tile), lambda j, s: (0, j))
    operands = [*hidden, down_weight]
    in_specs = [pl.BlockSpec(h.shape, lambda j, s: (0, 0)) for h in hidden]
    in_specs.append(pl.BlockSpec((pl.Element(width), pl.Element(tile)), lambda j, s: (start, j * tile)))
    if total is not None:
        operands.append(total)
        in_specs.append(rows)
    if last:
        out_shape = [jax.ShapeDtypeStruct((tok_dev, out_width), BF16)] * n_gx
        out_specs = [pl.BlockSpec((tok_dev, tile), lambda j, s: (0, j))] * n_gx
    else:
        out_shape, out_specs = jax.ShapeDtypeStruct((live, out_width), F32), rows
    return pl.pallas_call(
        functools.partial(down_kernel, len(hidden), n_gx, nx, total is None, last),
        out_shape=out_shape,
        grid_spec=pltpu.PrefetchScalarGridSpec(
            num_scalar_prefetch=1, grid=(out_width // tile,), in_specs=in_specs, out_specs=out_specs
        ),
        compiler_params=pltpu.CompilerParams(vmem_limit_bytes=32 * MIB),
        cost_estimate=pl.CostEstimate(
            flops=2 * live * width * out_width, bytes_accessed=2 * width * out_width, transcendentals=0
        ),
        name="down",
    )(lengths, *operands)


def column_chunks(cols, tile):
    tiles = cols // tile
    shares = (5, 7, 8, 6)
    edges = [round(tiles * sum(shares[:i]) / sum(shares)) for i in range(len(shares) + 1)]
    return [(a * tile, (b - a) * tile) for a, b in zip(edges, edges[1:]) if b > a]


def local(n_gx, n_gy, tokens, gate_weight, up_weight, down_weight, lengths):
    nx = n_gy // 2
    tok_dev = tokens.shape[0]
    live = 3 * tok_dev * n_gx // 4
    quarter = live // n_gy
    cols = gate_weight.shape[1]
    tile = 256 if cols % 256 == 0 else 128
    chunks = column_chunks(cols, tile)

    def over_z(block, k):
        return lax.ppermute(block, "gx", [(z, z ^ k) for z in range(n_gx)])

    def over_core(block):
        return lax.ppermute(block, "gy", [(i, i ^ 1) for i in range(n_gy)])

    def over_x(block, k):
        return lax.ppermute(block, "gy", [(i, (i + 2 * k) % n_gy) for i in range(n_gy)])

    blocks = [tokens] + [over_z(tokens, k) for k in range(1, n_gx)]
    tok = compact(lengths, blocks, live, nx)

    total = None
    for i, (start, width) in enumerate(chunks):
        send, keep = gate_up(tok, gate_weight, up_weight, start, width, tile)
        sums = keep + over_core(send).astype(F32)
        mine = sums[:, :quarter]
        for k in range(1, nx):
            block = sums[:, k * quarter:(k + 1) * quarter].astype(BF16)
            mine = mine + over_x(block, k).astype(F32)
        own = (jax.nn.silu(mine[0]) * mine[1]).astype(BF16)
        hidden = [own] + [over_x(own, -k) for k in range(1, nx)]
        hidden += [over_core(h) for h in hidden]
        last = i == len(chunks) - 1
        total = down(lengths, hidden, down_weight, total, start, width, n_gx, nx, tok_dev, last)

    out = total[0].astype(F32)
    for k in range(1, n_gx):
        out = out + over_z(total[k], k).astype(F32)
    return out.astype(BF16)


def solution(mesh):
    placed = (P(("group", "gx"), "gy"), P("gy", "gx"), P("gy", "gx"), P("gx", "gy"), P("group"))
    return jax.shard_map(
        functools.partial(local, mesh.shape["gx"], mesh.shape["gy"]),
        mesh=mesh, in_specs=placed, out_specs=P(("group", "gx"), "gy"), check_vma=False,
    )
```

time: 199 us -> 158 us (0.79)
  waiting for transfers between devices: 129 us -> 69 us
  Pallas kernels: 0 us -> 59.4 us
  matrix products: 36.7 us -> 0 us
  starting transfers between devices: 0.3 us -> 24.1 us
  between operations: 13.2 us -> 0.27 us
  other arithmetic: 11.9 us -> 2.03 us
  local copies, waits for them, and re-layouts: 7.54 us -> 2.7 us
    reduce_scatter x2 -> x0, waiting for transfers between devices: 77.4 us -> none  [the longest x1 50.1 us: local(): lax.psum_scatter(jnp.concatenate([gate_part, up_part], axis=1).astype(jnp...]
    ppermute x0 -> x26, waiting for transfers between devices: none -> 69 us  [the longest x6 40.7 us: over_z(): return lax.ppermute(block, 'gx', [(z, z ^ k) for z in range(n_gx)])]
    pallas_call x0 -> x9, Pallas kernels: none -> 59.4 us  [the longest x4 32.9 us: gate_up(): pl.pallas_call(gate_up_kernel, out_shape=[jax.ShapeDtypeStruct((2, half,...]
    all_gather x2 -> x0, waiting for transfers between devices: 50.8 us -> none  [the longest x1 25.7 us: local(): gathered = lax.all_gather(tokens, 'gx', axis=0, tiled=True)]
    dot_general x3 -> x0, matrix products: 36.7 us -> none  [the longest x1 13.3 us: local(): jnp.dot(lax.all_gather(hidden, 'gy', axis=0, tiled=True), down_weight, pr...]
    ppermute x0 -> x26, starting transfers between devices: none -> 24.1 us  [the longest x6 11.3 us: over_z(): return lax.ppermute(block, 'gx', [(z, z ^ k) for z in range(n_gx)])]
    gather x1 -> x0, local copies, waits for them, and re-layouts: 3.26 us -> none  [local(): compact = jnp.take(gathered, chosen, axis=0)]
    scatter x1 -> x0, local copies, waits for them, and re-layouts: 2.91 us -> none  [local(): jnp.zeros((all_rows, down_weight.shape[1]), jnp.float32).at[chosen]]
  transfers between devices with their start and end apart: 4 -> 26, of which waited for: 4 -> 10; matrix products, arithmetic and copies ran while one was open for 3% -> 1% of each run, Pallas kernels for 0% -> 22%
where the time goes in v1:
time: 158 us
  waiting for transfers between devices  69 us (44%)
  Pallas kernels  59.4 us (38%)
  starting transfers between devices  24.1 us (15%)
  local copies, waits for them, and re-layouts  2.7 us (2%)
  other arithmetic  2.03 us (1%)
    ppermute x6, waiting for transfers between devices, over_z(): return lax.ppermute(block, 'gx', [(z, z ^ k) for z in range(n_gx)])  40.7 us
    pallas_call x4, Pallas kernels, gate_up(): pl.pallas_call(gate_up_kernel, out_shape=[jax.ShapeDtypeStruct((2, half,...  32.9 us
    ppermute x8, waiting for transfers between devices, over_x(): lax.ppermute(block, 'gy', [(i, (i + 2 * k) % n_gy) for i in range(n_gy)])  28 us
    pallas_call x4, Pallas kernels, down(): pl.pallas_call(functools.partial(down_kernel, len(hidden), n_gx, nx, tota...  21.8 us
    ppermute x6, starting transfers between devices, over_z(): return lax.ppermute(block, 'gx', [(z, z ^ k) for z in range(n_gx)])  11.3 us
    ppermute x8, starting transfers between devices, over_x(): lax.ppermute(block, 'gy', [(i, (i + 2 * k) % n_gy) for i in range(n_gy)])  10.6 us
    pallas_call x1, Pallas kernels, compact(): pl.pallas_call(functools.partial(compact_kernel, n_gx, nx), out_shape=jax...  4.74 us
  transfers between devices with their start and end apart: 26, of which 10 were waited for; matrix products, arithmetic and copies ran while one was open for 1% of the time, Pallas kernels for 22%

profile of v1, /device:TPU:0, one launch (start us, length us, event | category | flops | bytes accessed | tf_op | source)
XLA Modules:
  0.0 157.5 jit_solution(4783610776340989501)
XLA Ops:
  0.0 3.0 %collective-permute-start = (bf16[64,2048]{1,0:T(8,128)(2,1)}, bf16[64,2048]{1,0:T(8,128)(2,1)S(1)}, u32[]{:S(2)}, u32[]{:S(2)}) collective-permute-start(bf16[64,2048]{1,0:T(8,128)(2,1)} %refs_0_.1), channel_id=1, source_target_pairs={{0,4},{4,0},{8,12},{12,8},{1,5},{5,1},{9,13},{13,9},{2,6},{6,2},{1... | collective-permute-start | bytes 786440 | tf_op jit(solution)/shard_map/ppermute | solution.py:161
  3.0 2.6 %collective-permute-start.1 = (bf16[64,2048]{1,0:T(8,128)(2,1)}, bf16[64,2048]{1,0:T(8,128)(2,1)S(1)}, u32[]{:S(2)}, u32[]{:S(2)}) collective-permute-start(bf16[64,2048]{1,0:T(8,128)(2,1)} %refs_0_.1), channel_id=1, source_target_pairs={{0,8},{4,12},{8,0},{12,4},{1,9},{5,13},{9,1},{13,5},{2,10},{6,14},... | collective-permute-start | bytes 786440 | tf_op jit(solution)/shard_map/ppermute | solution.py:161
  5.6 8.8 %collective-permute-done.refs_1_ = bf16[64,2048]{1,0:T(8,128)(2,1)S(1)} collective-permute-done((bf16[64,2048]{1,0:T(8,128)(2,1)}, bf16[64,2048]{1,0:T(8,128)(2,1)S(1)}, u32[]{:S(2)}, u32[]{:S(2)}) %collective-permute-start) | collective-permute-done | bytes 262176 | tf_op jit(solution)/shard_map/ppermute | solution.py:161
  14.4 10.2 %collective-permute-done.1.refs_2_ = bf16[64,2048]{1,0:T(8,128)(2,1)S(1)} collective-permute-done((bf16[64,2048]{1,0:T(8,128)(2,1)}, bf16[64,2048]{1,0:T(8,128)(2,1)S(1)}, u32[]{:S(2)}, u32[]{:S(2)}) %collective-permute-start.1) | collective-permute-done | bytes 262176 | tf_op jit(solution)/shard_map/ppermute | solution.py:161
  26.0 4.7 %compact.1.tok_ref = bf16[192,2048]{1,0:T(8,128)(2,1)} custom-call(s32[4]{0:T(128)} %lengths_ref.9, bf16[64,2048]{1,0:T(8,128)(2,1)} %refs_0_.1, bf16[64,2048]{1,0:T(8,128)(2,1)} %copy-done.2, bf16[64,2048]{1,0:T(8,128)(2,1)} %copy-done.3, bf16[64,2048]{1,0:T(8,128)(2,1)} %copy-done.4), custom_call_target="tpu_custom_call" | custom-call | tf_op jit(solution)/shard_map/compact/pallas_call | solution.py:53
  31.9 7.6 %gate_up.4 = (bf16[2,96,1536]{2,1,0:T(8,128)(2,1)S(1)}, f32[2,96,1536]{2,1,0:T(8,128)S(1)}) custom-call(bf16[192,2048]{1,0:T(8,128)(2,1)S(1)} %copy-done, bf16[2048,6656]{1,0:T(8,128)(2,1)} %gate_ref.7, bf16[2048,6656]{1,0:T(8,128)(2,1)} %up_ref.7), custom_call_target="tpu_custom_call" | custom-call | flops 2415919104 | bytes 12582912 | tf_op jit(solution)/shard_map/gate_up/pallas_call | solution.py:80
  39.5 6.6 %gate_up.7 = (bf16[2,96,1280]{2,1,0:T(8,128)(2,1)S(1)}, f32[2,96,1280]{2,1,0:T(8,128)S(1)}) custom-call(bf16[192,2048]{1,0:T(8,128)(2,1)S(1)} %copy-done, bf16[2048,6656]{1,0:T(8,128)(2,1)} %gate_ref.7, bf16[2048,6656]{1,0:T(8,128)(2,1)} %up_ref.7), custom_call_target="tpu_custom_call" | custom-call | flops 2013265920 | bytes 10485760 | tf_op jit(solution)/shard_map/gate_up/pallas_call | solution.py:80
  46.7 9.9 %gate_up.5 = (bf16[2,96,2048]{2,1,0:T(8,128)(2,1)S(1)}, f32[2,96,2048]{2,1,0:T(8,128)S(1)}) custom-call(bf16[192,2048]{1,0:T(8,128)(2,1)S(1)} %copy-done, bf16[2048,6656]{1,0:T(8,128)(2,1)} %gate_ref.7, bf16[2048,6656]{1,0:T(8,128)(2,1)} %up_ref.7), custom_call_target="tpu_custom_call" | custom-call | flops 3221225472 | bytes 16777216 | tf_op jit(solution)/shard_map/gate_up/pallas_call | solution.py:80
  56.5 8.9 %gate_up.6 = (bf16[2,96,1792]{2,1,0:T(8,128)(2,1)S(1)}, f32[2,96,1792]{2,1,0:T(8,128)S(1)}) custom-call(bf16[192,2048]{1,0:T(8,128)(2,1)S(1)} %copy-done, bf16[2048,6656]{1,0:T(8,128)(2,1)} %gate_ref.7, bf16[2048,6656]{1,0:T(8,128)(2,1)} %up_ref.7), custom_call_target="tpu_custom_call" | custom-call | flops 2818572288 | bytes 14680064 | tf_op jit(solution)/shard_map/gate_up/pallas_call | solution.py:80
  66.1 1.6 collective-permute-start.19
  69.0 1.6 collective-permute-start.14
  70.5 4.5 %collective-permute-done.19 = bf16[2,48,1280]{2,1,0:T(8,128)(2,1)S(1)} collective-permute-done((bf16[2,48,1280]{2,1,0:T(8,128)(2,1)S(1)}, bf16[2,48,1280]{2,1,0:T(8,128)(2,1)S(1)}, u32[]{:S(2)}, u32[]{:S(2)}) %collective-permute-start.19) | collective-permute-done | bytes 245792 | tf_op jit(solution)/shard_map/ppermute | solution.py:167
  75.1 1.6 collective-permute-start.20
  77.6 13.8 %collective-permute-done.20.refs_1_ = bf16[48,1280]{1,0:T(8,128)(2,1)S(1)} collective-permute-done((bf16[48,1280]{1,0:T(8,128)(2,1)S(1)}, bf16[48,1280]{1,0:T(8,128)(2,1)S(1)}, u32[]{:S(2)}, u32[]{:S(2)}) %collective-permute-start.20) | collective-permute-done | bytes 122912 | tf_op jit(solution)/shard_map/ppermute | solution.py:167
  93.4 6.4 %collective-permute-done.9 = bf16[2,48,2048]{2,1,0:T(8,128)(2,1)S(1)} collective-permute-done((bf16[2,48,2048]{2,1,0:T(8,128)(2,1)S(1)}, bf16[2,48,2048]{2,1,0:T(8,128)(2,1)S(1)}, u32[]{:S(2)}, u32[]{:S(2)}) %collective-permute-start.9) | collective-permute-done | bytes 393248 | tf_op jit(solution)/shard_map/ppermute | solution.py:167
  101.5 1.9 %collective-permute-done.15.refs_1_ = bf16[48,1792]{1,0:T(8,128)(2,1)S(1)} collective-permute-done((bf16[48,1792]{1,0:T(8,128)(2,1)S(1)}, bf16[48,1792]{1,0:T(8,128)(2,1)S(1)}, u32[]{:S(2)}, u32[]{:S(2)}) %collective-permute-start.15) | collective-permute-done | bytes 172064 | tf_op jit(solution)/shard_map/ppermute | solution.py:167
  106.8 4.7 %down.4.refs_5_ = f32[192,2048]{1,0:T(8,128)S(1)} custom-call(s32[4]{0:T(128)S(1)} %copy-done.1, bf16[48,1280]{1,0:T(8,128)(2,1)S(1)} %fusion.7.refs_0_, bf16[48,1280]{1,0:T(8,128)(2,1)S(1)} %collective-permute-done.20.refs_1_, bf16[48,1280]{1,0:T(8,128)(2,1)S(1)} %collective-permute-done.21.refs_2_, bf16[48,1280]{1,0:T(8,128)(2,1)S(1)} %collective-permute-done.22.refs_3_, ...), custom_call_target="tpu_custom_call" | custom-call | flops 1006632960 | bytes 5242880 | tf_op jit(solution)/shard_map/down/pallas_call | solution.py:130
  112.1 5.4 %down.5.refs_5_ = f32[192,2048]{1,0:T(8,128)S(1)} custom-call(s32[4]{0:T(128)S(1)} %copy-done.1, bf16[48,1792]{1,0:T(8,128)(2,1)S(1)} %fusion.3.refs_0_, bf16[48,1792]{1,0:T(8,128)(2,1)S(1)} %collective-permute-done.15.refs_1_, bf16[48,1792]{1,0:T(8,128)(2,1)S(1)} %collective-permute-done.16.refs_2_, bf16[48,1792]{1,0:T(8,128)(2,1)S(1)} %collective-permute-done.17.refs_3_, ...), custom_call_target="tpu_custom_call" | custom-call | flops 1409286144 | bytes 7340032 | tf_op jit(solution)/shard_map/down/pallas_call | solution.py:130
  117.6 5.9 %down.6.refs_5_ = f32[192,2048]{1,0:T(8,128)S(1)} custom-call(s32[4]{0:T(128)S(1)} %copy-done.1, bf16[48,2048]{1,0:T(8,128)(2,1)S(1)} %fusion.1.refs_0_, bf16[48,2048]{1,0:T(8,128)(2,1)S(1)} %collective-permute-done.10.refs_1_, bf16[48,2048]{1,0:T(8,128)(2,1)S(1)} %collective-permute-done.11.refs_2_, bf16[48,2048]{1,0:T(8,128)(2,1)S(1)} %collective-permute-done.12.refs_3_, ...), custom_call_target="tpu_custom_call" | custom-call | flops 1610612736 | bytes 8388608 | tf_op jit(solution)/shard_map/down/pallas_call | solution.py:130
  123.5 5.8 %down.7 = (bf16[64,2048]{1,0:T(8,128)(2,1)S(1)}, bf16[64,2048]{1,0:T(8,128)(2,1)S(1)}, bf16[64,2048]{1,0:T(8,128)(2,1)S(1)}, bf16[64,2048]{1,0:T(8,128)(2,1)S(1)}) custom-call(s32[4]{0:T(128)S(1)} %copy-done.1, bf16[48,1536]{1,0:T(8,128)(2,1)S(1)} %fusion.5.refs_0_, bf16[48,1536]{1,0:T(8,128)(2,1)S(1)} %collective-permute-done.5.refs_1_, ...), custom_call_target="tpu_custom_call" | custom-call | flops 1207959552 | bytes 6291456 | tf_op jit(solution)/shard_map/down/pallas_call | solution.py:130
  129.3 2.5 %collective-permute-start.25 = (bf16[64,2048]{1,0:T(8,128)(2,1)S(1)}, bf16[64,2048]{1,0:T(8,128)(2,1)S(1)}, u32[]{:S(2)}, u32[]{:S(2)}) collective-permute-start(bf16[64,2048]{1,0:T(8,128)(2,1)S(1)} %get-tuple-element.28), channel_id=1, source_target_pairs={{0,12},{4,8},{8,4},{12,0},{1,13},{5,9},{9,5},{13,1},{2,14},{6,10},... | collective-permute-start | bytes 786440 | tf_op jit(solution)/shard_map/ppermute | solution.py:161
  131.9 3.1 %collective-permute-start.24 = (bf16[64,2048]{1,0:T(8,128)(2,1)S(1)}, bf16[64,2048]{1,0:T(8,128)(2,1)S(1)}, u32[]{:S(2)}, u32[]{:S(2)}) collective-permute-start(bf16[64,2048]{1,0:T(8,128)(2,1)S(1)} %get-tuple-element.27), channel_id=1, source_target_pairs={{0,8},{4,12},{8,0},{12,4},{1,9},{5,13},{9,1},{13,5},{2,10},{6,14},... | collective-permute-start | bytes 786440 | tf_op jit(solution)/shard_map/ppermute | solution.py:161
  135.0 5.4 %collective-permute-done.25 = bf16[64,2048]{1,0:T(8,128)(2,1)S(1)} collective-permute-done((bf16[64,2048]{1,0:T(8,128)(2,1)S(1)}, bf16[64,2048]{1,0:T(8,128)(2,1)S(1)}, u32[]{:S(2)}, u32[]{:S(2)}) %collective-permute-start.25) | collective-permute-done | bytes 262176 | tf_op jit(solution)/shard_map/ppermute | solution.py:161
  140.4 16.3 %collective-permute-done.24 = bf16[64,2048]{1,0:T(8,128)(2,1)S(1)} collective-permute-done((bf16[64,2048]{1,0:T(8,128)(2,1)S(1)}, bf16[64,2048]{1,0:T(8,128)(2,1)S(1)}, u32[]{:S(2)}, u32[]{:S(2)}) %collective-permute-start.24) | collective-permute-done | bytes 262176 | tf_op jit(solution)/shard_map/ppermute | solution.py:161
  (64 shorter events, 14.7 us)
Async XLA Ops:
  0.0 14.4 %collective-permute-start = (bf16[64,2048]{1,0:T(8,128)(2,1)}, bf16[64,2048]{1,0:T(8,128)(2,1)S(1)}, u32[]{:S(2)}, u32[]{:S(2)}) collective-permute-start(bf16[64,2048]{1,0:T(8,128)(2,1)} %refs_0_.1), channel_id=1, source_target_pairs={{0,4},{4,0},{8,12},{12,8},{1,5},{5,1},{9,13},{13,9},{2,6},{6,2},{1... | collective-permute-start | bytes 786440 | tf_op jit(solution)/shard_map/ppermute | solution.py:161
  3.0 21.6 %collective-permute-start.1 = (bf16[64,2048]{1,0:T(8,128)(2,1)}, bf16[64,2048]{1,0:T(8,128)(2,1)S(1)}, u32[]{:S(2)}, u32[]{:S(2)}) collective-permute-start(bf16[64,2048]{1,0:T(8,128)(2,1)} %refs_0_.1), channel_id=1, source_target_pairs={{0,8},{4,12},{8,0},{12,4},{1,9},{5,13},{9,1},{13,5},{2,10},{6,14},... | collective-permute-start | bytes 786440 | tf_op jit(solution)/shard_map/ppermute | solution.py:161
  5.6 19.0 %collective-permute-start.2 = (bf16[64,2048]{1,0:T(8,128)(2,1)}, bf16[64,2048]{1,0:T(8,128)(2,1)S(1)}, u32[]{:S(2)}, u32[]{:S(2)}) collective-permute-start(bf16[64,2048]{1,0:T(8,128)(2,1)} %refs_0_.1), channel_id=1, source_target_pairs={{0,12},{4,8},{8,4},{12,0},{1,13},{5,9},{9,5},{13,1},{2,14},{6,10},... | collective-permute-start | bytes 786440 | tf_op jit(solution)/shard_map/ppermute | solution.py:161
  46.1 21.6 %collective-permute-start.3 = (bf16[2,96,1536]{2,1,0:T(8,128)(2,1)S(1)}, bf16[2,96,1536]{2,1,0:T(8,128)(2,1)S(1)}, u32[]{:S(2)}, u32[]{:S(2)}) collective-permute-start(bf16[2,96,1536]{2,1,0:T(8,128)(2,1)S(1)} %get-tuple-element.18), channel_id=1, source_target_pairs={{0,1},{1,0},{2,3},{3,2},{4,5},{5,4},{6,7},{7,6},{8,9},{9,8},{10,11... | collective-permute-start | bytes 1769480 | tf_op jit(solution)/shard_map/ppermute | solution.py:164
  46.2 19.8 %collective-permute-start.18 = (bf16[2,96,1280]{2,1,0:T(8,128)(2,1)S(1)}, bf16[2,96,1280]{2,1,0:T(8,128)(2,1)S(1)}, u32[]{:S(2)}, u32[]{:S(2)}) collective-permute-start(bf16[2,96,1280]{2,1,0:T(8,128)(2,1)S(1)} %get-tuple-element.24), channel_id=1, source_target_pairs={{0,1},{1,0},{2,3},{3,2},{4,5},{5,4},{6,7},{7,6},{8,9},{9,8},{10,11... | collective-permute-start | bytes 1474568 | tf_op jit(solution)/shard_map/ppermute | solution.py:164
  65.4 11.3 %collective-permute-start.8 = (bf16[2,96,2048]{2,1,0:T(8,128)(2,1)S(1)}, bf16[2,96,2048]{2,1,0:T(8,128)(2,1)S(1)}, u32[]{:S(2)}, u32[]{:S(2)}) collective-permute-start(bf16[2,96,2048]{2,1,0:T(8,128)(2,1)S(1)} %get-tuple-element.20), channel_id=1, source_target_pairs={{0,1},{1,0},{2,3},{3,2},{4,5},{5,4},{6,7},{7,6},{8,9},{9,8},{10,11... | collective-permute-start | bytes 2359304 | tf_op jit(solution)/shard_map/ppermute | solution.py:164
  66.1 8.9 %collective-permute-start.19 = (bf16[2,48,1280]{2,1,0:T(8,128)(2,1)S(1)}, bf16[2,48,1280]{2,1,0:T(8,128)(2,1)S(1)}, u32[]{:S(2)}, u32[]{:S(2)}) collective-permute-start(bf16[2,48,1280]{2,1,0:T(8,128)(2,1)S(1)} %slice.127), channel_id=1, source_target_pairs={{0,2},{1,3},{2,0},{3,1},{4,6},{5,7},{6,4},{7,5},{8,10},{9,11},{10,... | collective-permute-start | bytes 737288 | tf_op jit(solution)/shard_map/ppermute | solution.py:167
  67.9 23.5 %collective-permute-start.4 = (bf16[2,48,1536]{2,1,0:T(8,128)(2,1)S(1)}, bf16[2,48,1536]{2,1,0:T(8,128)(2,1)S(1)}, u32[]{:S(2)}, u32[]{:S(2)}) collective-permute-start(bf16[2,48,1536]{2,1,0:T(8,128)(2,1)S(1)} %slice.126), channel_id=1, source_target_pairs={{0,2},{1,3},{2,0},{3,1},{4,6},{5,7},{6,4},{7,5},{8,10},{9,11},{10,... | collective-permute-start | bytes 884744 | tf_op jit(solution)/shard_map/ppermute | solution.py:167
  69.0 22.4 %collective-permute-start.14 = (bf16[2,48,1792]{2,1,0:T(8,128)(2,1)S(1)}, bf16[2,48,1792]{2,1,0:T(8,128)(2,1)S(1)}, u32[]{:S(2)}, u32[]{:S(2)}) collective-permute-start(bf16[2,48,1792]{2,1,0:T(8,128)(2,1)S(1)} %slice.125), channel_id=1, source_target_pairs={{0,2},{1,3},{2,0},{3,1},{4,6},{5,7},{6,4},{7,5},{8,10},{9,11},{10,... | collective-permute-start | bytes 1032200 | tf_op jit(solution)/shard_map/ppermute | solution.py:167
  75.1 16.2 %collective-permute-start.20 = (bf16[48,1280]{1,0:T(8,128)(2,1)S(1)}, bf16[48,1280]{1,0:T(8,128)(2,1)S(1)}, u32[]{:S(2)}, u32[]{:S(2)}) collective-permute-start(bf16[48,1280]{1,0:T(8,128)(2,1)S(1)} %fusion.7.refs_0_), channel_id=1, source_target_pairs={{0,2},{1,3},{2,0},{3,1},{4,6},{5,7},{6,4},{7,5},{8,10},{9,11},{10,... | collective-permute-start | bytes 368648 | tf_op jit(solution)/shard_map/ppermute | solution.py:167
  76.7 26.8 %collective-permute-start.21 = (bf16[48,1280]{1,0:T(8,128)(2,1)S(1)}, bf16[48,1280]{1,0:T(8,128)(2,1)S(1)}, u32[]{:S(2)}, u32[]{:S(2)}) collective-permute-start(bf16[48,1280]{1,0:T(8,128)(2,1)S(1)} %fusion.7.refs_0_), channel_id=1, source_target_pairs={{0,1},{1,0},{2,3},{3,2},{4,5},{5,4},{6,7},{7,6},{8,9},{9,8},{10,11... | collective-permute-start | bytes 368648 | tf_op jit(solution)/shard_map/ppermute | solution.py:164
  77.0 22.8 %collective-permute-start.9 = (bf16[2,48,2048]{2,1,0:T(8,128)(2,1)S(1)}, bf16[2,48,2048]{2,1,0:T(8,128)(2,1)S(1)}, u32[]{:S(2)}, u32[]{:S(2)}) collective-permute-start(bf16[2,48,2048]{2,1,0:T(8,128)(2,1)S(1)} %slice.124), channel_id=1, source_target_pairs={{0,2},{1,3},{2,0},{3,1},{4,6},{5,7},{6,4},{7,5},{8,10},{9,11},{10,... | collective-permute-start | bytes 1179656 | tf_op jit(solution)/shard_map/ppermute | solution.py:167
  91.3 13.8 %collective-permute-start.22 = (bf16[48,1280]{1,0:T(8,128)(2,1)S(1)}, bf16[48,1280]{1,0:T(8,128)(2,1)S(1)}, u32[]{:S(2)}, u32[]{:S(2)}) collective-permute-start(bf16[48,1280]{1,0:T(8,128)(2,1)S(1)} %collective-permute-done.20.refs_1_), channel_id=1, source_target_pairs={{0,1},{1,0},{2,3},{3,2},{4,5},{5,4},{6,7},{7,6},{8,9},{9,8},{10,11... | collective-permute-start | bytes 368648 | tf_op jit(solution)/shard_map/ppermute | solution.py:164
  91.6 11.8 %collective-permute-start.15 = (bf16[48,1792]{1,0:T(8,128)(2,1)S(1)}, bf16[48,1792]{1,0:T(8,128)(2,1)S(1)}, u32[]{:S(2)}, u32[]{:S(2)}) collective-permute-start(bf16[48,1792]{1,0:T(8,128)(2,1)S(1)} %fusion.3.refs_0_), channel_id=1, source_target_pairs={{0,2},{1,3},{2,0},{3,1},{4,6},{5,7},{6,4},{7,5},{8,10},{9,11},{10,... | collective-permute-start | bytes 516104 | tf_op jit(solution)/shard_map/ppermute | solution.py:167
  93.2 18.9 %collective-permute-start.16 = (bf16[48,1792]{1,0:T(8,128)(2,1)S(1)}, bf16[48,1792]{1,0:T(8,128)(2,1)S(1)}, u32[]{:S(2)}, u32[]{:S(2)}) collective-permute-start(bf16[48,1792]{1,0:T(8,128)(2,1)S(1)} %fusion.3.refs_0_), channel_id=1, source_target_pairs={{0,1},{1,0},{2,3},{3,2},{4,5},{5,4},{6,7},{7,6},{8,9},{9,8},{10,11... | collective-permute-start | bytes 516104 | tf_op jit(solution)/shard_map/ppermute | solution.py:164
  103.4 8.7 %collective-permute-start.17 = (bf16[48,1792]{1,0:T(8,128)(2,1)S(1)}, bf16[48,1792]{1,0:T(8,128)(2,1)S(1)}, u32[]{:S(2)}, u32[]{:S(2)}) collective-permute-start(bf16[48,1792]{1,0:T(8,128)(2,1)S(1)} %collective-permute-done.15.refs_1_), channel_id=1, source_target_pairs={{0,1},{1,0},{2,3},{3,2},{4,5},{5,4},{6,7},{7,6},{8,9},{9,8},{10,11... | collective-permute-start | bytes 516104 | tf_op jit(solution)/shard_map/ppermute | solution.py:164
  103.6 7.9 %collective-permute-start.5 = (bf16[48,1536]{1,0:T(8,128)(2,1)S(1)}, bf16[48,1536]{1,0:T(8,128)(2,1)S(1)}, u32[]{:S(2)}, u32[]{:S(2)}) collective-permute-start(bf16[48,1536]{1,0:T(8,128)(2,1)S(1)} %fusion.5.refs_0_), channel_id=1, source_target_pairs={{0,2},{1,3},{2,0},{3,1},{4,6},{5,7},{6,4},{7,5},{8,10},{9,11},{10,... | collective-permute-start | bytes 442376 | tf_op jit(solution)/shard_map/ppermute | solution.py:167
  105.1 12.5 %collective-permute-start.11 = (bf16[48,2048]{1,0:T(8,128)(2,1)S(1)}, bf16[48,2048]{1,0:T(8,128)(2,1)S(1)}, u32[]{:S(2)}, u32[]{:S(2)}) collective-permute-start(bf16[48,2048]{1,0:T(8,128)(2,1)S(1)} %fusion.1.refs_0_), channel_id=1, source_target_pairs={{0,1},{1,0},{2,3},{3,2},{4,5},{5,4},{6,7},{7,6},{8,9},{9,8},{10,11... | collective-permute-start | bytes 589832 | tf_op jit(solution)/shard_map/ppermute | solution.py:164
  106.8 10.8 %collective-permute-start.12 = (bf16[48,2048]{1,0:T(8,128)(2,1)S(1)}, bf16[48,2048]{1,0:T(8,128)(2,1)S(1)}, u32[]{:S(2)}, u32[]{:S(2)}) collective-permute-start(bf16[48,2048]{1,0:T(8,128)(2,1)S(1)} %collective-permute-done.10.refs_1_), channel_id=1, source_target_pairs={{0,1},{1,0},{2,3},{3,2},{4,5},{5,4},{6,7},{7,6},{8,9},{9,8},{10,11... | collective-permute-start | bytes 589832 | tf_op jit(solution)/shard_map/ppermute | solution.py:164
  111.5 12.0 %collective-permute-start.6 = (bf16[48,1536]{1,0:T(8,128)(2,1)S(1)}, bf16[48,1536]{1,0:T(8,128)(2,1)S(1)}, u32[]{:S(2)}, u32[]{:S(2)}) collective-permute-start(bf16[48,1536]{1,0:T(8,128)(2,1)S(1)} %fusion.5.refs_0_), channel_id=1, source_target_pairs={{0,1},{1,0},{2,3},{3,2},{4,5},{5,4},{6,7},{7,6},{8,9},{9,8},{10,11... | collective-permute-start | bytes 442376 | tf_op jit(solution)/shard_map/ppermute | solution.py:164
  112.0 11.4 %collective-permute-start.7 = (bf16[48,1536]{1,0:T(8,128)(2,1)S(1)}, bf16[48,1536]{1,0:T(8,128)(2,1)S(1)}, u32[]{:S(2)}, u32[]{:S(2)}) collective-permute-start(bf16[48,1536]{1,0:T(8,128)(2,1)S(1)} %collective-permute-done.5.refs_1_), channel_id=1, source_target_pairs={{0,1},{1,0},{2,3},{3,2},{4,5},{5,4},{6,7},{7,6},{8,9},{9,8},{10,11... | collective-permute-start | bytes 442376 | tf_op jit(solution)/shard_map/ppermute | solution.py:164
  129.3 11.1 %collective-permute-start.25 = (bf16[64,2048]{1,0:T(8,128)(2,1)S(1)}, bf16[64,2048]{1,0:T(8,128)(2,1)S(1)}, u32[]{:S(2)}, u32[]{:S(2)}) collective-permute-start(bf16[64,2048]{1,0:T(8,128)(2,1)S(1)} %get-tuple-element.28), channel_id=1, source_target_pairs={{0,12},{4,8},{8,4},{12,0},{1,13},{5,9},{9,5},{13,1},{2,14},{6,10},... | collective-permute-start | bytes 786440 | tf_op jit(solution)/shard_map/ppermute | solution.py:161
  131.9 24.8 %collective-permute-start.24 = (bf16[64,2048]{1,0:T(8,128)(2,1)S(1)}, bf16[64,2048]{1,0:T(8,128)(2,1)S(1)}, u32[]{:S(2)}, u32[]{:S(2)}) collective-permute-start(bf16[64,2048]{1,0:T(8,128)(2,1)S(1)} %get-tuple-element.27), channel_id=1, source_target_pairs={{0,8},{4,12},{8,0},{12,4},{1,9},{5,13},{9,1},{13,5},{2,10},{6,14},... | collective-permute-start | bytes 786440 | tf_op jit(solution)/shard_map/ppermute | solution.py:161
  134.9 21.8 %collective-permute-start.23 = (bf16[64,2048]{1,0:T(8,128)(2,1)S(1)}, bf16[64,2048]{1,0:T(8,128)(2,1)S(1)}, u32[]{:S(2)}, u32[]{:S(2)}) collective-permute-start(bf16[64,2048]{1,0:T(8,128)(2,1)S(1)} %get-tuple-element.26), channel_id=1, source_target_pairs={{0,4},{4,0},{8,12},{12,8},{1,5},{5,1},{9,13},{13,9},{2,6},{6,2},{1... | collective-permute-start | bytes 786440 | tf_op jit(solution)/shard_map/ppermute | solution.py:161
  (7 other events, 38.0 us)

commit v2 on v1

v2 whole, which is shorter than its diff:
```python
import functools

import jax
import jax.numpy as jnp
from jax import lax
from jax.experimental import pallas as pl
from jax.experimental.pallas import tpu as pltpu
from jax.sharding import PartitionSpec as P

MIB = 1 << 20
BF16, F32 = jnp.bfloat16, jnp.float32


def row_sources(lengths_ref, rows, n_gx, tok_dev):
    start = jnp.int32(0)
    slot = rows
    for g in range(n_gx):
        slot = jnp.where(rows >= start, rows - start + g * tok_dev, slot)
        start = start + lengths_ref[g]
    return slot


def local_rows(shape, dim, quarter, nx):
    gy = lax.axis_index("gy")
    x, core = gy // 2, gy % 2
    j = lax.broadcasted_iota(jnp.int32, shape, dim)
    rows = jnp.zeros(shape, jnp.int32)
    for kc in range(2):
        for kx in range(nx):
            first = (kc * nx + kx) * quarter
            owner = lax.rem(x + kx, nx) * 2 + (1 - core if kc else core)
            rows = jnp.where(j >= first, owner * quarter + j - first, rows)
    return rows


def picks_kernel(n_gx, nx, tok_dev, lengths_ref, in_ref, out_ref):
    z = lax.axis_index("gx")
    live, slots = in_ref.shape
    quarter = live // (2 * nx)

    def slot_of(column):
        return (z ^ (column // tok_dev)) * tok_dev + column % tok_dev

    shape = (live, slots)
    source = row_sources(lengths_ref, local_rows(shape, 0, quarter, nx), n_gx, tok_dev)
    in_ref[...] = (source == slot_of(lax.broadcasted_iota(jnp.int32, shape, 1))).astype(F32).astype(BF16)
    shape = (slots, live)
    source = row_sources(lengths_ref, local_rows(shape, 1, quarter, nx), n_gx, tok_dev)
    out_ref[...] = (source == slot_of(lax.broadcasted_iota(jnp.int32, shape, 0))).astype(F32).astype(BF16)


def picks(lengths, n_gx, nx, tok_dev, live):
    slots = n_gx * tok_dev
    return pl.pallas_call(
        functools.partial(picks_kernel, n_gx, nx, tok_dev),
        out_shape=[jax.ShapeDtypeStruct((live, slots), BF16), jax.ShapeDtypeStruct((slots, live), BF16)],
        in_specs=[pl.BlockSpec(memory_space=pltpu.SMEM)],
        cost_estimate=pl.CostEstimate(flops=0, bytes_accessed=4 * live * slots, transcendentals=0),
        name="picks",
    )(lengths)


def compact_kernel(groups, pick_ref, *refs):
    refs, out_ref = list(refs[:-1]), refs[-1]
    blocks = []
    for n in groups:
        block = refs.pop(0)[...]
        for _ in range(n - 1):
            block = block + refs.pop(0)[...]
        blocks.append(block)
    rows = jnp.concatenate(blocks, axis=0)
    out_ref[...] = jnp.dot(pick_ref[...], rows, preferred_element_type=F32).astype(BF16)


def compact(pick, blocks):
    flat = [b for group in blocks for b in group]
    return pl.pallas_call(
        functools.partial(compact_kernel, [len(group) for group in blocks]),
        out_shape=jax.ShapeDtypeStruct((pick.shape[0], flat[0].shape[1]), BF16),
        cost_estimate=pl.CostEstimate(
            flops=2 * pick.size * flat[0].shape[1], bytes_accessed=2 * pick.size, transcendentals=0
        ),
        name="compact",
    )(pick, *flat)


def gate_up_kernel(tok_ref, gate_ref, up_ref, *refs):
    send_ref, keep_ref = refs[-2:]
    half = keep_ref.shape[1]
    rows = tok_ref[...]
    for i, w_ref in enumerate((gate_ref, up_ref)):
        part = jnp.dot(rows, w_ref[...], preferred_element_type=F32)
        keep_ref[i] = part[:half]
        send_ref[i] = part[half:].astype(BF16)


def gate_up(tok, gate_weight, up_weight, after, start, width, tile):
    live, depth = tok.shape
    half = live // 2
    weight = pl.BlockSpec((depth, tile), lambda j: (0, start // tile + j))
    out = pl.BlockSpec((2, half, tile), lambda j: (0, 0, j))
    return pl.pallas_call(
        gate_up_kernel,
        out_shape=[jax.ShapeDtypeStruct((2, half, width), BF16), jax.ShapeDtypeStruct((2, half, width), F32)],
        grid=(width // tile,),
        in_specs=[pl.BlockSpec((live, depth), lambda j: (0, 0)), weight, weight]
        + [pl.BlockSpec(memory_space=pl.ANY)] * len(after),
        out_specs=[out, out],
        compiler_params=pltpu.CompilerParams(vmem_limit_bytes=32 * MIB),
        cost_estimate=pl.CostEstimate(
            flops=0, bytes_accessed=0, transcendentals=0
        ),
        name="gate_up",
    )(tok, gate_weight, up_weight, *after)


def down_kernel(n_h, first, last, *refs):
    h_refs, w_ref, refs = refs[:n_h], refs[n_h], refs[n_h + 1:]
    h = jnp.concatenate([r[...] for r in h_refs], axis=0)
    total = jnp.dot(h, w_ref[...], preferred_element_type=F32)
    if not first:
        total += refs[0][...]
        refs = refs[1:]
    if not last:
        refs[0][...] = total
        return
    pick_ref, outs = refs[0], refs[1:]
    spread = jnp.dot(pick_ref[...], total.astype(BF16), preferred_element_type=F32).astype(BF16)
    rows = spread.shape[0] // len(outs)
    for k, out_ref in enumerate(outs):
        out_ref[...] = spread[k * rows:(k + 1) * rows]


def down(hidden, down_weight, total, pick, start, width, n_gx):
    live = sum(h.shape[0] for h in hidden)
    out_width = down_weight.shape[1]
    tile = min(out_width, 512)
    last = pick is not None
    rows = pl.BlockSpec((live, tile), lambda j: (0, j))
    operands = [*hidden, down_weight]
    in_specs = [pl.BlockSpec(h.shape, lambda j: (0, 0)) for h in hidden]
    in_specs.append(pl.BlockSpec((pl.Element(width), pl.Element(tile)), lambda j: (start, j * tile)))
    if total is not None:
        operands.append(total)
        in_specs.append(rows)
    if last:
        tok_dev = pick.shape[0] // n_gx
        operands.append(pick)
        in_specs.append(pl.BlockSpec(pick.shape, lambda j: (0, 0)))
        out_shape = [jax.ShapeDtypeStruct((tok_dev, out_width), BF16)] * n_gx
        out_specs = [pl.BlockSpec((tok_dev, tile), lambda j: (0, j))] * n_gx
    else:
        out_shape, out_specs = jax.ShapeDtypeStruct((live, out_width), F32), rows
    return pl.pallas_call(
        functools.partial(down_kernel, len(hidden), total is None, last),
        out_shape=out_shape,
        grid=(out_width // tile,),
        in_specs=in_specs,
        out_specs=out_specs,
        compiler_params=pltpu.CompilerParams(vmem_limit_bytes=32 * MIB),
        cost_estimate=pl.CostEstimate(
            flops=0, bytes_accessed=0, transcendentals=0
        ),
        name="down",
    )(*operands)


def column_chunks(cols, tile):
    tiles = cols // tile
    shares = (3, 5, 5)
    edges = [round(tiles * sum(shares[:i]) / sum(shares)) for i in range(len(shares) + 1)]
    return [(a * tile, (b - a) * tile) for a, b in zip(edges, edges[1:]) if b > a]


def local(n_gx, n_gy, tokens, gate_weight, up_weight, down_weight, lengths):
    nx = n_gy // 2
    tok_dev = tokens.shape[0]
    live = 3 * tok_dev * n_gx // 4
    quarter = live // n_gy
    cols = gate_weight.shape[1]
    tile = 512 if cols % 512 == 0 else 128
    chunks = column_chunks(cols, tile)

    def over_z(block, k, among=range(n_gx)):
        return lax.ppermute(block, "gx", [(z, z ^ k) for z in among])

    def over_core(block):
        return lax.ppermute(block, "gy", [(i, i ^ 1) for i in range(n_gy)])

    def over_x(block, k):
        return lax.ppermute(block, "gy", [(i, (i + 2 * k) % n_gy) for i in range(n_gy)])

    pick_in, pick_out = picks(lengths, n_gx, nx, tok_dev, live)
    if n_gx == 4:
        two = over_z(tokens, 2)
        one = over_z(tokens, 1)
        middle = over_z(tokens, 3, (1, 2))
        ends = over_z(two, 1, (1, 2))
        blocks = [[tokens], [one], [two], [middle, ends]]
    else:
        blocks = [[tokens]] + [[over_z(tokens, k)] for k in range(1, n_gx)]
    tok = compact(pick_in, blocks)

    total, after = None, []
    for i, (start, width) in enumerate(chunks):
        send, keep = gate_up(tok, gate_weight, up_weight, after, start, width, tile)
        sums = keep + over_core(send).astype(F32)
        mine = sums[:, :quarter]
        after = []
        for k in range(1, nx):
            block = sums[:, k * quarter:(k + 1) * quarter].astype(BF16)
            after.append(block)
            mine = mine + over_x(block, k).astype(F32)
        own = (jax.nn.silu(mine[0]) * mine[1]).astype(BF16)
        hidden = [own] + [over_x(own, -k) for k in range(1, nx)]
        hidden += [over_core(h) for h in hidden]
        last = i == len(chunks) - 1
        total = down(hidden, down_weight, total, pick_out if last else None, start, width, n_gx)

    if n_gx == 4:
        ends = over_z(total[3], 1, (0, 3))
        one = over_z(total[1], 1)
        middle = over_z(total[3], 3, (1, 2))
        two = over_z((total[2].astype(F32) + ends.astype(F32)).astype(BF16), 2)
        parts = [total[0], one, middle, two]
    else:
        parts = [total[0]] + [over_z(total[k], k) for k in range(1, n_gx)]
    return sum(p.astype(F32) for p in parts).astype(BF16)


def solution(mesh):
    placed = (P(("group", "gx"), "gy"), P("gy", "gx"), P("gy", "gx"), P("gx", "gy"), P("group"))
    return jax.shard_map(
        functools.partial(local, mesh.shape["gx"], mesh.shape["gy"]),
        mesh=mesh, in_specs=placed, out_specs=P(("group", "gx"), "gy"), check_vma=False,
    )
```

time: 158 us -> 140 us (0.89)
  Pallas kernels: 59.4 us -> 47.6 us
  waiting for transfers between devices: 69 us -> 59.8 us
  starting transfers between devices: 24.1 us -> 27.6 us
    ppermute x6 -> x8, waiting for transfers between devices: 40.7 us -> 29.3 us  [over_z(): return lax.ppermute(block, 'gx', [(z, z ^ k) for z in among])]
    ppermute x6 -> x8, starting transfers between devices: 11.3 us -> 19 us  [over_z(): return lax.ppermute(block, 'gx', [(z, z ^ k) for z in among])]
    pallas_call x4 -> x3, Pallas kernels: 32.9 us -> 26.6 us  [gate_up(): pl.pallas_call(gate_up_kernel, out_shape=[jax.ShapeDtypeStruct((2, half,...]
    pallas_call x5, Pallas kernels: 26.5 us -> 21 us  [the longest x3 17 us: down(): pl.pallas_call(functools.partial(down_kernel, len(hidden), total is None,...]
    ppermute x12 -> x9, waiting for transfers between devices: 0.33 us -> 4.24 us  [over_core(): return lax.ppermute(block, 'gy', [(i, i ^ 1) for i in range(n_gy)])]
    ppermute x8 -> x6, starting transfers between devices: 10.6 us -> 7.51 us  [over_x(): lax.ppermute(block, 'gy', [(i, (i + 2 * k) % n_gy) for i in range(n_gy)])]
    ppermute x8 -> x6, waiting for transfers between devices: 28 us -> 26.2 us  [over_x(): lax.ppermute(block, 'gy', [(i, (i + 2 * k) % n_gy) for i in range(n_gy)])]
  transfers between devices with their start and end apart: 26 -> 23, of which waited for: 10 -> 13; matrix products, arithmetic and copies ran while one was open for 1% -> 1% of each run, Pallas kernels for 22% -> 16%
where the time goes in v2:
time: 140 us; the launch traced here: 139 us
  waiting for transfers between devices  59.8 us (43%)
  Pallas kernels  47.6 us (34%)
  starting transfers between devices  27.6 us (20%)
  other arithmetic  2.11 us (2%)
  local copies, waits for them, and re-layouts  1.97 us (1%)
    ppermute x8, waiting for transfers between devices, over_z(): return lax.ppermute(block, 'gx', [(z, z ^ k) for z in among])  29.3 us
    pallas_call x3, Pallas kernels, gate_up(): pl.pallas_call(gate_up_kernel, out_shape=[jax.ShapeDtypeStruct((2, half,...  26.6 us
    ppermute x6, waiting for transfers between devices, over_x(): lax.ppermute(block, 'gy', [(i, (i + 2 * k) % n_gy) for i in range(n_gy)])  26.2 us
    ppermute x8, starting transfers between devices, over_z(): return lax.ppermute(block, 'gx', [(z, z ^ k) for z in among])  19 us
    pallas_call x3, Pallas kernels, down(): pl.pallas_call(functools.partial(down_kernel, len(hidden), total is None,...  17 us
    ppermute x6, starting transfers between devices, over_x(): lax.ppermute(block, 'gy', [(i, (i + 2 * k) % n_gy) for i in range(n_gy)])  7.51 us
    ppermute x9, waiting for transfers between devices, over_core(): return lax.ppermute(block, 'gy', [(i, i ^ 1) for i in range(n_gy)])  4.24 us
  transfers between devices with their start and end apart: 23, of which 13 were waited for; matrix products, arithmetic and copies ran while one was open for 1% of the time, Pallas kernels for 16%

profile of v2, /device:TPU:0, one launch (start us, length us, event | category | flops | bytes accessed | tf_op | source)
XLA Modules:
  0.0 139.4 jit_solution(8045378146990247201)
XLA Ops:
  0.0 4.0 %collective-permute-start.1 = (bf16[64,2048]{1,0:T(8,128)(2,1)}, bf16[64,2048]{1,0:T(8,128)(2,1)S(1)}, u32[]{:S(2)}, u32[]{:S(2)}) collective-permute-start(bf16[64,2048]{1,0:T(8,128)(2,1)} %refs_0_.1), channel_id=1, source_target_pairs={{0,8},{4,12},{8,0},{12,4},{1,9},{5,13},{9,1},{13,5},{2,10},{6,14},... | collective-permute-start | bytes 786440 | tf_op jit(solution)/shard_map/ppermute | solution.py:185
  4.0 1.6 %collective-permute-start = (bf16[64,2048]{1,0:T(8,128)(2,1)}, bf16[64,2048]{1,0:T(8,128)(2,1)S(1)}, u32[]{:S(2)}, u32[]{:S(2)}) collective-permute-start(bf16[64,2048]{1,0:T(8,128)(2,1)} %refs_0_.1), channel_id=1, source_target_pairs={{0,4},{4,0},{8,12},{12,8},{1,5},{5,1},{9,13},{13,9},{2,6},{6,2},{1... | collective-permute-start | bytes 786440 | tf_op jit(solution)/shard_map/ppermute | solution.py:185
  6.3 10.8 %collective-permute-done.1.refs_2_ = bf16[64,2048]{1,0:T(8,128)(2,1)S(1)} collective-permute-done((bf16[64,2048]{1,0:T(8,128)(2,1)}, bf16[64,2048]{1,0:T(8,128)(2,1)S(1)}, u32[]{:S(2)}, u32[]{:S(2)}) %collective-permute-start.1) | collective-permute-done | bytes 262176 | tf_op jit(solution)/shard_map/ppermute | solution.py:185
  19.8 5.8 %collective-permute-done.3.refs_4_ = bf16[64,2048]{1,0:T(8,128)(2,1)S(1)} collective-permute-done((bf16[64,2048]{1,0:T(8,128)(2,1)S(1)}, bf16[64,2048]{1,0:T(8,128)(2,1)S(1)}, u32[]{:S(2)}, u32[]{:S(2)}) %collective-permute-start.3) | collective-permute-done | bytes 262176 | tf_op jit(solution)/shard_map/ppermute | solution.py:185
  26.3 2.6 %compact.1.tok_ref = bf16[192,2048]{1,0:T(8,128)(2,1)} custom-call(bf16[192,256]{1,0:T(8,128)(2,1)} %get-tuple-element.17.pick_ref, bf16[64,2048]{1,0:T(8,128)(2,1)} %refs_0_.1, bf16[64,2048]{1,0:T(8,128)(2,1)} %copy-done.3, bf16[64,2048]{1,0:T(8,128)(2,1)} %copy-done.2, bf16[64,2048]{1,0:T(8,128)(2,1)} %copy-done.4, bf16[64,2048]{1,0:T(8,128)(2,1)} %copy-done.5), custom_call_target="tpu_custom_call" | custom-call | flops 201326592 | bytes 98304 | tf_op jit(solution)/shard_map/compact/pallas_call | solution.py:77
  30.0 6.6 %gate_up.3 = (bf16[2,96,1536]{2,1,0:T(8,128)(2,1)S(1)}, f32[2,96,1536]{2,1,0:T(8,128)S(1)}) custom-call(bf16[192,2048]{1,0:T(8,128)(2,1)S(1)} %copy-done, bf16[2048,6656]{1,0:T(8,128)(2,1)} %gate_ref.5, bf16[2048,6656]{1,0:T(8,128)(2,1)} %up_ref.5), custom_call_target="tpu_custom_call" | custom-call | tf_op jit(solution)/shard_map/gate_up/pallas_call | solution.py:102
  36.7 2.0 %collective-permute-done.4 = bf16[2,96,1536]{2,1,0:T(8,128)(2,1)S(1)} collective-permute-done((bf16[2,96,1536]{2,1,0:T(8,128)(2,1)S(1)}, bf16[2,96,1536]{2,1,0:T(8,128)(2,1)S(1)}, u32[]{:S(2)}, u32[]{:S(2)}) %collective-permute-start.4) | collective-permute-done | bytes 589856 | tf_op jit(solution)/shard_map/ppermute | solution.py:188
  38.9 10.0 %gate_up.4 = (bf16[2,96,2560]{2,1,0:T(8,128)(2,1)S(1)}, f32[2,96,2560]{2,1,0:T(8,128)S(1)}) custom-call(bf16[192,2048]{1,0:T(8,128)(2,1)S(1)} %copy-done, bf16[2048,6656]{1,0:T(8,128)(2,1)} %gate_ref.5, bf16[2048,6656]{1,0:T(8,128)(2,1)} %up_ref.5, bf16[2,48,1536]{2,1,0:T(8,128)(2,1)S(1)} %slice.95.refs_0_), custom_call_target="tpu_custom_call" | custom-call | tf_op jit(solution)/shard_map/gate_up/pallas_call | solution.py:102
  51.8 1.6 %collective-permute-start.11 = (bf16[2,48,2560]{2,1,0:T(8,128)(2,1)S(1)}, bf16[2,48,2560]{2,1,0:T(8,128)(2,1)S(1)}, u32[]{:S(2)}, u32[]{:S(2)}) collective-permute-start(bf16[2,48,2560]{2,1,0:T(8,128)(2,1)S(1)} %slice.94.refs_0_), channel_id=1, source_target_pairs={{0,2},{1,3},{2,0},{3,1},{4,6},{5,7},{6,4},{7,5},{8,10},{9,11},{10,... | collective-permute-start | bytes 1474568 | tf_op jit(solution)/shard_map/ppermute | solution.py:191
  53.5 10.0 %gate_up.5 = (bf16[2,96,2560]{2,1,0:T(8,128)(2,1)S(1)}, f32[2,96,2560]{2,1,0:T(8,128)S(1)}) custom-call(bf16[192,2048]{1,0:T(8,128)(2,1)S(1)} %copy-done, bf16[2048,6656]{1,0:T(8,128)(2,1)} %gate_ref.5, bf16[2048,6656]{1,0:T(8,128)(2,1)} %up_ref.5, bf16[2,48,2560]{2,1,0:T(8,128)(2,1)S(1)} %slice.94.refs_0_), custom_call_target="tpu_custom_call" | custom-call | tf_op jit(solution)/shard_map/gate_up/pallas_call | solution.py:102
  63.6 5.3 %collective-permute-done.11 = bf16[2,48,2560]{2,1,0:T(8,128)(2,1)S(1)} collective-permute-done((bf16[2,48,2560]{2,1,0:T(8,128)(2,1)S(1)}, bf16[2,48,2560]{2,1,0:T(8,128)(2,1)S(1)}, u32[]{:S(2)}, u32[]{:S(2)}) %collective-permute-start.11) | collective-permute-done | bytes 491552 | tf_op jit(solution)/shard_map/ppermute | solution.py:191
  69.3 1.6 %collective-permute-start.7 = (bf16[2,48,2560]{2,1,0:T(8,128)(2,1)S(1)}, bf16[2,48,2560]{2,1,0:T(8,128)(2,1)S(1)}, u32[]{:S(2)}, u32[]{:S(2)}) collective-permute-start(bf16[2,48,2560]{2,1,0:T(8,128)(2,1)S(1)} %slice.93), channel_id=1, source_target_pairs={{0,2},{1,3},{2,0},{3,1},{4,6},{5,7},{6,4},{7,5},{8,10},{9,11},{10,... | collective-permute-start | bytes 1474568 | tf_op jit(solution)/shard_map/ppermute | solution.py:191
  71.6 11.9 %collective-permute-done.7 = bf16[2,48,2560]{2,1,0:T(8,128)(2,1)S(1)} collective-permute-done((bf16[2,48,2560]{2,1,0:T(8,128)(2,1)S(1)}, bf16[2,48,2560]{2,1,0:T(8,128)(2,1)S(1)}, u32[]{:S(2)}, u32[]{:S(2)}) %collective-permute-start.7) | collective-permute-done | bytes 491552 | tf_op jit(solution)/shard_map/ppermute | solution.py:191
  83.8 1.6 %collective-permute-start.8 = (bf16[48,2560]{1,0:T(8,128)(2,1)S(1)}, bf16[48,2560]{1,0:T(8,128)(2,1)S(1)}, u32[]{:S(2)}, u32[]{:S(2)}) collective-permute-start(bf16[48,2560]{1,0:T(8,128)(2,1)S(1)} %fusion.3.refs_0_), channel_id=1, source_target_pairs={{0,2},{1,3},{2,0},{3,1},{4,6},{5,7},{6,4},{7,5},{8,10},{9,11},{10,... | collective-permute-start | bytes 737288 | tf_op jit(solution)/shard_map/ppermute | solution.py:191
  86.3 2.5 %collective-permute-done.12.refs_1_ = bf16[48,2560]{1,0:T(8,128)(2,1)S(1)} collective-permute-done((bf16[48,2560]{1,0:T(8,128)(2,1)S(1)}, bf16[48,2560]{1,0:T(8,128)(2,1)S(1)}, u32[]{:S(2)}, u32[]{:S(2)}) %collective-permute-start.12) | collective-permute-done | bytes 245792 | tf_op jit(solution)/shard_map/ppermute | solution.py:191
  89.3 4.8 %collective-permute-done.8.refs_1_ = bf16[48,2560]{1,0:T(8,128)(2,1)S(1)} collective-permute-done((bf16[48,2560]{1,0:T(8,128)(2,1)S(1)}, bf16[48,2560]{1,0:T(8,128)(2,1)S(1)}, u32[]{:S(2)}, u32[]{:S(2)}) %collective-permute-start.8) | collective-permute-done | bytes 245792 | tf_op jit(solution)/shard_map/ppermute | solution.py:191
  94.1 1.7 %collective-permute-done.16.refs_1_ = bf16[48,1536]{1,0:T(8,128)(2,1)S(1)} collective-permute-done((bf16[48,1536]{1,0:T(8,128)(2,1)S(1)}, bf16[48,1536]{1,0:T(8,128)(2,1)S(1)}, u32[]{:S(2)}, u32[]{:S(2)}) %collective-permute-start.16) | collective-permute-done | bytes 147488 | tf_op jit(solution)/shard_map/ppermute | solution.py:191
  97.1 4.5 %down.3.refs_5_ = f32[192,2048]{1,0:T(8,128)S(1)} custom-call(bf16[48,1536]{1,0:T(8,128)(2,1)S(1)} %fusion.5.refs_0_, bf16[48,1536]{1,0:T(8,128)(2,1)S(1)} %collective-permute-done.16.refs_1_, bf16[48,1536]{1,0:T(8,128)(2,1)S(1)} %collective-permute-done.17.refs_2_, bf16[48,1536]{1,0:T(8,128)(2,1)S(1)} %collective-permute-done.18.refs_3_, ...), custom_call_target="tpu_custom_call" | custom-call | tf_op jit(solution)/shard_map/down/pallas_call | solution.py:154
  101.7 6.0 %down.4.refs_5_ = f32[192,2048]{1,0:T(8,128)S(1)} custom-call(bf16[48,2560]{1,0:T(8,128)(2,1)S(1)} %fusion.1.refs_0_, bf16[48,2560]{1,0:T(8,128)(2,1)S(1)} %collective-permute-done.12.refs_1_, bf16[48,2560]{1,0:T(8,128)(2,1)S(1)} %collective-permute-done.13.refs_2_, bf16[48,2560]{1,0:T(8,128)(2,1)S(1)} %collective-permute-done.14.refs_3_, ...), custom_call_target="tpu_custom_call" | custom-call | tf_op jit(solution)/shard_map/down/pallas_call | solution.py:154
  107.7 6.5 %down.5 = (bf16[64,2048]{1,0:T(8,128)(2,1)S(1)}, bf16[64,2048]{1,0:T(8,128)(2,1)S(1)}, bf16[64,2048]{1,0:T(8,128)(2,1)S(1)}, bf16[64,2048]{1,0:T(8,128)(2,1)S(1)}) custom-call(bf16[48,2560]{1,0:T(8,128)(2,1)S(1)} %fusion.3.refs_0_, bf16[48,2560]{1,0:T(8,128)(2,1)S(1)} %collective-permute-done.8.refs_1_, bf16[48,2560]{1,0:T(8,128)(2,1)S(1)} %collective-permute-done.9.refs_2_, ...), custom_call_target="tpu_custom_call" | custom-call | tf_op jit(solution)/shard_map/down/pallas_call | solution.py:154
  116.3 4.0 %collective-permute-start.19 = (bf16[64,2048]{1,0:T(8,128)(2,1)S(1)}, bf16[64,2048]{1,0:T(8,128)(2,1)S(1)}, u32[]{:S(2)}, u32[]{:S(2)}) collective-permute-start(bf16[64,2048]{1,0:T(8,128)(2,1)S(1)} %get-tuple-element.26), channel_id=1, source_target_pairs={{0,4},{4,0},{8,12},{12,8},{1,5},{5,1},{9,13},{13,9},{2,6},{6,2},{1... | collective-permute-start | bytes 786440 | tf_op jit(solution)/shard_map/ppermute | solution.py:185
  120.4 1.9 %collective-permute-done.21 = bf16[64,2048]{1,0:T(8,128)(2,1)S(1)} collective-permute-done((bf16[64,2048]{1,0:T(8,128)(2,1)S(1)}, bf16[64,2048]{1,0:T(8,128)(2,1)S(1)}, u32[]{:S(2)}, u32[]{:S(2)}) %collective-permute-start.21) | collective-permute-done | bytes 262176 | tf_op jit(solution)/shard_map/ppermute | solution.py:185
  122.4 5.3 %collective-permute-start.22 = (bf16[64,2048]{1,0:T(8,128)(2,1)S(1)}, bf16[64,2048]{1,0:T(8,128)(2,1)S(1)}, u32[]{:S(2)}, u32[]{:S(2)}) collective-permute-start(bf16[64,2048]{1,0:T(8,128)(2,1)S(1)} %add_convert_fusion.1), channel_id=1, source_target_pairs={{0,8},{4,12},{8,0},{12,4},{1,9},{5,13},{9,1},{13,5},{2,10},{6,14},... | collective-permute-start | bytes 786440 | tf_op jit(solution)/shard_map/ppermute | solution.py:185
  127.8 10.7 %collective-permute-done.22 = bf16[64,2048]{1,0:T(8,128)(2,1)S(1)} collective-permute-done((bf16[64,2048]{1,0:T(8,128)(2,1)S(1)}, bf16[64,2048]{1,0:T(8,128)(2,1)S(1)}, u32[]{:S(2)}, u32[]{:S(2)}) %collective-permute-start.22) | collective-permute-done | bytes 262176 | tf_op jit(solution)/shard_map/ppermute | solution.py:185
  (56 shorter events, 15.8 us)
Async XLA Ops:
  0.0 17.0 %collective-permute-start.1 = (bf16[64,2048]{1,0:T(8,128)(2,1)}, bf16[64,2048]{1,0:T(8,128)(2,1)S(1)}, u32[]{:S(2)}, u32[]{:S(2)}) collective-permute-start(bf16[64,2048]{1,0:T(8,128)(2,1)} %refs_0_.1), channel_id=1, source_target_pairs={{0,8},{4,12},{8,0},{12,4},{1,9},{5,13},{9,1},{13,5},{2,10},{6,14},... | collective-permute-start | bytes 786440 | tf_op jit(solution)/shard_map/ppermute | solution.py:185
  4.0 15.8 %collective-permute-start = (bf16[64,2048]{1,0:T(8,128)(2,1)}, bf16[64,2048]{1,0:T(8,128)(2,1)S(1)}, u32[]{:S(2)}, u32[]{:S(2)}) collective-permute-start(bf16[64,2048]{1,0:T(8,128)(2,1)} %refs_0_.1), channel_id=1, source_target_pairs={{0,4},{4,0},{8,12},{12,8},{1,5},{5,1},{9,13},{13,9},{2,6},{6,2},{1... | collective-permute-start | bytes 786440 | tf_op jit(solution)/shard_map/ppermute | solution.py:185
  5.6 14.2 %collective-permute-start.2 = (bf16[64,2048]{1,0:T(8,128)(2,1)}, bf16[64,2048]{1,0:T(8,128)(2,1)S(1)}, u32[]{:S(2)}, u32[]{:S(2)}) collective-permute-start(bf16[64,2048]{1,0:T(8,128)(2,1)} %refs_0_.1), channel_id=1, source_target_pairs={{4,8},{8,4},{5,9},{9,5},{6,10},{10,6},{7,11},{11,7},{20,24},{24,20... | collective-permute-start | bytes 786440 | tf_op jit(solution)/shard_map/ppermute | solution.py:185
  17.0 8.6 %copy-start.2 = (bf16[64,2048]{1,0:T(8,128)(2,1)}, bf16[64,2048]{1,0:T(8,128)(2,1)S(1)}, u32[]{:S(2)}) copy-start(bf16[64,2048]{1,0:T(8,128)(2,1)S(1)} %collective-permute-done.1.refs_2_) | copy-start | bytes 786436
  17.0 8.5 %collective-permute-start.3 = (bf16[64,2048]{1,0:T(8,128)(2,1)S(1)}, bf16[64,2048]{1,0:T(8,128)(2,1)S(1)}, u32[]{:S(2)}, u32[]{:S(2)}) collective-permute-start(bf16[64,2048]{1,0:T(8,128)(2,1)S(1)} %collective-permute-done.1.refs_2_), channel_id=1, source_target_pairs={{4,0},{8,12},{5,1},{9,13},{6,2},{10,14},{7,3},{11,15},{20,16},{24,... | collective-permute-start | bytes 786440 | tf_op jit(solution)/shard_map/ppermute | solution.py:185
  36.6 2.1 %collective-permute-start.4 = (bf16[2,96,1536]{2,1,0:T(8,128)(2,1)S(1)}, bf16[2,96,1536]{2,1,0:T(8,128)(2,1)S(1)}, u32[]{:S(2)}, u32[]{:S(2)}) collective-permute-start(bf16[2,96,1536]{2,1,0:T(8,128)(2,1)S(1)} %get-tuple-element.19), channel_id=1, source_target_pairs={{0,1},{1,0},{2,3},{3,2},{4,5},{5,4},{6,7},{7,6},{8,9},{9,8},{10,11... | collective-permute-start | bytes 1769480 | tf_op jit(solution)/shard_map/ppermute | solution.py:188
  48.9 2.6 %collective-permute-start.5 = (bf16[2,96,2560]{2,1,0:T(8,128)(2,1)S(1)}, bf16[2,96,2560]{2,1,0:T(8,128)(2,1)S(1)}, u32[]{:S(2)}, u32[]{:S(2)}) collective-permute-start(bf16[2,96,2560]{2,1,0:T(8,128)(2,1)S(1)} %get-tuple-element.21), channel_id=1, source_target_pairs={{0,1},{1,0},{2,3},{3,2},{4,5},{5,4},{6,7},{7,6},{8,9},{9,8},{10,11... | collective-permute-start | bytes 2949128 | tf_op jit(solution)/shard_map/ppermute | solution.py:188
  49.1 14.4 %collective-permute-start.15 = (bf16[2,48,1536]{2,1,0:T(8,128)(2,1)S(1)}, bf16[2,48,1536]{2,1,0:T(8,128)(2,1)S(1)}, u32[]{:S(2)}, u32[]{:S(2)}) collective-permute-start(bf16[2,48,1536]{2,1,0:T(8,128)(2,1)S(1)} %slice.95.refs_0_), channel_id=1, source_target_pairs={{0,2},{1,3},{2,0},{3,1},{4,6},{5,7},{6,4},{7,5},{8,10},{9,11},{10,... | collective-permute-start | bytes 884744 | tf_op jit(solution)/shard_map/ppermute | solution.py:191
  51.8 17.1 %collective-permute-start.11 = (bf16[2,48,2560]{2,1,0:T(8,128)(2,1)S(1)}, bf16[2,48,2560]{2,1,0:T(8,128)(2,1)S(1)}, u32[]{:S(2)}, u32[]{:S(2)}) collective-permute-start(bf16[2,48,2560]{2,1,0:T(8,128)(2,1)S(1)} %slice.94.refs_0_), channel_id=1, source_target_pairs={{0,2},{1,3},{2,0},{3,1},{4,6},{5,7},{6,4},{7,5},{8,10},{9,11},{10,... | collective-permute-start | bytes 1474568 | tf_op jit(solution)/shard_map/ppermute | solution.py:191
  63.5 5.6 %collective-permute-start.6 = (bf16[2,96,2560]{2,1,0:T(8,128)(2,1)S(1)}, bf16[2,96,2560]{2,1,0:T(8,128)(2,1)S(1)}, u32[]{:S(2)}, u32[]{:S(2)}) collective-permute-start(bf16[2,96,2560]{2,1,0:T(8,128)(2,1)S(1)} %get-tuple-element.23), channel_id=1, source_target_pairs={{0,1},{1,0},{2,3},{3,2},{4,5},{5,4},{6,7},{7,6},{8,9},{9,8},{10,11... | collective-permute-start | bytes 2949128 | tf_op jit(solution)/shard_map/ppermute | solution.py:188
  69.3 14.2 %collective-permute-start.7 = (bf16[2,48,2560]{2,1,0:T(8,128)(2,1)S(1)}, bf16[2,48,2560]{2,1,0:T(8,128)(2,1)S(1)}, u32[]{:S(2)}, u32[]{:S(2)}) collective-permute-start(bf16[2,48,2560]{2,1,0:T(8,128)(2,1)S(1)} %slice.93), channel_id=1, source_target_pairs={{0,2},{1,3},{2,0},{3,1},{4,6},{5,7},{6,4},{7,5},{8,10},{9,11},{10,... | collective-permute-start | bytes 1474568 | tf_op jit(solution)/shard_map/ppermute | solution.py:191
  71.1 17.7 %collective-permute-start.12 = (bf16[48,2560]{1,0:T(8,128)(2,1)S(1)}, bf16[48,2560]{1,0:T(8,128)(2,1)S(1)}, u32[]{:S(2)}, u32[]{:S(2)}) collective-permute-start(bf16[48,2560]{1,0:T(8,128)(2,1)S(1)} %fusion.1.refs_0_), channel_id=1, source_target_pairs={{0,2},{1,3},{2,0},{3,1},{4,6},{5,7},{6,4},{7,5},{8,10},{9,11},{10,... | collective-permute-start | bytes 737288 | tf_op jit(solution)/shard_map/ppermute | solution.py:191
  83.8 10.3 %collective-permute-start.8 = (bf16[48,2560]{1,0:T(8,128)(2,1)S(1)}, bf16[48,2560]{1,0:T(8,128)(2,1)S(1)}, u32[]{:S(2)}, u32[]{:S(2)}) collective-permute-start(bf16[48,2560]{1,0:T(8,128)(2,1)S(1)} %fusion.3.refs_0_), channel_id=1, source_target_pairs={{0,2},{1,3},{2,0},{3,1},{4,6},{5,7},{6,4},{7,5},{8,10},{9,11},{10,... | collective-permute-start | bytes 737288 | tf_op jit(solution)/shard_map/ppermute | solution.py:191
  85.5 3.3 %collective-permute-start.17 = (bf16[48,1536]{1,0:T(8,128)(2,1)S(1)}, bf16[48,1536]{1,0:T(8,128)(2,1)S(1)}, u32[]{:S(2)}, u32[]{:S(2)}) collective-permute-start(bf16[48,1536]{1,0:T(8,128)(2,1)S(1)} %fusion.5.refs_0_), channel_id=1, source_target_pairs={{0,1},{1,0},{2,3},{3,2},{4,5},{5,4},{6,7},{7,6},{8,9},{9,8},{10,11... | collective-permute-start | bytes 442376 | tf_op jit(solution)/shard_map/ppermute | solution.py:188
  85.6 10.2 %collective-permute-start.16 = (bf16[48,1536]{1,0:T(8,128)(2,1)S(1)}, bf16[48,1536]{1,0:T(8,128)(2,1)S(1)}, u32[]{:S(2)}, u32[]{:S(2)}) collective-permute-start(bf16[48,1536]{1,0:T(8,128)(2,1)S(1)} %fusion.5.refs_0_), channel_id=1, source_target_pairs={{0,2},{1,3},{2,0},{3,1},{4,6},{5,7},{6,4},{7,5},{8,10},{9,11},{10,... | collective-permute-start | bytes 442376 | tf_op jit(solution)/shard_map/ppermute | solution.py:191
  86.1 15.5 %collective-permute-start.13 = (bf16[48,2560]{1,0:T(8,128)(2,1)S(1)}, bf16[48,2560]{1,0:T(8,128)(2,1)S(1)}, u32[]{:S(2)}, u32[]{:S(2)}) collective-permute-start(bf16[48,2560]{1,0:T(8,128)(2,1)S(1)} %fusion.1.refs_0_), channel_id=1, source_target_pairs={{0,1},{1,0},{2,3},{3,2},{4,5},{5,4},{6,7},{7,6},{8,9},{9,8},{10,11... | collective-permute-start | bytes 737288 | tf_op jit(solution)/shard_map/ppermute | solution.py:188
  88.8 12.8 %collective-permute-start.14 = (bf16[48,2560]{1,0:T(8,128)(2,1)S(1)}, bf16[48,2560]{1,0:T(8,128)(2,1)S(1)}, u32[]{:S(2)}, u32[]{:S(2)}) collective-permute-start(bf16[48,2560]{1,0:T(8,128)(2,1)S(1)} %collective-permute-done.12.refs_1_), channel_id=1, source_target_pairs={{0,1},{1,0},{2,3},{3,2},{4,5},{5,4},{6,7},{7,6},{8,9},{9,8},{10,11... | collective-permute-start | bytes 737288 | tf_op jit(solution)/shard_map/ppermute | solution.py:188
  88.8 18.8 %collective-permute-start.9 = (bf16[48,2560]{1,0:T(8,128)(2,1)S(1)}, bf16[48,2560]{1,0:T(8,128)(2,1)S(1)}, u32[]{:S(2)}, u32[]{:S(2)}) collective-permute-start(bf16[48,2560]{1,0:T(8,128)(2,1)S(1)} %fusion.3.refs_0_), channel_id=1, source_target_pairs={{0,1},{1,0},{2,3},{3,2},{4,5},{5,4},{6,7},{7,6},{8,9},{9,8},{10,11... | collective-permute-start | bytes 737288 | tf_op jit(solution)/shard_map/ppermute | solution.py:188
  94.1 13.6 %collective-permute-start.10 = (bf16[48,2560]{1,0:T(8,128)(2,1)S(1)}, bf16[48,2560]{1,0:T(8,128)(2,1)S(1)}, u32[]{:S(2)}, u32[]{:S(2)}) collective-permute-start(bf16[48,2560]{1,0:T(8,128)(2,1)S(1)} %collective-permute-done.8.refs_1_), channel_id=1, source_target_pairs={{0,1},{1,0},{2,3},{3,2},{4,5},{5,4},{6,7},{7,6},{8,9},{9,8},{10,11... | collective-permute-start | bytes 737288 | tf_op jit(solution)/shard_map/ppermute | solution.py:188
  95.8 1.4 collective-permute-start.18
  114.2 8.1 %collective-permute-start.21 = (bf16[64,2048]{1,0:T(8,128)(2,1)S(1)}, bf16[64,2048]{1,0:T(8,128)(2,1)S(1)}, u32[]{:S(2)}, u32[]{:S(2)}) collective-permute-start(bf16[64,2048]{1,0:T(8,128)(2,1)S(1)} %get-tuple-element.27), channel_id=1, source_target_pairs={{0,4},{12,8},{1,5},{13,9},{2,6},{14,10},{3,7},{15,11},{16,20},{28,... | collective-permute-start | bytes 786440 | tf_op jit(solution)/shard_map/ppermute | solution.py:185
  115.7 12.2 %collective-permute-start.20 = (bf16[64,2048]{1,0:T(8,128)(2,1)S(1)}, bf16[64,2048]{1,0:T(8,128)(2,1)S(1)}, u32[]{:S(2)}, u32[]{:S(2)}) collective-permute-start(bf16[64,2048]{1,0:T(8,128)(2,1)S(1)} %get-tuple-element.27), channel_id=1, source_target_pairs={{4,8},{8,4},{5,9},{9,5},{6,10},{10,6},{7,11},{11,7},{20,24},{24,20... | collective-permute-start | bytes 786440 | tf_op jit(solution)/shard_map/ppermute | solution.py:185
  116.3 11.5 %collective-permute-start.19 = (bf16[64,2048]{1,0:T(8,128)(2,1)S(1)}, bf16[64,2048]{1,0:T(8,128)(2,1)S(1)}, u32[]{:S(2)}, u32[]{:S(2)}) collective-permute-start(bf16[64,2048]{1,0:T(8,128)(2,1)S(1)} %get-tuple-element.26), channel_id=1, source_target_pairs={{0,4},{4,0},{8,12},{12,8},{1,5},{5,1},{9,13},{13,9},{2,6},{6,2},{1... | collective-permute-start | bytes 786440 | tf_op jit(solution)/shard_map/ppermute | solution.py:185
  122.4 16.2 %collective-permute-start.22 = (bf16[64,2048]{1,0:T(8,128)(2,1)S(1)}, bf16[64,2048]{1,0:T(8,128)(2,1)S(1)}, u32[]{:S(2)}, u32[]{:S(2)}) collective-permute-start(bf16[64,2048]{1,0:T(8,128)(2,1)S(1)} %add_convert_fusion.1), channel_id=1, source_target_pairs={{0,8},{4,12},{8,0},{12,4},{1,9},{5,13},{9,1},{13,5},{2,10},{6,14},... | collective-permute-start | bytes 786440 | tf_op jit(solution)/shard_map/ppermute | solution.py:185
  (5 other events, 19.5 us)

commit v3 on v2

--- a/solution.py
+++ b/solution.py
@@ -112,6 +112,53 @@
         ),
         name="gate_up",
     )(tok, gate_weight, up_weight, *after)
+
+
+def join_kernel(keep_ref, got_ref, *out_refs):
+    quarter = out_refs[0].shape[1]
+    for k, out_ref in enumerate(out_refs):
+        rows = pl.ds(k * quarter, quarter)
+        out_ref[...] = (keep_ref[:, rows] + got_ref[:, rows].astype(F32)).astype(out_ref.dtype)
+
+
+def join(keep, got, nx):
+    two, half, width = keep.shape
+    shape = (two, half // nx, width)
+    return pl.pallas_call(
+        join_kernel,
+        out_shape=[jax.ShapeDtypeStruct(shape, BF16 if k else F32) for k in range(nx)],
+        cost_estimate=pl.CostEstimate(flops=0, bytes_accessed=0, transcendentals=0),
+        name="join",
+    )(keep, got)
+
+
+def activate_kernel(n_got, mine_ref, *refs):
+    own_ref = refs[n_got]
+    both = mine_ref[...]
+    for got_ref in refs[:n_got]:
+        both = both + got_ref[...].astype(F32)
+    gate, up = both[0], both[1]
+    own_ref[...] = (gate / (1.0 + jnp.exp(-gate)) * up).astype(BF16)
+
+
+def activate(mine, got, handed, after):
+    def body(*refs):
+        n_in = 1 + len(got) + len(handed) + len(after)
+        activate_kernel(len(got), *refs[:1 + len(got)], refs[n_in])
+
+    held = [pl.BlockSpec(memory_space=pltpu.VMEM)] * (1 + len(got))
+    anywhere = pl.BlockSpec(memory_space=pl.ANY)
+    out = pl.pallas_call(
+        body,
+        out_shape=[jax.ShapeDtypeStruct(mine.shape[1:], BF16)]
+        + [jax.ShapeDtypeStruct(a.shape, a.dtype) for a in handed],
+        in_specs=held + [anywhere] * (len(handed) + len(after)),
+        out_specs=[pl.BlockSpec(memory_space=pltpu.VMEM)] + [anywhere] * len(handed),
+        input_output_aliases={1 + len(got) + i: 1 + i for i in range(len(handed))},
+        cost_estimate=pl.CostEstimate(flops=0, bytes_accessed=0, transcendentals=0),
+        name="activate",
+    )(mine, *got, *handed, *after)
+    return out[0], out[1:]
 
 
 def down_kernel(n_h, first, last, *refs):
@@ -134,12 +181,16 @@
 def down(hidden, down_weight, total, pick, start, width, n_gx):
     live = sum(h.shape[0] for h in hidden)
     out_width = down_weight.shape[1]
-    tile = min(out_width, 512)
+    tile = min(out_width, 256)
     last = pick is not None
     rows = pl.BlockSpec((live, tile), lambda j: (0, j))
     operands = [*hidden, down_weight]
     in_specs = [pl.BlockSpec(h.shape, lambda j: (0, 0)) for h in hidden]
-    in_specs.append(pl.BlockSpec((pl.Element(width), pl.Element(tile)), lambda j: (start, j * tile)))
+    in_specs.append(
+        pl.BlockSpec(
+            (pl.Element(width), pl.Element(tile)), lambda j: (start, j * tile)
+        )
+    )
     if total is not None:
         operands.append(total)
         in_specs.append(rows)
@@ -167,7 +218,7 @@
 
 def column_chunks(cols, tile):
     tiles = cols // tile
-    shares = (3, 5, 5)
+    shares = (2, 4, 4, 3)
     edges = [round(tiles * sum(shares[:i]) / sum(shares)) for i in range(len(shares) + 1)]
     return [(a * tile, (b - a) * tile) for a, b in zip(edges, edges[1:]) if b > a]
 
@@ -201,21 +252,31 @@
         blocks = [[tokens]] + [[over_z(tokens, k)] for k in range(1, n_gx)]
     tok = compact(pick_in, blocks)
 
-    total, after = None, []
-    for i, (start, width) in enumerate(chunks):
-        send, keep = gate_up(tok, gate_weight, up_weight, after, start, width, tile)
-        sums = keep + over_core(send).astype(F32)
-        mine = sums[:, :quarter]
-        after = []
-        for k in range(1, nx):
-            block = sums[:, k * quarter:(k + 1) * quarter].astype(BF16)
-            after.append(block)
-            mine = mine + over_x(block, k).astype(F32)
-        own = (jax.nn.silu(mine[0]) * mine[1]).astype(BF16)
-        hidden = [own] + [over_x(own, -k) for k in range(1, nx)]
-        hidden += [over_core(h) for h in hidden]
-        last = i == len(chunks) - 1
-        total = down(hidden, down_weight, total, pick_out if last else None, start, width, n_gx)
+    n = len(chunks)
+    send, keep = gate_up(tok, gate_weight, up_weight, [], *chunks[0], tile)
+    keeps, fars, hiddens, totals = [keep], [], [], []
+    for i in range(n):
+        mine, *blocks = join(keeps[i], over_core(send), nx)
+        got = [over_x(b, k + 1) for k, b in enumerate(blocks)]
+        handed = []
+        if i + 1 < n:
+            send, keep = gate_up(tok, gate_weight, up_weight, blocks, *chunks[i + 1], tile)
+            keeps.append(keep)
+            handed = [send]
+        after = (fars[i - 1] if i >= 1 else []) + (totals[i - 2:i - 1] if i >= 2 else [])
+        own, handed = activate(mine, got, handed, after)
+        if handed:
+            send = handed[0]
+        fars.append([over_x(own, -k) for k in range(1, nx)])
+        hiddens.append([own] + fars[i])
+        if i >= 1:
+            h = hiddens[i - 1]
+            h = h + [over_core(a) for a in h]
+            total = totals[-1] if totals else None
+            totals.append(down(h, down_weight, total, None, *chunks[i - 1], n_gx))
+    h = hiddens[-1]
+    h = h + [over_core(a) for a in h]
+    total = down(h, down_weight, totals[-1] if totals else None, pick_out, *chunks[-1], n_gx)
 
     if n_gx == 4:
         ends = over_z(total[3], 1, (0, 3))

time: 140 us -> 176 us (1.26)
  Pallas kernels: 47.6 us -> 76.9 us
  local copies, waits for them, and re-layouts: 1.97 us -> 20.3 us
  waiting for transfers between devices: 59.8 us -> 47.4 us
    ppermute x6 -> x8, waiting for transfers between devices: 26.2 us -> 7.66 us  [over_x(): lax.ppermute(block, 'gy', [(i, (i + 2 * k) % n_gy) for i in range(n_gy)])]
    unnamed x12 -> x78, local copies, waits for them, and re-layouts: 1.84 us -> 20.3 us
    pallas_call x0 -> x8, Pallas kernels: none -> 17.8 us  [the longest x4 9.91 us: join(): pl.pallas_call(join_kernel, out_shape=[jax.ShapeDtypeStruct(shape, BF16 i...]
    pallas_call x3 -> x4, Pallas kernels: 17 us -> 27.8 us  [down(): pl.pallas_call(functools.partial(down_kernel, len(hidden), total is None,...]
    ppermute x9 -> x12, waiting for transfers between devices: 4.24 us -> 9.52 us  [over_core(): return lax.ppermute(block, 'gy', [(i, i ^ 1) for i in range(n_gy)])]
    pallas_call x3 -> x4, Pallas kernels: 26.6 us -> 27.3 us  [gate_up(): pl.pallas_call(gate_up_kernel, out_shape=[jax.ShapeDtypeStruct((2, half,...]
    ppermute x6 -> x8, starting transfers between devices: 7.51 us -> 8.11 us  [over_x(): lax.ppermute(block, 'gy', [(i, (i + 2 * k) % n_gy) for i in range(n_gy)])]
  transfers between devices with their start and end apart: 23 -> 28, of which waited for: 13 -> 14; matrix products, arithmetic and copies ran while one was open for 1% -> 0% of each run, Pallas kernels for 16% -> 25%
where the time goes in v3:
time: 176 us; the launch traced here: 175 us
  Pallas kernels  76.9 us (44%)
  waiting for transfers between devices  47.4 us (27%)
  starting transfers between devices  28.8 us (16%)
  local copies, waits for them, and re-layouts  20.3 us (12%)
    ppermute x8, waiting for transfers between devices, over_z(): return lax.ppermute(block, 'gx', [(z, z ^ k) for z in among])  30.3 us
    pallas_call x4, Pallas kernels, down(): pl.pallas_call(functools.partial(down_kernel, len(hidden), total is None,...  27.8 us
    pallas_call x4, Pallas kernels, gate_up(): pl.pallas_call(gate_up_kernel, out_shape=[jax.ShapeDtypeStruct((2, half,...  27.3 us
    unnamed x78, local copies, waits for them, and re-layouts  20.3 us
    ppermute x8, starting transfers between devices, over_z(): return lax.ppermute(block, 'gx', [(z, z ^ k) for z in among])  18.8 us
    pallas_call x4, Pallas kernels, join(): pl.pallas_call(join_kernel, out_shape=[jax.ShapeDtypeStruct(shape, BF16 i...  9.91 us
    ppermute x12, waiting for transfers between devices, over_core(): return lax.ppermute(block, 'gy', [(i, i ^ 1) for i in range(n_gy)])  9.52 us
    ppermute x8, starting transfers between devices, over_x(): lax.ppermute(block, 'gy', [(i, (i + 2 * k) % n_gy) for i in range(n_gy)])  8.11 us
  transfers between devices with their start and end apart: 28, of which 14 were waited for; matrix products, arithmetic and copies ran while one was open for 0% of the time, Pallas kernels for 25%

profile of v3, /device:TPU:0, one launch (start us, length us, event | category | flops | bytes accessed | tf_op | source)
XLA Modules:
  0.0 174.6 jit_solution(7960162500991138482)
XLA Ops:
  0.0 4.0 %collective-permute-start.1 = (bf16[64,2048]{1,0:T(8,128)(2,1)}, bf16[64,2048]{1,0:T(8,128)(2,1)S(1)}, u32[]{:S(2)}, u32[]{:S(2)}) collective-permute-start(bf16[64,2048]{1,0:T(8,128)(2,1)} %refs_0_.1), channel_id=1, source_target_pairs={{0,8},{4,12},{8,0},{12,4},{1,9},{5,13},{9,1},{13,5},{2,10},{6,14},... | collective-permute-start | bytes 786440 | tf_op jit(solution)/shard_map/ppermute | solution.py:236
  6.3 10.8 %collective-permute-done.1.refs_2_ = bf16[64,2048]{1,0:T(8,128)(2,1)S(1)} collective-permute-done((bf16[64,2048]{1,0:T(8,128)(2,1)}, bf16[64,2048]{1,0:T(8,128)(2,1)S(1)}, u32[]{:S(2)}, u32[]{:S(2)}) %collective-permute-start.1) | collective-permute-done | bytes 262176 | tf_op jit(solution)/shard_map/ppermute | solution.py:236
  19.8 5.8 %collective-permute-done.3.refs_4_ = bf16[64,2048]{1,0:T(8,128)(2,1)S(1)} collective-permute-done((bf16[64,2048]{1,0:T(8,128)(2,1)S(1)}, bf16[64,2048]{1,0:T(8,128)(2,1)S(1)}, u32[]{:S(2)}, u32[]{:S(2)}) %collective-permute-start.3) | collective-permute-done | bytes 262176 | tf_op jit(solution)/shard_map/ppermute | solution.py:236
  26.3 2.6 %compact.1.tok_ref = bf16[192,2048]{1,0:T(8,128)(2,1)} custom-call(bf16[192,256]{1,0:T(8,128)(2,1)} %get-tuple-element.33.pick_ref, bf16[64,2048]{1,0:T(8,128)(2,1)} %refs_0_.1, bf16[64,2048]{1,0:T(8,128)(2,1)} %copy-done.35, bf16[64,2048]{1,0:T(8,128)(2,1)} %copy-done.34, bf16[64,2048]{1,0:T(8,128)(2,1)} %copy-done.36, bf16[64,2048]{1,0:T(8,128)(2,1)} %copy-done.37), custom_call_target="tpu_custom_call" | custom-call | flops 201326592 | bytes 98304 | tf_op jit(solution)/shard_map/compact/pallas_call | solution.py:77
  30.1 4.6 %gate_up.4 = (bf16[2,96,1024]{2,1,0:T(8,128)(2,1)S(1)}, f32[2,96,1024]{2,1,0:T(8,128)S(1)}) custom-call(bf16[192,2048]{1,0:T(8,128)(2,1)S(1)} %copy-done, bf16[2048,6656]{1,0:T(8,128)(2,1)} %gate_ref.7, bf16[2048,6656]{1,0:T(8,128)(2,1)} %up_ref.7), custom_call_target="tpu_custom_call" | custom-call | tf_op jit(solution)/shard_map/gate_up/pallas_call | solution.py:102
  38.0 2.1 %join.4 = (f32[2,48,1024]{2,1,0:T(8,128)}, bf16[2,48,1024]{2,1,0:T(8,128)(2,1)}) custom-call(f32[2,96,1024]{2,1,0:T(8,128)} %copy-done.13, bf16[2,96,1024]{2,1,0:T(8,128)(2,1)} %copy-done.31), custom_call_target="tpu_custom_call" | custom-call | tf_op jit(solution)/shard_map/join/pallas_call | solution.py:127
  42.6 8.0 %gate_up.5 = (bf16[2,96,2048]{2,1,0:T(8,128)(2,1)S(1)}, f32[2,96,2048]{2,1,0:T(8,128)S(1)}) custom-call(bf16[192,2048]{1,0:T(8,128)(2,1)S(1)} %copy-done.1, bf16[2048,6656]{1,0:T(8,128)(2,1)} %gate_ref.7, bf16[2048,6656]{1,0:T(8,128)(2,1)} %up_ref.7, bf16[2,48,1024]{2,1,0:T(8,128)(2,1)S(1)} %copy-done.24), custom_call_target="tpu_custom_call" | custom-call | tf_op jit(solution)/shard_map/gate_up/pallas_call | solution.py:102
  55.1 2.5 %collective-permute-done.6.got_ref = bf16[2,96,2048]{2,1,0:T(8,128)(2,1)S(1)} collective-permute-done((bf16[2,96,2048]{2,1,0:T(8,128)(2,1)}, bf16[2,96,2048]{2,1,0:T(8,128)(2,1)S(1)}, u32[]{:S(2)}, u32[]{:S(2)}) %collective-permute-start.6) | collective-permute-done | bytes 786464 | tf_op jit(solution)/shard_map/ppermute | solution.py:239
  58.5 2.7 %join.5 = (f32[2,48,2048]{2,1,0:T(8,128)}, bf16[2,48,2048]{2,1,0:T(8,128)(2,1)}) custom-call(f32[2,96,2048]{2,1,0:T(8,128)} %copy-done.7, bf16[2,96,2048]{2,1,0:T(8,128)(2,1)} %copy-done.27), custom_call_target="tpu_custom_call" | custom-call | tf_op jit(solution)/shard_map/join/pallas_call | solution.py:127
  64.3 8.1 %gate_up.6 = (bf16[2,96,2048]{2,1,0:T(8,128)(2,1)S(1)}, f32[2,96,2048]{2,1,0:T(8,128)S(1)}) custom-call(bf16[192,2048]{1,0:T(8,128)(2,1)S(1)} %copy-done.1, bf16[2048,6656]{1,0:T(8,128)(2,1)} %gate_ref.7, bf16[2048,6656]{1,0:T(8,128)(2,1)} %up_ref.7, bf16[2,48,2048]{2,1,0:T(8,128)(2,1)S(1)} %copy-done.19), custom_call_target="tpu_custom_call" | custom-call | tf_op jit(solution)/shard_map/gate_up/pallas_call | solution.py:102
  77.6 2.5 %collective-permute-done.9.got_ref = bf16[2,96,2048]{2,1,0:T(8,128)(2,1)S(1)} collective-permute-done((bf16[2,96,2048]{2,1,0:T(8,128)(2,1)}, bf16[2,96,2048]{2,1,0:T(8,128)(2,1)S(1)}, u32[]{:S(2)}, u32[]{:S(2)}) %collective-permute-start.9) | collective-permute-done | bytes 786464 | tf_op jit(solution)/shard_map/ppermute | solution.py:239
  80.9 2.7 %join.6 = (f32[2,48,2048]{2,1,0:T(8,128)}, bf16[2,48,2048]{2,1,0:T(8,128)(2,1)}) custom-call(f32[2,96,2048]{2,1,0:T(8,128)} %copy-done.6, bf16[2,96,2048]{2,1,0:T(8,128)(2,1)} %copy-done.28), custom_call_target="tpu_custom_call" | custom-call | tf_op jit(solution)/shard_map/join/pallas_call | solution.py:127
  87.2 5.7 %down.4.refs_4_.refs_5_ = f32[192,2048]{1,0:T(8,128)S(1)} custom-call(bf16[48,1024]{1,0:T(8,128)(2,1)S(1)} %copy-done.26, bf16[48,1024]{1,0:T(8,128)(2,1)S(1)} %copy-done.21, bf16[48,1024]{1,0:T(8,128)(2,1)S(1)} %collective-permute-done.12.refs_2_, bf16[48,1024]{1,0:T(8,128)(2,1)S(1)} %collective-permute-done.13.refs_3_, bf16[6656,2048]{1,0:T(8,128)(2,1)} %refs_4_.7), custom_call_target="tpu_custom_call" | custom-call | tf_op jit(solution)/shard_map/down/pallas_call | solution.py:205
  94.1 6.6 %gate_up.7 = (bf16[2,96,1536]{2,1,0:T(8,128)(2,1)S(1)}, f32[2,96,1536]{2,1,0:T(8,128)S(1)}) custom-call(bf16[192,2048]{1,0:T(8,128)(2,1)S(1)} %copy-done.1, bf16[2048,6656]{1,0:T(8,128)(2,1)} %gate_ref.7, bf16[2048,6656]{1,0:T(8,128)(2,1)} %up_ref.7, bf16[2,48,2048]{2,1,0:T(8,128)(2,1)S(1)} %copy-done.18), custom_call_target="tpu_custom_call" | custom-call | tf_op jit(solution)/shard_map/gate_up/pallas_call | solution.py:102
  103.4 2.1 %activate.6 = (bf16[48,2048]{1,0:T(8,128)(2,1)}, bf16[2,96,1536]{2,1,0:T(8,128)(2,1)}) custom-call(f32[2,48,2048]{2,1,0:T(8,128)} %get-tuple-element.49.refs_0_, bf16[2,48,2048]{2,1,0:T(8,128)(2,1)} %copy-done.30, bf16[2,96,1536]{2,1,0:T(8,128)(2,1)} %copy-done.17, bf16[48,2048]{1,0:T(8,128)(2,1)} %copy-done.9, ...), custom_call_target="tpu_custom_call", output_to_operand_aliasing={{1}: (2, {})} | custom-call | tf_op jit(solution)/shard_map/activate/pallas_call | solution.py:151
  108.5 2.4 %join.7 = (f32[2,48,1536]{2,1,0:T(8,128)}, bf16[2,48,1536]{2,1,0:T(8,128)(2,1)}) custom-call(f32[2,96,1536]{2,1,0:T(8,128)} %copy-done.8, bf16[2,96,1536]{2,1,0:T(8,128)(2,1)} %copy-done.29), custom_call_target="tpu_custom_call" | custom-call | tf_op jit(solution)/shard_map/join/pallas_call | solution.py:127
  113.5 7.2 %down.5.refs_3_.refs_5_ = f32[192,2048]{1,0:T(8,128)S(1)} custom-call(bf16[48,2048]{1,0:T(8,128)(2,1)S(1)} %copy-done.22, bf16[48,2048]{1,0:T(8,128)(2,1)S(1)} %copy-done.10, bf16[48,2048]{1,0:T(8,128)(2,1)S(1)} %collective-permute-done.17.refs_2_, bf16[48,2048]{1,0:T(8,128)(2,1)S(1)} %collective-permute-done.18.refs_3_, bf16[6656,2048]{1,0:T(8,128)(2,1)} %refs_4_.7, ...), custom_call_target="tpu_custom_call" | custom-call | tf_op jit(solution)/shard_map/down/pallas_call | solution.py:205
  121.8 2.8 %collective-permute-done.16.refs_2_.refs_1_ = bf16[48,2048]{1,0:T(8,128)(2,1)S(1)} collective-permute-done((bf16[48,2048]{1,0:T(8,128)(2,1)}, bf16[48,2048]{1,0:T(8,128)(2,1)S(1)}, u32[]{:S(2)}, u32[]{:S(2)}) %collective-permute-start.16) | collective-permute-done | bytes 196640 | tf_op jit(solution)/shard_map/ppermute | solution.py:242
  128.4 4.5 %collective-permute-done.19.refs_1_ = bf16[48,1536]{1,0:T(8,128)(2,1)S(1)} collective-permute-done((bf16[48,1536]{1,0:T(8,128)(2,1)}, bf16[48,1536]{1,0:T(8,128)(2,1)S(1)}, u32[]{:S(2)}, u32[]{:S(2)}) %collective-permute-start.19) | collective-permute-done | bytes 147488 | tf_op jit(solution)/shard_map/ppermute | solution.py:242
  133.8 7.2 %down.6.refs_5_ = f32[192,2048]{1,0:T(8,128)S(1)} custom-call(bf16[48,2048]{1,0:T(8,128)(2,1)S(1)} %copy-done.23, bf16[48,2048]{1,0:T(8,128)(2,1)S(1)} %copy-done.12, bf16[48,2048]{1,0:T(8,128)(2,1)S(1)} %collective-permute-done.22.refs_2_, bf16[48,2048]{1,0:T(8,128)(2,1)S(1)} %collective-permute-done.23.refs_3_, bf16[6656,2048]{1,0:T(8,128)(2,1)} %refs_4_.7, ...), custom_call_target="tpu_custom_call" | custom-call | tf_op jit(solution)/shard_map/down/pallas_call | solution.py:205
  141.1 7.6 %down.7 = (bf16[64,2048]{1,0:T(8,128)(2,1)S(1)}, bf16[64,2048]{1,0:T(8,128)(2,1)S(1)}, bf16[64,2048]{1,0:T(8,128)(2,1)S(1)}, bf16[64,2048]{1,0:T(8,128)(2,1)S(1)}) custom-call(bf16[48,1536]{1,0:T(8,128)(2,1)S(1)} %copy-done.16, bf16[48,1536]{1,0:T(8,128)(2,1)S(1)} %collective-permute-done.19.refs_1_, bf16[48,1536]{1,0:T(8,128)(2,1)S(1)} %collective-permute-done.20.refs_2_, ...), custom_call_target="tpu_custom_call" | custom-call | tf_op jit(solution)/shard_map/down/pallas_call | solution.py:205
  150.9 3.9 %collective-permute-start.24 = (bf16[64,2048]{1,0:T(8,128)(2,1)S(1)}, bf16[64,2048]{1,0:T(8,128)(2,1)S(1)}, u32[]{:S(2)}, u32[]{:S(2)}) collective-permute-start(bf16[64,2048]{1,0:T(8,128)(2,1)S(1)} %get-tuple-element.58), channel_id=1, source_target_pairs={{0,4},{4,0},{8,12},{12,8},{1,5},{5,1},{9,13},{13,9},{2,6},{6,2},{1... | collective-permute-start | bytes 786440 | tf_op jit(solution)/shard_map/ppermute | solution.py:236
  157.0 5.2 %collective-permute-start.27 = (bf16[64,2048]{1,0:T(8,128)(2,1)S(1)}, bf16[64,2048]{1,0:T(8,128)(2,1)S(1)}, u32[]{:S(2)}, u32[]{:S(2)}) collective-permute-start(bf16[64,2048]{1,0:T(8,128)(2,1)S(1)} %add_convert_fusion.1), channel_id=1, source_target_pairs={{0,8},{4,12},{8,0},{12,4},{1,9},{5,13},{9,1},{13,5},{2,10},{6,14},... | collective-permute-start | bytes 786440 | tf_op jit(solution)/shard_map/ppermute | solution.py:236
  162.4 11.4 %collective-permute-done.27 = bf16[64,2048]{1,0:T(8,128)(2,1)S(1)} collective-permute-done((bf16[64,2048]{1,0:T(8,128)(2,1)S(1)}, bf16[64,2048]{1,0:T(8,128)(2,1)S(1)}, u32[]{:S(2)}, u32[]{:S(2)}) %collective-permute-start.27) | collective-permute-done | bytes 262176 | tf_op jit(solution)/shard_map/ppermute | solution.py:236
  (130 shorter events, 51.3 us)
Async XLA Ops:
  0.0 17.0 %collective-permute-start.1 = (bf16[64,2048]{1,0:T(8,128)(2,1)}, bf16[64,2048]{1,0:T(8,128)(2,1)S(1)}, u32[]{:S(2)}, u32[]{:S(2)}) collective-permute-start(bf16[64,2048]{1,0:T(8,128)(2,1)} %refs_0_.1), channel_id=1, source_target_pairs={{0,8},{4,12},{8,0},{12,4},{1,9},{5,13},{9,1},{13,5},{2,10},{6,14},... | collective-permute-start | bytes 786440 | tf_op jit(solution)/shard_map/ppermute | solution.py:236
  4.0 15.7 %collective-permute-start = (bf16[64,2048]{1,0:T(8,128)(2,1)}, bf16[64,2048]{1,0:T(8,128)(2,1)S(1)}, u32[]{:S(2)}, u32[]{:S(2)}) collective-permute-start(bf16[64,2048]{1,0:T(8,128)(2,1)} %refs_0_.1), channel_id=1, source_target_pairs={{0,4},{4,0},{8,12},{12,8},{1,5},{5,1},{9,13},{13,9},{2,6},{6,2},{1... | collective-permute-start | bytes 786440 | tf_op jit(solution)/shard_map/ppermute | solution.py:236
  5.6 14.2 %collective-permute-start.2 = (bf16[64,2048]{1,0:T(8,128)(2,1)}, bf16[64,2048]{1,0:T(8,128)(2,1)S(1)}, u32[]{:S(2)}, u32[]{:S(2)}) collective-permute-start(bf16[64,2048]{1,0:T(8,128)(2,1)} %refs_0_.1), channel_id=1, source_target_pairs={{4,8},{8,4},{5,9},{9,5},{6,10},{10,6},{7,11},{11,7},{20,24},{24,20... | collective-permute-start | bytes 786440 | tf_op jit(solution)/shard_map/ppermute | solution.py:236
  17.0 8.5 %collective-permute-start.3 = (bf16[64,2048]{1,0:T(8,128)(2,1)S(1)}, bf16[64,2048]{1,0:T(8,128)(2,1)S(1)}, u32[]{:S(2)}, u32[]{:S(2)}) collective-permute-start(bf16[64,2048]{1,0:T(8,128)(2,1)S(1)} %collective-permute-done.1.refs_2_), channel_id=1, source_target_pairs={{4,0},{8,12},{5,1},{9,13},{6,2},{10,14},{7,3},{11,15},{20,16},{24,... | collective-permute-start | bytes 786440 | tf_op jit(solution)/shard_map/ppermute | solution.py:236
  40.1 12.6 %collective-permute-start.5 = (bf16[2,48,1024]{2,1,0:T(8,128)(2,1)}, bf16[2,48,1024]{2,1,0:T(8,128)(2,1)S(1)}, u32[]{:S(2)}, u32[]{:S(2)}) collective-permute-start(bf16[2,48,1024]{2,1,0:T(8,128)(2,1)} %get-tuple-element.36.refs_0_), channel_id=1, source_target_pairs={{0,2},{1,3},{2,0},{3,1},{4,6},{5,7},{6,4},{7,5},{8,10},{9,11},{10,... | collective-permute-start | bytes 589832 | tf_op jit(solution)/shard_map/ppermute | solution.py:242
  55.1 2.5 %collective-permute-start.6 = (bf16[2,96,2048]{2,1,0:T(8,128)(2,1)}, bf16[2,96,2048]{2,1,0:T(8,128)(2,1)S(1)}, u32[]{:S(2)}, u32[]{:S(2)}) collective-permute-start(bf16[2,96,2048]{2,1,0:T(8,128)(2,1)} %get-tuple-element.40), channel_id=1, source_target_pairs={{0,1},{1,0},{2,3},{3,2},{4,5},{5,4},{6,7},{7,6},{8,9},{9,8},{10,11... | collective-permute-start | bytes 2359304 | tf_op jit(solution)/shard_map/ppermute | solution.py:239
  61.2 13.5 %collective-permute-start.7 = (bf16[2,48,2048]{2,1,0:T(8,128)(2,1)}, bf16[2,48,2048]{2,1,0:T(8,128)(2,1)S(1)}, u32[]{:S(2)}, u32[]{:S(2)}) collective-permute-start(bf16[2,48,2048]{2,1,0:T(8,128)(2,1)} %get-tuple-element.41.refs_0_), channel_id=1, source_target_pairs={{0,2},{1,3},{2,0},{3,1},{4,6},{5,7},{6,4},{7,5},{8,10},{9,11},{10,... | collective-permute-start | bytes 1179656 | tf_op jit(solution)/shard_map/ppermute | solution.py:242
  61.7 13.0 %collective-permute-start.8 = (bf16[48,1024]{1,0:T(8,128)(2,1)S(1)}, bf16[48,1024]{1,0:T(8,128)(2,1)S(1)}, u32[]{:S(2)}, u32[]{:S(2)}) collective-permute-start(bf16[48,1024]{1,0:T(8,128)(2,1)S(1)} %copy-done.26), channel_id=1, source_target_pairs={{0,2},{1,3},{2,0},{3,1},{4,6},{5,7},{6,4},{7,5},{8,10},{9,11},{10,... | collective-permute-start | bytes 294920 | tf_op jit(solution)/shard_map/ppermute | solution.py:242
  77.6 2.5 %collective-permute-start.9 = (bf16[2,96,2048]{2,1,0:T(8,128)(2,1)}, bf16[2,96,2048]{2,1,0:T(8,128)(2,1)S(1)}, u32[]{:S(2)}, u32[]{:S(2)}) collective-permute-start(bf16[2,96,2048]{2,1,0:T(8,128)(2,1)} %get-tuple-element.46), channel_id=1, source_target_pairs={{0,1},{1,0},{2,3},{3,2},{4,5},{5,4},{6,7},{7,6},{8,9},{9,8},{10,11... | collective-permute-start | bytes 2359304 | tf_op jit(solution)/shard_map/ppermute | solution.py:239
  83.7 18.9 %collective-permute-start.10 = (bf16[2,48,2048]{2,1,0:T(8,128)(2,1)}, bf16[2,48,2048]{2,1,0:T(8,128)(2,1)S(1)}, u32[]{:S(2)}, u32[]{:S(2)}) collective-permute-start(bf16[2,48,2048]{2,1,0:T(8,128)(2,1)} %get-tuple-element.47.refs_0_), channel_id=1, source_target_pairs={{0,2},{1,3},{2,0},{3,1},{4,6},{5,7},{6,4},{7,5},{8,10},{9,11},{10,... | collective-permute-start | bytes 1179656 | tf_op jit(solution)/shard_map/ppermute | solution.py:242
  84.1 18.4 %collective-permute-start.11 = (bf16[48,2048]{1,0:T(8,128)(2,1)S(1)}, bf16[48,2048]{1,0:T(8,128)(2,1)S(1)}, u32[]{:S(2)}, u32[]{:S(2)}) collective-permute-start(bf16[48,2048]{1,0:T(8,128)(2,1)S(1)} %copy-done.22), channel_id=1, source_target_pairs={{0,2},{1,3},{2,0},{3,1},{4,6},{5,7},{6,4},{7,5},{8,10},{9,11},{10,... | collective-permute-start | bytes 589832 | tf_op jit(solution)/shard_map/ppermute | solution.py:242
  105.5 2.2 %collective-permute-start.14 = (bf16[2,96,1536]{2,1,0:T(8,128)(2,1)}, bf16[2,96,1536]{2,1,0:T(8,128)(2,1)S(1)}, u32[]{:S(2)}, u32[]{:S(2)}) collective-permute-start(bf16[2,96,1536]{2,1,0:T(8,128)(2,1)} %get-tuple-element.52), channel_id=1, source_target_pairs={{0,1},{1,0},{2,3},{3,2},{4,5},{5,4},{6,7},{7,6},{8,9},{9,8},{10,11... | collective-permute-start | bytes 1769480 | tf_op jit(solution)/shard_map/ppermute | solution.py:239
  110.9 13.7 %collective-permute-start.15 = (bf16[2,48,1536]{2,1,0:T(8,128)(2,1)}, bf16[2,48,1536]{2,1,0:T(8,128)(2,1)S(1)}, u32[]{:S(2)}, u32[]{:S(2)}) collective-permute-start(bf16[2,48,1536]{2,1,0:T(8,128)(2,1)} %get-tuple-element.54), channel_id=1, source_target_pairs={{0,2},{1,3},{2,0},{3,1},{4,6},{5,7},{6,4},{7,5},{8,10},{9,11},{10,... | collective-permute-start | bytes 884744 | tf_op jit(solution)/shard_map/ppermute | solution.py:242
  111.4 2.0 %collective-permute-start.17 = (bf16[48,2048]{1,0:T(8,128)(2,1)S(1)}, bf16[48,2048]{1,0:T(8,128)(2,1)S(1)}, u32[]{:S(2)}, u32[]{:S(2)}) collective-permute-start(bf16[48,2048]{1,0:T(8,128)(2,1)S(1)} %copy-done.22), channel_id=1, source_target_pairs={{0,1},{1,0},{2,3},{3,2},{4,5},{5,4},{6,7},{7,6},{8,9},{9,8},{10,11... | collective-permute-start | bytes 589832 | tf_op jit(solution)/shard_map/ppermute | solution.py:239
  111.9 12.7 %collective-permute-start.16 = (bf16[48,2048]{1,0:T(8,128)(2,1)}, bf16[48,2048]{1,0:T(8,128)(2,1)S(1)}, u32[]{:S(2)}, u32[]{:S(2)}) collective-permute-start(bf16[48,2048]{1,0:T(8,128)(2,1)} %get-tuple-element.55.refs_0_), channel_id=1, source_target_pairs={{0,2},{1,3},{2,0},{3,1},{4,6},{5,7},{6,4},{7,5},{8,10},{9,11},{10,... | collective-permute-start | bytes 589832 | tf_op jit(solution)/shard_map/ppermute | solution.py:242
  127.4 5.5 %collective-permute-start.19 = (bf16[48,1536]{1,0:T(8,128)(2,1)}, bf16[48,1536]{1,0:T(8,128)(2,1)S(1)}, u32[]{:S(2)}, u32[]{:S(2)}) collective-permute-start(bf16[48,1536]{1,0:T(8,128)(2,1)} %activate.7.refs_0_), channel_id=1, source_target_pairs={{0,2},{1,3},{2,0},{3,1},{4,6},{5,7},{6,4},{7,5},{8,10},{9,11},{10,... | collective-permute-start | bytes 442376 | tf_op jit(solution)/shard_map/ppermute | solution.py:242
  127.9 5.0 %collective-permute-start.22 = (bf16[48,2048]{1,0:T(8,128)(2,1)S(1)}, bf16[48,2048]{1,0:T(8,128)(2,1)S(1)}, u32[]{:S(2)}, u32[]{:S(2)}) collective-permute-start(bf16[48,2048]{1,0:T(8,128)(2,1)S(1)} %copy-done.23), channel_id=1, source_target_pairs={{0,1},{1,0},{2,3},{3,2},{4,5},{5,4},{6,7},{7,6},{8,9},{9,8},{10,11... | collective-permute-start | bytes 589832 | tf_op jit(solution)/shard_map/ppermute | solution.py:239
  127.9 5.0 %collective-permute-start.23 = (bf16[48,2048]{1,0:T(8,128)(2,1)}, bf16[48,2048]{1,0:T(8,128)(2,1)S(1)}, u32[]{:S(2)}, u32[]{:S(2)}) collective-permute-start(bf16[48,2048]{1,0:T(8,128)(2,1)} %copy-done.11), channel_id=1, source_target_pairs={{0,1},{1,0},{2,3},{3,2},{4,5},{5,4},{6,7},{7,6},{8,9},{9,8},{10,11... | collective-permute-start | bytes 589832 | tf_op jit(solution)/shard_map/ppermute | solution.py:239
  128.4 12.7 %collective-permute-start.20 = (bf16[48,1536]{1,0:T(8,128)(2,1)}, bf16[48,1536]{1,0:T(8,128)(2,1)S(1)}, u32[]{:S(2)}, u32[]{:S(2)}) collective-permute-start(bf16[48,1536]{1,0:T(8,128)(2,1)} %activate.7.refs_0_), channel_id=1, source_target_pairs={{0,1},{1,0},{2,3},{3,2},{4,5},{5,4},{6,7},{7,6},{8,9},{9,8},{10,11... | collective-permute-start | bytes 442376 | tf_op jit(solution)/shard_map/ppermute | solution.py:239
  132.9 8.2 %collective-permute-start.21 = (bf16[48,1536]{1,0:T(8,128)(2,1)S(1)}, bf16[48,1536]{1,0:T(8,128)(2,1)S(1)}, u32[]{:S(2)}, u32[]{:S(2)}) collective-permute-start(bf16[48,1536]{1,0:T(8,128)(2,1)S(1)} %collective-permute-done.19.refs_1_), channel_id=1, source_target_pairs={{0,1},{1,0},{2,3},{3,2},{4,5},{5,4},{6,7},{7,6},{8,9},{9,8},{10,11... | collective-permute-start | bytes 442376 | tf_op jit(solution)/shard_map/ppermute | solution.py:239
  148.7 8.1 %collective-permute-start.26 = (bf16[64,2048]{1,0:T(8,128)(2,1)S(1)}, bf16[64,2048]{1,0:T(8,128)(2,1)S(1)}, u32[]{:S(2)}, u32[]{:S(2)}) collective-permute-start(bf16[64,2048]{1,0:T(8,128)(2,1)S(1)} %get-tuple-element.59), channel_id=1, source_target_pairs={{0,4},{12,8},{1,5},{13,9},{2,6},{14,10},{3,7},{15,11},{16,20},{28,... | collective-permute-start | bytes 786440 | tf_op jit(solution)/shard_map/ppermute | solution.py:236
  150.2 11.9 %collective-permute-start.25 = (bf16[64,2048]{1,0:T(8,128)(2,1)S(1)}, bf16[64,2048]{1,0:T(8,128)(2,1)S(1)}, u32[]{:S(2)}, u32[]{:S(2)}) collective-permute-start(bf16[64,2048]{1,0:T(8,128)(2,1)S(1)} %get-tuple-element.59), channel_id=1, source_target_pairs={{4,8},{8,4},{5,9},{9,5},{6,10},{10,6},{7,11},{11,7},{20,24},{24,20... | collective-permute-start | bytes 786440 | tf_op jit(solution)/shard_map/ppermute | solution.py:236
  150.9 11.5 %collective-permute-start.24 = (bf16[64,2048]{1,0:T(8,128)(2,1)S(1)}, bf16[64,2048]{1,0:T(8,128)(2,1)S(1)}, u32[]{:S(2)}, u32[]{:S(2)}) collective-permute-start(bf16[64,2048]{1,0:T(8,128)(2,1)S(1)} %get-tuple-element.58), channel_id=1, source_target_pairs={{0,4},{4,0},{8,12},{12,8},{1,5},{5,1},{9,13},{13,9},{2,6},{6,2},{1... | collective-permute-start | bytes 786440 | tf_op jit(solution)/shard_map/ppermute | solution.py:236
  157.0 16.8 %collective-permute-start.27 = (bf16[64,2048]{1,0:T(8,128)(2,1)S(1)}, bf16[64,2048]{1,0:T(8,128)(2,1)S(1)}, u32[]{:S(2)}, u32[]{:S(2)}) collective-permute-start(bf16[64,2048]{1,0:T(8,128)(2,1)S(1)} %add_convert_fusion.1), channel_id=1, source_target_pairs={{0,8},{4,12},{8,0},{12,4},{1,9},{5,13},{9,1},{13,5},{2,10},{6,14},... | collective-permute-start | bytes 786440 | tf_op jit(solution)/shard_map/ppermute | solution.py:236
  (43 other events, 137.5 us)

commit v4 on v3

--- a/solution.py
+++ b/solution.py
@@ -56,6 +56,7 @@
         out_shape=[jax.ShapeDtypeStruct((live, slots), BF16), jax.ShapeDtypeStruct((slots, live), BF16)],
         in_specs=[pl.BlockSpec(memory_space=pltpu.SMEM)],
         cost_estimate=pl.CostEstimate(flops=0, bytes_accessed=4 * live * slots, transcendentals=0),
+        compiler_params=pltpu.CompilerParams(vmem_limit_bytes=8 * MIB),
         name="picks",
     )(lengths)
 
@@ -80,6 +81,7 @@
         cost_estimate=pl.CostEstimate(
             flops=2 * pick.size * flat[0].shape[1], bytes_accessed=2 * pick.size, transcendentals=0
         ),
+        compiler_params=pltpu.CompilerParams(vmem_limit_bytes=8 * MIB),
         name="compact",
     )(pick, *flat)
 
@@ -106,7 +108,7 @@
         in_specs=[pl.BlockSpec((live, depth), lambda j: (0, 0)), weight, weight]
         + [pl.BlockSpec(memory_space=pl.ANY)] * len(after),
         out_specs=[out, out],
-        compiler_params=pltpu.CompilerParams(vmem_limit_bytes=32 * MIB),
+        compiler_params=pltpu.CompilerParams(vmem_limit_bytes=20 * MIB),
         cost_estimate=pl.CostEstimate(
             flops=0, bytes_accessed=0, transcendentals=0
         ),
@@ -128,6 +130,7 @@
         join_kernel,
         out_shape=[jax.ShapeDtypeStruct(shape, BF16 if k else F32) for k in range(nx)],
         cost_estimate=pl.CostEstimate(flops=0, bytes_accessed=0, transcendentals=0),
+        compiler_params=pltpu.CompilerParams(vmem_limit_bytes=8 * MIB),
         name="join",
     )(keep, got)
 
@@ -156,6 +159,7 @@
         out_specs=[pl.BlockSpec(memory_space=pltpu.VMEM)] + [anywhere] * len(handed),
         input_output_aliases={1 + len(got) + i: 1 + i for i in range(len(handed))},
         cost_estimate=pl.CostEstimate(flops=0, bytes_accessed=0, transcendentals=0),
+        compiler_params=pltpu.CompilerParams(vmem_limit_bytes=8 * MIB),
         name="activate",
     )(mine, *got, *handed, *after)
     return out[0], out[1:]
@@ -208,7 +212,7 @@
         grid=(out_width // tile,),
         in_specs=in_specs,
         out_specs=out_specs,
-        compiler_params=pltpu.CompilerParams(vmem_limit_bytes=32 * MIB),
+        compiler_params=pltpu.CompilerParams(vmem_limit_bytes=20 * MIB),
         cost_estimate=pl.CostEstimate(
             flops=0, bytes_accessed=0, transcendentals=0
         ),

time: 176 us -> 177 us (level)
  Pallas kernels: 76.9 us -> 42.8 us
  local copies, waits for them, and re-layouts: 20.3 us -> 54.1 us
    unnamed x78 -> x16, local copies, waits for them, and re-layouts: 20.3 us -> 54.1 us
    pallas_call x4, Pallas kernels: 27.8 us -> 17.8 us  [down(): pl.pallas_call(functools.partial(down_kernel, len(hidden), total is None,...]
    pallas_call x4, Pallas kernels: 9.91 us -> 0.43 us  [join(): pl.pallas_call(join_kernel, out_shape=[jax.ShapeDtypeStruct(shape, BF16 i...]
    pallas_call x4, Pallas kernels: 7.85 us -> 0.54 us  [activate(): pl.pallas_call(body, out_shape=[jax.ShapeDtypeStruct(mine.shape[1:], BF16...]
    pallas_call x4, Pallas kernels: 27.3 us -> 23 us  [gate_up(): pl.pallas_call(gate_up_kernel, out_shape=[jax.ShapeDtypeStruct((2, half,...]
    pallas_call x1, Pallas kernels: 2.62 us -> 0.37 us  [compact(): pl.pallas_call(functools.partial(compact_kernel, [len(group) for group in...]
  transfers between devices with their start and end apart: 28 -> 28, of which waited for: 14 -> 13; matrix products, arithmetic and copies ran while one was open for 0% -> 0% of each run, Pallas kernels for 25% -> 18%
where the time goes in v4:
time: 177 us; the launch traced here: 176 us
  local copies, waits for them, and re-layouts  54.1 us (31%)
  waiting for transfers between devices  47.4 us (27%)
  Pallas kernels  42.8 us (24%)
  starting transfers between devices  30.4 us (17%)
    unnamed x16, local copies, waits for them, and re-layouts  54.1 us
    ppermute x8, waiting for transfers between devices, over_z(): return lax.ppermute(block, 'gx', [(z, z ^ k) for z in among])  30.2 us
    pallas_call x4, Pallas kernels, gate_up(): pl.pallas_call(gate_up_kernel, out_shape=[jax.ShapeDtypeStruct((2, half,...  23 us
    ppermute x8, starting transfers between devices, over_z(): return lax.ppermute(block, 'gx', [(z, z ^ k) for z in among])  19 us
    pallas_call x4, Pallas kernels, down(): pl.pallas_call(functools.partial(down_kernel, len(hidden), total is None,...  17.8 us
    ppermute x8, starting transfers between devices, over_x(): lax.ppermute(block, 'gy', [(i, (i + 2 * k) % n_gy) for i in range(n_gy)])  9.18 us
    ppermute x12, waiting for transfers between devices, over_core(): return lax.ppermute(block, 'gy', [(i, i ^ 1) for i in range(n_gy)])  8.86 us
    ppermute x8, waiting for transfers between devices, over_x(): lax.ppermute(block, 'gy', [(i, (i + 2 * k) % n_gy) for i in range(n_gy)])  8.33 us
  transfers between devices with their start and end apart: 28, of which 13 were waited for; matrix products, arithmetic and copies ran while one was open for 0% of the time, Pallas kernels for 18%

profile of v4, /device:TPU:0, one launch (start us, length us, event | category | flops | bytes accessed | tf_op | source)
XLA Modules:
  0.0 175.9 jit_solution(8118363806425768871)
XLA Ops:
  0.0 4.0 %collective-permute-start.1 = (bf16[64,2048]{1,0:T(8,128)(2,1)}, bf16[64,2048]{1,0:T(8,128)(2,1)S(1)}, u32[]{:S(2)}, u32[]{:S(2)}) collective-permute-start(bf16[64,2048]{1,0:T(8,128)(2,1)} %refs_0_.1), channel_id=1, source_target_pairs={{0,8},{4,12},{8,0},{12,4},{1,9},{5,13},{9,1},{13,5},{2,10},{6,14},... | collective-permute-start | bytes 786440 | tf_op jit(solution)/shard_map/ppermute | solution.py:240
  6.3 10.8 %collective-permute-done.1.refs_2_ = bf16[64,2048]{1,0:T(8,128)(2,1)S(1)} collective-permute-done((bf16[64,2048]{1,0:T(8,128)(2,1)}, bf16[64,2048]{1,0:T(8,128)(2,1)S(1)}, u32[]{:S(2)}, u32[]{:S(2)}) %collective-permute-start.1) | collective-permute-done | bytes 262176 | tf_op jit(solution)/shard_map/ppermute | solution.py:240
  19.7 5.9 %collective-permute-done.3.refs_4_ = bf16[64,2048]{1,0:T(8,128)(2,1)S(1)} collective-permute-done((bf16[64,2048]{1,0:T(8,128)(2,1)S(1)}, bf16[64,2048]{1,0:T(8,128)(2,1)S(1)}, u32[]{:S(2)}, u32[]{:S(2)}) %collective-permute-start.3) | collective-permute-done | bytes 262176 | tf_op jit(solution)/shard_map/ppermute | solution.py:240
  26.9 8.7 %copy-done.4 = bf16[2048,6656]{1,0:T(8,128)(2,1)S(1)} copy-done((bf16[2048,6656]{1,0:T(8,128)(2,1)S(1)}, bf16[2048,6656]{1,0:T(8,128)(2,1)}, u32[]{:S(2)}) %copy-start.4) | copy-done | bytes 27263000
  35.7 3.9 %gate_up.4 = (bf16[2,96,1024]{2,1,0:T(8,128)(2,1)S(1)}, f32[2,96,1024]{2,1,0:T(8,128)S(1)}) custom-call(bf16[192,2048]{1,0:T(8,128)(2,1)S(1)} %compact.1.tok_ref, bf16[2048,6656]{1,0:T(8,128)(2,1)S(1)} %copy-done.4, bf16[2048,6656]{1,0:T(8,128)(2,1)} %up_ref.7), custom_call_target="tpu_custom_call" | custom-call | tf_op jit(solution)/shard_map/gate_up/pallas_call | solution.py:104
  43.0 6.8 %gate_up.5 = (bf16[2,96,2048]{2,1,0:T(8,128)(2,1)S(1)}, f32[2,96,2048]{2,1,0:T(8,128)S(1)}) custom-call(bf16[192,2048]{1,0:T(8,128)(2,1)S(1)} %compact.1.tok_ref, bf16[2048,6656]{1,0:T(8,128)(2,1)S(1)} %copy-done.4, bf16[2048,6656]{1,0:T(8,128)(2,1)} %up_ref.7, bf16[2,48,1024]{2,1,0:T(8,128)(2,1)S(1)} %get-tuple-element.36.refs_0_), custom_call_target="tpu_custom_call" | custom-call | tf_op jit(solution)/shard_map/gate_up/pallas_call | solution.py:104
  50.0 2.3 %collective-permute-done.6.got_ref = bf16[2,96,2048]{2,1,0:T(8,128)(2,1)S(1)} collective-permute-done((bf16[2,96,2048]{2,1,0:T(8,128)(2,1)S(1)}, bf16[2,96,2048]{2,1,0:T(8,128)(2,1)S(1)}, u32[]{:S(2)}, u32[]{:S(2)}) %collective-permute-start.6) | collective-permute-done | bytes 786464 | tf_op jit(solution)/shard_map/ppermute | solution.py:243
  54.5 6.8 %gate_up.6 = (bf16[2,96,2048]{2,1,0:T(8,128)(2,1)S(1)}, f32[2,96,2048]{2,1,0:T(8,128)S(1)}) custom-call(bf16[192,2048]{1,0:T(8,128)(2,1)S(1)} %compact.1.tok_ref, bf16[2048,6656]{1,0:T(8,128)(2,1)S(1)} %copy-done.4, bf16[2048,6656]{1,0:T(8,128)(2,1)} %up_ref.7, bf16[2,48,2048]{2,1,0:T(8,128)(2,1)S(1)} %get-tuple-element.41.refs_0_), custom_call_target="tpu_custom_call" | custom-call | tf_op jit(solution)/shard_map/gate_up/pallas_call | solution.py:104
  61.4 4.4 %collective-permute-done.8.refs_3_.refs_1_ = bf16[48,1024]{1,0:T(8,128)(2,1)S(1)} collective-permute-done((bf16[48,1024]{1,0:T(8,128)(2,1)S(1)}, bf16[48,1024]{1,0:T(8,128)(2,1)S(1)}, u32[]{:S(2)}, u32[]{:S(2)}) %collective-permute-start.8) | collective-permute-done | bytes 98336 | tf_op jit(solution)/shard_map/ppermute | solution.py:246
  66.0 2.3 %collective-permute-done.9.got_ref = bf16[2,96,2048]{2,1,0:T(8,128)(2,1)S(1)} collective-permute-done((bf16[2,96,2048]{2,1,0:T(8,128)(2,1)S(1)}, bf16[2,96,2048]{2,1,0:T(8,128)(2,1)S(1)}, u32[]{:S(2)}, u32[]{:S(2)}) %collective-permute-start.9) | collective-permute-done | bytes 786464 | tf_op jit(solution)/shard_map/ppermute | solution.py:243
  72.0 8.8 %copy-done = bf16[6656,2048]{1,0:T(8,128)(2,1)S(1)} copy-done((bf16[6656,2048]{1,0:T(8,128)(2,1)S(1)}, bf16[6656,2048]{1,0:T(8,128)(2,1)}, u32[]{:S(2)}) %copy-start) | copy-done | bytes 27263000
  80.7 2.9 %down.4.refs_4_.refs_5_ = f32[192,2048]{1,0:T(8,128)S(1)} custom-call(bf16[48,1024]{1,0:T(8,128)(2,1)S(1)} %get-tuple-element.45.refs_0_, bf16[48,1024]{1,0:T(8,128)(2,1)S(1)} %collective-permute-done.8.refs_3_.refs_1_, bf16[48,1024]{1,0:T(8,128)(2,1)S(1)} %collective-permute-done.12.refs_2_, bf16[48,1024]{1,0:T(8,128)(2,1)S(1)} %collective-permute-done.13.refs_3_, ...), custom_call_target="tpu_custom_call" | custom-call | tf_op jit(solution)/shard_map/down/pallas_call | solution.py:209
  83.7 8.7 %copy-done.5 = bf16[2048,6656]{1,0:T(8,128)(2,1)S(1)} copy-done((bf16[2048,6656]{1,0:T(8,128)(2,1)S(1)}, bf16[2048,6656]{1,0:T(8,128)(2,1)}, u32[]{:S(2)}) %copy-start.5) | copy-done | bytes 27263000
  92.4 5.5 %gate_up.7 = (bf16[2,96,1536]{2,1,0:T(8,128)(2,1)S(1)}, f32[2,96,1536]{2,1,0:T(8,128)S(1)}) custom-call(bf16[192,2048]{1,0:T(8,128)(2,1)S(1)} %compact.1.tok_ref, bf16[2048,6656]{1,0:T(8,128)(2,1)S(1)} %copy-done.5, bf16[2048,6656]{1,0:T(8,128)(2,1)} %up_ref.7, bf16[2,48,2048]{2,1,0:T(8,128)(2,1)S(1)} %get-tuple-element.47.refs_0_), custom_call_target="tpu_custom_call" | custom-call | tf_op jit(solution)/shard_map/gate_up/pallas_call | solution.py:104
  103.0 8.8 %copy-done.1 = bf16[6656,2048]{1,0:T(8,128)(2,1)S(1)} copy-done((bf16[6656,2048]{1,0:T(8,128)(2,1)S(1)}, bf16[6656,2048]{1,0:T(8,128)(2,1)}, u32[]{:S(2)}) %copy-start.1) | copy-done | bytes 27263000
  111.7 4.6 %down.5.refs_3_.refs_5_ = f32[192,2048]{1,0:T(8,128)S(1)} custom-call(bf16[48,2048]{1,0:T(8,128)(2,1)S(1)} %get-tuple-element.51.refs_0_, bf16[48,2048]{1,0:T(8,128)(2,1)S(1)} %collective-permute-done.11.refs_3_.refs_1_, bf16[48,2048]{1,0:T(8,128)(2,1)S(1)} %collective-permute-done.17.refs_2_, bf16[48,2048]{1,0:T(8,128)(2,1)S(1)} %collective-permute-done.18.refs_3_, ...), custom_call_target="tpu_custom_call" | custom-call | tf_op jit(solution)/shard_map/down/pallas_call | solution.py:209
  118.3 3.9 %collective-permute-done.19.refs_1_ = bf16[48,1536]{1,0:T(8,128)(2,1)S(1)} collective-permute-done((bf16[48,1536]{1,0:T(8,128)(2,1)S(1)}, bf16[48,1536]{1,0:T(8,128)(2,1)S(1)}, u32[]{:S(2)}, u32[]{:S(2)}) %collective-permute-start.19) | collective-permute-done | bytes 147488 | tf_op jit(solution)/shard_map/ppermute | solution.py:246
  122.2 8.7 %copy-done.2 = bf16[6656,2048]{1,0:T(8,128)(2,1)S(1)} copy-done((bf16[6656,2048]{1,0:T(8,128)(2,1)S(1)}, bf16[6656,2048]{1,0:T(8,128)(2,1)}, u32[]{:S(2)}) %copy-start.2) | copy-done | bytes 27263000
  131.0 4.6 %down.6.refs_5_ = f32[192,2048]{1,0:T(8,128)S(1)} custom-call(bf16[48,2048]{1,0:T(8,128)(2,1)S(1)} %get-tuple-element.55.refs_0_, bf16[48,2048]{1,0:T(8,128)(2,1)S(1)} %collective-permute-done.16.refs_2_.refs_1_, bf16[48,2048]{1,0:T(8,128)(2,1)S(1)} %collective-permute-done.22.refs_2_, bf16[48,2048]{1,0:T(8,128)(2,1)S(1)} %collective-permute-done.23.refs_3_, ...), custom_call_target="tpu_custom_call" | custom-call | tf_op jit(solution)/shard_map/down/pallas_call | solution.py:209
  135.6 8.7 %copy-done.3 = bf16[6656,2048]{1,0:T(8,128)(2,1)S(1)} copy-done((bf16[6656,2048]{1,0:T(8,128)(2,1)S(1)}, bf16[6656,2048]{1,0:T(8,128)(2,1)}, u32[]{:S(2)}) %copy-start.3) | copy-done | bytes 27263000
  144.4 5.6 %down.7 = (bf16[64,2048]{1,0:T(8,128)(2,1)S(1)}, bf16[64,2048]{1,0:T(8,128)(2,1)S(1)}, bf16[64,2048]{1,0:T(8,128)(2,1)S(1)}, bf16[64,2048]{1,0:T(8,128)(2,1)S(1)}) custom-call(bf16[48,1536]{1,0:T(8,128)(2,1)S(1)} %activate.7.refs_0_, bf16[48,1536]{1,0:T(8,128)(2,1)S(1)} %collective-permute-done.19.refs_1_, ...), custom_call_target="tpu_custom_call" | custom-call | tf_op jit(solution)/shard_map/down/pallas_call | solution.py:209
  152.2 4.0 %collective-permute-start.24 = (bf16[64,2048]{1,0:T(8,128)(2,1)S(1)}, bf16[64,2048]{1,0:T(8,128)(2,1)S(1)}, u32[]{:S(2)}, u32[]{:S(2)}) collective-permute-start(bf16[64,2048]{1,0:T(8,128)(2,1)S(1)} %get-tuple-element.58), channel_id=1, source_target_pairs={{0,4},{4,0},{8,12},{12,8},{1,5},{5,1},{9,13},{13,9},{2,6},{6,2},{1... | collective-permute-start | bytes 786440 | tf_op jit(solution)/shard_map/ppermute | solution.py:240
  158.1 5.3 %collective-permute-start.27 = (bf16[64,2048]{1,0:T(8,128)(2,1)S(1)}, bf16[64,2048]{1,0:T(8,128)(2,1)S(1)}, u32[]{:S(2)}, u32[]{:S(2)}) collective-permute-start(bf16[64,2048]{1,0:T(8,128)(2,1)S(1)} %add_convert_fusion.1), channel_id=1, source_target_pairs={{0,8},{4,12},{8,0},{12,4},{1,9},{5,13},{9,1},{13,5},{2,10},{6,14},... | collective-permute-start | bytes 786440 | tf_op jit(solution)/shard_map/ppermute | solution.py:240
  163.7 11.4 %collective-permute-done.27 = bf16[64,2048]{1,0:T(8,128)(2,1)S(1)} collective-permute-done((bf16[64,2048]{1,0:T(8,128)(2,1)S(1)}, bf16[64,2048]{1,0:T(8,128)(2,1)S(1)}, u32[]{:S(2)}, u32[]{:S(2)}) %collective-permute-start.27) | collective-permute-done | bytes 262176 | tf_op jit(solution)/shard_map/ppermute | solution.py:240
  (68 shorter events, 28.0 us)
Async XLA Ops:
  0.0 17.0 %collective-permute-start.1 = (bf16[64,2048]{1,0:T(8,128)(2,1)}, bf16[64,2048]{1,0:T(8,128)(2,1)S(1)}, u32[]{:S(2)}, u32[]{:S(2)}) collective-permute-start(bf16[64,2048]{1,0:T(8,128)(2,1)} %refs_0_.1), channel_id=1, source_target_pairs={{0,8},{4,12},{8,0},{12,4},{1,9},{5,13},{9,1},{13,5},{2,10},{6,14},... | collective-permute-start | bytes 786440 | tf_op jit(solution)/shard_map/ppermute | solution.py:240
  4.0 15.6 %collective-permute-start = (bf16[64,2048]{1,0:T(8,128)(2,1)}, bf16[64,2048]{1,0:T(8,128)(2,1)S(1)}, u32[]{:S(2)}, u32[]{:S(2)}) collective-permute-start(bf16[64,2048]{1,0:T(8,128)(2,1)} %refs_0_.1), channel_id=1, source_target_pairs={{0,4},{4,0},{8,12},{12,8},{1,5},{5,1},{9,13},{13,9},{2,6},{6,2},{1... | collective-permute-start | bytes 786440 | tf_op jit(solution)/shard_map/ppermute | solution.py:240
  5.6 14.1 %collective-permute-start.2 = (bf16[64,2048]{1,0:T(8,128)(2,1)}, bf16[64,2048]{1,0:T(8,128)(2,1)S(1)}, u32[]{:S(2)}, u32[]{:S(2)}) collective-permute-start(bf16[64,2048]{1,0:T(8,128)(2,1)} %refs_0_.1), channel_id=1, source_target_pairs={{4,8},{8,4},{5,9},{9,5},{6,10},{10,6},{7,11},{11,7},{20,24},{24,20... | collective-permute-start | bytes 786440 | tf_op jit(solution)/shard_map/ppermute | solution.py:240
  17.0 8.5 %collective-permute-start.3 = (bf16[64,2048]{1,0:T(8,128)(2,1)S(1)}, bf16[64,2048]{1,0:T(8,128)(2,1)S(1)}, u32[]{:S(2)}, u32[]{:S(2)}) collective-permute-start(bf16[64,2048]{1,0:T(8,128)(2,1)S(1)} %collective-permute-done.1.refs_2_), channel_id=1, source_target_pairs={{4,0},{8,12},{5,1},{9,13},{6,2},{10,14},{7,3},{11,15},{20,16},{24,... | collective-permute-start | bytes 786440 | tf_op jit(solution)/shard_map/ppermute | solution.py:240
  41.4 8.4 %collective-permute-start.5 = (bf16[2,48,1024]{2,1,0:T(8,128)(2,1)S(1)}, bf16[2,48,1024]{2,1,0:T(8,128)(2,1)S(1)}, u32[]{:S(2)}, u32[]{:S(2)}) collective-permute-start(bf16[2,48,1024]{2,1,0:T(8,128)(2,1)S(1)} %get-tuple-element.36.refs_0_), channel_id=1, source_target_pairs={{0,2},{1,3},{2,0},{3,1},{4,6},{5,7},{6,4},{7,5},{8,10},{9,11},{10,... | collective-permute-start | bytes 589832 | tf_op jit(solution)/shard_map/ppermute | solution.py:246
  50.0 2.4 %collective-permute-start.6 = (bf16[2,96,2048]{2,1,0:T(8,128)(2,1)S(1)}, bf16[2,96,2048]{2,1,0:T(8,128)(2,1)S(1)}, u32[]{:S(2)}, u32[]{:S(2)}) collective-permute-start(bf16[2,96,2048]{2,1,0:T(8,128)(2,1)S(1)} %get-tuple-element.40), channel_id=1, source_target_pairs={{0,1},{1,0},{2,3},{3,2},{4,5},{5,4},{6,7},{7,6},{8,9},{9,8},{10,11... | collective-permute-start | bytes 2359304 | tf_op jit(solution)/shard_map/ppermute | solution.py:243
  52.4 13.3 %collective-permute-start.7 = (bf16[2,48,2048]{2,1,0:T(8,128)(2,1)S(1)}, bf16[2,48,2048]{2,1,0:T(8,128)(2,1)S(1)}, u32[]{:S(2)}, u32[]{:S(2)}) collective-permute-start(bf16[2,48,2048]{2,1,0:T(8,128)(2,1)S(1)} %get-tuple-element.41.refs_0_), channel_id=1, source_target_pairs={{0,2},{1,3},{2,0},{3,1},{4,6},{5,7},{6,4},{7,5},{8,10},{9,11},{10,... | collective-permute-start | bytes 1179656 | tf_op jit(solution)/shard_map/ppermute | solution.py:246
  53.0 12.8 %collective-permute-start.8 = (bf16[48,1024]{1,0:T(8,128)(2,1)S(1)}, bf16[48,1024]{1,0:T(8,128)(2,1)S(1)}, u32[]{:S(2)}, u32[]{:S(2)}) collective-permute-start(bf16[48,1024]{1,0:T(8,128)(2,1)S(1)} %get-tuple-element.45.refs_0_), channel_id=1, source_target_pairs={{0,2},{1,3},{2,0},{3,1},{4,6},{5,7},{6,4},{7,5},{8,10},{9,11},{10,... | collective-permute-start | bytes 294920 | tf_op jit(solution)/shard_map/ppermute | solution.py:246
  65.9 2.4 %collective-permute-start.9 = (bf16[2,96,2048]{2,1,0:T(8,128)(2,1)S(1)}, bf16[2,96,2048]{2,1,0:T(8,128)(2,1)S(1)}, u32[]{:S(2)}, u32[]{:S(2)}) collective-permute-start(bf16[2,96,2048]{2,1,0:T(8,128)(2,1)S(1)} %get-tuple-element.46), channel_id=1, source_target_pairs={{0,1},{1,0},{2,3},{3,2},{4,5},{5,4},{6,7},{7,6},{8,9},{9,8},{10,11... | collective-permute-start | bytes 2359304 | tf_op jit(solution)/shard_map/ppermute | solution.py:243
  68.4 29.6 %collective-permute-start.10 = (bf16[2,48,2048]{2,1,0:T(8,128)(2,1)S(1)}, bf16[2,48,2048]{2,1,0:T(8,128)(2,1)S(1)}, u32[]{:S(2)}, u32[]{:S(2)}) collective-permute-start(bf16[2,48,2048]{2,1,0:T(8,128)(2,1)S(1)} %get-tuple-element.47.refs_0_), channel_id=1, source_target_pairs={{0,2},{1,3},{2,0},{3,1},{4,6},{5,7},{6,4},{7,5},{8,10},{9,11},{10,... | collective-permute-start | bytes 1179656 | tf_op jit(solution)/shard_map/ppermute | solution.py:246
  69.0 29.0 %collective-permute-start.11 = (bf16[48,2048]{1,0:T(8,128)(2,1)S(1)}, bf16[48,2048]{1,0:T(8,128)(2,1)S(1)}, u32[]{:S(2)}, u32[]{:S(2)}) collective-permute-start(bf16[48,2048]{1,0:T(8,128)(2,1)S(1)} %get-tuple-element.51.refs_0_), channel_id=1, source_target_pairs={{0,2},{1,3},{2,0},{3,1},{4,6},{5,7},{6,4},{7,5},{8,10},{9,11},{10,... | collective-permute-start | bytes 589832 | tf_op jit(solution)/shard_map/ppermute | solution.py:246
  98.2 2.1 %collective-permute-start.14 = (bf16[2,96,1536]{2,1,0:T(8,128)(2,1)S(1)}, bf16[2,96,1536]{2,1,0:T(8,128)(2,1)S(1)}, u32[]{:S(2)}, u32[]{:S(2)}) collective-permute-start(bf16[2,96,1536]{2,1,0:T(8,128)(2,1)S(1)} %get-tuple-element.52), channel_id=1, source_target_pairs={{0,1},{1,0},{2,3},{3,2},{4,5},{5,4},{6,7},{7,6},{8,9},{9,8},{10,11... | collective-permute-start | bytes 1769480 | tf_op jit(solution)/shard_map/ppermute | solution.py:243
  100.3 16.0 %collective-permute-start.15 = (bf16[2,48,1536]{2,1,0:T(8,128)(2,1)S(1)}, bf16[2,48,1536]{2,1,0:T(8,128)(2,1)S(1)}, u32[]{:S(2)}, u32[]{:S(2)}) collective-permute-start(bf16[2,48,1536]{2,1,0:T(8,128)(2,1)S(1)} %get-tuple-element.54), channel_id=1, source_target_pairs={{0,2},{1,3},{2,0},{3,1},{4,6},{5,7},{6,4},{7,5},{8,10},{9,11},{10,... | collective-permute-start | bytes 884744 | tf_op jit(solution)/shard_map/ppermute | solution.py:246
  100.9 2.1 %collective-permute-start.17 = (bf16[48,2048]{1,0:T(8,128)(2,1)S(1)}, bf16[48,2048]{1,0:T(8,128)(2,1)S(1)}, u32[]{:S(2)}, u32[]{:S(2)}) collective-permute-start(bf16[48,2048]{1,0:T(8,128)(2,1)S(1)} %get-tuple-element.51.refs_0_), channel_id=1, source_target_pairs={{0,1},{1,0},{2,3},{3,2},{4,5},{5,4},{6,7},{7,6},{8,9},{9,8},{10,11... | collective-permute-start | bytes 589832 | tf_op jit(solution)/shard_map/ppermute | solution.py:243
  101.4 14.9 %collective-permute-start.16 = (bf16[48,2048]{1,0:T(8,128)(2,1)S(1)}, bf16[48,2048]{1,0:T(8,128)(2,1)S(1)}, u32[]{:S(2)}, u32[]{:S(2)}) collective-permute-start(bf16[48,2048]{1,0:T(8,128)(2,1)S(1)} %get-tuple-element.55.refs_0_), channel_id=1, source_target_pairs={{0,2},{1,3},{2,0},{3,1},{4,6},{5,7},{6,4},{7,5},{8,10},{9,11},{10,... | collective-permute-start | bytes 589832 | tf_op jit(solution)/shard_map/ppermute | solution.py:246
  116.5 5.7 %collective-permute-start.19 = (bf16[48,1536]{1,0:T(8,128)(2,1)S(1)}, bf16[48,1536]{1,0:T(8,128)(2,1)S(1)}, u32[]{:S(2)}, u32[]{:S(2)}) collective-permute-start(bf16[48,1536]{1,0:T(8,128)(2,1)S(1)} %activate.7.refs_0_), channel_id=1, source_target_pairs={{0,2},{1,3},{2,0},{3,1},{4,6},{5,7},{6,4},{7,5},{8,10},{9,11},{10,... | collective-permute-start | bytes 442376 | tf_op jit(solution)/shard_map/ppermute | solution.py:246
  117.8 4.4 %collective-permute-start.22 = (bf16[48,2048]{1,0:T(8,128)(2,1)S(1)}, bf16[48,2048]{1,0:T(8,128)(2,1)S(1)}, u32[]{:S(2)}, u32[]{:S(2)}) collective-permute-start(bf16[48,2048]{1,0:T(8,128)(2,1)S(1)} %get-tuple-element.55.refs_0_), channel_id=1, source_target_pairs={{0,1},{1,0},{2,3},{3,2},{4,5},{5,4},{6,7},{7,6},{8,9},{9,8},{10,11... | collective-permute-start | bytes 589832 | tf_op jit(solution)/shard_map/ppermute | solution.py:243
  117.8 4.4 %collective-permute-start.23 = (bf16[48,2048]{1,0:T(8,128)(2,1)S(1)}, bf16[48,2048]{1,0:T(8,128)(2,1)S(1)}, u32[]{:S(2)}, u32[]{:S(2)}) collective-permute-start(bf16[48,2048]{1,0:T(8,128)(2,1)S(1)} %collective-permute-done.16.refs_2_.refs_1_), channel_id=1, source_target_pairs={{0,1},{1,0},{2,3},{3,2},{4,5},{5,4},{6,7},{7,6},{8,9},{9,8},{10,11... | collective-permute-start | bytes 589832 | tf_op jit(solution)/shard_map/ppermute | solution.py:243
  118.3 17.3 %collective-permute-start.20 = (bf16[48,1536]{1,0:T(8,128)(2,1)S(1)}, bf16[48,1536]{1,0:T(8,128)(2,1)S(1)}, u32[]{:S(2)}, u32[]{:S(2)}) collective-permute-start(bf16[48,1536]{1,0:T(8,128)(2,1)S(1)} %activate.7.refs_0_), channel_id=1, source_target_pairs={{0,1},{1,0},{2,3},{3,2},{4,5},{5,4},{6,7},{7,6},{8,9},{9,8},{10,11... | collective-permute-start | bytes 442376 | tf_op jit(solution)/shard_map/ppermute | solution.py:243
  122.2 13.4 %collective-permute-start.21 = (bf16[48,1536]{1,0:T(8,128)(2,1)S(1)}, bf16[48,1536]{1,0:T(8,128)(2,1)S(1)}, u32[]{:S(2)}, u32[]{:S(2)}) collective-permute-start(bf16[48,1536]{1,0:T(8,128)(2,1)S(1)} %collective-permute-done.19.refs_1_), channel_id=1, source_target_pairs={{0,1},{1,0},{2,3},{3,2},{4,5},{5,4},{6,7},{7,6},{8,9},{9,8},{10,11... | collective-permute-start | bytes 442376 | tf_op jit(solution)/shard_map/ppermute | solution.py:243
  150.0 8.1 %collective-permute-start.26 = (bf16[64,2048]{1,0:T(8,128)(2,1)S(1)}, bf16[64,2048]{1,0:T(8,128)(2,1)S(1)}, u32[]{:S(2)}, u32[]{:S(2)}) collective-permute-start(bf16[64,2048]{1,0:T(8,128)(2,1)S(1)} %get-tuple-element.59), channel_id=1, source_target_pairs={{0,4},{12,8},{1,5},{13,9},{2,6},{14,10},{3,7},{15,11},{16,20},{28,... | collective-permute-start | bytes 786440 | tf_op jit(solution)/shard_map/ppermute | solution.py:240
  151.5 12.0 %collective-permute-start.25 = (bf16[64,2048]{1,0:T(8,128)(2,1)S(1)}, bf16[64,2048]{1,0:T(8,128)(2,1)S(1)}, u32[]{:S(2)}, u32[]{:S(2)}) collective-permute-start(bf16[64,2048]{1,0:T(8,128)(2,1)S(1)} %get-tuple-element.59), channel_id=1, source_target_pairs={{4,8},{8,4},{5,9},{9,5},{6,10},{10,6},{7,11},{11,7},{20,24},{24,20... | collective-permute-start | bytes 786440 | tf_op jit(solution)/shard_map/ppermute | solution.py:240
  152.2 11.5 %collective-permute-start.24 = (bf16[64,2048]{1,0:T(8,128)(2,1)S(1)}, bf16[64,2048]{1,0:T(8,128)(2,1)S(1)}, u32[]{:S(2)}, u32[]{:S(2)}) collective-permute-start(bf16[64,2048]{1,0:T(8,128)(2,1)S(1)} %get-tuple-element.58), channel_id=1, source_target_pairs={{0,4},{4,0},{8,12},{12,8},{1,5},{5,1},{9,13},{13,9},{2,6},{6,2},{1... | collective-permute-start | bytes 786440 | tf_op jit(solution)/shard_map/ppermute | solution.py:240
  158.1 17.0 %collective-permute-start.27 = (bf16[64,2048]{1,0:T(8,128)(2,1)S(1)}, bf16[64,2048]{1,0:T(8,128)(2,1)S(1)}, u32[]{:S(2)}, u32[]{:S(2)}) collective-permute-start(bf16[64,2048]{1,0:T(8,128)(2,1)S(1)} %add_convert_fusion.1), channel_id=1, source_target_pairs={{0,8},{4,12},{8,0},{12,4},{1,9},{5,13},{9,1},{13,5},{2,10},{6,14},... | collective-permute-start | bytes 786440 | tf_op jit(solution)/shard_map/ppermute | solution.py:240
  (12 other events, 60.7 us)

commit v5 on v2

--- a/solution.py
+++ b/solution.py
@@ -56,6 +56,7 @@
         out_shape=[jax.ShapeDtypeStruct((live, slots), BF16), jax.ShapeDtypeStruct((slots, live), BF16)],
         in_specs=[pl.BlockSpec(memory_space=pltpu.SMEM)],
         cost_estimate=pl.CostEstimate(flops=0, bytes_accessed=4 * live * slots, transcendentals=0),
+        compiler_params=pltpu.CompilerParams(vmem_limit_bytes=8 * MIB),
         name="picks",
     )(lengths)
 
@@ -80,6 +81,7 @@
         cost_estimate=pl.CostEstimate(
             flops=2 * pick.size * flat[0].shape[1], bytes_accessed=2 * pick.size, transcendentals=0
         ),
+        compiler_params=pltpu.CompilerParams(vmem_limit_bytes=8 * MIB),
         name="compact",
     )(pick, *flat)
 
@@ -106,7 +108,7 @@
         in_specs=[pl.BlockSpec((live, depth), lambda j: (0, 0)), weight, weight]
         + [pl.BlockSpec(memory_space=pl.ANY)] * len(after),
         out_specs=[out, out],
-        compiler_params=pltpu.CompilerParams(vmem_limit_bytes=32 * MIB),
+        compiler_params=pltpu.CompilerParams(vmem_limit_bytes=40 * MIB),
         cost_estimate=pl.CostEstimate(
             flops=0, bytes_accessed=0, transcendentals=0
         ),
@@ -114,8 +116,55 @@
     )(tok, gate_weight, up_weight, *after)
 
 
-def down_kernel(n_h, first, last, *refs):
-    h_refs, w_ref, refs = refs[:n_h], refs[n_h], refs[n_h + 1:]
+def join_kernel(n_handed, n_after, nx, keep_ref, got_ref, *refs):
+    out_refs = refs[n_handed + n_after:][:nx]
+    quarter = out_refs[0].shape[1]
+    for k, out_ref in enumerate(out_refs):
+        rows = pl.ds(k * quarter, quarter)
+        out_ref[...] = (keep_ref[:, rows] + got_ref[:, rows].astype(F32)).astype(out_ref.dtype)
+
+
+def join(keep, got, handed, after, nx):
+    two, half, width = keep.shape
+    shape = (two, half // nx, width)
+    held, anywhere = pl.BlockSpec(memory_space=pltpu.VMEM), pl.BlockSpec(memory_space=pl.ANY)
+    out = pl.pallas_call(
+        functools.partial(join_kernel, len(handed), len(after), nx),
+        out_shape=[jax.ShapeDtypeStruct(shape, BF16 if k else F32) for k in range(nx)]
+        + [jax.ShapeDtypeStruct(a.shape, a.dtype) for a in handed],
+        in_specs=[held, held] + [anywhere] * (len(handed) + len(after)),
+        out_specs=[held] * nx + [anywhere] * len(handed),
+        input_output_aliases={2 + i: nx + i for i in range(len(handed))},
+        compiler_params=pltpu.CompilerParams(vmem_limit_bytes=8 * MIB),
+        cost_estimate=pl.CostEstimate(flops=0, bytes_accessed=0, transcendentals=0),
+        name="join",
+    )(keep, got, *handed, *after)
+    return out[0], out[1:nx], out[nx:]
+
+
+def activate_kernel(n_got, mine_ref, *refs):
+    both = mine_ref[...]
+    for got_ref in refs[:n_got]:
+        both = both + got_ref[...].astype(F32)
+    gate, up = both[0], both[1]
+    refs[-1][...] = (gate / (1.0 + jnp.exp(-gate)) * up).astype(BF16)
+
+
+def activate(mine, got, after):
+    held, anywhere = pl.BlockSpec(memory_space=pltpu.VMEM), pl.BlockSpec(memory_space=pl.ANY)
+    return pl.pallas_call(
+        functools.partial(activate_kernel, len(got)),
+        out_shape=jax.ShapeDtypeStruct(mine.shape[1:], BF16),
+        in_specs=[held] * (1 + len(got)) + [anywhere] * len(after),
+        out_specs=held,
+        compiler_params=pltpu.CompilerParams(vmem_limit_bytes=8 * MIB),
+        cost_estimate=pl.CostEstimate(flops=0, bytes_accessed=0, transcendentals=0),
+        name="activate",
+    )(mine, *got, *after)
+
+
+def down_kernel(n_h, n_after, first, last, *refs):
+    h_refs, w_ref, refs = refs[:n_h], refs[n_h], refs[n_h + 1 + n_after:]
     h = jnp.concatenate([r[...] for r in h_refs], axis=0)
     total = jnp.dot(h, w_ref[...], preferred_element_type=F32)
     if not first:
@@ -131,7 +180,7 @@
         out_ref[...] = spread[k * rows:(k + 1) * rows]
 
 
-def down(hidden, down_weight, total, pick, start, width, n_gx):
+def down(hidden, down_weight, total, pick, after, start, width, n_gx):
     live = sum(h.shape[0] for h in hidden)
     out_width = down_weight.shape[1]
     tile = min(out_width, 512)
@@ -139,7 +188,13 @@
     rows = pl.BlockSpec((live, tile), lambda j: (0, j))
     operands = [*hidden, down_weight]
     in_specs = [pl.BlockSpec(h.shape, lambda j: (0, 0)) for h in hidden]
-    in_specs.append(pl.BlockSpec((pl.Element(width), pl.Element(tile)), lambda j: (start, j * tile)))
+    in_specs.append(
+        pl.BlockSpec(
+            (pl.Element(width), pl.Element(tile)), lambda j: (start, j * tile)
+        )
+    )
+    operands += after
+    in_specs += [pl.BlockSpec(memory_space=pl.ANY)] * len(after)
     if total is not None:
         operands.append(total)
         in_specs.append(rows)
@@ -152,12 +207,12 @@
     else:
         out_shape, out_specs = jax.ShapeDtypeStruct((live, out_width), F32), rows
     return pl.pallas_call(
-        functools.partial(down_kernel, len(hidden), total is None, last),
+        functools.partial(down_kernel, len(hidden), len(after), total is None, last),
         out_shape=out_shape,
         grid=(out_width // tile,),
         in_specs=in_specs,
         out_specs=out_specs,
-        compiler_params=pltpu.CompilerParams(vmem_limit_bytes=32 * MIB),
+        compiler_params=pltpu.CompilerParams(vmem_limit_bytes=40 * MIB),
         cost_estimate=pl.CostEstimate(
             flops=0, bytes_accessed=0, transcendentals=0
         ),
@@ -167,7 +222,7 @@
 
 def column_chunks(cols, tile):
     tiles = cols // tile
-    shares = (3, 5, 5)
+    shares = (2, 4, 4, 3)
     edges = [round(tiles * sum(shares[:i]) / sum(shares)) for i in range(len(shares) + 1)]
     return [(a * tile, (b - a) * tile) for a, b in zip(edges, edges[1:]) if b > a]
 
@@ -201,21 +256,35 @@
         blocks = [[tokens]] + [[over_z(tokens, k)] for k in range(1, n_gx)]
     tok = compact(pick_in, blocks)
 
-    total, after = None, []
-    for i, (start, width) in enumerate(chunks):
-        send, keep = gate_up(tok, gate_weight, up_weight, after, start, width, tile)
-        sums = keep + over_core(send).astype(F32)
-        mine = sums[:, :quarter]
-        after = []
-        for k in range(1, nx):
-            block = sums[:, k * quarter:(k + 1) * quarter].astype(BF16)
-            after.append(block)
-            mine = mine + over_x(block, k).astype(F32)
-        own = (jax.nn.silu(mine[0]) * mine[1]).astype(BF16)
-        hidden = [own] + [over_x(own, -k) for k in range(1, nx)]
-        hidden += [over_core(h) for h in hidden]
-        last = i == len(chunks) - 1
-        total = down(hidden, down_weight, total, pick_out if last else None, start, width, n_gx)
+    n = len(chunks)
+    first = [gate_up(tok, gate_weight, up_weight, [], *chunk, tile) for chunk in chunks[:2]]
+    sends, keeps = [list(a) for a in zip(*first)]
+    owns, fars, totals = [], [], []
+
+    def add_down(after):
+        i = len(totals)
+        h = [owns[i]] + fars[i]
+        h = h + [over_core(a) for a in h]
+        pick = pick_out if i == n - 1 else None
+        totals.append(down(h, down_weight, totals[-1] if totals else None, pick, after, *chunks[i], n_gx))
+
+    for j in range(n):
+        after = owns[j - 1:] + (fars[j - 2] if j >= 2 else []) + totals[-1:]
+        mine, blocks, handed = join(keeps[j], over_core(sends[j]), sends[j + 1:j + 2], after, nx)
+        sends[j + 1:j + 2] = handed
+        got = [over_x(b, k + 1) for k, b in enumerate(blocks)]
+        if j + 2 < n:
+            send, keep = gate_up(tok, gate_weight, up_weight, blocks, *chunks[j + 2], tile)
+            sends.append(send)
+            keeps.append(keep)
+        elif j >= n - 2 and len(totals) < n - 1:
+            add_down(list(blocks))
+        own = activate(mine, got, totals[-1:])
+        owns.append(own)
+        fars.append([over_x(own, -k) for k in range(1, nx)])
+    while len(totals) < n:
+        add_down([])
+    total = totals[-1]
 
     if n_gx == 4:
         ends = over_z(total[3], 1, (0, 3))

time: 140 us -> 133 us (0.950)
  waiting for transfers between devices: 59.8 us -> 51.2 us
  starting transfers between devices: 27.6 us -> 29.5 us
    ppermute x6 -> x8, waiting for transfers between devices: 26.2 us -> 19.9 us  [over_x(): lax.ppermute(block, 'gy', [(i, (i + 2 * k) % n_gy) for i in range(n_gy)])]
    pallas_call x3 -> x12, Pallas kernels: 17 us -> 20.4 us  [the longest x4 19.5 us: down(): pl.pallas_call(functools.partial(down_kernel, len(hidden), len(after), to...]
    ppermute x9 -> x12, waiting for transfers between devices: 4.24 us -> 0.97 us  [over_core(): return lax.ppermute(block, 'gy', [(i, i ^ 1) for i in range(n_gy)])]
    pallas_call x1, Pallas kernels: 2.59 us -> 0.37 us  [compact(): pl.pallas_call(functools.partial(compact_kernel, [len(group) for group in...]
    ppermute x6 -> x8, starting transfers between devices: 7.51 us -> 8.36 us  [over_x(): lax.ppermute(block, 'gy', [(i, (i + 2 * k) % n_gy) for i in range(n_gy)])]
    pallas_call x3 -> x4, Pallas kernels: 26.6 us -> 27.4 us  [gate_up(): pl.pallas_call(gate_up_kernel, out_shape=[jax.ShapeDtypeStruct((2, half,...]
  transfers between devices with their start and end apart: 23 -> 28, of which waited for: 13 -> 14; matrix products, arithmetic and copies ran while one was open for 1% -> 0% of each run, Pallas kernels for 16% -> 29%
where the time goes in v5:
time: 133 us; the launch traced here: 132 us
  waiting for transfers between devices  51.2 us (38%)
  Pallas kernels  48.8 us (37%)
  starting transfers between devices  29.5 us (22%)
  local copies, waits for them, and re-layouts  1.6 us (1%)
    ppermute x8, waiting for transfers between devices, over_z(): return lax.ppermute(block, 'gx', [(z, z ^ k) for z in among])  30.3 us
    pallas_call x4, Pallas kernels, gate_up(): pl.pallas_call(gate_up_kernel, out_shape=[jax.ShapeDtypeStruct((2, half,...  27.4 us
    ppermute x8, waiting for transfers between devices, over_x(): lax.ppermute(block, 'gy', [(i, (i + 2 * k) % n_gy) for i in range(n_gy)])  19.9 us
    pallas_call x4, Pallas kernels, down(): pl.pallas_call(functools.partial(down_kernel, len(hidden), len(after), to...  19.5 us
    ppermute x8, starting transfers between devices, over_z(): return lax.ppermute(block, 'gx', [(z, z ^ k) for z in among])  18.9 us
    ppermute x8, starting transfers between devices, over_x(): lax.ppermute(block, 'gy', [(i, (i + 2 * k) % n_gy) for i in range(n_gy)])  8.36 us
  transfers between devices with their start and end apart: 28, of which 14 were waited for; matrix products, arithmetic and copies ran while one was open for 0% of the time, Pallas kernels for 29%

profile of v5, /device:TPU:0, one launch (start us, length us, event | category | flops | bytes accessed | tf_op | source)
XLA Modules:
  0.0 132.3 jit_solution(8930937077023000440)
XLA Ops:
  0.0 4.0 %collective-permute-start.1 = (bf16[64,2048]{1,0:T(8,128)(2,1)}, bf16[64,2048]{1,0:T(8,128)(2,1)S(1)}, u32[]{:S(2)}, u32[]{:S(2)}) collective-permute-start(bf16[64,2048]{1,0:T(8,128)(2,1)} %refs_0_.1), channel_id=1, source_target_pairs={{0,8},{4,12},{8,0},{12,4},{1,9},{5,13},{9,1},{13,5},{2,10},{6,14},... | collective-permute-start | bytes 786440 | tf_op jit(solution)/shard_map/ppermute | solution.py:240
  4.0 1.6 %collective-permute-start = (bf16[64,2048]{1,0:T(8,128)(2,1)}, bf16[64,2048]{1,0:T(8,128)(2,1)S(1)}, u32[]{:S(2)}, u32[]{:S(2)}) collective-permute-start(bf16[64,2048]{1,0:T(8,128)(2,1)} %refs_0_.1), channel_id=1, source_target_pairs={{0,4},{4,0},{8,12},{12,8},{1,5},{5,1},{9,13},{13,9},{2,6},{6,2},{1... | collective-permute-start | bytes 786440 | tf_op jit(solution)/shard_map/ppermute | solution.py:240
  6.3 10.8 %collective-permute-done.1.refs_2_ = bf16[64,2048]{1,0:T(8,128)(2,1)S(1)} collective-permute-done((bf16[64,2048]{1,0:T(8,128)(2,1)}, bf16[64,2048]{1,0:T(8,128)(2,1)S(1)}, u32[]{:S(2)}, u32[]{:S(2)}) %collective-permute-start.1) | collective-permute-done | bytes 262176 | tf_op jit(solution)/shard_map/ppermute | solution.py:240
  19.7 5.9 %collective-permute-done.3.refs_4_ = bf16[64,2048]{1,0:T(8,128)(2,1)S(1)} collective-permute-done((bf16[64,2048]{1,0:T(8,128)(2,1)S(1)}, bf16[64,2048]{1,0:T(8,128)(2,1)S(1)}, u32[]{:S(2)}, u32[]{:S(2)}) %collective-permute-start.3) | collective-permute-done | bytes 262176 | tf_op jit(solution)/shard_map/ppermute | solution.py:240
  26.9 4.6 %gate_up.5 = (bf16[2,96,1024]{2,1,0:T(8,128)(2,1)S(1)}, f32[2,96,1024]{2,1,0:T(8,128)S(1)}) custom-call(bf16[192,2048]{1,0:T(8,128)(2,1)S(1)} %compact.1.tok_ref, bf16[2048,6656]{1,0:T(8,128)(2,1)} %gate_ref.7, bf16[2048,6656]{1,0:T(8,128)(2,1)} %up_ref.7), custom_call_target="tpu_custom_call" | custom-call | tf_op jit(solution)/shard_map/gate_up/pallas_call | solution.py:104
  31.6 8.1 %gate_up.4 = (bf16[2,96,2048]{2,1,0:T(8,128)(2,1)S(1)}, f32[2,96,2048]{2,1,0:T(8,128)S(1)}) custom-call(bf16[192,2048]{1,0:T(8,128)(2,1)S(1)} %compact.1.tok_ref, bf16[2048,6656]{1,0:T(8,128)(2,1)} %gate_ref.7, bf16[2048,6656]{1,0:T(8,128)(2,1)} %up_ref.7), custom_call_target="tpu_custom_call" | custom-call | tf_op jit(solution)/shard_map/gate_up/pallas_call | solution.py:104
  40.3 1.5 %collective-permute-start.6 = (bf16[2,48,1024]{2,1,0:T(8,128)(2,1)S(1)}, bf16[2,48,1024]{2,1,0:T(8,128)(2,1)S(1)}, u32[]{:S(2)}, u32[]{:S(2)}) collective-permute-start(bf16[2,48,1024]{2,1,0:T(8,128)(2,1)S(1)} %get-tuple-element.36.refs_0_), channel_id=1, source_target_pairs={{0,2},{1,3},{2,0},{3,1},{4,6},{5,7},{6,4},{7,5},{8,10},{9,11},{10,... | collective-permute-start | bytes 589832 | tf_op jit(solution)/shard_map/ppermute | solution.py:246
  41.8 8.1 %gate_up.6 = (bf16[2,96,2048]{2,1,0:T(8,128)(2,1)S(1)}, f32[2,96,2048]{2,1,0:T(8,128)S(1)}) custom-call(bf16[192,2048]{1,0:T(8,128)(2,1)S(1)} %compact.1.tok_ref, bf16[2048,6656]{1,0:T(8,128)(2,1)} %gate_ref.7, bf16[2048,6656]{1,0:T(8,128)(2,1)} %up_ref.7, bf16[2,48,1024]{2,1,0:T(8,128)(2,1)S(1)} %get-tuple-element.36.refs_0_), custom_call_target="tpu_custom_call" | custom-call | tf_op jit(solution)/shard_map/gate_up/pallas_call | solution.py:104
  50.8 1.5 %collective-permute-start.9 = (bf16[48,1024]{1,0:T(8,128)(2,1)S(1)}, bf16[48,1024]{1,0:T(8,128)(2,1)S(1)}, u32[]{:S(2)}, u32[]{:S(2)}) collective-permute-start(bf16[48,1024]{1,0:T(8,128)(2,1)S(1)} %activate.4.refs_1_.refs_0_), channel_id=1, source_target_pairs={{0,2},{1,3},{2,0},{3,1},{4,6},{5,7},{6,4},{7,5},{8,10},{9,11},{10,... | collective-permute-start | bytes 294920 | tf_op jit(solution)/shard_map/ppermute | solution.py:246
  52.3 6.6 %gate_up.7 = (bf16[2,96,1536]{2,1,0:T(8,128)(2,1)S(1)}, f32[2,96,1536]{2,1,0:T(8,128)S(1)}) custom-call(bf16[192,2048]{1,0:T(8,128)(2,1)S(1)} %compact.1.tok_ref, bf16[2048,6656]{1,0:T(8,128)(2,1)} %gate_ref.7, bf16[2048,6656]{1,0:T(8,128)(2,1)} %up_ref.7, bf16[2,48,2048]{2,1,0:T(8,128)(2,1)S(1)} %get-tuple-element.39.refs_0_), custom_call_target="tpu_custom_call" | custom-call | tf_op jit(solution)/shard_map/gate_up/pallas_call | solution.py:104
  59.0 3.2 %collective-permute-done.8.refs_0_ = bf16[2,48,2048]{2,1,0:T(8,128)(2,1)S(1)} collective-permute-done((bf16[2,48,2048]{2,1,0:T(8,128)(2,1)S(1)}, bf16[2,48,2048]{2,1,0:T(8,128)(2,1)S(1)}, u32[]{:S(2)}, u32[]{:S(2)}) %collective-permute-start.8) | collective-permute-done | bytes 393248 | tf_op jit(solution)/shard_map/ppermute | solution.py:246
  64.6 1.5 %collective-permute-start.14 = (bf16[48,2048]{1,0:T(8,128)(2,1)S(1)}, bf16[48,2048]{1,0:T(8,128)(2,1)S(1)}, u32[]{:S(2)}, u32[]{:S(2)}) collective-permute-start(bf16[48,2048]{1,0:T(8,128)(2,1)S(1)} %activate.5.refs_1_.refs_0_), channel_id=1, source_target_pairs={{0,2},{1,3},{2,0},{3,1},{4,6},{5,7},{6,4},{7,5},{8,10},{9,11},{10,... | collective-permute-start | bytes 589832 | tf_op jit(solution)/shard_map/ppermute | solution.py:246
  67.6 3.8 %down.4.refs_1_.refs_2_.refs_6_ = f32[192,2048]{1,0:T(8,128)S(1)} custom-call(bf16[48,1024]{1,0:T(8,128)(2,1)S(1)} %activate.4.refs_1_.refs_0_, bf16[48,1024]{1,0:T(8,128)(2,1)S(1)} %collective-permute-done.9.refs_2_.refs_1_, bf16[48,1024]{1,0:T(8,128)(2,1)S(1)} %collective-permute-done.12.refs_2_, bf16[48,1024]{1,0:T(8,128)(2,1)S(1)} %collective-permute-done.13.refs_3_, ...), custom_call_target="tpu_custom_call" | custom-call | tf_op jit(solution)/shard_map/down/pallas_call | solution.py:209
  71.4 4.6 %collective-permute-done.11.refs_0_ = bf16[2,48,2048]{2,1,0:T(8,128)(2,1)S(1)} collective-permute-done((bf16[2,48,2048]{2,1,0:T(8,128)(2,1)S(1)}, bf16[2,48,2048]{2,1,0:T(8,128)(2,1)S(1)}, u32[]{:S(2)}, u32[]{:S(2)}) %collective-permute-start.11) | collective-permute-done | bytes 393248 | tf_op jit(solution)/shard_map/ppermute | solution.py:246
  76.2 3.6 %collective-permute-done.14.refs_1_ = bf16[48,2048]{1,0:T(8,128)(2,1)S(1)} collective-permute-done((bf16[48,2048]{1,0:T(8,128)(2,1)S(1)}, bf16[48,2048]{1,0:T(8,128)(2,1)S(1)}, u32[]{:S(2)}, u32[]{:S(2)}) %collective-permute-start.14) | collective-permute-done | bytes 196640 | tf_op jit(solution)/shard_map/ppermute | solution.py:246
  82.6 5.2 %down.5.refs_1_.refs_5_ = f32[192,2048]{1,0:T(8,128)S(1)} custom-call(bf16[48,2048]{1,0:T(8,128)(2,1)S(1)} %activate.5.refs_1_.refs_0_, bf16[48,2048]{1,0:T(8,128)(2,1)S(1)} %collective-permute-done.14.refs_1_, bf16[48,2048]{1,0:T(8,128)(2,1)S(1)} %collective-permute-done.16.refs_2_, bf16[48,2048]{1,0:T(8,128)(2,1)S(1)} %collective-permute-done.17.refs_3_, ...), custom_call_target="tpu_custom_call" | custom-call | tf_op jit(solution)/shard_map/down/pallas_call | solution.py:209
  87.8 2.1 %collective-permute-done.15.refs_0_ = bf16[2,48,1536]{2,1,0:T(8,128)(2,1)S(1)} collective-permute-done((bf16[2,48,1536]{2,1,0:T(8,128)(2,1)S(1)}, bf16[2,48,1536]{2,1,0:T(8,128)(2,1)S(1)}, u32[]{:S(2)}, u32[]{:S(2)}) %collective-permute-start.15) | collective-permute-done | bytes 294944 | tf_op jit(solution)/shard_map/ppermute | solution.py:246
  90.6 3.5 %collective-permute-done.21.refs_1_ = bf16[48,2048]{1,0:T(8,128)(2,1)S(1)} collective-permute-done((bf16[48,2048]{1,0:T(8,128)(2,1)S(1)}, bf16[48,2048]{1,0:T(8,128)(2,1)S(1)}, u32[]{:S(2)}, u32[]{:S(2)}) %collective-permute-start.21) | collective-permute-done | bytes 196640 | tf_op jit(solution)/shard_map/ppermute | solution.py:246
  96.0 5.3 %down.6.refs_5_ = f32[192,2048]{1,0:T(8,128)S(1)} custom-call(bf16[48,2048]{1,0:T(8,128)(2,1)S(1)} %activate.6.refs_0_, bf16[48,2048]{1,0:T(8,128)(2,1)S(1)} %collective-permute-done.21.refs_1_, bf16[48,2048]{1,0:T(8,128)(2,1)S(1)} %collective-permute-done.22.refs_2_, bf16[48,2048]{1,0:T(8,128)(2,1)S(1)} %collective-permute-done.23.refs_3_, ...), custom_call_target="tpu_custom_call" | custom-call | tf_op jit(solution)/shard_map/down/pallas_call | solution.py:209
  101.3 5.2 %down.7 = (bf16[64,2048]{1,0:T(8,128)(2,1)S(1)}, bf16[64,2048]{1,0:T(8,128)(2,1)S(1)}, bf16[64,2048]{1,0:T(8,128)(2,1)S(1)}, bf16[64,2048]{1,0:T(8,128)(2,1)S(1)}) custom-call(bf16[48,1536]{1,0:T(8,128)(2,1)S(1)} %activate.7.refs_0_, bf16[48,1536]{1,0:T(8,128)(2,1)S(1)} %collective-permute-done.18.refs_1_, ...), custom_call_target="tpu_custom_call" | custom-call | tf_op jit(solution)/shard_map/down/pallas_call | solution.py:209
  108.6 3.9 %collective-permute-start.24 = (bf16[64,2048]{1,0:T(8,128)(2,1)S(1)}, bf16[64,2048]{1,0:T(8,128)(2,1)S(1)}, u32[]{:S(2)}, u32[]{:S(2)}) collective-permute-start(bf16[64,2048]{1,0:T(8,128)(2,1)S(1)} %get-tuple-element.52), channel_id=1, source_target_pairs={{0,4},{4,0},{8,12},{12,8},{1,5},{5,1},{9,13},{13,9},{2,6},{6,2},{1... | collective-permute-start | bytes 786440 | tf_op jit(solution)/shard_map/ppermute | solution.py:240
  112.5 2.0 %collective-permute-done.26 = bf16[64,2048]{1,0:T(8,128)(2,1)S(1)} collective-permute-done((bf16[64,2048]{1,0:T(8,128)(2,1)S(1)}, bf16[64,2048]{1,0:T(8,128)(2,1)S(1)}, u32[]{:S(2)}, u32[]{:S(2)}) %collective-permute-start.26) | collective-permute-done | bytes 262176 | tf_op jit(solution)/shard_map/ppermute | solution.py:240
  114.6 5.2 %collective-permute-start.27 = (bf16[64,2048]{1,0:T(8,128)(2,1)S(1)}, bf16[64,2048]{1,0:T(8,128)(2,1)S(1)}, u32[]{:S(2)}, u32[]{:S(2)}) collective-permute-start(bf16[64,2048]{1,0:T(8,128)(2,1)S(1)} %add_convert_fusion.1), channel_id=1, source_target_pairs={{0,8},{4,12},{8,0},{12,4},{1,9},{5,13},{9,1},{13,5},{2,10},{6,14},... | collective-permute-start | bytes 786440 | tf_op jit(solution)/shard_map/ppermute | solution.py:240
  120.1 11.4 %collective-permute-done.27 = bf16[64,2048]{1,0:T(8,128)(2,1)S(1)} collective-permute-done((bf16[64,2048]{1,0:T(8,128)(2,1)S(1)}, bf16[64,2048]{1,0:T(8,128)(2,1)S(1)}, u32[]{:S(2)}, u32[]{:S(2)}) %collective-permute-start.27) | collective-permute-done | bytes 262176 | tf_op jit(solution)/shard_map/ppermute | solution.py:240
  (56 shorter events, 18.7 us)
Async XLA Ops:
  0.0 17.0 %collective-permute-start.1 = (bf16[64,2048]{1,0:T(8,128)(2,1)}, bf16[64,2048]{1,0:T(8,128)(2,1)S(1)}, u32[]{:S(2)}, u32[]{:S(2)}) collective-permute-start(bf16[64,2048]{1,0:T(8,128)(2,1)} %refs_0_.1), channel_id=1, source_target_pairs={{0,8},{4,12},{8,0},{12,4},{1,9},{5,13},{9,1},{13,5},{2,10},{6,14},... | collective-permute-start | bytes 786440 | tf_op jit(solution)/shard_map/ppermute | solution.py:240
  4.0 15.6 %collective-permute-start = (bf16[64,2048]{1,0:T(8,128)(2,1)}, bf16[64,2048]{1,0:T(8,128)(2,1)S(1)}, u32[]{:S(2)}, u32[]{:S(2)}) collective-permute-start(bf16[64,2048]{1,0:T(8,128)(2,1)} %refs_0_.1), channel_id=1, source_target_pairs={{0,4},{4,0},{8,12},{12,8},{1,5},{5,1},{9,13},{13,9},{2,6},{6,2},{1... | collective-permute-start | bytes 786440 | tf_op jit(solution)/shard_map/ppermute | solution.py:240
  5.6 14.1 %collective-permute-start.2 = (bf16[64,2048]{1,0:T(8,128)(2,1)}, bf16[64,2048]{1,0:T(8,128)(2,1)S(1)}, u32[]{:S(2)}, u32[]{:S(2)}) collective-permute-start(bf16[64,2048]{1,0:T(8,128)(2,1)} %refs_0_.1), channel_id=1, source_target_pairs={{4,8},{8,4},{5,9},{9,5},{6,10},{10,6},{7,11},{11,7},{20,24},{24,20... | collective-permute-start | bytes 786440 | tf_op jit(solution)/shard_map/ppermute | solution.py:240
  17.0 8.5 %collective-permute-start.3 = (bf16[64,2048]{1,0:T(8,128)(2,1)S(1)}, bf16[64,2048]{1,0:T(8,128)(2,1)S(1)}, u32[]{:S(2)}, u32[]{:S(2)}) collective-permute-start(bf16[64,2048]{1,0:T(8,128)(2,1)S(1)} %collective-permute-done.1.refs_2_), channel_id=1, source_target_pairs={{4,0},{8,12},{5,1},{9,13},{6,2},{10,14},{7,3},{11,15},{20,16},{24,... | collective-permute-start | bytes 786440 | tf_op jit(solution)/shard_map/ppermute | solution.py:240
  31.5 8.2 %collective-permute-start.4 = (bf16[2,96,1024]{2,1,0:T(8,128)(2,1)S(1)}, bf16[2,96,1024]{2,1,0:T(8,128)(2,1)S(1)}, u32[]{:S(2)}, u32[]{:S(2)}) collective-permute-start(bf16[2,96,1024]{2,1,0:T(8,128)(2,1)S(1)} %get-tuple-element.33), channel_id=1, source_target_pairs={{0,1},{1,0},{2,3},{3,2},{4,5},{5,4},{6,7},{7,6},{8,9},{9,8},{10,11... | collective-permute-start | bytes 1179656 | tf_op jit(solution)/shard_map/ppermute | solution.py:243
  39.8 10.2 %collective-permute-start.5 = (bf16[2,96,2048]{2,1,0:T(8,128)(2,1)S(1)}, bf16[2,96,2048]{2,1,0:T(8,128)(2,1)S(1)}, u32[]{:S(2)}, u32[]{:S(2)}) collective-permute-start(bf16[2,96,2048]{2,1,0:T(8,128)(2,1)S(1)} %get-tuple-element.35), channel_id=1, source_target_pairs={{0,1},{1,0},{2,3},{3,2},{4,5},{5,4},{6,7},{7,6},{8,9},{9,8},{10,11... | collective-permute-start | bytes 2359304 | tf_op jit(solution)/shard_map/ppermute | solution.py:243
  40.3 9.6 %collective-permute-start.6 = (bf16[2,48,1024]{2,1,0:T(8,128)(2,1)S(1)}, bf16[2,48,1024]{2,1,0:T(8,128)(2,1)S(1)}, u32[]{:S(2)}, u32[]{:S(2)}) collective-permute-start(bf16[2,48,1024]{2,1,0:T(8,128)(2,1)S(1)} %get-tuple-element.36.refs_0_), channel_id=1, source_target_pairs={{0,2},{1,3},{2,0},{3,1},{4,6},{5,7},{6,4},{7,5},{8,10},{9,11},{10,... | collective-permute-start | bytes 589832 | tf_op jit(solution)/shard_map/ppermute | solution.py:246
  50.2 13.7 %collective-permute-start.7 = (bf16[2,96,2048]{2,1,0:T(8,128)(2,1)S(1)}, bf16[2,96,2048]{2,1,0:T(8,128)(2,1)S(1)}, u32[]{:S(2)}, u32[]{:S(2)}) collective-permute-start(bf16[2,96,2048]{2,1,0:T(8,128)(2,1)S(1)} %get-tuple-element.42), channel_id=1, source_target_pairs={{0,1},{1,0},{2,3},{3,2},{4,5},{5,4},{6,7},{7,6},{8,9},{9,8},{10,11... | collective-permute-start | bytes 2359304 | tf_op jit(solution)/shard_map/ppermute | solution.py:243
  50.2 12.0 %collective-permute-start.8 = (bf16[2,48,2048]{2,1,0:T(8,128)(2,1)S(1)}, bf16[2,48,2048]{2,1,0:T(8,128)(2,1)S(1)}, u32[]{:S(2)}, u32[]{:S(2)}) collective-permute-start(bf16[2,48,2048]{2,1,0:T(8,128)(2,1)S(1)} %get-tuple-element.39.refs_0_), channel_id=1, source_target_pairs={{0,2},{1,3},{2,0},{3,1},{4,6},{5,7},{6,4},{7,5},{8,10},{9,11},{10,... | collective-permute-start | bytes 1179656 | tf_op jit(solution)/shard_map/ppermute | solution.py:246
  50.8 13.1 %collective-permute-start.9 = (bf16[48,1024]{1,0:T(8,128)(2,1)S(1)}, bf16[48,1024]{1,0:T(8,128)(2,1)S(1)}, u32[]{:S(2)}, u32[]{:S(2)}) collective-permute-start(bf16[48,1024]{1,0:T(8,128)(2,1)S(1)} %activate.4.refs_1_.refs_0_), channel_id=1, source_target_pairs={{0,2},{1,3},{2,0},{3,1},{4,6},{5,7},{6,4},{7,5},{8,10},{9,11},{10,... | collective-permute-start | bytes 294920 | tf_op jit(solution)/shard_map/ppermute | solution.py:246
  64.0 15.8 %collective-permute-start.10 = (bf16[2,96,1536]{2,1,0:T(8,128)(2,1)S(1)}, bf16[2,96,1536]{2,1,0:T(8,128)(2,1)S(1)}, u32[]{:S(2)}, u32[]{:S(2)}) collective-permute-start(bf16[2,96,1536]{2,1,0:T(8,128)(2,1)S(1)} %get-tuple-element.45), channel_id=1, source_target_pairs={{0,1},{1,0},{2,3},{3,2},{4,5},{5,4},{6,7},{7,6},{8,9},{9,8},{10,11... | collective-permute-start | bytes 1769480 | tf_op jit(solution)/shard_map/ppermute | solution.py:243
  64.1 12.0 %collective-permute-start.11 = (bf16[2,48,2048]{2,1,0:T(8,128)(2,1)S(1)}, bf16[2,48,2048]{2,1,0:T(8,128)(2,1)S(1)}, u32[]{:S(2)}, u32[]{:S(2)}) collective-permute-start(bf16[2,48,2048]{2,1,0:T(8,128)(2,1)S(1)} %get-tuple-element.47.refs_5_), channel_id=1, source_target_pairs={{0,2},{1,3},{2,0},{3,1},{4,6},{5,7},{6,4},{7,5},{8,10},{9,11},{10,... | collective-permute-start | bytes 1179656 | tf_op jit(solution)/shard_map/ppermute | solution.py:246
  64.6 15.2 %collective-permute-start.14 = (bf16[48,2048]{1,0:T(8,128)(2,1)S(1)}, bf16[48,2048]{1,0:T(8,128)(2,1)S(1)}, u32[]{:S(2)}, u32[]{:S(2)}) collective-permute-start(bf16[48,2048]{1,0:T(8,128)(2,1)S(1)} %activate.5.refs_1_.refs_0_), channel_id=1, source_target_pairs={{0,2},{1,3},{2,0},{3,1},{4,6},{5,7},{6,4},{7,5},{8,10},{9,11},{10,... | collective-permute-start | bytes 589832 | tf_op jit(solution)/shard_map/ppermute | solution.py:246
  79.9 10.0 %collective-permute-start.15 = (bf16[2,48,1536]{2,1,0:T(8,128)(2,1)S(1)}, bf16[2,48,1536]{2,1,0:T(8,128)(2,1)S(1)}, u32[]{:S(2)}, u32[]{:S(2)}) collective-permute-start(bf16[2,48,1536]{2,1,0:T(8,128)(2,1)S(1)} %get-tuple-element.49.refs_5_), channel_id=1, source_target_pairs={{0,2},{1,3},{2,0},{3,1},{4,6},{5,7},{6,4},{7,5},{8,10},{9,11},{10,... | collective-permute-start | bytes 884744 | tf_op jit(solution)/shard_map/ppermute | solution.py:246
  80.5 2.1 %collective-permute-start.16 = (bf16[48,2048]{1,0:T(8,128)(2,1)S(1)}, bf16[48,2048]{1,0:T(8,128)(2,1)S(1)}, u32[]{:S(2)}, u32[]{:S(2)}) collective-permute-start(bf16[48,2048]{1,0:T(8,128)(2,1)S(1)} %activate.5.refs_1_.refs_0_), channel_id=1, source_target_pairs={{0,1},{1,0},{2,3},{3,2},{4,5},{5,4},{6,7},{7,6},{8,9},{9,8},{10,11... | collective-permute-start | bytes 589832 | tf_op jit(solution)/shard_map/ppermute | solution.py:243
  81.0 13.1 %collective-permute-start.21 = (bf16[48,2048]{1,0:T(8,128)(2,1)S(1)}, bf16[48,2048]{1,0:T(8,128)(2,1)S(1)}, u32[]{:S(2)}, u32[]{:S(2)}) collective-permute-start(bf16[48,2048]{1,0:T(8,128)(2,1)S(1)} %activate.6.refs_0_), channel_id=1, source_target_pairs={{0,2},{1,3},{2,0},{3,1},{4,6},{5,7},{6,4},{7,5},{8,10},{9,11},{10,... | collective-permute-start | bytes 589832 | tf_op jit(solution)/shard_map/ppermute | solution.py:246
  90.1 5.9 %collective-permute-start.18 = (bf16[48,1536]{1,0:T(8,128)(2,1)S(1)}, bf16[48,1536]{1,0:T(8,128)(2,1)S(1)}, u32[]{:S(2)}, u32[]{:S(2)}) collective-permute-start(bf16[48,1536]{1,0:T(8,128)(2,1)S(1)} %activate.7.refs_0_), channel_id=1, source_target_pairs={{0,2},{1,3},{2,0},{3,1},{4,6},{5,7},{6,4},{7,5},{8,10},{9,11},{10,... | collective-permute-start | bytes 442376 | tf_op jit(solution)/shard_map/ppermute | solution.py:246
  90.6 5.4 %collective-permute-start.22 = (bf16[48,2048]{1,0:T(8,128)(2,1)S(1)}, bf16[48,2048]{1,0:T(8,128)(2,1)S(1)}, u32[]{:S(2)}, u32[]{:S(2)}) collective-permute-start(bf16[48,2048]{1,0:T(8,128)(2,1)S(1)} %activate.6.refs_0_), channel_id=1, source_target_pairs={{0,1},{1,0},{2,3},{3,2},{4,5},{5,4},{6,7},{7,6},{8,9},{9,8},{10,11... | collective-permute-start | bytes 589832 | tf_op jit(solution)/shard_map/ppermute | solution.py:243
  94.1 7.1 %collective-permute-start.19 = (bf16[48,1536]{1,0:T(8,128)(2,1)S(1)}, bf16[48,1536]{1,0:T(8,128)(2,1)S(1)}, u32[]{:S(2)}, u32[]{:S(2)}) collective-permute-start(bf16[48,1536]{1,0:T(8,128)(2,1)S(1)} %activate.7.refs_0_), channel_id=1, source_target_pairs={{0,1},{1,0},{2,3},{3,2},{4,5},{5,4},{6,7},{7,6},{8,9},{9,8},{10,11... | collective-permute-start | bytes 442376 | tf_op jit(solution)/shard_map/ppermute | solution.py:243
  96.0 5.3 %collective-permute-start.20 = (bf16[48,1536]{1,0:T(8,128)(2,1)S(1)}, bf16[48,1536]{1,0:T(8,128)(2,1)S(1)}, u32[]{:S(2)}, u32[]{:S(2)}) collective-permute-start(bf16[48,1536]{1,0:T(8,128)(2,1)S(1)} %collective-permute-done.18.refs_1_), channel_id=1, source_target_pairs={{0,1},{1,0},{2,3},{3,2},{4,5},{5,4},{6,7},{7,6},{8,9},{9,8},{10,11... | collective-permute-start | bytes 442376 | tf_op jit(solution)/shard_map/ppermute | solution.py:243
  106.4 8.1 %collective-permute-start.26 = (bf16[64,2048]{1,0:T(8,128)(2,1)S(1)}, bf16[64,2048]{1,0:T(8,128)(2,1)S(1)}, u32[]{:S(2)}, u32[]{:S(2)}) collective-permute-start(bf16[64,2048]{1,0:T(8,128)(2,1)S(1)} %get-tuple-element.53), channel_id=1, source_target_pairs={{0,4},{12,8},{1,5},{13,9},{2,6},{14,10},{3,7},{15,11},{16,20},{28,... | collective-permute-start | bytes 786440 | tf_op jit(solution)/shard_map/ppermute | solution.py:240
  107.9 12.2 %collective-permute-start.25 = (bf16[64,2048]{1,0:T(8,128)(2,1)S(1)}, bf16[64,2048]{1,0:T(8,128)(2,1)S(1)}, u32[]{:S(2)}, u32[]{:S(2)}) collective-permute-start(bf16[64,2048]{1,0:T(8,128)(2,1)S(1)} %get-tuple-element.53), channel_id=1, source_target_pairs={{4,8},{8,4},{5,9},{9,5},{6,10},{10,6},{7,11},{11,7},{20,24},{24,20... | collective-permute-start | bytes 786440 | tf_op jit(solution)/shard_map/ppermute | solution.py:240
  108.6 11.5 %collective-permute-start.24 = (bf16[64,2048]{1,0:T(8,128)(2,1)S(1)}, bf16[64,2048]{1,0:T(8,128)(2,1)S(1)}, u32[]{:S(2)}, u32[]{:S(2)}) collective-permute-start(bf16[64,2048]{1,0:T(8,128)(2,1)S(1)} %get-tuple-element.52), channel_id=1, source_target_pairs={{0,4},{4,0},{8,12},{12,8},{1,5},{5,1},{9,13},{13,9},{2,6},{6,2},{1... | collective-permute-start | bytes 786440 | tf_op jit(solution)/shard_map/ppermute | solution.py:240
  114.6 16.9 %collective-permute-start.27 = (bf16[64,2048]{1,0:T(8,128)(2,1)S(1)}, bf16[64,2048]{1,0:T(8,128)(2,1)S(1)}, u32[]{:S(2)}, u32[]{:S(2)}) collective-permute-start(bf16[64,2048]{1,0:T(8,128)(2,1)S(1)} %add_convert_fusion.1), channel_id=1, source_target_pairs={{0,8},{4,12},{8,0},{12,4},{1,9},{5,13},{9,1},{13,5},{2,10},{6,14},... | collective-permute-start | bytes 786440 | tf_op jit(solution)/shard_map/ppermute | solution.py:240
  (6 other events, 8.2 us)

commit v6 on v5

v6 whole, which is shorter than its diff:
```python
import functools

import jax
import jax.numpy as jnp
from jax import lax
from jax.experimental import pallas as pl
from jax.experimental.pallas import tpu as pltpu
from jax.sharding import PartitionSpec as P

MIB = 1 << 20
BF16, F32 = jnp.bfloat16, jnp.float32


def row_sources(lengths_ref, rows, n_gx, tok_dev):
    start = jnp.int32(0)
    slot = rows
    for g in range(n_gx):
        slot = jnp.where(rows >= start, rows - start + g * tok_dev, slot)
        start = start + lengths_ref[g]
    return slot


def local_rows(shape, dim, quarter, nx):
    gy = lax.axis_index("gy")
    x, core = gy // 2, gy % 2
    j = lax.broadcasted_iota(jnp.int32, shape, dim)
    rows = jnp.zeros(shape, jnp.int32)
    for kc in range(2):
        for kx in range(nx):
            first = (kc * nx + kx) * quarter
            owner = lax.rem(x + kx, nx) * 2 + (1 - core if kc else core)
            rows = jnp.where(j >= first, owner * quarter + j - first, rows)
    return rows


def picks_kernel(n_gx, nx, tok_dev, lengths_ref, tok_ref, in_ref, out_ref, held_ref):
    z = lax.axis_index("gx")
    live, slots = in_ref.shape
    held_ref[...] = tok_ref[...]
    quarter = live // (2 * nx)

    def slot_of(column):
        return (z ^ (column // tok_dev)) * tok_dev + column % tok_dev

    shape = (live, slots)
    source = row_sources(lengths_ref, local_rows(shape, 0, quarter, nx), n_gx, tok_dev)
    in_ref[...] = (source == slot_of(lax.broadcasted_iota(jnp.int32, shape, 1))).astype(F32).astype(BF16)
    shape = (slots, live)
    source = row_sources(lengths_ref, local_rows(shape, 1, quarter, nx), n_gx, tok_dev)
    out_ref[...] = (source == slot_of(lax.broadcasted_iota(jnp.int32, shape, 0))).astype(F32).astype(BF16)


def picks(lengths, tokens, n_gx, nx, live):
    tok_dev = tokens.shape[0]
    slots = n_gx * tok_dev
    held = pl.BlockSpec(memory_space=pltpu.VMEM)
    return pl.pallas_call(
        functools.partial(picks_kernel, n_gx, nx, tok_dev),
        out_shape=[
            jax.ShapeDtypeStruct((live, slots), BF16),
            jax.ShapeDtypeStruct((slots, live), BF16),
            jax.ShapeDtypeStruct(tokens.shape, tokens.dtype),
        ],
        in_specs=[pl.BlockSpec(memory_space=pltpu.SMEM), held],
        out_specs=[held] * 3,
        cost_estimate=pl.CostEstimate(flops=0, bytes_accessed=4 * live * slots, transcendentals=0),
        compiler_params=pltpu.CompilerParams(vmem_limit_bytes=8 * MIB),
        name="picks",
    )(lengths, tokens)


def compact_kernel(groups, pick_ref, *refs):
    refs = list(refs)
    out_ref = refs.pop()

    def rows_of(n):
        return jnp.concatenate([refs.pop(0)[...] for _ in range(n)], axis=0)

    blocks = []
    for group in groups:
        block = rows_of(group[0])
        for n in group[1:]:
            block = block + rows_of(n)
        blocks.append(block)
    rows = jnp.concatenate(blocks, axis=0)
    out_ref[...] = jnp.dot(pick_ref[...], rows, preferred_element_type=F32).astype(BF16)


def compact(pick, blocks):
    flat = [piece for group in blocks for pieces in group for piece in pieces]
    return pl.pallas_call(
        functools.partial(compact_kernel, [[len(pieces) for pieces in group] for group in blocks]),
        out_shape=jax.ShapeDtypeStruct((pick.shape[0], flat[0].shape[1]), BF16),
        compiler_params=pltpu.CompilerParams(vmem_limit_bytes=8 * MIB),
        cost_estimate=pl.CostEstimate(
            flops=2 * pick.size * flat[0].shape[1], bytes_accessed=2 * pick.size, transcendentals=0
        ),
        name="compact",
    )(pick, *flat)


def gate_up_kernel(tok_ref, gate_ref, up_ref, *refs):
    send_ref, keep_ref = refs[-2:]
    half = keep_ref.shape[1]
    rows = tok_ref[...]
    for i, w_ref in enumerate((gate_ref, up_ref)):
        part = jnp.dot(rows, w_ref[...], preferred_element_type=F32)
        keep_ref[i] = part[:half]
        send_ref[i] = part[half:].astype(BF16)


def gate_up(tok, gate_weight, up_weight, after, start, width, tile):
    live, depth = tok.shape
    half = live // 2
    weight = pl.BlockSpec((depth, tile), lambda j: (0, start // tile + j))
    out = pl.BlockSpec((2, half, tile), lambda j: (0, 0, j))
    return pl.pallas_call(
        gate_up_kernel,
        out_shape=[jax.ShapeDtypeStruct((2, half, width), BF16), jax.ShapeDtypeStruct((2, half, width), F32)],
        grid=(width // tile,),
        in_specs=[pl.BlockSpec((live, depth), lambda j: (0, 0)), weight, weight]
        + [pl.BlockSpec(memory_space=pl.ANY)] * len(after),
        out_specs=[out, out],
        compiler_params=pltpu.CompilerParams(vmem_limit_bytes=40 * MIB),
        cost_estimate=pl.CostEstimate(
            flops=0, bytes_accessed=0, transcendentals=0
        ),
        name="gate_up",
    )(tok, gate_weight, up_weight, *after)


def join_kernel(n_handed, n_after, nx, keep_ref, got_ref, *refs):
    out_refs = refs[n_handed + n_after:][:nx]
    quarter = out_refs[0].shape[1]
    for k, out_ref in enumerate(out_refs):
        rows = pl.ds(k * quarter, quarter)
        out_ref[...] = (keep_ref[:, rows] + got_ref[:, rows].astype(F32)).astype(out_ref.dtype)


def join(keep, got, handed, after, nx):
    two, half, width = keep.shape
    shape = (two, half // nx, width)
    held, anywhere = pl.BlockSpec(memory_space=pltpu.VMEM), pl.BlockSpec(memory_space=pl.ANY)
    out = pl.pallas_call(
        functools.partial(join_kernel, len(handed), len(after), nx),
        out_shape=[jax.ShapeDtypeStruct(shape, BF16 if k else F32) for k in range(nx)]
        + [jax.ShapeDtypeStruct(a.shape, a.dtype) for a in handed],
        in_specs=[held, held] + [anywhere] * (len(handed) + len(after)),
        out_specs=[held] * nx + [anywhere] * len(handed),
        input_output_aliases={2 + i: nx + i for i in range(len(handed))},
        compiler_params=pltpu.CompilerParams(vmem_limit_bytes=8 * MIB),
        cost_estimate=pl.CostEstimate(flops=0, bytes_accessed=0, transcendentals=0),
        name="join",
    )(keep, got, *handed, *after)
    return out[0], out[1:nx], out[nx:]


def activate_kernel(n_got, n_unread, mine_ref, *refs):
    both = mine_ref[...]
    for got_ref in refs[:n_got]:
        both = both + got_ref[...].astype(F32)
    gate, up = both[0], both[1]
    refs[n_got + n_unread][...] = (gate / (1.0 + jnp.exp(-gate)) * up).astype(BF16)


def activate(mine, got, handed, after):
    held, anywhere = pl.BlockSpec(memory_space=pltpu.VMEM), pl.BlockSpec(memory_space=pl.ANY)
    out = pl.pallas_call(
        functools.partial(activate_kernel, len(got), len(handed) + len(after)),
        out_shape=[jax.ShapeDtypeStruct(mine.shape[1:], BF16)]
        + [jax.ShapeDtypeStruct(a.shape, a.dtype) for a in handed],
        in_specs=[held] * (1 + len(got)) + [anywhere] * (len(handed) + len(after)),
        out_specs=[held] + [anywhere] * len(handed),
        input_output_aliases={1 + len(got) + i: 1 + i for i in range(len(handed))},
        compiler_params=pltpu.CompilerParams(vmem_limit_bytes=8 * MIB),
        cost_estimate=pl.CostEstimate(flops=0, bytes_accessed=0, transcendentals=0),
        name="activate",
    )(mine, *got, *handed, *after)
    return out[0], out[1:]


def relay_kernel(own_ref, got_ref, *refs):
    out_ref = refs[len(refs) // 2]
    out_ref[...] = (own_ref[...].astype(F32) + got_ref[...].astype(F32)).astype(BF16)


def relay(own, got, handed, after):
    held, anywhere = pl.BlockSpec(memory_space=pltpu.VMEM), pl.BlockSpec(memory_space=pl.ANY)
    out = pl.pallas_call(
        relay_kernel,
        out_shape=[jax.ShapeDtypeStruct(a.shape, a.dtype) for a in (own, *handed)],
        in_specs=[held, held] + [anywhere] * (1 + len(handed)),
        out_specs=[held] + [anywhere] * len(handed),
        input_output_aliases={2 + i: 1 + i for i in range(len(handed))},
        compiler_params=pltpu.CompilerParams(vmem_limit_bytes=8 * MIB),
        cost_estimate=pl.CostEstimate(flops=0, bytes_accessed=0, transcendentals=0),
        name="relay",
    )(own, got, *handed, after)
    return out[0], out[1:]


def down_kernel(pieces, n_after, first, last, *refs):
    refs, hidden = list(refs[:-1]), refs[-1]
    h_refs = [[refs.pop(0) for _ in range(n)] for n in pieces]
    w_ref, refs = refs[0], refs[1 + n_after:]

    @pl.when(pl.program_id(0) == 0)
    def _():
        column = 0
        for chunk in h_refs:
            row = 0
            for r in chunk:
                n, width = r.shape
                hidden[row:row + n, column:column + width] = r[...]
                row += n
            column += width

    total = jnp.dot(hidden[...], w_ref[...], preferred_element_type=F32)
    if not first:
        total += refs[0][...]
        refs = refs[1:]
    if not last:
        refs[0][...] = total
        return
    pick_ref, outs = refs[0], refs[1:]
    spread = jnp.dot(pick_ref[...], total.astype(BF16), preferred_element_type=F32).astype(BF16)
    row = 0
    for out_ref in outs:
        n = out_ref.shape[0]
        out_ref[...] = spread[row:row + n]
        row += n


def down(hidden, down_weight, total, pick, out_rows, after, start):
    live = sum(h.shape[0] for h in hidden[0])
    width = sum(chunk[0].shape[1] for chunk in hidden)
    out_width = down_weight.shape[1]
    tile = min(out_width, 512 if width <= 2560 else 256)
    last = pick is not None
    rows = pl.BlockSpec((live, tile), lambda j: (0, j))
    flat = [h for chunk in hidden for h in chunk]
    operands = [*flat, down_weight, *after]
    in_specs = [pl.BlockSpec(h.shape, lambda j: (0, 0)) for h in flat]
    in_specs.append(pl.BlockSpec((pl.Element(width), pl.Element(tile)), lambda j: (start, j * tile)))
    in_specs += [pl.BlockSpec(memory_space=pl.ANY)] * len(after)
    if total is not None:
        operands.append(total)
        in_specs.append(rows)
    if last:
        operands.append(pick)
        in_specs.append(pl.BlockSpec(pick.shape, lambda j: (0, 0)))
        out_shape = [jax.ShapeDtypeStruct((n, out_width), BF16) for n in out_rows]
        out_specs = [pl.BlockSpec((n, tile), lambda j: (0, j)) for n in out_rows]
    else:
        out_shape, out_specs = jax.ShapeDtypeStruct((live, out_width), F32), rows
    return pl.pallas_call(
        functools.partial(down_kernel, [len(c) for c in hidden], len(after), total is None, last),
        out_shape=out_shape,
        grid=(out_width // tile,),
        in_specs=in_specs,
        out_specs=out_specs,
        scratch_shapes=[pltpu.VMEM((live, width), BF16)],
        compiler_params=pltpu.CompilerParams(vmem_limit_bytes=40 * MIB),
        cost_estimate=pl.CostEstimate(flops=0, bytes_accessed=0, transcendentals=0),
        name="down",
    )(*operands)


def column_chunks(cols, tile):
    tiles = cols // tile
    shares = (4, 5, 4)
    edges = [round(tiles * sum(shares[:i]) / sum(shares)) for i in range(len(shares) + 1)]
    return [(a * tile, (b - a) * tile) for a, b in zip(edges, edges[1:]) if b > a]


def local(n_gx, n_gy, tokens, gate_weight, up_weight, down_weight, lengths):
    nx = n_gy // 2
    tok_dev = tokens.shape[0]
    live = 3 * tok_dev * n_gx // 4
    cols = gate_weight.shape[1]
    tile = 512 if cols % 512 == 0 else 128
    chunks = column_chunks(cols, tile)
    n = len(chunks)
    line = n_gx == 4
    part = tok_dev // 2

    def over_z(block, k, among=range(n_gx)):
        return lax.ppermute(block, "gx", [(z, z ^ k) for z in among])

    def over_core(block):
        return lax.ppermute(block, "gy", [(i, i ^ 1) for i in range(n_gy)])

    def over_x(block, k):
        return lax.ppermute(block, "gy", [(i, (i + 2 * k) % n_gy) for i in range(n_gy)])

    pick_in, pick_out, held = picks(lengths, tokens, n_gx, nx, live)
    if line:
        two = [over_z(tokens[:part], 2), over_z(tokens[part:], 2)]
        one = over_z(tokens, 1)
        middle = over_z(tokens, 3, (1, 2))
        ends = [over_z(piece, 1, (1, 2)) for piece in two]
        blocks = [[[held]], [[one]], [two], [[middle], ends]]
    else:
        blocks = [[[held]]] + [[[over_z(tokens, k)]] for k in range(1, n_gx)]
    tok = compact(pick_in, blocks)

    send, keep = gate_up(tok, gate_weight, up_weight, [], *chunks[0], tile)
    hidden, fars, total = [], [], None

    def pieces(own, far):
        h = [own] + far
        return h + [over_core(a) for a in h]

    for j in range(n):
        mine, blocks, _ = join(keep, over_core(send), [], [], nx)
        got = [over_x(b, k + 1) for k, b in enumerate(blocks)]
        handed, after = [], fars[-1] if fars else []
        if j + 1 < n:
            send, keep = gate_up(tok, gate_weight, up_weight, blocks, *chunks[j + 1], tile)
            handed = [send]
        elif n > 1:
            total = down(hidden, down_weight, None, None, None, list(blocks), chunks[0][0])
            after = [total]
        own, handed = activate(mine, got, handed, after)
        if handed:
            send = handed[0]
        far = [over_x(own, -k) for k in range(1, nx)]
        fars.append(far)
        hidden.append(pieces(own, far))
    out_rows = [tok_dev, part, part, tok_dev, tok_dev] if line else [tok_dev] * n_gx
    spread = down(hidden[-1:], down_weight, total, pick_out, out_rows, [], chunks[-1][0])

    if line:
        own, low, high, two, three = spread
        ends = over_z(three, 1, (0, 3))
        middle = over_z(three, 3, (1, 2))
        two, near = relay(two, ends, [low, high], middle)
        far = over_z(two, 2)
        near = [over_z(a, 1) for a in near]
        parts = [own, jnp.concatenate(near, axis=0), far, middle]
    else:
        parts = [spread[0]] + [over_z(spread[k], k) for k in range(1, n_gx)]
    return sum(p.astype(F32) for p in parts).astype(BF16)


def solution(mesh):
    placed = (P(("group", "gx"), "gy"), P("gy", "gx"), P("gy", "gx"), P("gx", "gy"), P("group"))
    return jax.shard_map(
        functools.partial(local, mesh.shape["gx"], mesh.shape["gy"]),
        mesh=mesh, in_specs=placed, out_specs=P(("group", "gx"), "gy"), check_vma=False,
    )
```

time: 133 us -> 130 us (0.977)
  Pallas kernels: 48.8 us -> 44.7 us
  waiting for transfers between devices: 51.2 us -> 54.6 us
  starting transfers between devices: 29.5 us -> 27.1 us
    ppermute x12 -> x9, waiting for transfers between devices: 0.97 us -> 8.91 us  [over_core(): return lax.ppermute(block, 'gy', [(i, i ^ 1) for i in range(n_gy)])]
    ppermute x8 -> x11, waiting for transfers between devices: 30.3 us -> 27.3 us  [over_z(): return lax.ppermute(block, 'gx', [(z, z ^ k) for z in among])]
    pallas_call x9 -> x7, Pallas kernels: 20.4 us -> 17.5 us  [the longest x2 16.6 us: down(): pl.pallas_call(functools.partial(down_kernel, [len(c) for c in hidden], l...]
    ppermute x12 -> x9, starting transfers between devices: 2.27 us -> 0.73 us  [over_core(): return lax.ppermute(block, 'gy', [(i, i ^ 1) for i in range(n_gy)])]
    ppermute x8 -> x6, waiting for transfers between devices: 19.9 us -> 18.4 us  [over_x(): lax.ppermute(block, 'gy', [(i, (i + 2 * k) % n_gy) for i in range(n_gy)])]
    pallas_call x4 -> x3, Pallas kernels: 27.4 us -> 26.1 us  [gate_up(): pl.pallas_call(gate_up_kernel, out_shape=[jax.ShapeDtypeStruct((2, half,...]
    ppermute x8 -> x6, starting transfers between devices: 8.36 us -> 7.53 us  [over_x(): lax.ppermute(block, 'gy', [(i, (i + 2 * k) % n_gy) for i in range(n_gy)])]
    ppermute x8 -> x11, starting transfers between devices: 18.9 us -> 18.8 us  [over_z(): return lax.ppermute(block, 'gx', [(z, z ^ k) for z in among])]
  transfers between devices with their start and end apart: 28 -> 26, of which waited for: 14 -> 17; matrix products, arithmetic and copies ran while one was open for 0% -> 0% of each run, Pallas kernels for 29% -> 23%
where the time goes in v6:
time: 130 us
  waiting for transfers between devices  54.6 us (42%)
  Pallas kernels  44.7 us (34%)
  starting transfers between devices  27.1 us (21%)
  local copies, waits for them, and re-layouts  2.58 us (2%)
    ppermute x11, waiting for transfers between devices, over_z(): return lax.ppermute(block, 'gx', [(z, z ^ k) for z in among])  27.3 us
    pallas_call x3, Pallas kernels, gate_up(): pl.pallas_call(gate_up_kernel, out_shape=[jax.ShapeDtypeStruct((2, half,...  26.1 us
    ppermute x11, starting transfers between devices, over_z(): return lax.ppermute(block, 'gx', [(z, z ^ k) for z in among])  18.8 us
    ppermute x6, waiting for transfers between devices, over_x(): lax.ppermute(block, 'gy', [(i, (i + 2 * k) % n_gy) for i in range(n_gy)])  18.4 us
    pallas_call x2, Pallas kernels, down(): pl.pallas_call(functools.partial(down_kernel, [len(c) for c in hidden], l...  16.6 us
    ppermute x9, waiting for transfers between devices, over_core(): return lax.ppermute(block, 'gy', [(i, i ^ 1) for i in range(n_gy)])  8.91 us
    ppermute x6, starting transfers between devices, over_x(): lax.ppermute(block, 'gy', [(i, (i + 2 * k) % n_gy) for i in range(n_gy)])  7.53 us
  transfers between devices with their start and end apart: 26, of which 17 were waited for; matrix products, arithmetic and copies ran while one was open for 0% of the time, Pallas kernels for 23%

profile of v6, /device:TPU:0, one launch (start us, length us, event | category | flops | bytes accessed | tf_op | source)
XLA Modules:
  0.0 130.1 jit_solution(6603236457504756082)
XLA Ops:
  1.0 4.1 %collective-permute-start.2 = (bf16[32,2048]{1,0:T(8,128)(2,1)S(1)}, bf16[32,2048]{1,0:T(8,128)(2,1)S(1)}, u32[]{:S(2)}, u32[]{:S(2)}) collective-permute-start(bf16[32,2048]{1,0:T(8,128)(2,1)S(1)} %get-tuple-element.59), channel_id=1, source_target_pairs={{0,8},{4,12},{8,0},{12,4},{1,9},{5,13},{9,1},{13,5},{2,10},{6,14},... | collective-permute-start | bytes 393224 | tf_op jit(solution)/shard_map/ppermute | solution.py:288
  5.2 1.8 %collective-permute-start = (bf16[64,2048]{1,0:T(8,128)(2,1)}, bf16[64,2048]{1,0:T(8,128)(2,1)S(1)}, u32[]{:S(2)}, u32[]{:S(2)}) collective-permute-start(bf16[64,2048]{1,0:T(8,128)(2,1)} %tok_ref.1), channel_id=1, source_target_pairs={{0,4},{4,0},{8,12},{12,8},{1,5},{5,1},{9,13},{13,9},{2,6},{6,2},{1... | collective-permute-start | bytes 786440 | tf_op jit(solution)/shard_map/ppermute | solution.py:288
  7.7 7.5 %collective-permute-done.2.refs_3_ = bf16[32,2048]{1,0:T(8,128)(2,1)S(1)} collective-permute-done((bf16[32,2048]{1,0:T(8,128)(2,1)S(1)}, bf16[32,2048]{1,0:T(8,128)(2,1)S(1)}, u32[]{:S(2)}, u32[]{:S(2)}) %collective-permute-start.2) | collective-permute-done | bytes 131104 | tf_op jit(solution)/shard_map/ppermute | solution.py:288
  16.4 1.5 %collective-permute-done.1.refs_2_ = bf16[32,2048]{1,0:T(8,128)(2,1)S(1)} collective-permute-done((bf16[32,2048]{1,0:T(8,128)(2,1)S(1)}, bf16[32,2048]{1,0:T(8,128)(2,1)S(1)}, u32[]{:S(2)}, u32[]{:S(2)}) %collective-permute-start.1) | collective-permute-done | bytes 131104 | tf_op jit(solution)/shard_map/ppermute | solution.py:288
  21.5 1.7 %collective-permute-done.5.refs_6_ = bf16[32,2048]{1,0:T(8,128)(2,1)S(1)} collective-permute-done((bf16[32,2048]{1,0:T(8,128)(2,1)S(1)}, bf16[32,2048]{1,0:T(8,128)(2,1)S(1)}, u32[]{:S(2)}, u32[]{:S(2)}) %collective-permute-start.5) | collective-permute-done | bytes 131104 | tf_op jit(solution)/shard_map/ppermute | solution.py:288
  23.2 1.6 %collective-permute-done.4.refs_5_ = bf16[32,2048]{1,0:T(8,128)(2,1)S(1)} collective-permute-done((bf16[32,2048]{1,0:T(8,128)(2,1)S(1)}, bf16[32,2048]{1,0:T(8,128)(2,1)S(1)}, u32[]{:S(2)}, u32[]{:S(2)}) %collective-permute-start.4) | collective-permute-done | bytes 131104 | tf_op jit(solution)/shard_map/ppermute | solution.py:288
  25.2 8.1 %gate_up.3 = (bf16[2,96,2048]{2,1,0:T(8,128)(2,1)S(1)}, f32[2,96,2048]{2,1,0:T(8,128)S(1)}) custom-call(bf16[192,2048]{1,0:T(8,128)(2,1)S(1)} %compact.1.tok_ref, bf16[2048,6656]{1,0:T(8,128)(2,1)} %gate_ref.5, bf16[2048,6656]{1,0:T(8,128)(2,1)} %up_ref.5), custom_call_target="tpu_custom_call" | custom-call | tf_op jit(solution)/shard_map/gate_up/pallas_call | solution.py:117
  33.3 2.3 %collective-permute-done.6.got_ref = bf16[2,96,2048]{2,1,0:T(8,128)(2,1)S(1)} collective-permute-done((bf16[2,96,2048]{2,1,0:T(8,128)(2,1)S(1)}, bf16[2,96,2048]{2,1,0:T(8,128)(2,1)S(1)}, u32[]{:S(2)}, u32[]{:S(2)}) %collective-permute-start.6) | collective-permute-done | bytes 786464 | tf_op jit(solution)/shard_map/ppermute | solution.py:291
  35.7 1.9 %collective-permute-start.7 = (bf16[2,48,2048]{2,1,0:T(8,128)(2,1)S(1)}, bf16[2,48,2048]{2,1,0:T(8,128)(2,1)S(1)}, u32[]{:S(2)}, u32[]{:S(2)}) collective-permute-start(bf16[2,48,2048]{2,1,0:T(8,128)(2,1)S(1)} %get-tuple-element.36.refs_0_), channel_id=1, source_target_pairs={{0,2},{1,3},{2,0},{3,1},{4,6},{5,7},{6,4},{7,5},{8,10},{9,11},{10,... | collective-permute-start | bytes 1179656 | tf_op jit(solution)/shard_map/ppermute | solution.py:294
  37.6 10.0 %gate_up.4 = (bf16[2,96,2560]{2,1,0:T(8,128)(2,1)S(1)}, f32[2,96,2560]{2,1,0:T(8,128)S(1)}) custom-call(bf16[192,2048]{1,0:T(8,128)(2,1)S(1)} %compact.1.tok_ref, bf16[2048,6656]{1,0:T(8,128)(2,1)} %gate_ref.5, bf16[2048,6656]{1,0:T(8,128)(2,1)} %up_ref.5, bf16[2,48,2048]{2,1,0:T(8,128)(2,1)S(1)} %get-tuple-element.36.refs_0_), custom_call_target="tpu_custom_call" | custom-call | tf_op jit(solution)/shard_map/gate_up/pallas_call | solution.py:117
  47.9 2.6 %collective-permute-done.8.got_ref = bf16[2,96,2560]{2,1,0:T(8,128)(2,1)S(1)} collective-permute-done((bf16[2,96,2560]{2,1,0:T(8,128)(2,1)S(1)}, bf16[2,96,2560]{2,1,0:T(8,128)(2,1)S(1)}, u32[]{:S(2)}, u32[]{:S(2)}) %collective-permute-start.8) | collective-permute-done | bytes 983072 | tf_op jit(solution)/shard_map/ppermute | solution.py:291
  52.7 8.1 %gate_up.5 = (bf16[2,96,2048]{2,1,0:T(8,128)(2,1)S(1)}, f32[2,96,2048]{2,1,0:T(8,128)S(1)}) custom-call(bf16[192,2048]{1,0:T(8,128)(2,1)S(1)} %compact.1.tok_ref, bf16[2048,6656]{1,0:T(8,128)(2,1)} %gate_ref.5, bf16[2048,6656]{1,0:T(8,128)(2,1)} %up_ref.5, bf16[2,48,2560]{2,1,0:T(8,128)(2,1)S(1)} %get-tuple-element.41.refs_0_), custom_call_target="tpu_custom_call" | custom-call | tf_op jit(solution)/shard_map/gate_up/pallas_call | solution.py:117
  60.7 7.4 %collective-permute-done.10.refs_2_.refs_1_ = bf16[48,2048]{1,0:T(8,128)(2,1)S(1)} collective-permute-done((bf16[48,2048]{1,0:T(8,128)(2,1)S(1)}, bf16[48,2048]{1,0:T(8,128)(2,1)S(1)}, u32[]{:S(2)}, u32[]{:S(2)}) %collective-permute-start.10) | collective-permute-done | bytes 196640 | tf_op jit(solution)/shard_map/ppermute | solution.py:294
  72.0 5.2 %collective-permute-done.15.refs_5_ = bf16[48,2560]{1,0:T(8,128)(2,1)S(1)} collective-permute-done((bf16[48,2560]{1,0:T(8,128)(2,1)S(1)}, bf16[48,2560]{1,0:T(8,128)(2,1)S(1)}, u32[]{:S(2)}, u32[]{:S(2)}) %collective-permute-start.15) | collective-permute-done | bytes 245792 | tf_op jit(solution)/shard_map/ppermute | solution.py:294
  79.3 10.7 %down.2.refs_1_.refs_5_ = f32[192,2048]{1,0:T(8,128)S(1)} custom-call(bf16[48,2048]{1,0:T(8,128)(2,1)S(1)} %get-tuple-element.45.refs_0_, bf16[48,2048]{1,0:T(8,128)(2,1)S(1)} %collective-permute-done.10.refs_2_.refs_1_, bf16[48,2048]{1,0:T(8,128)(2,1)S(1)} %collective-permute-done.13.refs_2_, bf16[48,2048]{1,0:T(8,128)(2,1)S(1)} %collective-permute-done.14.refs_3_, ...), custom_call_target="tpu_custom_call" | custom-call | tf_op jit(solution)/shard_map/down/pallas_call | solution.py:256
  91.4 5.8 %collective-permute-done.18.refs_1_ = bf16[48,2048]{1,0:T(8,128)(2,1)S(1)} collective-permute-done((bf16[48,2048]{1,0:T(8,128)(2,1)S(1)}, bf16[48,2048]{1,0:T(8,128)(2,1)S(1)}, u32[]{:S(2)}, u32[]{:S(2)}) %collective-permute-start.18) | collective-permute-done | bytes 196640 | tf_op jit(solution)/shard_map/ppermute | solution.py:294
  97.2 1.4 %collective-permute-done.20.refs_3_ = bf16[48,2048]{1,0:T(8,128)(2,1)S(1)} collective-permute-done((bf16[48,2048]{1,0:T(8,128)(2,1)S(1)}, bf16[48,2048]{1,0:T(8,128)(2,1)S(1)}, u32[]{:S(2)}, u32[]{:S(2)}) %collective-permute-start.20) | collective-permute-done | bytes 196640 | tf_op jit(solution)/shard_map/ppermute | solution.py:291
  98.6 5.9 %down.3 = (bf16[64,2048]{1,0:T(8,128)(2,1)S(1)}, bf16[32,2048]{1,0:T(8,128)(2,1)S(1)}, bf16[32,2048]{1,0:T(8,128)(2,1)S(1)}, bf16[64,2048]{1,0:T(8,128)(2,1)S(1)}, bf16[64,2048]{1,0:T(8,128)(2,1)S(1)}) custom-call(bf16[48,2048]{1,0:T(8,128)(2,1)S(1)} %activate.5.refs_0_, bf16[48,2048]{1,0:T(8,128)(2,1)S(1)} %collective-permute-done.18.refs_1_, ...), custom_call_target="tpu_custom_call" | custom-call | tf_op jit(solution)/shard_map/down/pallas_call | solution.py:256
  105.2 4.6 %collective-permute-start.21 = (bf16[64,2048]{1,0:T(8,128)(2,1)S(1)}, bf16[64,2048]{1,0:T(8,128)(2,1)S(1)}, u32[]{:S(2)}, u32[]{:S(2)}) collective-permute-start(bf16[64,2048]{1,0:T(8,128)(2,1)S(1)} %get-tuple-element.53), channel_id=1, source_target_pairs={{0,4},{12,8},{1,5},{13,9},{2,6},{14,10},{3,7},{15,11},{16,20},{28,... | collective-permute-start | bytes 786440 | tf_op jit(solution)/shard_map/ppermute | solution.py:288
  109.8 5.5 %collective-permute-done.21.got_ref = bf16[64,2048]{1,0:T(8,128)(2,1)S(1)} collective-permute-done((bf16[64,2048]{1,0:T(8,128)(2,1)S(1)}, bf16[64,2048]{1,0:T(8,128)(2,1)S(1)}, u32[]{:S(2)}, u32[]{:S(2)}) %collective-permute-start.21) | collective-permute-done | bytes 262176 | tf_op jit(solution)/shard_map/ppermute | solution.py:288
  115.4 2.3 %collective-permute-start.25 = (bf16[64,2048]{1,0:T(8,128)(2,1)S(1)}, bf16[64,2048]{1,0:T(8,128)(2,1)S(1)}, u32[]{:S(2)}, u32[]{:S(2)}) collective-permute-start(bf16[64,2048]{1,0:T(8,128)(2,1)S(1)} %get-tuple-element.58), channel_id=1, source_target_pairs={{0,8},{4,12},{8,0},{12,4},{1,9},{5,13},{9,1},{13,5},{2,10},{6,14},... | collective-permute-start | bytes 786440 | tf_op jit(solution)/shard_map/ppermute | solution.py:288
  118.1 1.7 %collective-permute-start.24 = (bf16[32,2048]{1,0:T(8,128)(2,1)S(1)}, bf16[32,2048]{1,0:T(8,128)(2,1)S(1)}, u32[]{:S(2)}, u32[]{:S(2)}) collective-permute-start(bf16[32,2048]{1,0:T(8,128)(2,1)S(1)} %get-tuple-element.57), channel_id=1, source_target_pairs={{0,4},{4,0},{8,12},{12,8},{1,5},{5,1},{9,13},{13,9},{2,6},{6,2},{1... | collective-permute-start | bytes 393224 | tf_op jit(solution)/shard_map/ppermute | solution.py:288
  119.7 7.1 %collective-permute-done.23 = bf16[32,2048]{1,0:T(8,128)(2,1)S(1)} collective-permute-done((bf16[32,2048]{1,0:T(8,128)(2,1)S(1)}, bf16[32,2048]{1,0:T(8,128)(2,1)S(1)}, u32[]{:S(2)}, u32[]{:S(2)}) %collective-permute-start.23) | collective-permute-done | bytes 131104 | tf_op jit(solution)/shard_map/ppermute | solution.py:288
  126.9 1.4 %collective-permute-done.24 = bf16[32,2048]{1,0:T(8,128)(2,1)S(1)} collective-permute-done((bf16[32,2048]{1,0:T(8,128)(2,1)S(1)}, bf16[32,2048]{1,0:T(8,128)(2,1)S(1)}, u32[]{:S(2)}, u32[]{:S(2)}) %collective-permute-start.24) | collective-permute-done | bytes 131104 | tf_op jit(solution)/shard_map/ppermute | solution.py:288
  (48 shorter events, 19.8 us)
Async XLA Ops:
  1.0 14.1 %collective-permute-start.2 = (bf16[32,2048]{1,0:T(8,128)(2,1)S(1)}, bf16[32,2048]{1,0:T(8,128)(2,1)S(1)}, u32[]{:S(2)}, u32[]{:S(2)}) collective-permute-start(bf16[32,2048]{1,0:T(8,128)(2,1)S(1)} %get-tuple-element.59), channel_id=1, source_target_pairs={{0,8},{4,12},{8,0},{12,4},{1,9},{5,13},{9,1},{13,5},{2,10},{6,14},... | collective-permute-start | bytes 393224 | tf_op jit(solution)/shard_map/ppermute | solution.py:288
  5.1 12.8 %collective-permute-start.1 = (bf16[32,2048]{1,0:T(8,128)(2,1)S(1)}, bf16[32,2048]{1,0:T(8,128)(2,1)S(1)}, u32[]{:S(2)}, u32[]{:S(2)}) collective-permute-start(bf16[32,2048]{1,0:T(8,128)(2,1)S(1)} %get-tuple-element.60), channel_id=1, source_target_pairs={{0,8},{4,12},{8,0},{12,4},{1,9},{5,13},{9,1},{13,5},{2,10},{6,14},... | collective-permute-start | bytes 393224 | tf_op jit(solution)/shard_map/ppermute | solution.py:288
  5.2 19.6 %collective-permute-start = (bf16[64,2048]{1,0:T(8,128)(2,1)}, bf16[64,2048]{1,0:T(8,128)(2,1)S(1)}, u32[]{:S(2)}, u32[]{:S(2)}) collective-permute-start(bf16[64,2048]{1,0:T(8,128)(2,1)} %tok_ref.1), channel_id=1, source_target_pairs={{0,4},{4,0},{8,12},{12,8},{1,5},{5,1},{9,13},{13,9},{2,6},{6,2},{1... | collective-permute-start | bytes 786440 | tf_op jit(solution)/shard_map/ppermute | solution.py:288
  7.0 17.8 %collective-permute-start.3 = (bf16[64,2048]{1,0:T(8,128)(2,1)}, bf16[64,2048]{1,0:T(8,128)(2,1)S(1)}, u32[]{:S(2)}, u32[]{:S(2)}) collective-permute-start(bf16[64,2048]{1,0:T(8,128)(2,1)} %tok_ref.1), channel_id=1, source_target_pairs={{4,8},{8,4},{5,9},{9,5},{6,10},{10,6},{7,11},{11,7},{20,24},{24,20... | collective-permute-start | bytes 786440 | tf_op jit(solution)/shard_map/ppermute | solution.py:288
  15.1 8.0 %collective-permute-start.5 = (bf16[32,2048]{1,0:T(8,128)(2,1)S(1)}, bf16[32,2048]{1,0:T(8,128)(2,1)S(1)}, u32[]{:S(2)}, u32[]{:S(2)}) collective-permute-start(bf16[32,2048]{1,0:T(8,128)(2,1)S(1)} %collective-permute-done.2.refs_3_), channel_id=1, source_target_pairs={{4,0},{8,12},{5,1},{9,13},{6,2},{10,14},{7,3},{11,15},{20,16},{24,... | collective-permute-start | bytes 393224 | tf_op jit(solution)/shard_map/ppermute | solution.py:288
  17.9 6.9 %collective-permute-start.4 = (bf16[32,2048]{1,0:T(8,128)(2,1)S(1)}, bf16[32,2048]{1,0:T(8,128)(2,1)S(1)}, u32[]{:S(2)}, u32[]{:S(2)}) collective-permute-start(bf16[32,2048]{1,0:T(8,128)(2,1)S(1)} %collective-permute-done.1.refs_2_), channel_id=1, source_target_pairs={{4,0},{8,12},{5,1},{9,13},{6,2},{10,14},{7,3},{11,15},{20,16},{24,... | collective-permute-start | bytes 393224 | tf_op jit(solution)/shard_map/ppermute | solution.py:288
  33.3 2.4 %collective-permute-start.6 = (bf16[2,96,2048]{2,1,0:T(8,128)(2,1)S(1)}, bf16[2,96,2048]{2,1,0:T(8,128)(2,1)S(1)}, u32[]{:S(2)}, u32[]{:S(2)}) collective-permute-start(bf16[2,96,2048]{2,1,0:T(8,128)(2,1)S(1)} %get-tuple-element.35), channel_id=1, source_target_pairs={{0,1},{1,0},{2,3},{3,2},{4,5},{5,4},{6,7},{7,6},{8,9},{9,8},{10,11... | collective-permute-start | bytes 2359304 | tf_op jit(solution)/shard_map/ppermute | solution.py:291
  35.7 11.9 %collective-permute-start.7 = (bf16[2,48,2048]{2,1,0:T(8,128)(2,1)S(1)}, bf16[2,48,2048]{2,1,0:T(8,128)(2,1)S(1)}, u32[]{:S(2)}, u32[]{:S(2)}) collective-permute-start(bf16[2,48,2048]{2,1,0:T(8,128)(2,1)S(1)} %get-tuple-element.36.refs_0_), channel_id=1, source_target_pairs={{0,2},{1,3},{2,0},{3,1},{4,6},{5,7},{6,4},{7,5},{8,10},{9,11},{10,... | collective-permute-start | bytes 1179656 | tf_op jit(solution)/shard_map/ppermute | solution.py:294
  47.8 2.6 %collective-permute-start.8 = (bf16[2,96,2560]{2,1,0:T(8,128)(2,1)S(1)}, bf16[2,96,2560]{2,1,0:T(8,128)(2,1)S(1)}, u32[]{:S(2)}, u32[]{:S(2)}) collective-permute-start(bf16[2,96,2560]{2,1,0:T(8,128)(2,1)S(1)} %get-tuple-element.40), channel_id=1, source_target_pairs={{0,1},{1,0},{2,3},{3,2},{4,5},{5,4},{6,7},{7,6},{8,9},{9,8},{10,11... | collective-permute-start | bytes 2949128 | tf_op jit(solution)/shard_map/ppermute | solution.py:291
  50.6 17.5 %collective-permute-start.9 = (bf16[2,48,2560]{2,1,0:T(8,128)(2,1)S(1)}, bf16[2,48,2560]{2,1,0:T(8,128)(2,1)S(1)}, u32[]{:S(2)}, u32[]{:S(2)}) collective-permute-start(bf16[2,48,2560]{2,1,0:T(8,128)(2,1)S(1)} %get-tuple-element.41.refs_0_), channel_id=1, source_target_pairs={{0,2},{1,3},{2,0},{3,1},{4,6},{5,7},{6,4},{7,5},{8,10},{9,11},{10,... | collective-permute-start | bytes 1474568 | tf_op jit(solution)/shard_map/ppermute | solution.py:294
  51.8 16.4 %collective-permute-start.10 = (bf16[48,2048]{1,0:T(8,128)(2,1)S(1)}, bf16[48,2048]{1,0:T(8,128)(2,1)S(1)}, u32[]{:S(2)}, u32[]{:S(2)}) collective-permute-start(bf16[48,2048]{1,0:T(8,128)(2,1)S(1)} %get-tuple-element.45.refs_0_), channel_id=1, source_target_pairs={{0,2},{1,3},{2,0},{3,1},{4,6},{5,7},{6,4},{7,5},{8,10},{9,11},{10,... | collective-permute-start | bytes 589832 | tf_op jit(solution)/shard_map/ppermute | solution.py:294
  68.3 2.4 %collective-permute-start.11 = (bf16[2,96,2048]{2,1,0:T(8,128)(2,1)S(1)}, bf16[2,96,2048]{2,1,0:T(8,128)(2,1)S(1)}, u32[]{:S(2)}, u32[]{:S(2)}) collective-permute-start(bf16[2,96,2048]{2,1,0:T(8,128)(2,1)S(1)} %get-tuple-element.46), channel_id=1, source_target_pairs={{0,1},{1,0},{2,3},{3,2},{4,5},{5,4},{6,7},{7,6},{8,9},{9,8},{10,11... | collective-permute-start | bytes 2359304 | tf_op jit(solution)/shard_map/ppermute | solution.py:291
  68.4 8.8 %collective-permute-start.15 = (bf16[48,2560]{1,0:T(8,128)(2,1)S(1)}, bf16[48,2560]{1,0:T(8,128)(2,1)S(1)}, u32[]{:S(2)}, u32[]{:S(2)}) collective-permute-start(bf16[48,2560]{1,0:T(8,128)(2,1)S(1)} %get-tuple-element.49.refs_4_), channel_id=1, source_target_pairs={{0,2},{1,3},{2,0},{3,1},{4,6},{5,7},{6,4},{7,5},{8,10},{9,11},{10,... | collective-permute-start | bytes 737288 | tf_op jit(solution)/shard_map/ppermute | solution.py:294
  70.8 19.2 %collective-permute-start.12 = (bf16[2,48,2048]{2,1,0:T(8,128)(2,1)S(1)}, bf16[2,48,2048]{2,1,0:T(8,128)(2,1)S(1)}, u32[]{:S(2)}, u32[]{:S(2)}) collective-permute-start(bf16[2,48,2048]{2,1,0:T(8,128)(2,1)S(1)} %get-tuple-element.48.refs_9_), channel_id=1, source_target_pairs={{0,2},{1,3},{2,0},{3,1},{4,6},{5,7},{6,4},{7,5},{8,10},{9,11},{10,... | collective-permute-start | bytes 1179656 | tf_op jit(solution)/shard_map/ppermute | solution.py:294
  72.0 7.3 %collective-permute-start.16 = (bf16[48,2560]{1,0:T(8,128)(2,1)S(1)}, bf16[48,2560]{1,0:T(8,128)(2,1)S(1)}, u32[]{:S(2)}, u32[]{:S(2)}) collective-permute-start(bf16[48,2560]{1,0:T(8,128)(2,1)S(1)} %get-tuple-element.49.refs_4_), channel_id=1, source_target_pairs={{0,1},{1,0},{2,3},{3,2},{4,5},{5,4},{6,7},{7,6},{8,9},{9,8},{10,11... | collective-permute-start | bytes 737288 | tf_op jit(solution)/shard_map/ppermute | solution.py:291
  77.2 2.1 %collective-permute-start.17 = (bf16[48,2560]{1,0:T(8,128)(2,1)S(1)}, bf16[48,2560]{1,0:T(8,128)(2,1)S(1)}, u32[]{:S(2)}, u32[]{:S(2)}) collective-permute-start(bf16[48,2560]{1,0:T(8,128)(2,1)S(1)} %collective-permute-done.15.refs_5_), channel_id=1, source_target_pairs={{0,1},{1,0},{2,3},{3,2},{4,5},{5,4},{6,7},{7,6},{8,9},{9,8},{10,11... | collective-permute-start | bytes 737288 | tf_op jit(solution)/shard_map/ppermute | solution.py:291
  77.2 1.8 %collective-permute-start.13 = (bf16[48,2048]{1,0:T(8,128)(2,1)S(1)}, bf16[48,2048]{1,0:T(8,128)(2,1)S(1)}, u32[]{:S(2)}, u32[]{:S(2)}) collective-permute-start(bf16[48,2048]{1,0:T(8,128)(2,1)S(1)} %get-tuple-element.45.refs_0_), channel_id=1, source_target_pairs={{0,1},{1,0},{2,3},{3,2},{4,5},{5,4},{6,7},{7,6},{8,9},{9,8},{10,11... | collective-permute-start | bytes 589832 | tf_op jit(solution)/shard_map/ppermute | solution.py:291
  90.2 7.0 %collective-permute-start.18 = (bf16[48,2048]{1,0:T(8,128)(2,1)S(1)}, bf16[48,2048]{1,0:T(8,128)(2,1)S(1)}, u32[]{:S(2)}, u32[]{:S(2)}) collective-permute-start(bf16[48,2048]{1,0:T(8,128)(2,1)S(1)} %activate.5.refs_0_), channel_id=1, source_target_pairs={{0,2},{1,3},{2,0},{3,1},{4,6},{5,7},{6,4},{7,5},{8,10},{9,11},{10,... | collective-permute-start | bytes 589832 | tf_op jit(solution)/shard_map/ppermute | solution.py:294
  91.3 5.8 %collective-permute-start.19 = (bf16[48,2048]{1,0:T(8,128)(2,1)S(1)}, bf16[48,2048]{1,0:T(8,128)(2,1)S(1)}, u32[]{:S(2)}, u32[]{:S(2)}) collective-permute-start(bf16[48,2048]{1,0:T(8,128)(2,1)S(1)} %activate.5.refs_0_), channel_id=1, source_target_pairs={{0,1},{1,0},{2,3},{3,2},{4,5},{5,4},{6,7},{7,6},{8,9},{9,8},{10,11... | collective-permute-start | bytes 589832 | tf_op jit(solution)/shard_map/ppermute | solution.py:291
  104.6 5.3 %collective-permute-start.22 = (bf16[64,2048]{1,0:T(8,128)(2,1)S(1)}, bf16[64,2048]{1,0:T(8,128)(2,1)S(1)}, u32[]{:S(2)}, u32[]{:S(2)}) collective-permute-start(bf16[64,2048]{1,0:T(8,128)(2,1)S(1)} %get-tuple-element.53), channel_id=1, source_target_pairs={{4,8},{8,4},{5,9},{9,5},{6,10},{10,6},{7,11},{11,7},{20,24},{24,20... | collective-permute-start | bytes 786440 | tf_op jit(solution)/shard_map/ppermute | solution.py:288
  105.2 10.1 %collective-permute-start.21 = (bf16[64,2048]{1,0:T(8,128)(2,1)S(1)}, bf16[64,2048]{1,0:T(8,128)(2,1)S(1)}, u32[]{:S(2)}, u32[]{:S(2)}) collective-permute-start(bf16[64,2048]{1,0:T(8,128)(2,1)S(1)} %get-tuple-element.53), channel_id=1, source_target_pairs={{0,4},{12,8},{1,5},{13,9},{2,6},{14,10},{3,7},{15,11},{16,20},{28,... | collective-permute-start | bytes 786440 | tf_op jit(solution)/shard_map/ppermute | solution.py:288
  115.4 13.8 %collective-permute-start.25 = (bf16[64,2048]{1,0:T(8,128)(2,1)S(1)}, bf16[64,2048]{1,0:T(8,128)(2,1)S(1)}, u32[]{:S(2)}, u32[]{:S(2)}) collective-permute-start(bf16[64,2048]{1,0:T(8,128)(2,1)S(1)} %get-tuple-element.58), channel_id=1, source_target_pairs={{0,8},{4,12},{8,0},{12,4},{1,9},{5,13},{9,1},{13,5},{2,10},{6,14},... | collective-permute-start | bytes 786440 | tf_op jit(solution)/shard_map/ppermute | solution.py:288
  117.7 9.1 %collective-permute-start.23 = (bf16[32,2048]{1,0:T(8,128)(2,1)S(1)}, bf16[32,2048]{1,0:T(8,128)(2,1)S(1)}, u32[]{:S(2)}, u32[]{:S(2)}) collective-permute-start(bf16[32,2048]{1,0:T(8,128)(2,1)S(1)} %get-tuple-element.56), channel_id=1, source_target_pairs={{0,4},{4,0},{8,12},{12,8},{1,5},{5,1},{9,13},{13,9},{2,6},{6,2},{1... | collective-permute-start | bytes 393224 | tf_op jit(solution)/shard_map/ppermute | solution.py:288
  118.1 10.2 %collective-permute-start.24 = (bf16[32,2048]{1,0:T(8,128)(2,1)S(1)}, bf16[32,2048]{1,0:T(8,128)(2,1)S(1)}, u32[]{:S(2)}, u32[]{:S(2)}) collective-permute-start(bf16[32,2048]{1,0:T(8,128)(2,1)S(1)} %get-tuple-element.57), channel_id=1, source_target_pairs={{0,4},{4,0},{8,12},{12,8},{1,5},{5,1},{9,13},{13,9},{2,6},{6,2},{1... | collective-permute-start | bytes 393224 | tf_op jit(solution)/shard_map/ppermute | solution.py:288
  (4 other events, 4.6 us)

commit v7 on v6

--- a/solution.py
+++ b/solution.py
@@ -33,11 +33,19 @@
     return rows
 
 
-def picks_kernel(n_gx, nx, tok_dev, lengths_ref, tok_ref, in_ref, out_ref, held_ref):
+def prepare_kernel(n_gx, nx, lengths_ref, tok_ref, gate_ref, up_ref, in_ref, out_ref, held_ref, gate_out, up_out, sems):
+    fetched = pl.ds(0, gate_out.shape[1])
+    copies = [
+        pltpu.make_async_copy(src.at[:, fetched], dst, sems.at[i])
+        for i, (src, dst) in enumerate(((gate_ref, gate_out), (up_ref, up_out)))
+    ]
+    for copy in copies:
+        copy.start()
+    tok_dev = tok_ref.shape[0]
     z = lax.axis_index("gx")
     live, slots = in_ref.shape
+    quarter = live // (2 * nx)
     held_ref[...] = tok_ref[...]
-    quarter = live // (2 * nx)
 
     def slot_of(column):
         return (z ^ (column // tok_dev)) * tok_dev + column % tok_dev
@@ -48,25 +56,44 @@
     shape = (slots, live)
     source = row_sources(lengths_ref, local_rows(shape, 1, quarter, nx), n_gx, tok_dev)
     out_ref[...] = (source == slot_of(lax.broadcasted_iota(jnp.int32, shape, 0))).astype(F32).astype(BF16)
-
-
-def picks(lengths, tokens, n_gx, nx, live):
-    tok_dev = tokens.shape[0]
-    slots = n_gx * tok_dev
-    held = pl.BlockSpec(memory_space=pltpu.VMEM)
-    return pl.pallas_call(
-        functools.partial(picks_kernel, n_gx, nx, tok_dev),
+    for copy in copies:
+        copy.wait()
+
+
+def prepare(lengths, tokens, gate_weight, up_weight, fetched, n_gx, nx, live):
+    slots = n_gx * tokens.shape[0]
+    held, anywhere = pl.BlockSpec(memory_space=pltpu.VMEM), pl.BlockSpec(memory_space=pl.ANY)
+    weight = jax.ShapeDtypeStruct((gate_weight.shape[0], fetched), BF16)
+    return pl.pallas_call(
+        functools.partial(prepare_kernel, n_gx, nx),
         out_shape=[
             jax.ShapeDtypeStruct((live, slots), BF16),
             jax.ShapeDtypeStruct((slots, live), BF16),
             jax.ShapeDtypeStruct(tokens.shape, tokens.dtype),
+            weight,
+            weight,
         ],
-        in_specs=[pl.BlockSpec(memory_space=pltpu.SMEM), held],
-        out_specs=[held] * 3,
-        cost_estimate=pl.CostEstimate(flops=0, bytes_accessed=4 * live * slots, transcendentals=0),
-        compiler_params=pltpu.CompilerParams(vmem_limit_bytes=8 * MIB),
-        name="picks",
-    )(lengths, tokens)
+        in_specs=[pl.BlockSpec(memory_space=pltpu.SMEM), held, anywhere, anywhere],
+        out_specs=[held] * 5,
+        scratch_shapes=[pltpu.SemaphoreType.DMA((2,))],
+        cost_estimate=pl.CostEstimate(flops=0, bytes_accessed=0, transcendentals=0),
+        compiler_params=pltpu.CompilerParams(vmem_limit_bytes=8 * MIB),
+        name="prepare",
+    )(lengths, tokens, gate_weight, up_weight)
+
+
+def follow(handed, after):
+    anywhere = pl.BlockSpec(memory_space=pl.ANY)
+    return pl.pallas_call(
+        lambda *refs: None,
+        out_shape=jax.ShapeDtypeStruct(handed.shape, handed.dtype),
+        in_specs=[anywhere] * (1 + len(after)),
+        out_specs=anywhere,
+        input_output_aliases={0: 0},
+        compiler_params=pltpu.CompilerParams(vmem_limit_bytes=8 * MIB),
+        cost_estimate=pl.CostEstimate(flops=0, bytes_accessed=0, transcendentals=0),
+        name="follow",
+    )(handed, *after)
 
 
 def compact_kernel(groups, pick_ref, *refs):
@@ -127,6 +154,30 @@
         ),
         name="gate_up",
     )(tok, gate_weight, up_weight, *after)
+
+
+def gate_up_held_kernel(start, width, tile, tok_ref, gate_ref, up_ref, send_ref, keep_ref):
+    half = keep_ref.shape[1]
+    rows = tok_ref[...]
+    for j in range(0, width, tile):
+        for i, w_ref in enumerate((gate_ref, up_ref)):
+            part = jnp.dot(rows, w_ref[:, start + j:start + j + tile], preferred_element_type=F32)
+            keep_ref[i, :, j:j + tile] = part[:half]
+            send_ref[i, :, j:j + tile] = part[half:].astype(BF16)
+
+
+def gate_up_held(tok, gate_held, up_held, start, width, tile):
+    half = tok.shape[0] // 2
+    held = pl.BlockSpec(memory_space=pltpu.VMEM)
+    return pl.pallas_call(
+        functools.partial(gate_up_held_kernel, start, width, tile),
+        out_shape=[jax.ShapeDtypeStruct((2, half, width), BF16), jax.ShapeDtypeStruct((2, half, width), F32)],
+        in_specs=[held] * 3,
+        out_specs=[held] * 2,
+        compiler_params=pltpu.CompilerParams(vmem_limit_bytes=12 * MIB),
+        cost_estimate=pl.CostEstimate(flops=0, bytes_accessed=0, transcendentals=0),
+        name="gate_up_held",
+    )(tok, gate_held, up_held)
 
 
 def join_kernel(n_handed, n_after, nx, keep_ref, got_ref, *refs):
@@ -268,7 +319,7 @@
 
 def column_chunks(cols, tile):
     tiles = cols // tile
-    shares = (4, 5, 4)
+    shares = (3, 3, 4, 3)
     edges = [round(tiles * sum(shares[:i]) / sum(shares)) for i in range(len(shares) + 1)]
     return [(a * tile, (b - a) * tile) for a, b in zip(edges, edges[1:]) if b > a]
 
@@ -293,40 +344,51 @@
     def over_x(block, k):
         return lax.ppermute(block, "gy", [(i, (i + 2 * k) % n_gy) for i in range(n_gy)])
 
-    pick_in, pick_out, held = picks(lengths, tokens, n_gx, nx, live)
+    first = sum(width for _, width in chunks[:2])
+    pick_in, pick_out, held, gate_held, up_held = prepare(
+        lengths, tokens, gate_weight, up_weight, first, n_gx, nx, live
+    )
     if line:
         two = [over_z(tokens[:part], 2), over_z(tokens[part:], 2)]
         one = over_z(tokens, 1)
         middle = over_z(tokens, 3, (1, 2))
+        two = [follow(piece, [pick_in]) for piece in two]
         ends = [over_z(piece, 1, (1, 2)) for piece in two]
         blocks = [[[held]], [[one]], [two], [[middle], ends]]
     else:
         blocks = [[[held]]] + [[[over_z(tokens, k)]] for k in range(1, n_gx)]
     tok = compact(pick_in, blocks)
 
-    send, keep = gate_up(tok, gate_weight, up_weight, [], *chunks[0], tile)
-    hidden, fars, total = [], [], None
-
-    def pieces(own, far):
+    made = [gate_up_held(tok, gate_held, up_held, *chunk, tile) for chunk in chunks[:2]]
+    sends, keeps = [list(a) for a in zip(*made)]
+    mines, gots, owns, fars, hidden, total = [], [], [], [], [], None
+
+    def exchange(j, handed):
+        mine, blocks, handed = join(keeps[j], over_core(sends[j]), handed, [], nx)
+        mines.append(mine)
+        gots.append([over_x(b, k + 1) for k, b in enumerate(blocks)])
+        return list(blocks), handed
+
+    def finish(j, handed, after):
+        own, handed = activate(mines[j], gots[j], handed, after)
+        far = [over_x(own, -k) for k in range(1, nx)]
+        owns.append(own)
+        fars.append(far)
         h = [own] + far
-        return h + [over_core(a) for a in h]
-
-    for j in range(n):
-        mine, blocks, _ = join(keep, over_core(send), [], [], nx)
-        got = [over_x(b, k + 1) for k, b in enumerate(blocks)]
-        handed, after = [], fars[-1] if fars else []
-        if j + 1 < n:
-            send, keep = gate_up(tok, gate_weight, up_weight, blocks, *chunks[j + 1], tile)
-            handed = [send]
-        elif n > 1:
-            total = down(hidden, down_weight, None, None, None, list(blocks), chunks[0][0])
-            after = [total]
-        own, handed = activate(mine, got, handed, after)
-        if handed:
-            send = handed[0]
-        far = [over_x(own, -k) for k in range(1, nx)]
-        fars.append(far)
-        hidden.append(pieces(own, far))
+        hidden.append(h + [over_core(a) for a in h])
+        return handed
+
+    ready, sends[1:2] = exchange(0, sends[1:2])
+    ready += exchange(1, [])[0]
+    for j in range(2, n):
+        send, keep = gate_up(tok, gate_weight, up_weight, ready, *chunks[j], tile)
+        keeps.append(keep)
+        sends += finish(j - 2, [send], [])
+        ready = exchange(j, [])[0]
+    finish(n - 2, [], ready)
+    total = down(hidden[:n - 2], down_weight, None, None, None, [owns[n - 2]], chunks[0][0])
+    finish(n - 1, [], [total])
+    total = down(hidden[n - 2:n - 1], down_weight, total, None, None, [], chunks[n - 2][0])
     out_rows = [tok_dev, part, part, tok_dev, tok_dev] if line else [tok_dev] * n_gx
     spread = down(hidden[-1:], down_weight, total, pick_out, out_rows, [], chunks[-1][0])
 

time: 130 us -> 129 us (level)
  waiting for transfers between devices: 54.6 us -> 41.5 us
  starting transfers between devices: 27.1 us -> 33.9 us
  Pallas kernels: 44.7 us -> 49.4 us
    pallas_call x1 -> x5, Pallas kernels: 0.67 us -> 14.1 us  [the longest x1 8.92 us: prepare(): pl.pallas_call(functools.partial(prepare_kernel, n_gx, nx), out_shape=[ja...]
    pallas_call x3 -> x2, Pallas kernels: 26.1 us -> 14.7 us  [gate_up(): pl.pallas_call(gate_up_kernel, out_shape=[jax.ShapeDtypeStruct((2, half,...]
    ppermute x9 -> x12, waiting for transfers between devices: 8.91 us -> 0.41 us  [over_core(): return lax.ppermute(block, 'gy', [(i, i ^ 1) for i in range(n_gy)])]
    ppermute x11, waiting for transfers between devices: 27.3 us -> 22.6 us  [over_z(): return lax.ppermute(block, 'gx', [(z, z ^ k) for z in among])]
    ppermute x11, starting transfers between devices: 18.8 us -> 21.8 us  [over_z(): return lax.ppermute(block, 'gx', [(z, z ^ k) for z in among])]
    pallas_call x2 -> x3, Pallas kernels: 16.6 us -> 19.1 us  [down(): pl.pallas_call(functools.partial(down_kernel, [len(c) for c in hidden], l...]
    ppermute x6 -> x8, starting transfers between devices: 7.53 us -> 9.82 us  [over_x(): lax.ppermute(block, 'gy', [(i, (i + 2 * k) % n_gy) for i in range(n_gy)])]
    ppermute x9 -> x12, starting transfers between devices: 0.73 us -> 2.26 us  [over_core(): return lax.ppermute(block, 'gy', [(i, i ^ 1) for i in range(n_gy)])]
  transfers between devices with their start and end apart: 26 -> 31, of which waited for: 17 -> 12; matrix products, arithmetic and copies ran while one was open for 0% -> 0% of each run, Pallas kernels for 23% -> 32%
where the time goes in v7:
time: 129 us; the launch traced here: 128 us
  Pallas kernels  49.4 us (38%)
  waiting for transfers between devices  41.5 us (32%)
  starting transfers between devices  33.9 us (26%)
  local copies, waits for them, and re-layouts  2.59 us (2%)
    ppermute x11, waiting for transfers between devices, over_z(): return lax.ppermute(block, 'gx', [(z, z ^ k) for z in among])  22.6 us
    ppermute x11, starting transfers between devices, over_z(): return lax.ppermute(block, 'gx', [(z, z ^ k) for z in among])  21.8 us
    pallas_call x3, Pallas kernels, down(): pl.pallas_call(functools.partial(down_kernel, [len(c) for c in hidden], l...  19.1 us
    ppermute x8, waiting for transfers between devices, over_x(): lax.ppermute(block, 'gy', [(i, (i + 2 * k) % n_gy) for i in range(n_gy)])  18.5 us
    pallas_call x2, Pallas kernels, gate_up(): pl.pallas_call(gate_up_kernel, out_shape=[jax.ShapeDtypeStruct((2, half,...  14.7 us
    ppermute x8, starting transfers between devices, over_x(): lax.ppermute(block, 'gy', [(i, (i + 2 * k) % n_gy) for i in range(n_gy)])  9.82 us
    pallas_call x1, Pallas kernels, prepare(): pl.pallas_call(functools.partial(prepare_kernel, n_gx, nx), out_shape=[ja...  8.92 us
    pallas_call x2, Pallas kernels, gate_up_held(): pl.pallas_call(functools.partial(gate_up_held_kernel, start, width, tile)...  5.22 us
  transfers between devices with their start and end apart: 31, of which 12 were waited for; matrix products, arithmetic and copies ran while one was open for 0% of the time, Pallas kernels for 32%

profile of v7, /device:TPU:0, one launch (start us, length us, event | category | flops | bytes accessed | tf_op | source)
XLA Modules:
  0.0 128.5 jit_solution(7891623291503309765)
XLA Ops:
  1.0 4.1 %collective-permute-start.1 = (bf16[32,2048]{1,0:T(8,128)(2,1)S(1)}, bf16[32,2048]{1,0:T(8,128)(2,1)S(1)}, u32[]{:S(2)}, u32[]{:S(2)}) collective-permute-start(bf16[32,2048]{1,0:T(8,128)(2,1)S(1)} %get-tuple-element.74), channel_id=1, source_target_pairs={{0,8},{4,12},{8,0},{12,4},{1,9},{5,13},{9,1},{13,5},{2,10},{6,14},... | collective-permute-start | bytes 393224 | tf_op jit(solution)/shard_map/ppermute | solution.py:339
  5.1 1.6 %collective-permute-start = (bf16[64,2048]{1,0:T(8,128)(2,1)}, bf16[64,2048]{1,0:T(8,128)(2,1)S(1)}, u32[]{:S(2)}, u32[]{:S(2)}) collective-permute-start(bf16[64,2048]{1,0:T(8,128)(2,1)} %tok_ref.1), channel_id=1, source_target_pairs={{0,4},{4,0},{8,12},{12,8},{1,5},{5,1},{9,13},{13,9},{2,6},{6,2},{1... | collective-permute-start | bytes 786440 | tf_op jit(solution)/shard_map/ppermute | solution.py:339
  7.3 3.2 %collective-permute-start.2 = (bf16[32,2048]{1,0:T(8,128)(2,1)S(1)}, bf16[32,2048]{1,0:T(8,128)(2,1)S(1)}, u32[]{:S(2)}, u32[]{:S(2)}) collective-permute-start(bf16[32,2048]{1,0:T(8,128)(2,1)S(1)} %get-tuple-element.73), channel_id=1, source_target_pairs={{0,8},{4,12},{8,0},{12,4},{1,9},{5,13},{9,1},{13,5},{2,10},{6,14},... | collective-permute-start | bytes 393224 | tf_op jit(solution)/shard_map/ppermute | solution.py:339
  12.2 8.9 %prepare.1 = (bf16[192,256]{1,0:T(8,128)(2,1)S(1)}, bf16[256,192]{1,0:T(8,128)(2,1)S(1)}, bf16[64,2048]{1,0:T(8,128)(2,1)S(1)}, bf16[2048,3072]{1,0:T(8,128)(2,1)S(1)}, bf16[2048,3072]{1,0:T(8,128)(2,1)S(1)}) custom-call(s32[4]{0:T(128)S(1)} %copy-done.1, bf16[64,2048]{1,0:T(8,128)(2,1)S(1)} %copy-done, bf16[2048,6656]{1,0:T(8,128)(2,1)} %gate_ref.5, ...), custom_call_target="tpu_custom_call" | custom-call | tf_op jit(solution)/shard_map/prepare/pallas_call | solution.py:67
  23.9 5.2 %collective-permute-done.4.refs_5_ = bf16[32,2048]{1,0:T(8,128)(2,1)S(1)} collective-permute-done((bf16[32,2048]{1,0:T(8,128)(2,1)S(1)}, bf16[32,2048]{1,0:T(8,128)(2,1)S(1)}, u32[]{:S(2)}, u32[]{:S(2)}) %collective-permute-start.4) | collective-permute-done | bytes 131104 | tf_op jit(solution)/shard_map/ppermute | solution.py:339
  30.9 2.6 %gate_up_held.2 = (bf16[2,96,1536]{2,1,0:T(8,128)(2,1)S(1)}, f32[2,96,1536]{2,1,0:T(8,128)S(1)}) custom-call(bf16[192,2048]{1,0:T(8,128)(2,1)S(1)} %compact.1.tok_ref, bf16[2048,3072]{1,0:T(8,128)(2,1)S(1)} %get-tuple-element.41.gate_ref, bf16[2048,3072]{1,0:T(8,128)(2,1)S(1)} %get-tuple-element.42.up_ref), custom_call_target="tpu_custom_call" | custom-call | tf_op jit(solution)/shard_map/gate_up_held/pallas_call | solution.py:172
  33.6 2.6 %gate_up_held.3 = (bf16[2,96,1536]{2,1,0:T(8,128)(2,1)S(1)}, f32[2,96,1536]{2,1,0:T(8,128)S(1)}) custom-call(bf16[192,2048]{1,0:T(8,128)(2,1)S(1)} %compact.1.tok_ref, bf16[2048,3072]{1,0:T(8,128)(2,1)S(1)} %get-tuple-element.41.gate_ref, bf16[2048,3072]{1,0:T(8,128)(2,1)S(1)} %get-tuple-element.42.up_ref), custom_call_target="tpu_custom_call" | custom-call | tf_op jit(solution)/shard_map/gate_up_held/pallas_call | solution.py:172
  36.9 1.6 %collective-permute-start.8 = (bf16[2,48,1536]{2,1,0:T(8,128)(2,1)S(1)}, bf16[2,48,1536]{2,1,0:T(8,128)(2,1)S(1)}, u32[]{:S(2)}, u32[]{:S(2)}) collective-permute-start(bf16[2,48,1536]{2,1,0:T(8,128)(2,1)S(1)} %get-tuple-element.46.refs_0_), channel_id=1, source_target_pairs={{0,2},{1,3},{2,0},{3,1},{4,6},{5,7},{6,4},{7,5},{8,10},{9,11},{10,... | collective-permute-start | bytes 884744 | tf_op jit(solution)/shard_map/ppermute | solution.py:345
  38.7 8.1 %gate_up.2 = (bf16[2,96,2048]{2,1,0:T(8,128)(2,1)S(1)}, f32[2,96,2048]{2,1,0:T(8,128)S(1)}) custom-call(bf16[192,2048]{1,0:T(8,128)(2,1)S(1)} %compact.1.tok_ref, bf16[2048,6656]{1,0:T(8,128)(2,1)} %gate_ref.5, bf16[2048,6656]{1,0:T(8,128)(2,1)} %up_ref.5, bf16[2,48,1536]{2,1,0:T(8,128)(2,1)S(1)} %get-tuple-element.46.refs_0_, ...), custom_call_target="tpu_custom_call" | custom-call | tf_op jit(solution)/shard_map/gate_up/pallas_call | solution.py:144
  49.4 6.7 %gate_up.3 = (bf16[2,96,1536]{2,1,0:T(8,128)(2,1)S(1)}, f32[2,96,1536]{2,1,0:T(8,128)S(1)}) custom-call(bf16[192,2048]{1,0:T(8,128)(2,1)S(1)} %compact.1.tok_ref, bf16[2048,6656]{1,0:T(8,128)(2,1)} %gate_ref.5, bf16[2048,6656]{1,0:T(8,128)(2,1)} %up_ref.5, bf16[2,48,2048]{2,1,0:T(8,128)(2,1)S(1)} %get-tuple-element.54.refs_0_), custom_call_target="tpu_custom_call" | custom-call | tf_op jit(solution)/shard_map/gate_up/pallas_call | solution.py:144
  56.6 1.6 %collective-permute-start.19 = (bf16[2,48,2048]{2,1,0:T(8,128)(2,1)S(1)}, bf16[2,48,2048]{2,1,0:T(8,128)(2,1)S(1)}, u32[]{:S(2)}, u32[]{:S(2)}) collective-permute-start(bf16[2,48,2048]{2,1,0:T(8,128)(2,1)S(1)} %get-tuple-element.54.refs_0_), channel_id=1, source_target_pairs={{0,2},{1,3},{2,0},{3,1},{4,6},{5,7},{6,4},{7,5},{8,10},{9,11},{10,... | collective-permute-start | bytes 1179656 | tf_op jit(solution)/shard_map/ppermute | solution.py:345
  58.7 1.6 %collective-permute-start.16 = (bf16[48,1536]{1,0:T(8,128)(2,1)S(1)}, bf16[48,1536]{1,0:T(8,128)(2,1)S(1)}, u32[]{:S(2)}, u32[]{:S(2)}) collective-permute-start(bf16[48,1536]{1,0:T(8,128)(2,1)S(1)} %get-tuple-element.62.refs_4_), channel_id=1, source_target_pairs={{0,2},{1,3},{2,0},{3,1},{4,6},{5,7},{6,4},{7,5},{8,10},{9,11},{10,... | collective-permute-start | bytes 442376 | tf_op jit(solution)/shard_map/ppermute | solution.py:345
  60.9 10.8 %collective-permute-done.13.refs_1_ = bf16[48,1536]{1,0:T(8,128)(2,1)S(1)} collective-permute-done((bf16[48,1536]{1,0:T(8,128)(2,1)S(1)}, bf16[48,1536]{1,0:T(8,128)(2,1)S(1)}, u32[]{:S(2)}, u32[]{:S(2)}) %collective-permute-start.13) | collective-permute-done | bytes 147488 | tf_op jit(solution)/shard_map/ppermute | solution.py:345
  71.7 3.2 %collective-permute-done.16.refs_5_ = bf16[48,1536]{1,0:T(8,128)(2,1)S(1)} collective-permute-done((bf16[48,1536]{1,0:T(8,128)(2,1)S(1)}, bf16[48,1536]{1,0:T(8,128)(2,1)S(1)}, u32[]{:S(2)}, u32[]{:S(2)}) %collective-permute-start.16) | collective-permute-done | bytes 147488 | tf_op jit(solution)/shard_map/ppermute | solution.py:345
  75.6 1.7 %collective-permute-start.23 = (bf16[48,2048]{1,0:T(8,128)(2,1)S(1)}, bf16[48,2048]{1,0:T(8,128)(2,1)S(1)}, u32[]{:S(2)}, u32[]{:S(2)}) collective-permute-start(bf16[48,2048]{1,0:T(8,128)(2,1)S(1)} %activate.6.refs_9_.refs_0_), channel_id=1, source_target_pairs={{0,2},{1,3},{2,0},{3,1},{4,6},{5,7},{6,4},{7,5},{8,10},{9,11},{10,... | collective-permute-start | bytes 589832 | tf_op jit(solution)/shard_map/ppermute | solution.py:345
  77.2 8.6 %down.3.refs_1_.refs_5_ = f32[192,2048]{1,0:T(8,128)S(1)} custom-call(bf16[48,1536]{1,0:T(8,128)(2,1)S(1)} %get-tuple-element.61.refs_0_, bf16[48,1536]{1,0:T(8,128)(2,1)S(1)} %collective-permute-done.13.refs_1_, bf16[48,1536]{1,0:T(8,128)(2,1)S(1)} %collective-permute-done.14.refs_2_, bf16[48,1536]{1,0:T(8,128)(2,1)S(1)} %collective-permute-done.15.refs_3_, ...), custom_call_target="tpu_custom_call" | custom-call | tf_op jit(solution)/shard_map/down/pallas_call | solution.py:307
  87.4 4.1 %collective-permute-done.20.refs_1_ = bf16[48,1536]{1,0:T(8,128)(2,1)S(1)} collective-permute-done((bf16[48,1536]{1,0:T(8,128)(2,1)S(1)}, bf16[48,1536]{1,0:T(8,128)(2,1)S(1)}, u32[]{:S(2)}, u32[]{:S(2)}) %collective-permute-start.20) | collective-permute-done | bytes 147488 | tf_op jit(solution)/shard_map/ppermute | solution.py:345
  91.6 5.3 %down.4.refs_5_ = f32[192,2048]{1,0:T(8,128)S(1)} custom-call(bf16[48,2048]{1,0:T(8,128)(2,1)S(1)} %activate.6.refs_9_.refs_0_, bf16[48,2048]{1,0:T(8,128)(2,1)S(1)} %collective-permute-done.23.refs_1_, bf16[48,2048]{1,0:T(8,128)(2,1)S(1)} %collective-permute-done.24.refs_2_, bf16[48,2048]{1,0:T(8,128)(2,1)S(1)} %collective-permute-done.25.refs_3_, ...), custom_call_target="tpu_custom_call" | custom-call | tf_op jit(solution)/shard_map/down/pallas_call | solution.py:307
  96.9 5.2 %down.5 = (bf16[64,2048]{1,0:T(8,128)(2,1)S(1)}, bf16[32,2048]{1,0:T(8,128)(2,1)S(1)}, bf16[32,2048]{1,0:T(8,128)(2,1)S(1)}, bf16[64,2048]{1,0:T(8,128)(2,1)S(1)}, bf16[64,2048]{1,0:T(8,128)(2,1)S(1)}) custom-call(bf16[48,1536]{1,0:T(8,128)(2,1)S(1)} %activate.7.refs_0_, bf16[48,1536]{1,0:T(8,128)(2,1)S(1)} %collective-permute-done.20.refs_1_, ...), custom_call_target="tpu_custom_call" | custom-call | tf_op jit(solution)/shard_map/down/pallas_call | solution.py:307
  102.8 4.7 %collective-permute-start.26 = (bf16[64,2048]{1,0:T(8,128)(2,1)S(1)}, bf16[64,2048]{1,0:T(8,128)(2,1)S(1)}, u32[]{:S(2)}, u32[]{:S(2)}) collective-permute-start(bf16[64,2048]{1,0:T(8,128)(2,1)S(1)} %get-tuple-element.67), channel_id=1, source_target_pairs={{0,4},{12,8},{1,5},{13,9},{2,6},{14,10},{3,7},{15,11},{16,20},{28,... | collective-permute-start | bytes 786440 | tf_op jit(solution)/shard_map/ppermute | solution.py:339
  107.5 5.9 %collective-permute-done.26.got_ref = bf16[64,2048]{1,0:T(8,128)(2,1)S(1)} collective-permute-done((bf16[64,2048]{1,0:T(8,128)(2,1)S(1)}, bf16[64,2048]{1,0:T(8,128)(2,1)S(1)}, u32[]{:S(2)}, u32[]{:S(2)}) %collective-permute-start.26) | collective-permute-done | bytes 262176 | tf_op jit(solution)/shard_map/ppermute | solution.py:339
  113.4 2.3 %collective-permute-start.30 = (bf16[64,2048]{1,0:T(8,128)(2,1)S(1)}, bf16[64,2048]{1,0:T(8,128)(2,1)S(1)}, u32[]{:S(2)}, u32[]{:S(2)}) collective-permute-start(bf16[64,2048]{1,0:T(8,128)(2,1)S(1)} %get-tuple-element.72), channel_id=1, source_target_pairs={{0,8},{4,12},{8,0},{12,4},{1,9},{5,13},{9,1},{13,5},{2,10},{6,14},... | collective-permute-start | bytes 786440 | tf_op jit(solution)/shard_map/ppermute | solution.py:339
  116.1 1.7 %collective-permute-start.29 = (bf16[32,2048]{1,0:T(8,128)(2,1)S(1)}, bf16[32,2048]{1,0:T(8,128)(2,1)S(1)}, u32[]{:S(2)}, u32[]{:S(2)}) collective-permute-start(bf16[32,2048]{1,0:T(8,128)(2,1)S(1)} %get-tuple-element.71), channel_id=1, source_target_pairs={{0,4},{4,0},{8,12},{12,8},{1,5},{5,1},{9,13},{13,9},{2,6},{6,2},{1... | collective-permute-start | bytes 393224 | tf_op jit(solution)/shard_map/ppermute | solution.py:339
  117.8 7.5 %collective-permute-done.28 = bf16[32,2048]{1,0:T(8,128)(2,1)S(1)} collective-permute-done((bf16[32,2048]{1,0:T(8,128)(2,1)S(1)}, bf16[32,2048]{1,0:T(8,128)(2,1)S(1)}, u32[]{:S(2)}, u32[]{:S(2)}) %collective-permute-start.28) | collective-permute-done | bytes 131104 | tf_op jit(solution)/shard_map/ppermute | solution.py:339
  (64 shorter events, 19.4 us)
Async XLA Ops:
  1.0 20.1 %collective-permute-start.1 = (bf16[32,2048]{1,0:T(8,128)(2,1)S(1)}, bf16[32,2048]{1,0:T(8,128)(2,1)S(1)}, u32[]{:S(2)}, u32[]{:S(2)}) collective-permute-start(bf16[32,2048]{1,0:T(8,128)(2,1)S(1)} %get-tuple-element.74), channel_id=1, source_target_pairs={{0,8},{4,12},{8,0},{12,4},{1,9},{5,13},{9,1},{13,5},{2,10},{6,14},... | collective-permute-start | bytes 393224 | tf_op jit(solution)/shard_map/ppermute | solution.py:339
  5.1 18.8 %collective-permute-start = (bf16[64,2048]{1,0:T(8,128)(2,1)}, bf16[64,2048]{1,0:T(8,128)(2,1)S(1)}, u32[]{:S(2)}, u32[]{:S(2)}) collective-permute-start(bf16[64,2048]{1,0:T(8,128)(2,1)} %tok_ref.1), channel_id=1, source_target_pairs={{0,4},{4,0},{8,12},{12,8},{1,5},{5,1},{9,13},{13,9},{2,6},{6,2},{1... | collective-permute-start | bytes 786440 | tf_op jit(solution)/shard_map/ppermute | solution.py:339
  6.7 17.3 %collective-permute-start.3 = (bf16[64,2048]{1,0:T(8,128)(2,1)}, bf16[64,2048]{1,0:T(8,128)(2,1)S(1)}, u32[]{:S(2)}, u32[]{:S(2)}) collective-permute-start(bf16[64,2048]{1,0:T(8,128)(2,1)} %tok_ref.1), channel_id=1, source_target_pairs={{4,8},{8,4},{5,9},{9,5},{6,10},{10,6},{7,11},{11,7},{20,24},{24,20... | collective-permute-start | bytes 786440 | tf_op jit(solution)/shard_map/ppermute | solution.py:339
  7.3 15.3 %collective-permute-start.2 = (bf16[32,2048]{1,0:T(8,128)(2,1)S(1)}, bf16[32,2048]{1,0:T(8,128)(2,1)S(1)}, u32[]{:S(2)}, u32[]{:S(2)}) collective-permute-start(bf16[32,2048]{1,0:T(8,128)(2,1)S(1)} %get-tuple-element.73), channel_id=1, source_target_pairs={{0,8},{4,12},{8,0},{12,4},{1,9},{5,13},{9,1},{13,5},{2,10},{6,14},... | collective-permute-start | bytes 393224 | tf_op jit(solution)/shard_map/ppermute | solution.py:339
  21.1 8.0 %collective-permute-start.4 = (bf16[32,2048]{1,0:T(8,128)(2,1)S(1)}, bf16[32,2048]{1,0:T(8,128)(2,1)S(1)}, u32[]{:S(2)}, u32[]{:S(2)}) collective-permute-start(bf16[32,2048]{1,0:T(8,128)(2,1)S(1)} %follow.2.refs_2_), channel_id=1, source_target_pairs={{4,0},{8,12},{5,1},{9,13},{6,2},{10,14},{7,3},{11,15},{20,16},{24,... | collective-permute-start | bytes 393224 | tf_op jit(solution)/shard_map/ppermute | solution.py:339
  22.6 7.9 %collective-permute-start.5 = (bf16[32,2048]{1,0:T(8,128)(2,1)S(1)}, bf16[32,2048]{1,0:T(8,128)(2,1)S(1)}, u32[]{:S(2)}, u32[]{:S(2)}) collective-permute-start(bf16[32,2048]{1,0:T(8,128)(2,1)S(1)} %follow.3.refs_3_), channel_id=1, source_target_pairs={{4,0},{8,12},{5,1},{9,13},{6,2},{10,14},{7,3},{11,15},{20,16},{24,... | collective-permute-start | bytes 393224 | tf_op jit(solution)/shard_map/ppermute | solution.py:339
  36.9 9.8 %collective-permute-start.8 = (bf16[2,48,1536]{2,1,0:T(8,128)(2,1)S(1)}, bf16[2,48,1536]{2,1,0:T(8,128)(2,1)S(1)}, u32[]{:S(2)}, u32[]{:S(2)}) collective-permute-start(bf16[2,48,1536]{2,1,0:T(8,128)(2,1)S(1)} %get-tuple-element.46.refs_0_), channel_id=1, source_target_pairs={{0,2},{1,3},{2,0},{3,1},{4,6},{5,7},{6,4},{7,5},{8,10},{9,11},{10,... | collective-permute-start | bytes 884744 | tf_op jit(solution)/shard_map/ppermute | solution.py:345
  47.3 9.0 %collective-permute-start.10 = (bf16[2,48,1536]{2,1,0:T(8,128)(2,1)S(1)}, bf16[2,48,1536]{2,1,0:T(8,128)(2,1)S(1)}, u32[]{:S(2)}, u32[]{:S(2)}) collective-permute-start(bf16[2,48,1536]{2,1,0:T(8,128)(2,1)S(1)} %get-tuple-element.49.refs_1_), channel_id=1, source_target_pairs={{0,2},{1,3},{2,0},{3,1},{4,6},{5,7},{6,4},{7,5},{8,10},{9,11},{10,... | collective-permute-start | bytes 884744 | tf_op jit(solution)/shard_map/ppermute | solution.py:345
  56.6 18.3 %collective-permute-start.19 = (bf16[2,48,2048]{2,1,0:T(8,128)(2,1)S(1)}, bf16[2,48,2048]{2,1,0:T(8,128)(2,1)S(1)}, u32[]{:S(2)}, u32[]{:S(2)}) collective-permute-start(bf16[2,48,2048]{2,1,0:T(8,128)(2,1)S(1)} %get-tuple-element.54.refs_0_), channel_id=1, source_target_pairs={{0,2},{1,3},{2,0},{3,1},{4,6},{5,7},{6,4},{7,5},{8,10},{9,11},{10,... | collective-permute-start | bytes 1179656 | tf_op jit(solution)/shard_map/ppermute | solution.py:345
  58.2 13.5 %collective-permute-start.13 = (bf16[48,1536]{1,0:T(8,128)(2,1)S(1)}, bf16[48,1536]{1,0:T(8,128)(2,1)S(1)}, u32[]{:S(2)}, u32[]{:S(2)}) collective-permute-start(bf16[48,1536]{1,0:T(8,128)(2,1)S(1)} %get-tuple-element.61.refs_0_), channel_id=1, source_target_pairs={{0,2},{1,3},{2,0},{3,1},{4,6},{5,7},{6,4},{7,5},{8,10},{9,11},{10,... | collective-permute-start | bytes 442376 | tf_op jit(solution)/shard_map/ppermute | solution.py:345
  58.7 16.2 %collective-permute-start.16 = (bf16[48,1536]{1,0:T(8,128)(2,1)S(1)}, bf16[48,1536]{1,0:T(8,128)(2,1)S(1)}, u32[]{:S(2)}, u32[]{:S(2)}) collective-permute-start(bf16[48,1536]{1,0:T(8,128)(2,1)S(1)} %get-tuple-element.62.refs_4_), channel_id=1, source_target_pairs={{0,2},{1,3},{2,0},{3,1},{4,6},{5,7},{6,4},{7,5},{8,10},{9,11},{10,... | collective-permute-start | bytes 442376 | tf_op jit(solution)/shard_map/ppermute | solution.py:345
  60.4 25.5 %collective-permute-start.12 = (bf16[2,48,1536]{2,1,0:T(8,128)(2,1)S(1)}, bf16[2,48,1536]{2,1,0:T(8,128)(2,1)S(1)}, u32[]{:S(2)}, u32[]{:S(2)}) collective-permute-start(bf16[2,48,1536]{2,1,0:T(8,128)(2,1)S(1)} %get-tuple-element.60.refs_1_), channel_id=1, source_target_pairs={{0,2},{1,3},{2,0},{3,1},{4,6},{5,7},{6,4},{7,5},{8,10},{9,11},{10,... | collective-permute-start | bytes 884744 | tf_op jit(solution)/shard_map/ppermute | solution.py:345
  60.9 14.7 %collective-permute-start.14 = (bf16[48,1536]{1,0:T(8,128)(2,1)S(1)}, bf16[48,1536]{1,0:T(8,128)(2,1)S(1)}, u32[]{:S(2)}, u32[]{:S(2)}) collective-permute-start(bf16[48,1536]{1,0:T(8,128)(2,1)S(1)} %get-tuple-element.61.refs_0_), channel_id=1, source_target_pairs={{0,1},{1,0},{2,3},{3,2},{4,5},{5,4},{6,7},{7,6},{8,9},{9,8},{10,11... | collective-permute-start | bytes 442376 | tf_op jit(solution)/shard_map/ppermute | solution.py:342
  71.7 5.5 %collective-permute-start.15 = (bf16[48,1536]{1,0:T(8,128)(2,1)S(1)}, bf16[48,1536]{1,0:T(8,128)(2,1)S(1)}, u32[]{:S(2)}, u32[]{:S(2)}) collective-permute-start(bf16[48,1536]{1,0:T(8,128)(2,1)S(1)} %collective-permute-done.13.refs_1_), channel_id=1, source_target_pairs={{0,1},{1,0},{2,3},{3,2},{4,5},{5,4},{6,7},{7,6},{8,9},{9,8},{10,11... | collective-permute-start | bytes 442376 | tf_op jit(solution)/shard_map/ppermute | solution.py:342
  75.6 11.3 %collective-permute-start.23 = (bf16[48,2048]{1,0:T(8,128)(2,1)S(1)}, bf16[48,2048]{1,0:T(8,128)(2,1)S(1)}, u32[]{:S(2)}, u32[]{:S(2)}) collective-permute-start(bf16[48,2048]{1,0:T(8,128)(2,1)S(1)} %activate.6.refs_9_.refs_0_), channel_id=1, source_target_pairs={{0,2},{1,3},{2,0},{3,1},{4,6},{5,7},{6,4},{7,5},{8,10},{9,11},{10,... | collective-permute-start | bytes 589832 | tf_op jit(solution)/shard_map/ppermute | solution.py:345
  86.0 5.5 %collective-permute-start.20 = (bf16[48,1536]{1,0:T(8,128)(2,1)S(1)}, bf16[48,1536]{1,0:T(8,128)(2,1)S(1)}, u32[]{:S(2)}, u32[]{:S(2)}) collective-permute-start(bf16[48,1536]{1,0:T(8,128)(2,1)S(1)} %activate.7.refs_0_), channel_id=1, source_target_pairs={{0,2},{1,3},{2,0},{3,1},{4,6},{5,7},{6,4},{7,5},{8,10},{9,11},{10,... | collective-permute-start | bytes 442376 | tf_op jit(solution)/shard_map/ppermute | solution.py:345
  86.9 4.7 %collective-permute-start.24 = (bf16[48,2048]{1,0:T(8,128)(2,1)S(1)}, bf16[48,2048]{1,0:T(8,128)(2,1)S(1)}, u32[]{:S(2)}, u32[]{:S(2)}) collective-permute-start(bf16[48,2048]{1,0:T(8,128)(2,1)S(1)} %activate.6.refs_9_.refs_0_), channel_id=1, source_target_pairs={{0,1},{1,0},{2,3},{3,2},{4,5},{5,4},{6,7},{7,6},{8,9},{9,8},{10,11... | collective-permute-start | bytes 589832 | tf_op jit(solution)/shard_map/ppermute | solution.py:342
  87.4 9.5 %collective-permute-start.21 = (bf16[48,1536]{1,0:T(8,128)(2,1)S(1)}, bf16[48,1536]{1,0:T(8,128)(2,1)S(1)}, u32[]{:S(2)}, u32[]{:S(2)}) collective-permute-start(bf16[48,1536]{1,0:T(8,128)(2,1)S(1)} %activate.7.refs_0_), channel_id=1, source_target_pairs={{0,1},{1,0},{2,3},{3,2},{4,5},{5,4},{6,7},{7,6},{8,9},{9,8},{10,11... | collective-permute-start | bytes 442376 | tf_op jit(solution)/shard_map/ppermute | solution.py:342
  91.6 5.4 %collective-permute-start.22 = (bf16[48,1536]{1,0:T(8,128)(2,1)S(1)}, bf16[48,1536]{1,0:T(8,128)(2,1)S(1)}, u32[]{:S(2)}, u32[]{:S(2)}) collective-permute-start(bf16[48,1536]{1,0:T(8,128)(2,1)S(1)} %collective-permute-done.20.refs_1_), channel_id=1, source_target_pairs={{0,1},{1,0},{2,3},{3,2},{4,5},{5,4},{6,7},{7,6},{8,9},{9,8},{10,11... | collective-permute-start | bytes 442376 | tf_op jit(solution)/shard_map/ppermute | solution.py:342
  102.1 5.4 %collective-permute-start.27 = (bf16[64,2048]{1,0:T(8,128)(2,1)S(1)}, bf16[64,2048]{1,0:T(8,128)(2,1)S(1)}, u32[]{:S(2)}, u32[]{:S(2)}) collective-permute-start(bf16[64,2048]{1,0:T(8,128)(2,1)S(1)} %get-tuple-element.67), channel_id=1, source_target_pairs={{4,8},{8,4},{5,9},{9,5},{6,10},{10,6},{7,11},{11,7},{20,24},{24,20... | collective-permute-start | bytes 786440 | tf_op jit(solution)/shard_map/ppermute | solution.py:339
  102.8 10.6 %collective-permute-start.26 = (bf16[64,2048]{1,0:T(8,128)(2,1)S(1)}, bf16[64,2048]{1,0:T(8,128)(2,1)S(1)}, u32[]{:S(2)}, u32[]{:S(2)}) collective-permute-start(bf16[64,2048]{1,0:T(8,128)(2,1)S(1)} %get-tuple-element.67), channel_id=1, source_target_pairs={{0,4},{12,8},{1,5},{13,9},{2,6},{14,10},{3,7},{15,11},{16,20},{28,... | collective-permute-start | bytes 786440 | tf_op jit(solution)/shard_map/ppermute | solution.py:339
  113.4 14.2 %collective-permute-start.30 = (bf16[64,2048]{1,0:T(8,128)(2,1)S(1)}, bf16[64,2048]{1,0:T(8,128)(2,1)S(1)}, u32[]{:S(2)}, u32[]{:S(2)}) collective-permute-start(bf16[64,2048]{1,0:T(8,128)(2,1)S(1)} %get-tuple-element.72), channel_id=1, source_target_pairs={{0,8},{4,12},{8,0},{12,4},{1,9},{5,13},{9,1},{13,5},{2,10},{6,14},... | collective-permute-start | bytes 786440 | tf_op jit(solution)/shard_map/ppermute | solution.py:339
  115.7 9.5 %collective-permute-start.28 = (bf16[32,2048]{1,0:T(8,128)(2,1)S(1)}, bf16[32,2048]{1,0:T(8,128)(2,1)S(1)}, u32[]{:S(2)}, u32[]{:S(2)}) collective-permute-start(bf16[32,2048]{1,0:T(8,128)(2,1)S(1)} %get-tuple-element.70), channel_id=1, source_target_pairs={{0,4},{4,0},{8,12},{12,8},{1,5},{5,1},{9,13},{13,9},{2,6},{6,2},{1... | collective-permute-start | bytes 393224 | tf_op jit(solution)/shard_map/ppermute | solution.py:339
  116.1 10.7 %collective-permute-start.29 = (bf16[32,2048]{1,0:T(8,128)(2,1)S(1)}, bf16[32,2048]{1,0:T(8,128)(2,1)S(1)}, u32[]{:S(2)}, u32[]{:S(2)}) collective-permute-start(bf16[32,2048]{1,0:T(8,128)(2,1)S(1)} %get-tuple-element.71), channel_id=1, source_target_pairs={{0,4},{4,0},{8,12},{12,8},{1,5},{5,1},{9,13},{13,9},{2,6},{6,2},{1... | collective-permute-start | bytes 393224 | tf_op jit(solution)/shard_map/ppermute | solution.py:339
  (9 other events, 22.0 us)

commit v8 on v7

--- a/solution.py
+++ b/solution.py
@@ -82,20 +82,6 @@
     )(lengths, tokens, gate_weight, up_weight)
 
 
-def follow(handed, after):
-    anywhere = pl.BlockSpec(memory_space=pl.ANY)
-    return pl.pallas_call(
-        lambda *refs: None,
-        out_shape=jax.ShapeDtypeStruct(handed.shape, handed.dtype),
-        in_specs=[anywhere] * (1 + len(after)),
-        out_specs=anywhere,
-        input_output_aliases={0: 0},
-        compiler_params=pltpu.CompilerParams(vmem_limit_bytes=8 * MIB),
-        cost_estimate=pl.CostEstimate(flops=0, bytes_accessed=0, transcendentals=0),
-        name="follow",
-    )(handed, *after)
-
-
 def compact_kernel(groups, pick_ref, *refs):
     refs = list(refs)
     out_ref = refs.pop()
@@ -206,27 +192,34 @@
     return out[0], out[1:nx], out[nx:]
 
 
-def activate_kernel(n_got, n_unread, mine_ref, *refs):
-    both = mine_ref[...]
-    for got_ref in refs[:n_got]:
-        both = both + got_ref[...].astype(F32)
-    gate, up = both[0], both[1]
-    refs[n_got + n_unread][...] = (gate / (1.0 + jnp.exp(-gate)) * up).astype(BF16)
-
-
-def activate(mine, got, handed, after):
+def activate_kernel(n_got, n_chunks, n_unread, *refs):
+    own_ref = refs[n_chunks * (1 + n_got) + n_unread]
+    column = 0
+    for c in range(n_chunks):
+        mine_ref, *got_refs = refs[c * (1 + n_got):(c + 1) * (1 + n_got)]
+        both = mine_ref[...]
+        for got_ref in got_refs:
+            both = both + got_ref[...].astype(F32)
+        gate, up = both[0], both[1]
+        own_ref[:, column:column + gate.shape[1]] = (gate / (1.0 + jnp.exp(-gate)) * up).astype(BF16)
+        column += gate.shape[1]
+
+
+def activate(sums, handed, after):
     held, anywhere = pl.BlockSpec(memory_space=pltpu.VMEM), pl.BlockSpec(memory_space=pl.ANY)
+    flat = [a for chunk in sums for a in chunk]
+    width = sum(chunk[0].shape[2] for chunk in sums)
     out = pl.pallas_call(
-        functools.partial(activate_kernel, len(got), len(handed) + len(after)),
-        out_shape=[jax.ShapeDtypeStruct(mine.shape[1:], BF16)]
+        functools.partial(activate_kernel, len(sums[0]) - 1, len(sums), len(handed) + len(after)),
+        out_shape=[jax.ShapeDtypeStruct((flat[0].shape[1], width), BF16)]
         + [jax.ShapeDtypeStruct(a.shape, a.dtype) for a in handed],
-        in_specs=[held] * (1 + len(got)) + [anywhere] * (len(handed) + len(after)),
+        in_specs=[held] * len(flat) + [anywhere] * (len(handed) + len(after)),
         out_specs=[held] + [anywhere] * len(handed),
-        input_output_aliases={1 + len(got) + i: 1 + i for i in range(len(handed))},
+        input_output_aliases={len(flat) + i: 1 + i for i in range(len(handed))},
         compiler_params=pltpu.CompilerParams(vmem_limit_bytes=8 * MIB),
         cost_estimate=pl.CostEstimate(flops=0, bytes_accessed=0, transcendentals=0),
         name="activate",
-    )(mine, *got, *handed, *after)
+    )(*flat, *handed, *after)
     return out[0], out[1:]
 
 
@@ -250,71 +243,105 @@
     return out[0], out[1:]
 
 
-def down_kernel(pieces, n_after, first, last, *refs):
-    refs, hidden = list(refs[:-1]), refs[-1]
-    h_refs = [[refs.pop(0) for _ in range(n)] for n in pieces]
-    w_ref, refs = refs[0], refs[1 + n_after:]
+def put_rows(h_refs, hidden):
+    row = 0
+    for r in h_refs:
+        hidden[row:row + r.shape[0]] = r[...]
+        row += r.shape[0]
+
+
+def down_kernel(n_h, *refs):
+    h_refs, w_ref, out_ref, hidden = refs[:n_h], refs[n_h], refs[-2], refs[-1]
 
     @pl.when(pl.program_id(0) == 0)
     def _():
-        column = 0
-        for chunk in h_refs:
-            row = 0
-            for r in chunk:
-                n, width = r.shape
-                hidden[row:row + n, column:column + width] = r[...]
-                row += n
-            column += width
-
-    total = jnp.dot(hidden[...], w_ref[...], preferred_element_type=F32)
-    if not first:
-        total += refs[0][...]
-        refs = refs[1:]
-    if not last:
-        refs[0][...] = total
-        return
-    pick_ref, outs = refs[0], refs[1:]
-    spread = jnp.dot(pick_ref[...], total.astype(BF16), preferred_element_type=F32).astype(BF16)
-    row = 0
-    for out_ref in outs:
-        n = out_ref.shape[0]
-        out_ref[...] = spread[row:row + n]
-        row += n
-
-
-def down(hidden, down_weight, total, pick, out_rows, after, start):
-    live = sum(h.shape[0] for h in hidden[0])
-    width = sum(chunk[0].shape[1] for chunk in hidden)
+        put_rows(h_refs, hidden)
+
+    out_ref[...] = jnp.dot(hidden[...], w_ref[...], preferred_element_type=F32)
+
+
+def down(hidden, down_weight, after, start):
+    live = sum(h.shape[0] for h in hidden)
+    width = hidden[0].shape[1]
     out_width = down_weight.shape[1]
-    tile = min(out_width, 512 if width <= 2560 else 256)
+    tile = min(out_width, 512)
+    weight = pl.BlockSpec((pl.Element(width), pl.Element(tile)), lambda j: (start, j * tile))
+    return pl.pallas_call(
+        functools.partial(down_kernel, len(hidden)),
+        out_shape=jax.ShapeDtypeStruct((live, out_width), F32),
+        grid=(out_width // tile,),
+        in_specs=[pl.BlockSpec(h.shape, lambda j: (0, 0)) for h in hidden]
+        + [weight]
+        + [pl.BlockSpec(memory_space=pl.ANY)] * len(after),
+        out_specs=pl.BlockSpec((live, tile), lambda j: (0, j)),
+        scratch_shapes=[pltpu.VMEM((live, width), BF16)],
+        compiler_params=pltpu.CompilerParams(vmem_limit_bytes=28 * MIB),
+        cost_estimate=pl.CostEstimate(flops=0, bytes_accessed=0, transcendentals=0),
+        name="down",
+    )(*hidden, down_weight, *after)
+
+
+def fetch_kernel(starts, src_ref, *refs):
+    outs, sems = refs[-1 - len(starts):-1], refs[-1]
+    copies = [
+        pltpu.make_async_copy(src_ref.at[pl.ds(start, out.shape[0])], out, sems.at[i])
+        for i, (start, out) in enumerate(zip(starts, outs))
+    ]
+    for copy in copies:
+        copy.start()
+    for copy in copies:
+        copy.wait()
+
+
+def fetch(down_weight, chunks, after):
+    held, anywhere = pl.BlockSpec(memory_space=pltpu.VMEM), pl.BlockSpec(memory_space=pl.ANY)
+    return pl.pallas_call(
+        functools.partial(fetch_kernel, [start for start, _ in chunks]),
+        out_shape=[jax.ShapeDtypeStruct((width, down_weight.shape[1]), BF16) for _, width in chunks],
+        in_specs=[anywhere] * (1 + len(after)),
+        out_specs=[held] * len(chunks),
+        scratch_shapes=[pltpu.SemaphoreType.DMA((len(chunks),))],
+        compiler_params=pltpu.CompilerParams(vmem_limit_bytes=28 * MIB),
+        cost_estimate=pl.CostEstimate(flops=0, bytes_accessed=0, transcendentals=0),
+        name="fetch",
+    )(down_weight, *after)
+
+
+def down_held_kernel(n_h, last, tile, *refs):
+    h_refs, w_ref, total_ref, outs, hidden = refs[:n_h], refs[n_h], refs[n_h + 1], refs[n_h + 2:-1], refs[-1]
+    put_rows(h_refs, hidden)
+    for j in range(0, total_ref.shape[1], tile):
+        total = jnp.dot(hidden[...], w_ref[:, j:j + tile], preferred_element_type=F32) + total_ref[:, j:j + tile]
+        if not last:
+            outs[0][:, j:j + tile] = total
+            continue
+        pick_ref = outs[0]
+        spread = jnp.dot(pick_ref[...], total.astype(BF16), preferred_element_type=F32).astype(BF16)
+        row = 0
+        for out_ref in outs[1:]:
+            n = out_ref.shape[0]
+            out_ref[:, j:j + tile] = spread[row:row + n]
+            row += n
+
+
+def down_held(hidden, weight_held, total, pick, out_rows):
+    live, out_width = total.shape
+    held = pl.BlockSpec(memory_space=pltpu.VMEM)
     last = pick is not None
-    rows = pl.BlockSpec((live, tile), lambda j: (0, j))
-    flat = [h for chunk in hidden for h in chunk]
-    operands = [*flat, down_weight, *after]
-    in_specs = [pl.BlockSpec(h.shape, lambda j: (0, 0)) for h in flat]
-    in_specs.append(pl.BlockSpec((pl.Element(width), pl.Element(tile)), lambda j: (start, j * tile)))
-    in_specs += [pl.BlockSpec(memory_space=pl.ANY)] * len(after)
-    if total is not None:
-        operands.append(total)
-        in_specs.append(rows)
     if last:
-        operands.append(pick)
-        in_specs.append(pl.BlockSpec(pick.shape, lambda j: (0, 0)))
         out_shape = [jax.ShapeDtypeStruct((n, out_width), BF16) for n in out_rows]
-        out_specs = [pl.BlockSpec((n, tile), lambda j: (0, j)) for n in out_rows]
     else:
-        out_shape, out_specs = jax.ShapeDtypeStruct((live, out_width), F32), rows
-    return pl.pallas_call(
-        functools.partial(down_kernel, [len(c) for c in hidden], len(after), total is None, last),
+        out_shape = jax.ShapeDtypeStruct((live, out_width), F32)
+    return pl.pallas_call(
+        functools.partial(down_held_kernel, len(hidden), last, min(out_width, 512)),
         out_shape=out_shape,
-        grid=(out_width // tile,),
-        in_specs=in_specs,
-        out_specs=out_specs,
-        scratch_shapes=[pltpu.VMEM((live, width), BF16)],
-        compiler_params=pltpu.CompilerParams(vmem_limit_bytes=40 * MIB),
-        cost_estimate=pl.CostEstimate(flops=0, bytes_accessed=0, transcendentals=0),
-        name="down",
-    )(*operands)
+        in_specs=[held] * (len(hidden) + (3 if last else 2)),
+        out_specs=[held] * len(out_rows) if last else held,
+        scratch_shapes=[pltpu.VMEM((live, hidden[0].shape[1]), BF16)],
+        compiler_params=pltpu.CompilerParams(vmem_limit_bytes=12 * MIB),
+        cost_estimate=pl.CostEstimate(flops=0, bytes_accessed=0, transcendentals=0),
+        name="down_held",
+    )(*hidden, weight_held, total, *([pick] if last else []))
 
 
 def column_chunks(cols, tile):
@@ -331,7 +358,6 @@
     cols = gate_weight.shape[1]
     tile = 512 if cols % 512 == 0 else 128
     chunks = column_chunks(cols, tile)
-    n = len(chunks)
     line = n_gx == 4
     part = tok_dev // 2
 
@@ -348,49 +374,40 @@
     pick_in, pick_out, held, gate_held, up_held = prepare(
         lengths, tokens, gate_weight, up_weight, first, n_gx, nx, live
     )
-    if line:
-        two = [over_z(tokens[:part], 2), over_z(tokens[part:], 2)]
-        one = over_z(tokens, 1)
-        middle = over_z(tokens, 3, (1, 2))
-        two = [follow(piece, [pick_in]) for piece in two]
-        ends = [over_z(piece, 1, (1, 2)) for piece in two]
-        blocks = [[[held]], [[one]], [two], [[middle], ends]]
-    else:
-        blocks = [[[held]]] + [[[over_z(tokens, k)]] for k in range(1, n_gx)]
+    blocks = [[[held]]] + [[[over_z(tokens, k)]] for k in range(1, n_gx)]
     tok = compact(pick_in, blocks)
 
     made = [gate_up_held(tok, gate_held, up_held, *chunk, tile) for chunk in chunks[:2]]
     sends, keeps = [list(a) for a in zip(*made)]
-    mines, gots, owns, fars, hidden, total = [], [], [], [], [], None
+    sums = []
 
     def exchange(j, handed):
         mine, blocks, handed = join(keeps[j], over_core(sends[j]), handed, [], nx)
-        mines.append(mine)
-        gots.append([over_x(b, k + 1) for k, b in enumerate(blocks)])
+        sums.append([mine] + [over_x(b, k + 1) for k, b in enumerate(blocks)])
         return list(blocks), handed
 
-    def finish(j, handed, after):
-        own, handed = activate(mines[j], gots[j], handed, after)
-        far = [over_x(own, -k) for k in range(1, nx)]
-        owns.append(own)
-        fars.append(far)
-        h = [own] + far
-        hidden.append(h + [over_core(a) for a in h])
-        return handed
+    def finish(first, last, handed, after):
+        own, handed = activate(sums[first:last], handed, after)
+        h = [own] + [over_x(own, -k) for k in range(1, nx)]
+        return h + [over_core(a) for a in h], handed
 
     ready, sends[1:2] = exchange(0, sends[1:2])
     ready += exchange(1, [])[0]
-    for j in range(2, n):
-        send, keep = gate_up(tok, gate_weight, up_weight, ready, *chunks[j], tile)
+    for chunk in chunks[2:]:
+        send, keep = gate_up(tok, gate_weight, up_weight, ready, *chunk, tile)
+        sends.append(send)
         keeps.append(keep)
-        sends += finish(j - 2, [send], [])
-        ready = exchange(j, [])[0]
-    finish(n - 2, [], ready)
-    total = down(hidden[:n - 2], down_weight, None, None, None, [owns[n - 2]], chunks[0][0])
-    finish(n - 1, [], [total])
-    total = down(hidden[n - 2:n - 1], down_weight, total, None, None, [], chunks[n - 2][0])
+        ready = [send]
+    hidden, sends[2:] = finish(0, 2, sends[2:], [])
+    ready, sends[3:] = exchange(2, sends[3:])
+    ready += exchange(3, [])[0]
+    rows_held = fetch(down_weight, chunks[2:], ready)
+    total = down(hidden, down_weight, [rows_held[0]], chunks[0][0])
+    hidden, _ = finish(2, 3, [], [total])
+    total = down_held(hidden, rows_held[0], total, None, None)
+    hidden, _ = finish(3, 4, [], [])
     out_rows = [tok_dev, part, part, tok_dev, tok_dev] if line else [tok_dev] * n_gx
-    spread = down(hidden[-1:], down_weight, total, pick_out, out_rows, [], chunks[-1][0])
+    spread = down_held(hidden, rows_held[1], total, pick_out, out_rows)
 
     if line:
         own, low, high, two, three = spread

time: 129 us -> 120 us (0.930)
  starting transfers between devices: 33.9 us -> 24.8 us
  waiting for transfers between devices: 41.5 us -> 45.9 us
  Pallas kernels: 49.4 us -> 46.1 us
    ppermute x11 -> x8, starting transfers between devices: 21.8 us -> 15.4 us  [over_z(): return lax.ppermute(block, 'gx', [(z, z ^ k) for z in among])]
    ppermute x11 -> x8, waiting for transfers between devices: 22.6 us -> 28.3 us  [over_z(): return lax.ppermute(block, 'gx', [(z, z ^ k) for z in among])]
    pallas_call x9 -> x7, Pallas kernels: 19.7 us -> 16.4 us  [the longest x1 6.64 us: down(): pl.pallas_call(functools.partial(down_kernel, len(hidden)), out_shape=jax...]
    ppermute x8 -> x7, waiting for transfers between devices: 18.5 us -> 15.3 us  [over_x(): lax.ppermute(block, 'gy', [(i, (i + 2 * k) % n_gy) for i in range(n_gy)])]
    ppermute x8 -> x7, starting transfers between devices: 9.82 us -> 7.87 us  [over_x(): lax.ppermute(block, 'gy', [(i, (i + 2 * k) % n_gy) for i in range(n_gy)])]
    ppermute x12 -> x10, waiting for transfers between devices: 0.41 us -> 2.35 us  [over_core(): return lax.ppermute(block, 'gy', [(i, i ^ 1) for i in range(n_gy)])]
  transfers between devices with their start and end apart: 31 -> 25, of which waited for: 12 -> 10; matrix products, arithmetic and copies ran while one was open for 0% -> 0% of each run, Pallas kernels for 32% -> 34%
where the time goes in v8:
time: 120 us; the launch traced here: 119 us
  Pallas kernels  46.1 us (38%)
  waiting for transfers between devices  45.9 us (38%)
  starting transfers between devices  24.8 us (21%)
  local copies, waits for them, and re-layouts  1.64 us (1%)
    ppermute x8, waiting for transfers between devices, over_z(): return lax.ppermute(block, 'gx', [(z, z ^ k) for z in among])  28.3 us
    ppermute x8, starting transfers between devices, over_z(): return lax.ppermute(block, 'gx', [(z, z ^ k) for z in among])  15.4 us
    ppermute x7, waiting for transfers between devices, over_x(): lax.ppermute(block, 'gy', [(i, (i + 2 * k) % n_gy) for i in range(n_gy)])  15.3 us
    pallas_call x2, Pallas kernels, gate_up(): pl.pallas_call(gate_up_kernel, out_shape=[jax.ShapeDtypeStruct((2, half,...  14.7 us
    pallas_call x1, Pallas kernels, prepare(): pl.pallas_call(functools.partial(prepare_kernel, n_gx, nx), out_shape=[ja...  8.92 us
    ppermute x7, starting transfers between devices, over_x(): lax.ppermute(block, 'gy', [(i, (i + 2 * k) % n_gy) for i in range(n_gy)])  7.87 us
    pallas_call x1, Pallas kernels, down(): pl.pallas_call(functools.partial(down_kernel, len(hidden)), out_shape=jax...  6.64 us
    pallas_call x2, Pallas kernels, gate_up_held(): pl.pallas_call(functools.partial(gate_up_held_kernel, start, width, tile)...  5.22 us
  transfers between devices with their start and end apart: 25, of which 10 were waited for; matrix products, arithmetic and copies ran while one was open for 0% of the time, Pallas kernels for 34%

profile of v8, /device:TPU:0, one launch (start us, length us, event | category | flops | bytes accessed | tf_op | source)
XLA Modules:
  0.0 119.5 jit_solution(5391105094898849665)
XLA Ops:
  0.0 3.0 %collective-permute-start = (bf16[64,2048]{1,0:T(8,128)(2,1)}, bf16[64,2048]{1,0:T(8,128)(2,1)S(1)}, u32[]{:S(2)}, u32[]{:S(2)}) collective-permute-start(bf16[64,2048]{1,0:T(8,128)(2,1)} %tok_ref.1), channel_id=1, source_target_pairs={{0,4},{4,0},{8,12},{12,8},{1,5},{5,1},{9,13},{13,9},{2,6},{6,2},{1... | collective-permute-start | bytes 786440 | tf_op jit(solution)/shard_map/ppermute | solution.py:365
  3.0 2.5 %collective-permute-start.2 = (bf16[64,2048]{1,0:T(8,128)(2,1)}, bf16[64,2048]{1,0:T(8,128)(2,1)S(1)}, u32[]{:S(2)}, u32[]{:S(2)}) collective-permute-start(bf16[64,2048]{1,0:T(8,128)(2,1)} %tok_ref.1), channel_id=1, source_target_pairs={{0,12},{4,8},{8,4},{12,0},{1,13},{5,9},{9,5},{13,1},{2,14},{6,10},... | collective-permute-start | bytes 786440 | tf_op jit(solution)/shard_map/ppermute | solution.py:365
  7.3 8.9 %prepare.1 = (bf16[192,256]{1,0:T(8,128)(2,1)S(1)}, bf16[256,192]{1,0:T(8,128)(2,1)S(1)}, bf16[64,2048]{1,0:T(8,128)(2,1)S(1)}, bf16[2048,3072]{1,0:T(8,128)(2,1)S(1)}, bf16[2048,3072]{1,0:T(8,128)(2,1)S(1)}) custom-call(s32[4]{0:T(128)S(1)} %copy-done.1, bf16[64,2048]{1,0:T(8,128)(2,1)S(1)} %copy-done, bf16[2048,6656]{1,0:T(8,128)(2,1)} %gate_ref.5, ...), custom_call_target="tpu_custom_call" | custom-call | tf_op jit(solution)/shard_map/prepare/pallas_call | solution.py:67
  16.2 2.4 %collective-permute-done.2.refs_3_ = bf16[64,2048]{1,0:T(8,128)(2,1)S(1)} collective-permute-done((bf16[64,2048]{1,0:T(8,128)(2,1)}, bf16[64,2048]{1,0:T(8,128)(2,1)S(1)}, u32[]{:S(2)}, u32[]{:S(2)}) %collective-permute-start.2) | collective-permute-done | bytes 262176 | tf_op jit(solution)/shard_map/ppermute | solution.py:365
  18.6 10.1 %collective-permute-done.1.refs_2_ = bf16[64,2048]{1,0:T(8,128)(2,1)S(1)} collective-permute-done((bf16[64,2048]{1,0:T(8,128)(2,1)}, bf16[64,2048]{1,0:T(8,128)(2,1)S(1)}, u32[]{:S(2)}, u32[]{:S(2)}) %collective-permute-start.1) | collective-permute-done | bytes 262176 | tf_op jit(solution)/shard_map/ppermute | solution.py:365
  29.1 2.6 %gate_up_held.2 = (bf16[2,96,1536]{2,1,0:T(8,128)(2,1)S(1)}, f32[2,96,1536]{2,1,0:T(8,128)S(1)}) custom-call(bf16[192,2048]{1,0:T(8,128)(2,1)S(1)} %compact.1.tok_ref, bf16[2048,3072]{1,0:T(8,128)(2,1)S(1)} %get-tuple-element.43.gate_ref, bf16[2048,3072]{1,0:T(8,128)(2,1)S(1)} %get-tuple-element.44.up_ref), custom_call_target="tpu_custom_call" | custom-call | tf_op jit(solution)/shard_map/gate_up_held/pallas_call | solution.py:158
  31.8 2.6 %gate_up_held.3 = (bf16[2,96,1536]{2,1,0:T(8,128)(2,1)S(1)}, f32[2,96,1536]{2,1,0:T(8,128)S(1)}) custom-call(bf16[192,2048]{1,0:T(8,128)(2,1)S(1)} %compact.1.tok_ref, bf16[2048,3072]{1,0:T(8,128)(2,1)S(1)} %get-tuple-element.43.gate_ref, bf16[2048,3072]{1,0:T(8,128)(2,1)S(1)} %get-tuple-element.44.up_ref), custom_call_target="tpu_custom_call" | custom-call | tf_op jit(solution)/shard_map/gate_up_held/pallas_call | solution.py:158
  36.8 1.6 %collective-permute-start.6 = (bf16[2,48,1536]{2,1,0:T(8,128)(2,1)S(1)}, bf16[2,48,1536]{2,1,0:T(8,128)(2,1)S(1)}, u32[]{:S(2)}, u32[]{:S(2)}) collective-permute-start(bf16[2,48,1536]{2,1,0:T(8,128)(2,1)S(1)} %get-tuple-element.51.refs_1_), channel_id=1, source_target_pairs={{0,2},{1,3},{2,0},{3,1},{4,6},{5,7},{6,4},{7,5},{8,10},{9,11},{10,... | collective-permute-start | bytes 884744 | tf_op jit(solution)/shard_map/ppermute | solution.py:371
  38.4 8.0 %gate_up.2 = (bf16[2,96,2048]{2,1,0:T(8,128)(2,1)S(1)}, f32[2,96,2048]{2,1,0:T(8,128)S(1)}) custom-call(bf16[192,2048]{1,0:T(8,128)(2,1)S(1)} %compact.1.tok_ref, bf16[2048,6656]{1,0:T(8,128)(2,1)} %gate_ref.5, bf16[2048,6656]{1,0:T(8,128)(2,1)} %up_ref.5, bf16[2,48,1536]{2,1,0:T(8,128)(2,1)S(1)} %get-tuple-element.48.refs_0_, ...), custom_call_target="tpu_custom_call" | custom-call | tf_op jit(solution)/shard_map/gate_up/pallas_call | solution.py:130
  46.5 6.7 %gate_up.3 = (bf16[2,96,1536]{2,1,0:T(8,128)(2,1)S(1)}, f32[2,96,1536]{2,1,0:T(8,128)S(1)}) custom-call(bf16[192,2048]{1,0:T(8,128)(2,1)S(1)} %compact.1.tok_ref, bf16[2048,6656]{1,0:T(8,128)(2,1)} %gate_ref.5, bf16[2048,6656]{1,0:T(8,128)(2,1)} %up_ref.5, bf16[2,96,2048]{2,1,0:T(8,128)(2,1)S(1)} %get-tuple-element.52.refs_0_.refs_4_), custom_call_target="tpu_custom_call" | custom-call | tf_op jit(solution)/shard_map/gate_up/pallas_call | solution.py:130
  53.6 2.2 %collective-permute-done.7.got_ref = bf16[2,96,2048]{2,1,0:T(8,128)(2,1)S(1)} collective-permute-done((bf16[2,96,2048]{2,1,0:T(8,128)(2,1)S(1)}, bf16[2,96,2048]{2,1,0:T(8,128)(2,1)S(1)}, u32[]{:S(2)}, u32[]{:S(2)}) %collective-permute-start.7) | collective-permute-done | bytes 786464 | tf_op jit(solution)/shard_map/ppermute | solution.py:368
  58.1 7.8 %collective-permute-done.14.refs_1_ = bf16[48,3072]{1,0:T(8,128)(2,1)S(1)} collective-permute-done((bf16[48,3072]{1,0:T(8,128)(2,1)S(1)}, bf16[48,3072]{1,0:T(8,128)(2,1)S(1)}, u32[]{:S(2)}, u32[]{:S(2)}) %collective-permute-start.14) | collective-permute-done | bytes 294944 | tf_op jit(solution)/shard_map/ppermute | solution.py:371
  66.6 5.2 %fetch.1 = (bf16[2048,2048]{1,0:T(8,128)(2,1)S(1)}, bf16[1536,2048]{1,0:T(8,128)(2,1)S(1)}) custom-call(bf16[6656,2048]{1,0:T(8,128)(2,1)} %refs_4_.1, bf16[2,48,2048]{2,1,0:T(8,128)(2,1)S(1)} %get-tuple-element.63.refs_0_, bf16[2,48,1536]{2,1,0:T(8,128)(2,1)S(1)} %get-tuple-element.62.refs_1_), custom_call_target="tpu_custom_call" | custom-call | tf_op jit(solution)/shard_map/fetch/pallas_call | solution.py:298
  71.8 6.6 %down.1.refs_2_.refs_5_ = f32[192,2048]{1,0:T(8,128)S(1)} custom-call(bf16[48,3072]{1,0:T(8,128)(2,1)S(1)} %get-tuple-element.66.refs_0_, bf16[48,3072]{1,0:T(8,128)(2,1)S(1)} %collective-permute-done.14.refs_1_, bf16[48,3072]{1,0:T(8,128)(2,1)S(1)} %collective-permute-done.15.refs_2_, bf16[48,3072]{1,0:T(8,128)(2,1)S(1)} %collective-permute-done.16.refs_3_, ...), custom_call_target="tpu_custom_call" | custom-call | tf_op jit(solution)/shard_map/down/pallas_call | solution.py:269
  81.0 5.5 %collective-permute-done.17.refs_1_ = bf16[48,2048]{1,0:T(8,128)(2,1)S(1)} collective-permute-done((bf16[48,2048]{1,0:T(8,128)(2,1)S(1)}, bf16[48,2048]{1,0:T(8,128)(2,1)S(1)}, u32[]{:S(2)}, u32[]{:S(2)}) %collective-permute-start.17) | collective-permute-done | bytes 196640 | tf_op jit(solution)/shard_map/ppermute | solution.py:371
  87.0 1.9 %collective-permute-done.10.refs_1_ = bf16[48,1536]{1,0:T(8,128)(2,1)S(1)} collective-permute-done((bf16[48,1536]{1,0:T(8,128)(2,1)S(1)}, bf16[48,1536]{1,0:T(8,128)(2,1)S(1)}, u32[]{:S(2)}, u32[]{:S(2)}) %collective-permute-start.10) | collective-permute-done | bytes 147488 | tf_op jit(solution)/shard_map/ppermute | solution.py:371
  88.9 1.8 %down_held.2.refs_5_ = f32[192,2048]{1,0:T(8,128)S(1)} custom-call(bf16[48,2048]{1,0:T(8,128)(2,1)S(1)} %activate.5.refs_0_, bf16[48,2048]{1,0:T(8,128)(2,1)S(1)} %collective-permute-done.17.refs_1_, bf16[48,2048]{1,0:T(8,128)(2,1)S(1)} %collective-permute-done.18.refs_2_, bf16[48,2048]{1,0:T(8,128)(2,1)S(1)} %collective-permute-done.19.refs_3_, ...), custom_call_target="tpu_custom_call" | custom-call | tf_op jit(solution)/shard_map/down_held/pallas_call | solution.py:335
  90.8 2.2 %down_held.3 = (bf16[64,2048]{1,0:T(8,128)(2,1)S(1)}, bf16[32,2048]{1,0:T(8,128)(2,1)S(1)}, bf16[32,2048]{1,0:T(8,128)(2,1)S(1)}, bf16[64,2048]{1,0:T(8,128)(2,1)S(1)}, bf16[64,2048]{1,0:T(8,128)(2,1)S(1)}) custom-call(bf16[48,1536]{1,0:T(8,128)(2,1)S(1)} %activate.4.refs_0_, bf16[48,1536]{1,0:T(8,128)(2,1)S(1)} %collective-permute-done.10.refs_1_, ...), custom_call_target="tpu_custom_call" | custom-call | tf_op jit(solution)/shard_map/down_held/pallas_call | solution.py:335
  93.7 3.4 %collective-permute-start.20 = (bf16[64,2048]{1,0:T(8,128)(2,1)S(1)}, bf16[64,2048]{1,0:T(8,128)(2,1)S(1)}, u32[]{:S(2)}, u32[]{:S(2)}) collective-permute-start(bf16[64,2048]{1,0:T(8,128)(2,1)S(1)} %get-tuple-element.71), channel_id=1, source_target_pairs={{0,4},{12,8},{1,5},{13,9},{2,6},{14,10},{3,7},{15,11},{16,20},{28,... | collective-permute-start | bytes 786440 | tf_op jit(solution)/shard_map/ppermute | solution.py:365
  97.1 5.9 %collective-permute-done.20.got_ref = bf16[64,2048]{1,0:T(8,128)(2,1)S(1)} collective-permute-done((bf16[64,2048]{1,0:T(8,128)(2,1)S(1)}, bf16[64,2048]{1,0:T(8,128)(2,1)S(1)}, u32[]{:S(2)}, u32[]{:S(2)}) %collective-permute-start.20) | collective-permute-done | bytes 262176 | tf_op jit(solution)/shard_map/ppermute | solution.py:365
  103.1 3.7 %collective-permute-start.24 = (bf16[64,2048]{1,0:T(8,128)(2,1)S(1)}, bf16[64,2048]{1,0:T(8,128)(2,1)S(1)}, u32[]{:S(2)}, u32[]{:S(2)}) collective-permute-start(bf16[64,2048]{1,0:T(8,128)(2,1)S(1)} %get-tuple-element.76), channel_id=1, source_target_pairs={{0,8},{4,12},{8,0},{12,4},{1,9},{5,13},{9,1},{13,5},{2,10},{6,14},... | collective-permute-start | bytes 786440 | tf_op jit(solution)/shard_map/ppermute | solution.py:365
  106.7 2.0 %collective-permute-start.23 = (bf16[32,2048]{1,0:T(8,128)(2,1)S(1)}, bf16[32,2048]{1,0:T(8,128)(2,1)S(1)}, u32[]{:S(2)}, u32[]{:S(2)}) collective-permute-start(bf16[32,2048]{1,0:T(8,128)(2,1)S(1)} %get-tuple-element.75), channel_id=1, source_target_pairs={{0,4},{4,0},{8,12},{12,8},{1,5},{5,1},{9,13},{13,9},{2,6},{6,2},{1... | collective-permute-start | bytes 393224 | tf_op jit(solution)/shard_map/ppermute | solution.py:365
  108.8 7.4 %collective-permute-done.22 = bf16[32,2048]{1,0:T(8,128)(2,1)S(1)} collective-permute-done((bf16[32,2048]{1,0:T(8,128)(2,1)S(1)}, bf16[32,2048]{1,0:T(8,128)(2,1)S(1)}, u32[]{:S(2)}, u32[]{:S(2)}) %collective-permute-start.22) | collective-permute-done | bytes 131104 | tf_op jit(solution)/shard_map/ppermute | solution.py:365
  116.1 2.5 %collective-permute-done.23 = bf16[32,2048]{1,0:T(8,128)(2,1)S(1)} collective-permute-done((bf16[32,2048]{1,0:T(8,128)(2,1)S(1)}, bf16[32,2048]{1,0:T(8,128)(2,1)S(1)}, u32[]{:S(2)}, u32[]{:S(2)}) %collective-permute-start.23) | collective-permute-done | bytes 131104 | tf_op jit(solution)/shard_map/ppermute | solution.py:365
  (49 shorter events, 12.6 us)
Async XLA Ops:
  0.0 16.2 %collective-permute-start = (bf16[64,2048]{1,0:T(8,128)(2,1)}, bf16[64,2048]{1,0:T(8,128)(2,1)S(1)}, u32[]{:S(2)}, u32[]{:S(2)}) collective-permute-start(bf16[64,2048]{1,0:T(8,128)(2,1)} %tok_ref.1), channel_id=1, source_target_pairs={{0,4},{4,0},{8,12},{12,8},{1,5},{5,1},{9,13},{13,9},{2,6},{6,2},{1... | collective-permute-start | bytes 786440 | tf_op jit(solution)/shard_map/ppermute | solution.py:365
  3.0 15.6 %collective-permute-start.2 = (bf16[64,2048]{1,0:T(8,128)(2,1)}, bf16[64,2048]{1,0:T(8,128)(2,1)S(1)}, u32[]{:S(2)}, u32[]{:S(2)}) collective-permute-start(bf16[64,2048]{1,0:T(8,128)(2,1)} %tok_ref.1), channel_id=1, source_target_pairs={{0,12},{4,8},{8,4},{12,0},{1,13},{5,9},{9,5},{13,1},{2,14},{6,10},... | collective-permute-start | bytes 786440 | tf_op jit(solution)/shard_map/ppermute | solution.py:365
  5.5 23.2 %collective-permute-start.1 = (bf16[64,2048]{1,0:T(8,128)(2,1)}, bf16[64,2048]{1,0:T(8,128)(2,1)S(1)}, u32[]{:S(2)}, u32[]{:S(2)}) collective-permute-start(bf16[64,2048]{1,0:T(8,128)(2,1)} %tok_ref.1), channel_id=1, source_target_pairs={{0,8},{4,12},{8,0},{12,4},{1,9},{5,13},{9,1},{13,5},{2,10},{6,14},... | collective-permute-start | bytes 786440 | tf_op jit(solution)/shard_map/ppermute | solution.py:365
  31.7 2.7 %collective-permute-start.3 = (bf16[2,96,1536]{2,1,0:T(8,128)(2,1)S(1)}, bf16[2,96,1536]{2,1,0:T(8,128)(2,1)S(1)}, u32[]{:S(2)}, u32[]{:S(2)}) collective-permute-start(bf16[2,96,1536]{2,1,0:T(8,128)(2,1)S(1)} %get-tuple-element.46), channel_id=1, source_target_pairs={{0,1},{1,0},{2,3},{3,2},{4,5},{5,4},{6,7},{7,6},{8,9},{9,8},{10,11... | collective-permute-start | bytes 1769480 | tf_op jit(solution)/shard_map/ppermute | solution.py:368
  34.5 2.2 %collective-permute-start.4 = (bf16[2,96,1536]{2,1,0:T(8,128)(2,1)S(1)}, bf16[2,96,1536]{2,1,0:T(8,128)(2,1)S(1)}, u32[]{:S(2)}, u32[]{:S(2)}) collective-permute-start(bf16[2,96,1536]{2,1,0:T(8,128)(2,1)S(1)} %get-tuple-element.50), channel_id=1, source_target_pairs={{0,1},{1,0},{2,3},{3,2},{4,5},{5,4},{6,7},{7,6},{8,9},{9,8},{10,11... | collective-permute-start | bytes 1769480 | tf_op jit(solution)/shard_map/ppermute | solution.py:368
  35.1 18.0 %collective-permute-start.5 = (bf16[2,48,1536]{2,1,0:T(8,128)(2,1)S(1)}, bf16[2,48,1536]{2,1,0:T(8,128)(2,1)S(1)}, u32[]{:S(2)}, u32[]{:S(2)}) collective-permute-start(bf16[2,48,1536]{2,1,0:T(8,128)(2,1)S(1)} %get-tuple-element.48.refs_0_), channel_id=1, source_target_pairs={{0,2},{1,3},{2,0},{3,1},{4,6},{5,7},{6,4},{7,5},{8,10},{9,11},{10,... | collective-permute-start | bytes 884744 | tf_op jit(solution)/shard_map/ppermute | solution.py:371
  36.8 16.3 %collective-permute-start.6 = (bf16[2,48,1536]{2,1,0:T(8,128)(2,1)S(1)}, bf16[2,48,1536]{2,1,0:T(8,128)(2,1)S(1)}, u32[]{:S(2)}, u32[]{:S(2)}) collective-permute-start(bf16[2,48,1536]{2,1,0:T(8,128)(2,1)S(1)} %get-tuple-element.51.refs_1_), channel_id=1, source_target_pairs={{0,2},{1,3},{2,0},{3,1},{4,6},{5,7},{6,4},{7,5},{8,10},{9,11},{10,... | collective-permute-start | bytes 884744 | tf_op jit(solution)/shard_map/ppermute | solution.py:371
  53.4 2.4 %collective-permute-start.7 = (bf16[2,96,2048]{2,1,0:T(8,128)(2,1)S(1)}, bf16[2,96,2048]{2,1,0:T(8,128)(2,1)S(1)}, u32[]{:S(2)}, u32[]{:S(2)}) collective-permute-start(bf16[2,96,2048]{2,1,0:T(8,128)(2,1)S(1)} %get-tuple-element.58), channel_id=1, source_target_pairs={{0,1},{1,0},{2,3},{3,2},{4,5},{5,4},{6,7},{7,6},{8,9},{9,8},{10,11... | collective-permute-start | bytes 2359304 | tf_op jit(solution)/shard_map/ppermute | solution.py:368
  55.9 10.0 %collective-permute-start.8 = (bf16[2,96,1536]{2,1,0:T(8,128)(2,1)S(1)}, bf16[2,96,1536]{2,1,0:T(8,128)(2,1)S(1)}, u32[]{:S(2)}, u32[]{:S(2)}) collective-permute-start(bf16[2,96,1536]{2,1,0:T(8,128)(2,1)S(1)} %get-tuple-element.60), channel_id=1, source_target_pairs={{0,1},{1,0},{2,3},{3,2},{4,5},{5,4},{6,7},{7,6},{8,9},{9,8},{10,11... | collective-permute-start | bytes 1769480 | tf_op jit(solution)/shard_map/ppermute | solution.py:368
  56.1 9.8 %collective-permute-start.14 = (bf16[48,3072]{1,0:T(8,128)(2,1)S(1)}, bf16[48,3072]{1,0:T(8,128)(2,1)S(1)}, u32[]{:S(2)}, u32[]{:S(2)}) collective-permute-start(bf16[48,3072]{1,0:T(8,128)(2,1)S(1)} %get-tuple-element.66.refs_0_), channel_id=1, source_target_pairs={{0,2},{1,3},{2,0},{3,1},{4,6},{5,7},{6,4},{7,5},{8,10},{9,11},{10,... | collective-permute-start | bytes 884744 | tf_op jit(solution)/shard_map/ppermute | solution.py:371
  56.6 21.9 %collective-permute-start.13 = (bf16[2,48,2048]{2,1,0:T(8,128)(2,1)S(1)}, bf16[2,48,2048]{2,1,0:T(8,128)(2,1)S(1)}, u32[]{:S(2)}, u32[]{:S(2)}) collective-permute-start(bf16[2,48,2048]{2,1,0:T(8,128)(2,1)S(1)} %get-tuple-element.63.refs_0_), channel_id=1, source_target_pairs={{0,2},{1,3},{2,0},{3,1},{4,6},{5,7},{6,4},{7,5},{8,10},{9,11},{10,... | collective-permute-start | bytes 1179656 | tf_op jit(solution)/shard_map/ppermute | solution.py:371
  58.1 13.7 %collective-permute-start.15 = (bf16[48,3072]{1,0:T(8,128)(2,1)S(1)}, bf16[48,3072]{1,0:T(8,128)(2,1)S(1)}, u32[]{:S(2)}, u32[]{:S(2)}) collective-permute-start(bf16[48,3072]{1,0:T(8,128)(2,1)S(1)} %get-tuple-element.66.refs_0_), channel_id=1, source_target_pairs={{0,1},{1,0},{2,3},{3,2},{4,5},{5,4},{6,7},{7,6},{8,9},{9,8},{10,11... | collective-permute-start | bytes 884744 | tf_op jit(solution)/shard_map/ppermute | solution.py:368
  65.9 5.9 %collective-permute-start.16 = (bf16[48,3072]{1,0:T(8,128)(2,1)S(1)}, bf16[48,3072]{1,0:T(8,128)(2,1)S(1)}, u32[]{:S(2)}, u32[]{:S(2)}) collective-permute-start(bf16[48,3072]{1,0:T(8,128)(2,1)S(1)} %collective-permute-done.14.refs_1_), channel_id=1, source_target_pairs={{0,1},{1,0},{2,3},{3,2},{4,5},{5,4},{6,7},{7,6},{8,9},{9,8},{10,11... | collective-permute-start | bytes 884744 | tf_op jit(solution)/shard_map/ppermute | solution.py:368
  66.0 14.2 %collective-permute-start.9 = (bf16[2,48,1536]{2,1,0:T(8,128)(2,1)S(1)}, bf16[2,48,1536]{2,1,0:T(8,128)(2,1)S(1)}, u32[]{:S(2)}, u32[]{:S(2)}) collective-permute-start(bf16[2,48,1536]{2,1,0:T(8,128)(2,1)S(1)} %get-tuple-element.62.refs_1_), channel_id=1, source_target_pairs={{0,2},{1,3},{2,0},{3,1},{4,6},{5,7},{6,4},{7,5},{8,10},{9,11},{10,... | collective-permute-start | bytes 884744 | tf_op jit(solution)/shard_map/ppermute | solution.py:371
  78.7 7.8 %collective-permute-start.17 = (bf16[48,2048]{1,0:T(8,128)(2,1)S(1)}, bf16[48,2048]{1,0:T(8,128)(2,1)S(1)}, u32[]{:S(2)}, u32[]{:S(2)}) collective-permute-start(bf16[48,2048]{1,0:T(8,128)(2,1)S(1)} %activate.5.refs_0_), channel_id=1, source_target_pairs={{0,2},{1,3},{2,0},{3,1},{4,6},{5,7},{6,4},{7,5},{8,10},{9,11},{10,... | collective-permute-start | bytes 589832 | tf_op jit(solution)/shard_map/ppermute | solution.py:371
  80.4 8.6 %collective-permute-start.10 = (bf16[48,1536]{1,0:T(8,128)(2,1)S(1)}, bf16[48,1536]{1,0:T(8,128)(2,1)S(1)}, u32[]{:S(2)}, u32[]{:S(2)}) collective-permute-start(bf16[48,1536]{1,0:T(8,128)(2,1)S(1)} %activate.4.refs_0_), channel_id=1, source_target_pairs={{0,2},{1,3},{2,0},{3,1},{4,6},{5,7},{6,4},{7,5},{8,10},{9,11},{10,... | collective-permute-start | bytes 442376 | tf_op jit(solution)/shard_map/ppermute | solution.py:371
  81.0 8.0 %collective-permute-start.18 = (bf16[48,2048]{1,0:T(8,128)(2,1)S(1)}, bf16[48,2048]{1,0:T(8,128)(2,1)S(1)}, u32[]{:S(2)}, u32[]{:S(2)}) collective-permute-start(bf16[48,2048]{1,0:T(8,128)(2,1)S(1)} %activate.5.refs_0_), channel_id=1, source_target_pairs={{0,1},{1,0},{2,3},{3,2},{4,5},{5,4},{6,7},{7,6},{8,9},{9,8},{10,11... | collective-permute-start | bytes 589832 | tf_op jit(solution)/shard_map/ppermute | solution.py:368
  86.5 2.5 %collective-permute-start.19 = (bf16[48,2048]{1,0:T(8,128)(2,1)S(1)}, bf16[48,2048]{1,0:T(8,128)(2,1)S(1)}, u32[]{:S(2)}, u32[]{:S(2)}) collective-permute-start(bf16[48,2048]{1,0:T(8,128)(2,1)S(1)} %collective-permute-done.17.refs_1_), channel_id=1, source_target_pairs={{0,1},{1,0},{2,3},{3,2},{4,5},{5,4},{6,7},{7,6},{8,9},{9,8},{10,11... | collective-permute-start | bytes 589832 | tf_op jit(solution)/shard_map/ppermute | solution.py:368
  86.5 4.3 %collective-permute-start.11 = (bf16[48,1536]{1,0:T(8,128)(2,1)S(1)}, bf16[48,1536]{1,0:T(8,128)(2,1)S(1)}, u32[]{:S(2)}, u32[]{:S(2)}) collective-permute-start(bf16[48,1536]{1,0:T(8,128)(2,1)S(1)} %activate.4.refs_0_), channel_id=1, source_target_pairs={{0,1},{1,0},{2,3},{3,2},{4,5},{5,4},{6,7},{7,6},{8,9},{9,8},{10,11... | collective-permute-start | bytes 442376 | tf_op jit(solution)/shard_map/ppermute | solution.py:368
  93.0 4.1 %collective-permute-start.21 = (bf16[64,2048]{1,0:T(8,128)(2,1)S(1)}, bf16[64,2048]{1,0:T(8,128)(2,1)S(1)}, u32[]{:S(2)}, u32[]{:S(2)}) collective-permute-start(bf16[64,2048]{1,0:T(8,128)(2,1)S(1)} %get-tuple-element.71), channel_id=1, source_target_pairs={{4,8},{8,4},{5,9},{9,5},{6,10},{10,6},{7,11},{11,7},{20,24},{24,20... | collective-permute-start | bytes 786440 | tf_op jit(solution)/shard_map/ppermute | solution.py:365
  93.7 9.3 %collective-permute-start.20 = (bf16[64,2048]{1,0:T(8,128)(2,1)S(1)}, bf16[64,2048]{1,0:T(8,128)(2,1)S(1)}, u32[]{:S(2)}, u32[]{:S(2)}) collective-permute-start(bf16[64,2048]{1,0:T(8,128)(2,1)S(1)} %get-tuple-element.71), channel_id=1, source_target_pairs={{0,4},{12,8},{1,5},{13,9},{2,6},{14,10},{3,7},{15,11},{16,20},{28,... | collective-permute-start | bytes 786440 | tf_op jit(solution)/shard_map/ppermute | solution.py:365
  103.1 15.6 %collective-permute-start.24 = (bf16[64,2048]{1,0:T(8,128)(2,1)S(1)}, bf16[64,2048]{1,0:T(8,128)(2,1)S(1)}, u32[]{:S(2)}, u32[]{:S(2)}) collective-permute-start(bf16[64,2048]{1,0:T(8,128)(2,1)S(1)} %get-tuple-element.76), channel_id=1, source_target_pairs={{0,8},{4,12},{8,0},{12,4},{1,9},{5,13},{9,1},{13,5},{2,10},{6,14},... | collective-permute-start | bytes 786440 | tf_op jit(solution)/shard_map/ppermute | solution.py:365
  106.7 9.4 %collective-permute-start.22 = (bf16[32,2048]{1,0:T(8,128)(2,1)S(1)}, bf16[32,2048]{1,0:T(8,128)(2,1)S(1)}, u32[]{:S(2)}, u32[]{:S(2)}) collective-permute-start(bf16[32,2048]{1,0:T(8,128)(2,1)S(1)} %get-tuple-element.74), channel_id=1, source_target_pairs={{0,4},{4,0},{8,12},{12,8},{1,5},{5,1},{9,13},{13,9},{2,6},{6,2},{1... | collective-permute-start | bytes 393224 | tf_op jit(solution)/shard_map/ppermute | solution.py:365
  106.7 11.9 %collective-permute-start.23 = (bf16[32,2048]{1,0:T(8,128)(2,1)S(1)}, bf16[32,2048]{1,0:T(8,128)(2,1)S(1)}, u32[]{:S(2)}, u32[]{:S(2)}) collective-permute-start(bf16[32,2048]{1,0:T(8,128)(2,1)S(1)} %get-tuple-element.75), channel_id=1, source_target_pairs={{0,4},{4,0},{8,12},{12,8},{1,5},{5,1},{9,13},{13,9},{2,6},{6,2},{1... | collective-permute-start | bytes 393224 | tf_op jit(solution)/shard_map/ppermute | solution.py:365
  (3 other events, 3.5 us)

commit v9 on v8

--- a/solution.py
+++ b/solution.py
@@ -33,19 +33,34 @@
     return rows
 
 
-def prepare_kernel(n_gx, nx, lengths_ref, tok_ref, gate_ref, up_ref, in_ref, out_ref, held_ref, gate_out, up_out, sems):
-    fetched = pl.ds(0, gate_out.shape[1])
-    copies = [
-        pltpu.make_async_copy(src.at[:, fetched], dst, sems.at[i])
-        for i, (src, dst) in enumerate(((gate_ref, gate_out), (up_ref, up_out)))
-    ]
+def hold_kernel(tok_ref, out_ref):
+    out_ref[...] = tok_ref[...]
+
+
+def hold(tokens):
+    held = pl.BlockSpec(memory_space=pltpu.VMEM)
+    return pl.pallas_call(
+        hold_kernel,
+        out_shape=jax.ShapeDtypeStruct(tokens.shape, tokens.dtype),
+        in_specs=[held],
+        out_specs=held,
+        cost_estimate=pl.CostEstimate(flops=0, bytes_accessed=0, transcendentals=0),
+        compiler_params=pltpu.CompilerParams(vmem_limit_bytes=4 * MIB),
+        name="hold",
+    )(tokens)
+
+
+def prepare_kernel(n_gx, nx, tok_dev, chunks, lengths_ref, gate_ref, up_ref, in_ref, out_ref, *refs):
+    outs, sems = refs[:-1], refs[-1]
+    copies = []
+    for i, (start, width) in enumerate(chunks):
+        for k, src in enumerate((gate_ref, up_ref)):
+            copies.append(pltpu.make_async_copy(src.at[:, pl.ds(start, width)], outs[2 * i + k], sems.at[2 * i + k]))
     for copy in copies:
         copy.start()
-    tok_dev = tok_ref.shape[0]
     z = lax.axis_index("gx")
     live, slots = in_ref.shape
     quarter = live // (2 * nx)
-    held_ref[...] = tok_ref[...]
 
     def slot_of(column):
         return (z ^ (column // tok_dev)) * tok_dev + column % tok_dev
@@ -60,56 +75,36 @@
         copy.wait()
 
 
-def prepare(lengths, tokens, gate_weight, up_weight, fetched, n_gx, nx, live):
-    slots = n_gx * tokens.shape[0]
-    held, anywhere = pl.BlockSpec(memory_space=pltpu.VMEM), pl.BlockSpec(memory_space=pl.ANY)
-    weight = jax.ShapeDtypeStruct((gate_weight.shape[0], fetched), BF16)
-    return pl.pallas_call(
-        functools.partial(prepare_kernel, n_gx, nx),
-        out_shape=[
-            jax.ShapeDtypeStruct((live, slots), BF16),
-            jax.ShapeDtypeStruct((slots, live), BF16),
-            jax.ShapeDtypeStruct(tokens.shape, tokens.dtype),
-            weight,
-            weight,
-        ],
-        in_specs=[pl.BlockSpec(memory_space=pltpu.SMEM), held, anywhere, anywhere],
-        out_specs=[held] * 5,
-        scratch_shapes=[pltpu.SemaphoreType.DMA((2,))],
-        cost_estimate=pl.CostEstimate(flops=0, bytes_accessed=0, transcendentals=0),
-        compiler_params=pltpu.CompilerParams(vmem_limit_bytes=8 * MIB),
+def prepare(lengths, gate_weight, up_weight, chunks, n_gx, nx, tok_dev, live):
+    slots = n_gx * tok_dev
+    held, anywhere = pl.BlockSpec(memory_space=pltpu.VMEM), pl.BlockSpec(memory_space=pl.ANY)
+    weights = [jax.ShapeDtypeStruct((gate_weight.shape[0], width), BF16) for _, width in chunks for _ in range(2)]
+    out = pl.pallas_call(
+        functools.partial(prepare_kernel, n_gx, nx, tok_dev, chunks),
+        out_shape=[jax.ShapeDtypeStruct((live, slots), BF16), jax.ShapeDtypeStruct((slots, live), BF16)] + weights,
+        in_specs=[pl.BlockSpec(memory_space=pltpu.SMEM), anywhere, anywhere],
+        out_specs=[held] * (2 + len(weights)),
+        scratch_shapes=[pltpu.SemaphoreType.DMA((len(weights),))],
+        cost_estimate=pl.CostEstimate(flops=0, bytes_accessed=0, transcendentals=0),
+        compiler_params=pltpu.CompilerParams(vmem_limit_bytes=4 * MIB),
         name="prepare",
-    )(lengths, tokens, gate_weight, up_weight)
-
-
-def compact_kernel(groups, pick_ref, *refs):
-    refs = list(refs)
-    out_ref = refs.pop()
-
-    def rows_of(n):
-        return jnp.concatenate([refs.pop(0)[...] for _ in range(n)], axis=0)
-
-    blocks = []
-    for group in groups:
-        block = rows_of(group[0])
-        for n in group[1:]:
-            block = block + rows_of(n)
-        blocks.append(block)
-    rows = jnp.concatenate(blocks, axis=0)
-    out_ref[...] = jnp.dot(pick_ref[...], rows, preferred_element_type=F32).astype(BF16)
+    )(lengths, gate_weight, up_weight)
+    return out[0], out[1], [out[2 + 2 * i:4 + 2 * i] for i in range(len(chunks))]
+
+
+def compact_kernel(pick_ref, *refs):
+    rows = jnp.concatenate([r[...] for r in refs[:-1]], axis=0)
+    refs[-1][...] = jnp.dot(pick_ref[...], rows, preferred_element_type=F32).astype(BF16)
 
 
 def compact(pick, blocks):
-    flat = [piece for group in blocks for pieces in group for piece in pieces]
-    return pl.pallas_call(
-        functools.partial(compact_kernel, [[len(pieces) for pieces in group] for group in blocks]),
-        out_shape=jax.ShapeDtypeStruct((pick.shape[0], flat[0].shape[1]), BF16),
-        compiler_params=pltpu.CompilerParams(vmem_limit_bytes=8 * MIB),
-        cost_estimate=pl.CostEstimate(
-            flops=2 * pick.size * flat[0].shape[1], bytes_accessed=2 * pick.size, transcendentals=0
-        ),
+    return pl.pallas_call(
+        compact_kernel,
+        out_shape=jax.ShapeDtypeStruct((pick.shape[0], blocks[0].shape[1]), BF16),
+        compiler_params=pltpu.CompilerParams(vmem_limit_bytes=5 * MIB),
+        cost_estimate=pl.CostEstimate(flops=0, bytes_accessed=0, transcendentals=0),
         name="compact",
-    )(pick, *flat)
+    )(pick, *blocks)
 
 
 def gate_up_kernel(tok_ref, gate_ref, up_ref, *refs):
@@ -142,28 +137,29 @@
     )(tok, gate_weight, up_weight, *after)
 
 
-def gate_up_held_kernel(start, width, tile, tok_ref, gate_ref, up_ref, send_ref, keep_ref):
-    half = keep_ref.shape[1]
+def gate_up_held_kernel(tile, tok_ref, gate_ref, up_ref, *refs):
+    send_ref, keep_ref = refs[-2:]
+    half, width = keep_ref.shape[1:]
     rows = tok_ref[...]
     for j in range(0, width, tile):
         for i, w_ref in enumerate((gate_ref, up_ref)):
-            part = jnp.dot(rows, w_ref[:, start + j:start + j + tile], preferred_element_type=F32)
+            part = jnp.dot(rows, w_ref[:, j:j + tile], preferred_element_type=F32)
             keep_ref[i, :, j:j + tile] = part[:half]
             send_ref[i, :, j:j + tile] = part[half:].astype(BF16)
 
 
-def gate_up_held(tok, gate_held, up_held, start, width, tile):
-    half = tok.shape[0] // 2
-    held = pl.BlockSpec(memory_space=pltpu.VMEM)
-    return pl.pallas_call(
-        functools.partial(gate_up_held_kernel, start, width, tile),
+def gate_up_held(tok, gate_held, up_held, after, tile):
+    half, width = tok.shape[0] // 2, gate_held.shape[1]
+    held, anywhere = pl.BlockSpec(memory_space=pltpu.VMEM), pl.BlockSpec(memory_space=pl.ANY)
+    return pl.pallas_call(
+        functools.partial(gate_up_held_kernel, tile),
         out_shape=[jax.ShapeDtypeStruct((2, half, width), BF16), jax.ShapeDtypeStruct((2, half, width), F32)],
-        in_specs=[held] * 3,
+        in_specs=[held] * 3 + [anywhere] * len(after),
         out_specs=[held] * 2,
-        compiler_params=pltpu.CompilerParams(vmem_limit_bytes=12 * MIB),
+        compiler_params=pltpu.CompilerParams(vmem_limit_bytes=6 * MIB),
         cost_estimate=pl.CostEstimate(flops=0, bytes_accessed=0, transcendentals=0),
         name="gate_up_held",
-    )(tok, gate_held, up_held)
+    )(tok, gate_held, up_held, *after)
 
 
 def join_kernel(n_handed, n_after, nx, keep_ref, got_ref, *refs):
@@ -370,14 +366,12 @@
     def over_x(block, k):
         return lax.ppermute(block, "gy", [(i, (i + 2 * k) % n_gy) for i in range(n_gy)])
 
-    first = sum(width for _, width in chunks[:2])
-    pick_in, pick_out, held, gate_held, up_held = prepare(
-        lengths, tokens, gate_weight, up_weight, first, n_gx, nx, live
-    )
-    blocks = [[[held]]] + [[[over_z(tokens, k)]] for k in range(1, n_gx)]
+    mine = hold(tokens)
+    blocks = [mine] + [over_z(mine, k) for k in range(1, n_gx)]
+    pick_in, pick_out, weights = prepare(lengths, gate_weight, up_weight, chunks[:3], n_gx, nx, tok_dev, live)
     tok = compact(pick_in, blocks)
 
-    made = [gate_up_held(tok, gate_held, up_held, *chunk, tile) for chunk in chunks[:2]]
+    made = [gate_up_held(tok, *weights[i], [], tile) for i in range(2)]
     sends, keeps = [list(a) for a in zip(*made)]
     sums = []
 
@@ -393,11 +387,11 @@
 
     ready, sends[1:2] = exchange(0, sends[1:2])
     ready += exchange(1, [])[0]
-    for chunk in chunks[2:]:
-        send, keep = gate_up(tok, gate_weight, up_weight, ready, *chunk, tile)
+    made = [gate_up_held(tok, *weights[2], ready, tile)]
+    made.append(gate_up(tok, gate_weight, up_weight, made[0][:1], *chunks[3], tile))
+    for send, keep in made:
         sends.append(send)
         keeps.append(keep)
-        ready = [send]
     hidden, sends[2:] = finish(0, 2, sends[2:], [])
     ready, sends[3:] = exchange(2, sends[3:])
     ready += exchange(3, [])[0]

time: 120 us -> 117 us (0.975)
  waiting for transfers between devices: 45.9 us -> 42.4 us
    pallas_call x4 -> x6, Pallas kernels: 14.5 us -> 22.8 us  [the longest x1 13.6 us: prepare(): pl.pallas_call(functools.partial(prepare_kernel, n_gx, nx, tok_dev, chunk...]
    pallas_call x2 -> x1, Pallas kernels: 14.7 us -> 6.83 us  [gate_up(): pl.pallas_call(gate_up_kernel, out_shape=[jax.ShapeDtypeStruct((2, half,...]
    ppermute x8, waiting for transfers between devices: 28.3 us -> 23 us  [over_z(): return lax.ppermute(block, 'gx', [(z, z ^ k) for z in among])]
    ppermute x7, waiting for transfers between devices: 15.3 us -> 16.9 us  [over_x(): lax.ppermute(block, 'gy', [(i, (i + 2 * k) % n_gy) for i in range(n_gy)])]
  transfers between devices with their start and end apart: 25 -> 25, of which waited for: 10 -> 10; matrix products, arithmetic and copies ran while one was open for 0% -> 0% of each run, Pallas kernels for 34% -> 35%
where the time goes in v9:
time: 117 us
  Pallas kernels  46.4 us (40%)
  waiting for transfers between devices  42.4 us (36%)
  starting transfers between devices  25.5 us (22%)
  local copies, waits for them, and re-layouts  1.6 us (1%)
    ppermute x8, waiting for transfers between devices, over_z(): return lax.ppermute(block, 'gx', [(z, z ^ k) for z in among])  23 us
    ppermute x7, waiting for transfers between devices, over_x(): lax.ppermute(block, 'gy', [(i, (i + 2 * k) % n_gy) for i in range(n_gy)])  16.9 us
    ppermute x8, starting transfers between devices, over_z(): return lax.ppermute(block, 'gx', [(z, z ^ k) for z in among])  15.3 us
    pallas_call x1, Pallas kernels, prepare(): pl.pallas_call(functools.partial(prepare_kernel, n_gx, nx, tok_dev, chunk...  13.6 us
    ppermute x7, starting transfers between devices, over_x(): lax.ppermute(block, 'gy', [(i, (i + 2 * k) % n_gy) for i in range(n_gy)])  8.79 us
    pallas_call x3, Pallas kernels, gate_up_held(): pl.pallas_call(functools.partial(gate_up_held_kernel, tile), out_shape=[j...  8.73 us
    pallas_call x1, Pallas kernels, gate_up(): pl.pallas_call(gate_up_kernel, out_shape=[jax.ShapeDtypeStruct((2, half,...  6.83 us
    pallas_call x1, Pallas kernels, down(): pl.pallas_call(functools.partial(down_kernel, len(hidden)), out_shape=jax...  6.64 us
  transfers between devices with their start and end apart: 25, of which 10 were waited for; matrix products, arithmetic and copies ran while one was open for 0% of the time, Pallas kernels for 35%

profile of v9, /device:TPU:0, one launch (start us, length us, event | category | flops | bytes accessed | tf_op | source)
XLA Modules:
  0.0 117.0 jit_solution(14111956184193413612)
XLA Ops:
  1.0 5.1 %collective-permute-start.2 = (bf16[64,2048]{1,0:T(8,128)(2,1)S(1)}, bf16[64,2048]{1,0:T(8,128)(2,1)S(1)}, u32[]{:S(2)}, u32[]{:S(2)}) collective-permute-start(bf16[64,2048]{1,0:T(8,128)(2,1)S(1)} %hold.1.refs_0_), channel_id=1, source_target_pairs={{0,12},{4,8},{8,4},{12,0},{1,13},{5,9},{9,5},{13,1},{2,14},{6,10},... | collective-permute-start | bytes 786440 | tf_op jit(solution)/shard_map/ppermute | solution.py:361
  7.4 13.6 %prepare.1 = (bf16[192,256]{1,0:T(8,128)(2,1)S(1)}, bf16[256,192]{1,0:T(8,128)(2,1)S(1)}, bf16[2048,1536]{1,0:T(8,128)(2,1)S(1)}, bf16[2048,1536]{1,0:T(8,128)(2...) custom-call(s32[4]{0:T(128)S(1)} %copy-done.1, ...), custom_call_target="tpu_custom_call" | custom-call | tf_op jit(solution)/shard_map/prepare/pallas_call | solution.py:82
  21.0 7.4 %collective-permute-done.1.refs_2_ = bf16[64,2048]{1,0:T(8,128)(2,1)S(1)} collective-permute-done((bf16[64,2048]{1,0:T(8,128)(2,1)S(1)}, bf16[64,2048]{1,0:T(8,128)(2,1)S(1)}, u32[]{:S(2)}, u32[]{:S(2)}) %collective-permute-start.1) | collective-permute-done | bytes 262176 | tf_op jit(solution)/shard_map/ppermute | solution.py:361
  28.8 2.6 %gate_up_held.3 = (bf16[2,96,1536]{2,1,0:T(8,128)(2,1)S(1)}, f32[2,96,1536]{2,1,0:T(8,128)S(1)}) custom-call(bf16[192,2048]{1,0:T(8,128)(2,1)S(1)} %compact.1.tok_ref, bf16[2048,1536]{1,0:T(8,128)(2,1)S(1)} %get-tuple-element.47.gate_ref, bf16[2048,1536]{1,0:T(8,128)(2,1)S(1)} %get-tuple-element.48.up_ref), custom_call_target="tpu_custom_call" | custom-call | tf_op jit(solution)/shard_map/gate_up_held/pallas_call | solution.py:154
  31.5 2.6 %gate_up_held.4 = (bf16[2,96,1536]{2,1,0:T(8,128)(2,1)S(1)}, f32[2,96,1536]{2,1,0:T(8,128)S(1)}) custom-call(bf16[192,2048]{1,0:T(8,128)(2,1)S(1)} %compact.1.tok_ref, bf16[2048,1536]{1,0:T(8,128)(2,1)S(1)} %get-tuple-element.51.gate_ref, bf16[2048,1536]{1,0:T(8,128)(2,1)S(1)} %get-tuple-element.52.up_ref), custom_call_target="tpu_custom_call" | custom-call | tf_op jit(solution)/shard_map/gate_up_held/pallas_call | solution.py:154
  36.5 1.6 %collective-permute-start.6 = (bf16[2,48,1536]{2,1,0:T(8,128)(2,1)S(1)}, bf16[2,48,1536]{2,1,0:T(8,128)(2,1)S(1)}, u32[]{:S(2)}, u32[]{:S(2)}) collective-permute-start(bf16[2,48,1536]{2,1,0:T(8,128)(2,1)S(1)} %get-tuple-element.57.refs_1_), channel_id=1, source_target_pairs={{0,2},{1,3},{2,0},{3,1},{4,6},{5,7},{6,4},{7,5},{8,10},{9,11},{10,... | collective-permute-start | bytes 884744 | tf_op jit(solution)/shard_map/ppermute | solution.py:367
  38.1 3.5 %gate_up_held.5 = (bf16[2,96,2048]{2,1,0:T(8,128)(2,1)S(1)}, f32[2,96,2048]{2,1,0:T(8,128)S(1)}) custom-call(bf16[192,2048]{1,0:T(8,128)(2,1)S(1)} %compact.1.tok_ref, bf16[2048,2048]{1,0:T(8,128)(2,1)S(1)} %get-tuple-element.45.gate_ref, bf16[2048,2048]{1,0:T(8,128)(2,1)S(1)} %get-tuple-element.46.up_ref, ...), custom_call_target="tpu_custom_call" | custom-call | tf_op jit(solution)/shard_map/gate_up_held/pallas_call | solution.py:154
  41.6 6.8 %gate_up.1 = (bf16[2,96,1536]{2,1,0:T(8,128)(2,1)S(1)}, f32[2,96,1536]{2,1,0:T(8,128)S(1)}) custom-call(bf16[192,2048]{1,0:T(8,128)(2,1)S(1)} %compact.1.tok_ref, bf16[2048,6656]{1,0:T(8,128)(2,1)} %gate_ref.3, bf16[2048,6656]{1,0:T(8,128)(2,1)} %up_ref.3, bf16[2,96,2048]{2,1,0:T(8,128)(2,1)S(1)} %get-tuple-element.58.refs_0_.refs_4_), custom_call_target="tpu_custom_call" | custom-call | tf_op jit(solution)/shard_map/gate_up/pallas_call | solution.py:125
  48.4 1.7 %collective-permute-done.6.refs_3_ = bf16[2,48,1536]{2,1,0:T(8,128)(2,1)S(1)} collective-permute-done((bf16[2,48,1536]{2,1,0:T(8,128)(2,1)S(1)}, bf16[2,48,1536]{2,1,0:T(8,128)(2,1)S(1)}, u32[]{:S(2)}, u32[]{:S(2)}) %collective-permute-start.6) | collective-permute-done | bytes 294944 | tf_op jit(solution)/shard_map/ppermute | solution.py:367
  50.4 2.3 %collective-permute-done.7.got_ref = bf16[2,96,2048]{2,1,0:T(8,128)(2,1)S(1)} collective-permute-done((bf16[2,96,2048]{2,1,0:T(8,128)(2,1)S(1)}, bf16[2,96,2048]{2,1,0:T(8,128)(2,1)S(1)}, u32[]{:S(2)}, u32[]{:S(2)}) %collective-permute-start.7) | collective-permute-done | bytes 786464 | tf_op jit(solution)/shard_map/ppermute | solution.py:364
  55.1 7.8 %collective-permute-done.14.refs_1_ = bf16[48,3072]{1,0:T(8,128)(2,1)S(1)} collective-permute-done((bf16[48,3072]{1,0:T(8,128)(2,1)S(1)}, bf16[48,3072]{1,0:T(8,128)(2,1)S(1)}, u32[]{:S(2)}, u32[]{:S(2)}) %collective-permute-start.14) | collective-permute-done | bytes 294944 | tf_op jit(solution)/shard_map/ppermute | solution.py:367
  63.0 1.5 %collective-permute-start.9 = (bf16[2,48,1536]{2,1,0:T(8,128)(2,1)S(1)}, bf16[2,48,1536]{2,1,0:T(8,128)(2,1)S(1)}, u32[]{:S(2)}, u32[]{:S(2)}) collective-permute-start(bf16[2,48,1536]{2,1,0:T(8,128)(2,1)S(1)} %get-tuple-element.68.refs_1_), channel_id=1, source_target_pairs={{0,2},{1,3},{2,0},{3,1},{4,6},{5,7},{6,4},{7,5},{8,10},{9,11},{10,... | collective-permute-start | bytes 884744 | tf_op jit(solution)/shard_map/ppermute | solution.py:367
  64.6 5.2 %fetch.1 = (bf16[2048,2048]{1,0:T(8,128)(2,1)S(1)}, bf16[1536,2048]{1,0:T(8,128)(2,1)S(1)}) custom-call(bf16[6656,2048]{1,0:T(8,128)(2,1)} %refs_4_.1, bf16[2,48,2048]{2,1,0:T(8,128)(2,1)S(1)} %get-tuple-element.69.refs_0_, bf16[2,48,1536]{2,1,0:T(8,128)(2,1)S(1)} %get-tuple-element.68.refs_1_), custom_call_target="tpu_custom_call" | custom-call | tf_op jit(solution)/shard_map/fetch/pallas_call | solution.py:294
  69.8 6.6 %down.1.refs_2_.refs_5_ = f32[192,2048]{1,0:T(8,128)S(1)} custom-call(bf16[48,3072]{1,0:T(8,128)(2,1)S(1)} %get-tuple-element.72.refs_0_, bf16[48,3072]{1,0:T(8,128)(2,1)S(1)} %collective-permute-done.14.refs_1_, bf16[48,3072]{1,0:T(8,128)(2,1)S(1)} %collective-permute-done.15.refs_2_, bf16[48,3072]{1,0:T(8,128)(2,1)S(1)} %collective-permute-done.16.refs_3_, ...), custom_call_target="tpu_custom_call" | custom-call | tf_op jit(solution)/shard_map/down/pallas_call | solution.py:265
  78.9 5.5 %collective-permute-done.17.refs_1_ = bf16[48,2048]{1,0:T(8,128)(2,1)S(1)} collective-permute-done((bf16[48,2048]{1,0:T(8,128)(2,1)S(1)}, bf16[48,2048]{1,0:T(8,128)(2,1)S(1)}, u32[]{:S(2)}, u32[]{:S(2)}) %collective-permute-start.17) | collective-permute-done | bytes 196640 | tf_op jit(solution)/shard_map/ppermute | solution.py:367
  84.9 1.9 %collective-permute-done.10.refs_1_ = bf16[48,1536]{1,0:T(8,128)(2,1)S(1)} collective-permute-done((bf16[48,1536]{1,0:T(8,128)(2,1)S(1)}, bf16[48,1536]{1,0:T(8,128)(2,1)S(1)}, u32[]{:S(2)}, u32[]{:S(2)}) %collective-permute-start.10) | collective-permute-done | bytes 147488 | tf_op jit(solution)/shard_map/ppermute | solution.py:367
  86.9 1.8 %down_held.2.refs_5_ = f32[192,2048]{1,0:T(8,128)S(1)} custom-call(bf16[48,2048]{1,0:T(8,128)(2,1)S(1)} %activate.5.refs_0_, bf16[48,2048]{1,0:T(8,128)(2,1)S(1)} %collective-permute-done.17.refs_1_, bf16[48,2048]{1,0:T(8,128)(2,1)S(1)} %collective-permute-done.18.refs_2_, bf16[48,2048]{1,0:T(8,128)(2,1)S(1)} %collective-permute-done.19.refs_3_, ...), custom_call_target="tpu_custom_call" | custom-call | tf_op jit(solution)/shard_map/down_held/pallas_call | solution.py:331
  88.7 2.2 %down_held.3 = (bf16[64,2048]{1,0:T(8,128)(2,1)S(1)}, bf16[32,2048]{1,0:T(8,128)(2,1)S(1)}, bf16[32,2048]{1,0:T(8,128)(2,1)S(1)}, bf16[64,2048]{1,0:T(8,128)(2,1)S(1)}, bf16[64,2048]{1,0:T(8,128)(2,1)S(1)}) custom-call(bf16[48,1536]{1,0:T(8,128)(2,1)S(1)} %activate.4.refs_0_, bf16[48,1536]{1,0:T(8,128)(2,1)S(1)} %collective-permute-done.10.refs_1_, ...), custom_call_target="tpu_custom_call" | custom-call | tf_op jit(solution)/shard_map/down_held/pallas_call | solution.py:331
  91.6 3.3 %collective-permute-start.20 = (bf16[64,2048]{1,0:T(8,128)(2,1)S(1)}, bf16[64,2048]{1,0:T(8,128)(2,1)S(1)}, u32[]{:S(2)}, u32[]{:S(2)}) collective-permute-start(bf16[64,2048]{1,0:T(8,128)(2,1)S(1)} %get-tuple-element.77), channel_id=1, source_target_pairs={{0,4},{12,8},{1,5},{13,9},{2,6},{14,10},{3,7},{15,11},{16,20},{28,... | collective-permute-start | bytes 786440 | tf_op jit(solution)/shard_map/ppermute | solution.py:361
  94.9 5.9 %collective-permute-done.20.got_ref = bf16[64,2048]{1,0:T(8,128)(2,1)S(1)} collective-permute-done((bf16[64,2048]{1,0:T(8,128)(2,1)S(1)}, bf16[64,2048]{1,0:T(8,128)(2,1)S(1)}, u32[]{:S(2)}, u32[]{:S(2)}) %collective-permute-start.20) | collective-permute-done | bytes 262176 | tf_op jit(solution)/shard_map/ppermute | solution.py:361
  100.9 3.5 %collective-permute-start.24 = (bf16[64,2048]{1,0:T(8,128)(2,1)S(1)}, bf16[64,2048]{1,0:T(8,128)(2,1)S(1)}, u32[]{:S(2)}, u32[]{:S(2)}) collective-permute-start(bf16[64,2048]{1,0:T(8,128)(2,1)S(1)} %get-tuple-element.82), channel_id=1, source_target_pairs={{0,8},{4,12},{8,0},{12,4},{1,9},{5,13},{9,1},{13,5},{2,10},{6,14},... | collective-permute-start | bytes 786440 | tf_op jit(solution)/shard_map/ppermute | solution.py:361
  104.4 2.0 %collective-permute-start.23 = (bf16[32,2048]{1,0:T(8,128)(2,1)S(1)}, bf16[32,2048]{1,0:T(8,128)(2,1)S(1)}, u32[]{:S(2)}, u32[]{:S(2)}) collective-permute-start(bf16[32,2048]{1,0:T(8,128)(2,1)S(1)} %get-tuple-element.81), channel_id=1, source_target_pairs={{0,4},{4,0},{8,12},{12,8},{1,5},{5,1},{9,13},{13,9},{2,6},{6,2},{1... | collective-permute-start | bytes 393224 | tf_op jit(solution)/shard_map/ppermute | solution.py:361
  106.4 7.4 %collective-permute-done.22 = bf16[32,2048]{1,0:T(8,128)(2,1)S(1)} collective-permute-done((bf16[32,2048]{1,0:T(8,128)(2,1)S(1)}, bf16[32,2048]{1,0:T(8,128)(2,1)S(1)}, u32[]{:S(2)}, u32[]{:S(2)}) %collective-permute-start.22) | collective-permute-done | bytes 131104 | tf_op jit(solution)/shard_map/ppermute | solution.py:361
  113.8 2.4 %collective-permute-done.23 = bf16[32,2048]{1,0:T(8,128)(2,1)S(1)} collective-permute-done((bf16[32,2048]{1,0:T(8,128)(2,1)S(1)}, bf16[32,2048]{1,0:T(8,128)(2,1)S(1)}, u32[]{:S(2)}, u32[]{:S(2)}) %collective-permute-start.23) | collective-permute-done | bytes 131104 | tf_op jit(solution)/shard_map/ppermute | solution.py:361
  (50 shorter events, 12.5 us)
Async XLA Ops:
  1.0 20.1 %collective-permute-start.2 = (bf16[64,2048]{1,0:T(8,128)(2,1)S(1)}, bf16[64,2048]{1,0:T(8,128)(2,1)S(1)}, u32[]{:S(2)}, u32[]{:S(2)}) collective-permute-start(bf16[64,2048]{1,0:T(8,128)(2,1)S(1)} %hold.1.refs_0_), channel_id=1, source_target_pairs={{0,12},{4,8},{8,4},{12,0},{1,13},{5,9},{9,5},{13,1},{2,14},{6,10},... | collective-permute-start | bytes 786440 | tf_op jit(solution)/shard_map/ppermute | solution.py:361
  6.1 22.3 %collective-permute-start.1 = (bf16[64,2048]{1,0:T(8,128)(2,1)S(1)}, bf16[64,2048]{1,0:T(8,128)(2,1)S(1)}, u32[]{:S(2)}, u32[]{:S(2)}) collective-permute-start(bf16[64,2048]{1,0:T(8,128)(2,1)S(1)} %hold.1.refs_0_), channel_id=1, source_target_pairs={{0,8},{4,12},{8,0},{12,4},{1,9},{5,13},{9,1},{13,5},{2,10},{6,14},... | collective-permute-start | bytes 786440 | tf_op jit(solution)/shard_map/ppermute | solution.py:361
  6.1 22.3 %collective-permute-start = (bf16[64,2048]{1,0:T(8,128)(2,1)S(1)}, bf16[64,2048]{1,0:T(8,128)(2,1)S(1)}, u32[]{:S(2)}, u32[]{:S(2)}) collective-permute-start(bf16[64,2048]{1,0:T(8,128)(2,1)S(1)} %hold.1.refs_0_), channel_id=1, source_target_pairs={{0,4},{4,0},{8,12},{12,8},{1,5},{5,1},{9,13},{13,9},{2,6},{6,2},{1... | collective-permute-start | bytes 786440 | tf_op jit(solution)/shard_map/ppermute | solution.py:361
  31.4 2.7 %collective-permute-start.3 = (bf16[2,96,1536]{2,1,0:T(8,128)(2,1)S(1)}, bf16[2,96,1536]{2,1,0:T(8,128)(2,1)S(1)}, u32[]{:S(2)}, u32[]{:S(2)}) collective-permute-start(bf16[2,96,1536]{2,1,0:T(8,128)(2,1)S(1)} %get-tuple-element.50), channel_id=1, source_target_pairs={{0,1},{1,0},{2,3},{3,2},{4,5},{5,4},{6,7},{7,6},{8,9},{9,8},{10,11... | collective-permute-start | bytes 1769480 | tf_op jit(solution)/shard_map/ppermute | solution.py:364
  34.3 2.2 %collective-permute-start.4 = (bf16[2,96,1536]{2,1,0:T(8,128)(2,1)S(1)}, bf16[2,96,1536]{2,1,0:T(8,128)(2,1)S(1)}, u32[]{:S(2)}, u32[]{:S(2)}) collective-permute-start(bf16[2,96,1536]{2,1,0:T(8,128)(2,1)S(1)} %get-tuple-element.56), channel_id=1, source_target_pairs={{0,1},{1,0},{2,3},{3,2},{4,5},{5,4},{6,7},{7,6},{8,9},{9,8},{10,11... | collective-permute-start | bytes 1769480 | tf_op jit(solution)/shard_map/ppermute | solution.py:364
  34.8 13.6 %collective-permute-start.5 = (bf16[2,48,1536]{2,1,0:T(8,128)(2,1)S(1)}, bf16[2,48,1536]{2,1,0:T(8,128)(2,1)S(1)}, u32[]{:S(2)}, u32[]{:S(2)}) collective-permute-start(bf16[2,48,1536]{2,1,0:T(8,128)(2,1)S(1)} %get-tuple-element.54.refs_0_), channel_id=1, source_target_pairs={{0,2},{1,3},{2,0},{3,1},{4,6},{5,7},{6,4},{7,5},{8,10},{9,11},{10,... | collective-permute-start | bytes 884744 | tf_op jit(solution)/shard_map/ppermute | solution.py:367
  36.5 13.6 %collective-permute-start.6 = (bf16[2,48,1536]{2,1,0:T(8,128)(2,1)S(1)}, bf16[2,48,1536]{2,1,0:T(8,128)(2,1)S(1)}, u32[]{:S(2)}, u32[]{:S(2)}) collective-permute-start(bf16[2,48,1536]{2,1,0:T(8,128)(2,1)S(1)} %get-tuple-element.57.refs_1_), channel_id=1, source_target_pairs={{0,2},{1,3},{2,0},{3,1},{4,6},{5,7},{6,4},{7,5},{8,10},{9,11},{10,... | collective-permute-start | bytes 884744 | tf_op jit(solution)/shard_map/ppermute | solution.py:367
  50.4 2.4 %collective-permute-start.7 = (bf16[2,96,2048]{2,1,0:T(8,128)(2,1)S(1)}, bf16[2,96,2048]{2,1,0:T(8,128)(2,1)S(1)}, u32[]{:S(2)}, u32[]{:S(2)}) collective-permute-start(bf16[2,96,2048]{2,1,0:T(8,128)(2,1)S(1)} %get-tuple-element.64), channel_id=1, source_target_pairs={{0,1},{1,0},{2,3},{3,2},{4,5},{5,4},{6,7},{7,6},{8,9},{9,8},{10,11... | collective-permute-start | bytes 2359304 | tf_op jit(solution)/shard_map/ppermute | solution.py:364
  52.8 10.0 %collective-permute-start.8 = (bf16[2,96,1536]{2,1,0:T(8,128)(2,1)S(1)}, bf16[2,96,1536]{2,1,0:T(8,128)(2,1)S(1)}, u32[]{:S(2)}, u32[]{:S(2)}) collective-permute-start(bf16[2,96,1536]{2,1,0:T(8,128)(2,1)S(1)} %get-tuple-element.66), channel_id=1, source_target_pairs={{0,1},{1,0},{2,3},{3,2},{4,5},{5,4},{6,7},{7,6},{8,9},{9,8},{10,11... | collective-permute-start | bytes 1769480 | tf_op jit(solution)/shard_map/ppermute | solution.py:364
  53.1 9.8 %collective-permute-start.14 = (bf16[48,3072]{1,0:T(8,128)(2,1)S(1)}, bf16[48,3072]{1,0:T(8,128)(2,1)S(1)}, u32[]{:S(2)}, u32[]{:S(2)}) collective-permute-start(bf16[48,3072]{1,0:T(8,128)(2,1)S(1)} %get-tuple-element.72.refs_0_), channel_id=1, source_target_pairs={{0,2},{1,3},{2,0},{3,1},{4,6},{5,7},{6,4},{7,5},{8,10},{9,11},{10,... | collective-permute-start | bytes 884744 | tf_op jit(solution)/shard_map/ppermute | solution.py:367
  54.5 21.9 %collective-permute-start.13 = (bf16[2,48,2048]{2,1,0:T(8,128)(2,1)S(1)}, bf16[2,48,2048]{2,1,0:T(8,128)(2,1)S(1)}, u32[]{:S(2)}, u32[]{:S(2)}) collective-permute-start(bf16[2,48,2048]{2,1,0:T(8,128)(2,1)S(1)} %get-tuple-element.69.refs_0_), channel_id=1, source_target_pairs={{0,2},{1,3},{2,0},{3,1},{4,6},{5,7},{6,4},{7,5},{8,10},{9,11},{10,... | collective-permute-start | bytes 1179656 | tf_op jit(solution)/shard_map/ppermute | solution.py:367
  55.1 14.7 %collective-permute-start.15 = (bf16[48,3072]{1,0:T(8,128)(2,1)S(1)}, bf16[48,3072]{1,0:T(8,128)(2,1)S(1)}, u32[]{:S(2)}, u32[]{:S(2)}) collective-permute-start(bf16[48,3072]{1,0:T(8,128)(2,1)S(1)} %get-tuple-element.72.refs_0_), channel_id=1, source_target_pairs={{0,1},{1,0},{2,3},{3,2},{4,5},{5,4},{6,7},{7,6},{8,9},{9,8},{10,11... | collective-permute-start | bytes 884744 | tf_op jit(solution)/shard_map/ppermute | solution.py:364
  62.9 6.9 %collective-permute-start.16 = (bf16[48,3072]{1,0:T(8,128)(2,1)S(1)}, bf16[48,3072]{1,0:T(8,128)(2,1)S(1)}, u32[]{:S(2)}, u32[]{:S(2)}) collective-permute-start(bf16[48,3072]{1,0:T(8,128)(2,1)S(1)} %collective-permute-done.14.refs_1_), channel_id=1, source_target_pairs={{0,1},{1,0},{2,3},{3,2},{4,5},{5,4},{6,7},{7,6},{8,9},{9,8},{10,11... | collective-permute-start | bytes 884744 | tf_op jit(solution)/shard_map/ppermute | solution.py:364
  63.0 14.2 %collective-permute-start.9 = (bf16[2,48,1536]{2,1,0:T(8,128)(2,1)S(1)}, bf16[2,48,1536]{2,1,0:T(8,128)(2,1)S(1)}, u32[]{:S(2)}, u32[]{:S(2)}) collective-permute-start(bf16[2,48,1536]{2,1,0:T(8,128)(2,1)S(1)} %get-tuple-element.68.refs_1_), channel_id=1, source_target_pairs={{0,2},{1,3},{2,0},{3,1},{4,6},{5,7},{6,4},{7,5},{8,10},{9,11},{10,... | collective-permute-start | bytes 884744 | tf_op jit(solution)/shard_map/ppermute | solution.py:367
  76.6 7.8 %collective-permute-start.17 = (bf16[48,2048]{1,0:T(8,128)(2,1)S(1)}, bf16[48,2048]{1,0:T(8,128)(2,1)S(1)}, u32[]{:S(2)}, u32[]{:S(2)}) collective-permute-start(bf16[48,2048]{1,0:T(8,128)(2,1)S(1)} %activate.5.refs_0_), channel_id=1, source_target_pairs={{0,2},{1,3},{2,0},{3,1},{4,6},{5,7},{6,4},{7,5},{8,10},{9,11},{10,... | collective-permute-start | bytes 589832 | tf_op jit(solution)/shard_map/ppermute | solution.py:367
  77.3 9.5 %collective-permute-start.10 = (bf16[48,1536]{1,0:T(8,128)(2,1)S(1)}, bf16[48,1536]{1,0:T(8,128)(2,1)S(1)}, u32[]{:S(2)}, u32[]{:S(2)}) collective-permute-start(bf16[48,1536]{1,0:T(8,128)(2,1)S(1)} %activate.4.refs_0_), channel_id=1, source_target_pairs={{0,2},{1,3},{2,0},{3,1},{4,6},{5,7},{6,4},{7,5},{8,10},{9,11},{10,... | collective-permute-start | bytes 442376 | tf_op jit(solution)/shard_map/ppermute | solution.py:367
  78.9 8.0 %collective-permute-start.18 = (bf16[48,2048]{1,0:T(8,128)(2,1)S(1)}, bf16[48,2048]{1,0:T(8,128)(2,1)S(1)}, u32[]{:S(2)}, u32[]{:S(2)}) collective-permute-start(bf16[48,2048]{1,0:T(8,128)(2,1)S(1)} %activate.5.refs_0_), channel_id=1, source_target_pairs={{0,1},{1,0},{2,3},{3,2},{4,5},{5,4},{6,7},{7,6},{8,9},{9,8},{10,11... | collective-permute-start | bytes 589832 | tf_op jit(solution)/shard_map/ppermute | solution.py:364
  84.4 2.5 %collective-permute-start.19 = (bf16[48,2048]{1,0:T(8,128)(2,1)S(1)}, bf16[48,2048]{1,0:T(8,128)(2,1)S(1)}, u32[]{:S(2)}, u32[]{:S(2)}) collective-permute-start(bf16[48,2048]{1,0:T(8,128)(2,1)S(1)} %collective-permute-done.17.refs_1_), channel_id=1, source_target_pairs={{0,1},{1,0},{2,3},{3,2},{4,5},{5,4},{6,7},{7,6},{8,9},{9,8},{10,11... | collective-permute-start | bytes 589832 | tf_op jit(solution)/shard_map/ppermute | solution.py:364
  84.4 4.3 %collective-permute-start.11 = (bf16[48,1536]{1,0:T(8,128)(2,1)S(1)}, bf16[48,1536]{1,0:T(8,128)(2,1)S(1)}, u32[]{:S(2)}, u32[]{:S(2)}) collective-permute-start(bf16[48,1536]{1,0:T(8,128)(2,1)S(1)} %activate.4.refs_0_), channel_id=1, source_target_pairs={{0,1},{1,0},{2,3},{3,2},{4,5},{5,4},{6,7},{7,6},{8,9},{9,8},{10,11... | collective-permute-start | bytes 442376 | tf_op jit(solution)/shard_map/ppermute | solution.py:364
  90.9 4.0 %collective-permute-start.21 = (bf16[64,2048]{1,0:T(8,128)(2,1)S(1)}, bf16[64,2048]{1,0:T(8,128)(2,1)S(1)}, u32[]{:S(2)}, u32[]{:S(2)}) collective-permute-start(bf16[64,2048]{1,0:T(8,128)(2,1)S(1)} %get-tuple-element.77), channel_id=1, source_target_pairs={{4,8},{8,4},{5,9},{9,5},{6,10},{10,6},{7,11},{11,7},{20,24},{24,20... | collective-permute-start | bytes 786440 | tf_op jit(solution)/shard_map/ppermute | solution.py:361
  91.6 9.2 %collective-permute-start.20 = (bf16[64,2048]{1,0:T(8,128)(2,1)S(1)}, bf16[64,2048]{1,0:T(8,128)(2,1)S(1)}, u32[]{:S(2)}, u32[]{:S(2)}) collective-permute-start(bf16[64,2048]{1,0:T(8,128)(2,1)S(1)} %get-tuple-element.77), channel_id=1, source_target_pairs={{0,4},{12,8},{1,5},{13,9},{2,6},{14,10},{3,7},{15,11},{16,20},{28,... | collective-permute-start | bytes 786440 | tf_op jit(solution)/shard_map/ppermute | solution.py:361
  100.9 15.3 %collective-permute-start.24 = (bf16[64,2048]{1,0:T(8,128)(2,1)S(1)}, bf16[64,2048]{1,0:T(8,128)(2,1)S(1)}, u32[]{:S(2)}, u32[]{:S(2)}) collective-permute-start(bf16[64,2048]{1,0:T(8,128)(2,1)S(1)} %get-tuple-element.82), channel_id=1, source_target_pairs={{0,8},{4,12},{8,0},{12,4},{1,9},{5,13},{9,1},{13,5},{2,10},{6,14},... | collective-permute-start | bytes 786440 | tf_op jit(solution)/shard_map/ppermute | solution.py:361
  104.4 9.4 %collective-permute-start.22 = (bf16[32,2048]{1,0:T(8,128)(2,1)S(1)}, bf16[32,2048]{1,0:T(8,128)(2,1)S(1)}, u32[]{:S(2)}, u32[]{:S(2)}) collective-permute-start(bf16[32,2048]{1,0:T(8,128)(2,1)S(1)} %get-tuple-element.80), channel_id=1, source_target_pairs={{0,4},{4,0},{8,12},{12,8},{1,5},{5,1},{9,13},{13,9},{2,6},{6,2},{1... | collective-permute-start | bytes 393224 | tf_op jit(solution)/shard_map/ppermute | solution.py:361
  104.4 11.8 %collective-permute-start.23 = (bf16[32,2048]{1,0:T(8,128)(2,1)S(1)}, bf16[32,2048]{1,0:T(8,128)(2,1)S(1)}, u32[]{:S(2)}, u32[]{:S(2)}) collective-permute-start(bf16[32,2048]{1,0:T(8,128)(2,1)S(1)} %get-tuple-element.81), channel_id=1, source_target_pairs={{0,4},{4,0},{8,12},{12,8},{1,5},{5,1},{9,13},{13,9},{2,6},{6,2},{1... | collective-permute-start | bytes 393224 | tf_op jit(solution)/shard_map/ppermute | solution.py:361
  (3 other events, 3.4 us)

commit v10 on v9

--- a/solution.py
+++ b/solution.py
@@ -33,24 +33,7 @@
     return rows
 
 
-def hold_kernel(tok_ref, out_ref):
-    out_ref[...] = tok_ref[...]
-
-
-def hold(tokens):
-    held = pl.BlockSpec(memory_space=pltpu.VMEM)
-    return pl.pallas_call(
-        hold_kernel,
-        out_shape=jax.ShapeDtypeStruct(tokens.shape, tokens.dtype),
-        in_specs=[held],
-        out_specs=held,
-        cost_estimate=pl.CostEstimate(flops=0, bytes_accessed=0, transcendentals=0),
-        compiler_params=pltpu.CompilerParams(vmem_limit_bytes=4 * MIB),
-        name="hold",
-    )(tokens)
-
-
-def prepare_kernel(n_gx, nx, tok_dev, chunks, lengths_ref, gate_ref, up_ref, in_ref, out_ref, *refs):
+def prepare_kernel(n_gx, nx, chunks, lengths_ref, tok_ref, gate_ref, up_ref, in_ref, out_ref, held_ref, *refs):
     outs, sems = refs[:-1], refs[-1]
     copies = []
     for i, (start, width) in enumerate(chunks):
@@ -58,6 +41,8 @@
             copies.append(pltpu.make_async_copy(src.at[:, pl.ds(start, width)], outs[2 * i + k], sems.at[2 * i + k]))
     for copy in copies:
         copy.start()
+    held_ref[...] = tok_ref[...]
+    tok_dev = tok_ref.shape[0]
     z = lax.axis_index("gx")
     live, slots = in_ref.shape
     quarter = live // (2 * nx)
@@ -75,21 +60,26 @@
         copy.wait()
 
 
-def prepare(lengths, gate_weight, up_weight, chunks, n_gx, nx, tok_dev, live):
-    slots = n_gx * tok_dev
+def prepare(lengths, tokens, gate_weight, up_weight, chunks, n_gx, nx, live):
+    slots = n_gx * tokens.shape[0]
     held, anywhere = pl.BlockSpec(memory_space=pltpu.VMEM), pl.BlockSpec(memory_space=pl.ANY)
     weights = [jax.ShapeDtypeStruct((gate_weight.shape[0], width), BF16) for _, width in chunks for _ in range(2)]
     out = pl.pallas_call(
-        functools.partial(prepare_kernel, n_gx, nx, tok_dev, chunks),
-        out_shape=[jax.ShapeDtypeStruct((live, slots), BF16), jax.ShapeDtypeStruct((slots, live), BF16)] + weights,
-        in_specs=[pl.BlockSpec(memory_space=pltpu.SMEM), anywhere, anywhere],
-        out_specs=[held] * (2 + len(weights)),
+        functools.partial(prepare_kernel, n_gx, nx, chunks),
+        out_shape=[
+            jax.ShapeDtypeStruct((live, slots), BF16),
+            jax.ShapeDtypeStruct((slots, live), BF16),
+            jax.ShapeDtypeStruct(tokens.shape, tokens.dtype),
+        ]
+        + weights,
+        in_specs=[pl.BlockSpec(memory_space=pltpu.SMEM), held, anywhere, anywhere],
+        out_specs=[held] * (3 + len(weights)),
         scratch_shapes=[pltpu.SemaphoreType.DMA((len(weights),))],
         cost_estimate=pl.CostEstimate(flops=0, bytes_accessed=0, transcendentals=0),
         compiler_params=pltpu.CompilerParams(vmem_limit_bytes=4 * MIB),
         name="prepare",
-    )(lengths, gate_weight, up_weight)
-    return out[0], out[1], [out[2 + 2 * i:4 + 2 * i] for i in range(len(chunks))]
+    )(lengths, tokens, gate_weight, up_weight)
+    return out[0], out[1], out[2], [out[3 + 2 * i:5 + 2 * i] for i in range(len(chunks))]
 
 
 def compact_kernel(pick_ref, *refs):
@@ -107,85 +97,97 @@
     )(pick, *blocks)
 
 
-def gate_up_kernel(tok_ref, gate_ref, up_ref, *refs):
-    send_ref, keep_ref = refs[-2:]
+def send_shapes(half, nx, width):
+    return [jax.ShapeDtypeStruct((half // nx, width), BF16)] * (2 * nx)
+
+
+def put_part(i, part, columns, keep_ref, send_refs):
     half = keep_ref.shape[1]
+    nx = len(send_refs) // 2
+    quarter = half // nx
+    keep_ref[i, :, columns] = part[:half]
+    for k in range(nx):
+        first = half + k * quarter
+        send_refs[i * nx + k][:, columns] = part[first:first + quarter].astype(BF16)
+
+
+def gate_up_held_kernel(n_after, tile, tok_ref, gate_ref, up_ref, *refs):
+    keep_ref, *send_refs = refs[n_after:]
+    rows = tok_ref[...]
+    for j in range(0, keep_ref.shape[2], tile):
+        columns = slice(j, j + tile)
+        for i, w_ref in enumerate((gate_ref, up_ref)):
+            part = jnp.dot(rows, w_ref[:, columns], preferred_element_type=F32)
+            put_part(i, part, columns, keep_ref, send_refs)
+
+
+def gate_up_held(tok, gate_held, up_held, after, nx, tile):
+    half, width = tok.shape[0] // 2, gate_held.shape[1]
+    held, anywhere = pl.BlockSpec(memory_space=pltpu.VMEM), pl.BlockSpec(memory_space=pl.ANY)
+    keep, *send = pl.pallas_call(
+        functools.partial(gate_up_held_kernel, len(after), tile),
+        out_shape=[jax.ShapeDtypeStruct((2, half, width), F32)] + send_shapes(half, nx, width),
+        in_specs=[held] * 3 + [anywhere] * len(after),
+        out_specs=[held] * (1 + 2 * nx),
+        compiler_params=pltpu.CompilerParams(vmem_limit_bytes=6 * MIB),
+        cost_estimate=pl.CostEstimate(flops=0, bytes_accessed=0, transcendentals=0),
+        name="gate_up_held",
+    )(tok, gate_held, up_held, *after)
+    return send, keep
+
+
+def gate_up_kernel(n_after, tok_ref, gate_ref, up_ref, *refs):
+    keep_ref, *send_refs = refs[n_after:]
     rows = tok_ref[...]
     for i, w_ref in enumerate((gate_ref, up_ref)):
         part = jnp.dot(rows, w_ref[...], preferred_element_type=F32)
-        keep_ref[i] = part[:half]
-        send_ref[i] = part[half:].astype(BF16)
-
-
-def gate_up(tok, gate_weight, up_weight, after, start, width, tile):
+        put_part(i, part, slice(None), keep_ref, send_refs)
+
+
+def gate_up(tok, gate_weight, up_weight, after, start, width, nx, tile):
     live, depth = tok.shape
     half = live // 2
     weight = pl.BlockSpec((depth, tile), lambda j: (0, start // tile + j))
-    out = pl.BlockSpec((2, half, tile), lambda j: (0, 0, j))
-    return pl.pallas_call(
-        gate_up_kernel,
-        out_shape=[jax.ShapeDtypeStruct((2, half, width), BF16), jax.ShapeDtypeStruct((2, half, width), F32)],
+    keep, *send = pl.pallas_call(
+        functools.partial(gate_up_kernel, len(after)),
+        out_shape=[jax.ShapeDtypeStruct((2, half, width), F32)] + send_shapes(half, nx, width),
         grid=(width // tile,),
         in_specs=[pl.BlockSpec((live, depth), lambda j: (0, 0)), weight, weight]
         + [pl.BlockSpec(memory_space=pl.ANY)] * len(after),
-        out_specs=[out, out],
+        out_specs=[pl.BlockSpec((2, half, tile), lambda j: (0, 0, j))]
+        + [pl.BlockSpec((half // nx, tile), lambda j: (0, j))] * (2 * nx),
         compiler_params=pltpu.CompilerParams(vmem_limit_bytes=40 * MIB),
-        cost_estimate=pl.CostEstimate(
-            flops=0, bytes_accessed=0, transcendentals=0
-        ),
+        cost_estimate=pl.CostEstimate(flops=0, bytes_accessed=0, transcendentals=0),
         name="gate_up",
     )(tok, gate_weight, up_weight, *after)
-
-
-def gate_up_held_kernel(tile, tok_ref, gate_ref, up_ref, *refs):
-    send_ref, keep_ref = refs[-2:]
-    half, width = keep_ref.shape[1:]
-    rows = tok_ref[...]
-    for j in range(0, width, tile):
-        for i, w_ref in enumerate((gate_ref, up_ref)):
-            part = jnp.dot(rows, w_ref[:, j:j + tile], preferred_element_type=F32)
-            keep_ref[i, :, j:j + tile] = part[:half]
-            send_ref[i, :, j:j + tile] = part[half:].astype(BF16)
-
-
-def gate_up_held(tok, gate_held, up_held, after, tile):
-    half, width = tok.shape[0] // 2, gate_held.shape[1]
-    held, anywhere = pl.BlockSpec(memory_space=pltpu.VMEM), pl.BlockSpec(memory_space=pl.ANY)
-    return pl.pallas_call(
-        functools.partial(gate_up_held_kernel, tile),
-        out_shape=[jax.ShapeDtypeStruct((2, half, width), BF16), jax.ShapeDtypeStruct((2, half, width), F32)],
-        in_specs=[held] * 3 + [anywhere] * len(after),
-        out_specs=[held] * 2,
-        compiler_params=pltpu.CompilerParams(vmem_limit_bytes=6 * MIB),
-        cost_estimate=pl.CostEstimate(flops=0, bytes_accessed=0, transcendentals=0),
-        name="gate_up_held",
-    )(tok, gate_held, up_held, *after)
-
-
-def join_kernel(n_handed, n_after, nx, keep_ref, got_ref, *refs):
-    out_refs = refs[n_handed + n_after:][:nx]
+    return send, keep
+
+
+def join_kernel(n_unread, nx, keep_ref, *refs):
+    got_refs, out_refs = refs[:2 * nx], refs[2 * nx + n_unread:][:nx]
     quarter = out_refs[0].shape[1]
-    for k, out_ref in enumerate(out_refs):
-        rows = pl.ds(k * quarter, quarter)
-        out_ref[...] = (keep_ref[:, rows] + got_ref[:, rows].astype(F32)).astype(out_ref.dtype)
-
-
-def join(keep, got, handed, after, nx):
+    for i in range(2):
+        for k, out_ref in enumerate(out_refs):
+            rows = pl.ds(k * quarter, quarter)
+            out_ref[i] = (keep_ref[i, rows] + got_refs[i * nx + k][...].astype(F32)).astype(out_ref.dtype)
+
+
+def join(keep, got, handed, nx):
     two, half, width = keep.shape
     shape = (two, half // nx, width)
     held, anywhere = pl.BlockSpec(memory_space=pltpu.VMEM), pl.BlockSpec(memory_space=pl.ANY)
     out = pl.pallas_call(
-        functools.partial(join_kernel, len(handed), len(after), nx),
+        functools.partial(join_kernel, len(handed), nx),
         out_shape=[jax.ShapeDtypeStruct(shape, BF16 if k else F32) for k in range(nx)]
         + [jax.ShapeDtypeStruct(a.shape, a.dtype) for a in handed],
-        in_specs=[held, held] + [anywhere] * (len(handed) + len(after)),
+        in_specs=[held] * (1 + len(got)) + [anywhere] * len(handed),
         out_specs=[held] * nx + [anywhere] * len(handed),
-        input_output_aliases={2 + i: nx + i for i in range(len(handed))},
+        input_output_aliases={1 + len(got) + i: nx + i for i in range(len(handed))},
         compiler_params=pltpu.CompilerParams(vmem_limit_bytes=8 * MIB),
         cost_estimate=pl.CostEstimate(flops=0, bytes_accessed=0, transcendentals=0),
         name="join",
-    )(keep, got, *handed, *after)
-    return out[0], out[1:nx], out[nx:]
+    )(keep, *got, *handed)
+    return out[0], list(out[1:nx]), list(out[nx:])
 
 
 def activate_kernel(n_got, n_chunks, n_unread, *refs):
@@ -366,35 +368,35 @@
     def over_x(block, k):
         return lax.ppermute(block, "gy", [(i, (i + 2 * k) % n_gy) for i in range(n_gy)])
 
-    mine = hold(tokens)
-    blocks = [mine] + [over_z(mine, k) for k in range(1, n_gx)]
-    pick_in, pick_out, weights = prepare(lengths, gate_weight, up_weight, chunks[:3], n_gx, nx, tok_dev, live)
+    far = [over_z(tokens, k) for k in range(1, n_gx)]
+    pick_in, pick_out, held, weights = prepare(lengths, tokens, gate_weight, up_weight, chunks[:3], n_gx, nx, live)
+    blocks = [held] + far
     tok = compact(pick_in, blocks)
 
-    made = [gate_up_held(tok, *weights[i], [], tile) for i in range(2)]
+    made = [gate_up_held(tok, *weights[i], [], nx, tile) for i in range(2)]
     sends, keeps = [list(a) for a in zip(*made)]
     sums = []
 
     def exchange(j, handed):
-        mine, blocks, handed = join(keeps[j], over_core(sends[j]), handed, [], nx)
+        mine, blocks, handed = join(keeps[j], [over_core(a) for a in sends[j]], handed, nx)
         sums.append([mine] + [over_x(b, k + 1) for k, b in enumerate(blocks)])
-        return list(blocks), handed
+        return blocks, handed
 
     def finish(first, last, handed, after):
         own, handed = activate(sums[first:last], handed, after)
         h = [own] + [over_x(own, -k) for k in range(1, nx)]
         return h + [over_core(a) for a in h], handed
 
-    ready, sends[1:2] = exchange(0, sends[1:2])
-    ready += exchange(1, [])[0]
-    made = [gate_up_held(tok, *weights[2], ready, tile)]
-    made.append(gate_up(tok, gate_weight, up_weight, made[0][:1], *chunks[3], tile))
-    for send, keep in made:
-        sends.append(send)
-        keeps.append(keep)
-    hidden, sends[2:] = finish(0, 2, sends[2:], [])
-    ready, sends[3:] = exchange(2, sends[3:])
-    ready += exchange(3, [])[0]
+    ready, sends[1] = exchange(0, sends[1])
+    ready = ready + exchange(1, [])[0]
+    made = [gate_up_held(tok, *weights[2], ready, nx, tile)]
+    made.append(gate_up(tok, gate_weight, up_weight, made[0][0][:1], *chunks[3], nx, tile))
+    pieces = len(sends[0])
+    hidden, handed = finish(0, 2, made[0][0] + made[1][0], [])
+    sends += [handed[:pieces], handed[pieces:]]
+    keeps += [keep for _, keep in made]
+    ready, sends[3] = exchange(2, sends[3])
+    ready = ready + exchange(3, [])[0]
     rows_held = fetch(down_weight, chunks[2:], ready)
     total = down(hidden, down_weight, [rows_held[0]], chunks[0][0])
     hidden, _ = finish(2, 3, [], [total])

time: 117 us -> 119 us (1.017)
  starting transfers between devices: 25.5 us -> 29.3 us
  waiting for transfers between devices: 42.4 us -> 40.2 us
    ppermute x10 -> x22, starting transfers between devices: 1.43 us -> 4.91 us  [over_core(): return lax.ppermute(block, 'gy', [(i, i ^ 1) for i in range(n_gy)])]
    ppermute x10 -> x22, waiting for transfers between devices: 2.44 us -> 0.84 us  [over_core(): return lax.ppermute(block, 'gy', [(i, i ^ 1) for i in range(n_gy)])]
    ppermute x7, waiting for transfers between devices: 16.9 us -> 15.7 us  [over_x(): lax.ppermute(block, 'gy', [(i, (i + 2 * k) % n_gy) for i in range(n_gy)])]
    pallas_call x10 -> x9, Pallas kernels: 29.6 us -> 29.6 us  [the longest x1 13.6 us: prepare(): pl.pallas_call(functools.partial(prepare_kernel, n_gx, nx, chunks), out_s...]
  transfers between devices with their start and end apart: 25 -> 37, of which waited for: 10 -> 9; matrix products, arithmetic and copies ran while one was open for 0% -> 0% of each run, Pallas kernels for 35% -> 34%
where the time goes in v10:
time: 119 us
  Pallas kernels  46.4 us (39%)
  waiting for transfers between devices  40.2 us (34%)
  starting transfers between devices  29.3 us (25%)
  local copies, waits for them, and re-layouts  1.64 us (1%)
    ppermute x8, waiting for transfers between devices, over_z(): return lax.ppermute(block, 'gx', [(z, z ^ k) for z in among])  23.6 us
    ppermute x7, waiting for transfers between devices, over_x(): lax.ppermute(block, 'gy', [(i, (i + 2 * k) % n_gy) for i in range(n_gy)])  15.7 us
    ppermute x8, starting transfers between devices, over_z(): return lax.ppermute(block, 'gx', [(z, z ^ k) for z in among])  15.4 us
    pallas_call x1, Pallas kernels, prepare(): pl.pallas_call(functools.partial(prepare_kernel, n_gx, nx, chunks), out_s...  13.6 us
    ppermute x7, starting transfers between devices, over_x(): lax.ppermute(block, 'gy', [(i, (i + 2 * k) % n_gy) for i in range(n_gy)])  9.05 us
    pallas_call x3, Pallas kernels, gate_up_held(): pl.pallas_call(functools.partial(gate_up_held_kernel, len(after), tile),...  8.69 us
    pallas_call x1, Pallas kernels, gate_up(): pl.pallas_call(functools.partial(gate_up_kernel, len(after)), out_shape=[...  6.83 us
    pallas_call x1, Pallas kernels, down(): pl.pallas_call(functools.partial(down_kernel, len(hidden)), out_shape=jax...  6.64 us
  transfers between devices with their start and end apart: 37, of which 9 were waited for; matrix products, arithmetic and copies ran while one was open for 0% of the time, Pallas kernels for 34%

profile of v10, /device:TPU:0, one launch (start us, length us, event | category | flops | bytes accessed | tf_op | source)
XLA Modules:
  0.0 118.7 jit_solution(18358999007934202038)
XLA Ops:
  0.0 3.0 %collective-permute-start = (bf16[64,2048]{1,0:T(8,128)(2,1)}, bf16[64,2048]{1,0:T(8,128)(2,1)S(1)}, u32[]{:S(2)}, u32[]{:S(2)}) collective-permute-start(bf16[64,2048]{1,0:T(8,128)(2,1)} %tok_ref.1), channel_id=1, source_target_pairs={{0,4},{4,0},{8,12},{12,8},{1,5},{5,1},{9,13},{13,9},{2,6},{6,2},{1... | collective-permute-start | bytes 786440 | tf_op jit(solution)/shard_map/ppermute | solution.py:363
  3.0 2.5 %collective-permute-start.2 = (bf16[64,2048]{1,0:T(8,128)(2,1)}, bf16[64,2048]{1,0:T(8,128)(2,1)S(1)}, u32[]{:S(2)}, u32[]{:S(2)}) collective-permute-start(bf16[64,2048]{1,0:T(8,128)(2,1)} %tok_ref.1), channel_id=1, source_target_pairs={{0,12},{4,8},{8,4},{12,0},{1,13},{5,9},{9,5},{13,1},{2,14},{6,10},... | collective-permute-start | bytes 786440 | tf_op jit(solution)/shard_map/ppermute | solution.py:363
  7.3 13.6 %prepare.1 = (bf16[192,256]{1,0:T(8,128)(2,1)S(1)}, bf16[256,192]{1,0:T(8,128)(2,1)S(1)}, bf16[64,2048]{1,0:T(8,128)(2,1)S(1)}, bf16[2048,1536]{1,0:T(8,128)(2,1...) custom-call(s32[4]{0:T(128)S(1)} %copy-done.1, ...), custom_call_target="tpu_custom_call" | custom-call | tf_op jit(solution)/shard_map/prepare/pallas_call | solution.py:67
  20.9 7.8 %collective-permute-done.1.refs_2_ = bf16[64,2048]{1,0:T(8,128)(2,1)S(1)} collective-permute-done((bf16[64,2048]{1,0:T(8,128)(2,1)}, bf16[64,2048]{1,0:T(8,128)(2,1)S(1)}, u32[]{:S(2)}, u32[]{:S(2)}) %collective-permute-start.1) | collective-permute-done | bytes 262176 | tf_op jit(solution)/shard_map/ppermute | solution.py:363
  29.1 2.6 %gate_up_held.3 = (f32[2,96,1536]{2,1,0:T(8,128)S(1)}, bf16[48,1536]{1,0:T(8,128)(2,1)S(1)}, bf16[48,1536]{1,0:T(8,128)(2,1)S(1)}, bf16[48,1536]{1,0:T(8,128)(2,1)S(1)}, bf16[48,1536]{1,0:T(8,128)(2,1)S(1)}) custom-call(bf16[192,2048]{1,0:T(8,128)(2,1)S(1)} %compact.1.tok_ref, bf16[2048,1536]{1,0:T(8,128)(2,1)S(1)} %get-tuple-element.73.gate_ref, ...), custom_call_target="tpu_custom_call" | custom-call | tf_op jit(solution)/shard_map/gate_up_held/pallas_call | solution.py:127
  32.8 2.6 %gate_up_held.4 = (f32[2,96,1536]{2,1,0:T(8,128)S(1)}, bf16[48,1536]{1,0:T(8,128)(2,1)S(1)}, bf16[48,1536]{1,0:T(8,128)(2,1)S(1)}, bf16[48,1536]{1,0:T(8,128)(2,1)S(1)}, bf16[48,1536]{1,0:T(8,128)(2,1)S(1)}) custom-call(bf16[192,2048]{1,0:T(8,128)(2,1)S(1)} %compact.1.tok_ref, bf16[2048,1536]{1,0:T(8,128)(2,1)S(1)} %get-tuple-element.80.gate_ref, ...), custom_call_target="tpu_custom_call" | custom-call | tf_op jit(solution)/shard_map/gate_up_held/pallas_call | solution.py:127
  39.4 3.5 %gate_up_held.5 = (f32[2,96,2048]{2,1,0:T(8,128)S(1)}, bf16[48,2048]{1,0:T(8,128)(2,1)S(1)}, bf16[48,2048]{1,0:T(8,128)(2,1)S(1)}, bf16[48,2048]{1,0:T(8,128)(2,1)S(1)}, bf16[48,2048]{1,0:T(8,128)(2,1)S(1)}) custom-call(bf16[192,2048]{1,0:T(8,128)(2,1)S(1)} %compact.1.tok_ref, bf16[2048,2048]{1,0:T(8,128)(2,1)S(1)} %get-tuple-element.71.gate_ref, ...), custom_call_target="tpu_custom_call" | custom-call | tf_op jit(solution)/shard_map/gate_up_held/pallas_call | solution.py:127
  42.9 6.8 %gate_up.1 = (f32[2,96,1536]{2,1,0:T(8,128)S(1)}, bf16[48,1536]{1,0:T(8,128)(2,1)S(1)}, bf16[48,1536]{1,0:T(8,128)(2,1)S(1)}, bf16[48,1536]{1,0:T(8,128)(2,1)S(1)}, bf16[48,1536]{1,0:T(8,128)(2,1)S(1)}) custom-call(bf16[192,2048]{1,0:T(8,128)(2,1)S(1)} %compact.1.tok_ref, bf16[2048,6656]{1,0:T(8,128)(2,1)} %gate_ref.3, bf16[2048,6656]{1,0:T(8,128)(2,1)} %up_ref.3, ...), custom_call_target="tpu_custom_call" | custom-call | tf_op jit(solution)/shard_map/gate_up/pallas_call | solution.py:151
  49.7 2.2 %collective-permute-done.12.refs_3_ = bf16[2,48,1536]{2,1,0:T(8,128)(2,1)S(1)} collective-permute-done((bf16[2,48,1536]{2,1,0:T(8,128)(2,1)S(1)}, bf16[2,48,1536]{2,1,0:T(8,128)(2,1)S(1)}, u32[]{:S(2)}, u32[]{:S(2)}) %collective-permute-start.12) | collective-permute-done | bytes 294944 | tf_op jit(solution)/shard_map/ppermute | solution.py:369
  56.8 6.4 %collective-permute-done.26.refs_1_ = bf16[48,3072]{1,0:T(8,128)(2,1)S(1)} collective-permute-done((bf16[48,3072]{1,0:T(8,128)(2,1)S(1)}, bf16[48,3072]{1,0:T(8,128)(2,1)S(1)}, u32[]{:S(2)}, u32[]{:S(2)}) %collective-permute-start.26) | collective-permute-done | bytes 294944 | tf_op jit(solution)/shard_map/ppermute | solution.py:369
  64.6 1.6 %collective-permute-start.21 = (bf16[2,48,1536]{2,1,0:T(8,128)(2,1)S(1)}, bf16[2,48,1536]{2,1,0:T(8,128)(2,1)S(1)}, u32[]{:S(2)}, u32[]{:S(2)}) collective-permute-start(bf16[2,48,1536]{2,1,0:T(8,128)(2,1)S(1)} %get-tuple-element.118.refs_1_), channel_id=1, source_target_pairs={{0,2},{1,3},{2,0},{3,1},{4,6},{5,7},{6,4},{7,5},{8,10},{9,11},{10,... | collective-permute-start | bytes 884744 | tf_op jit(solution)/shard_map/ppermute | solution.py:369
  66.2 5.2 %fetch.1 = (bf16[2048,2048]{1,0:T(8,128)(2,1)S(1)}, bf16[1536,2048]{1,0:T(8,128)(2,1)S(1)}) custom-call(bf16[6656,2048]{1,0:T(8,128)(2,1)} %refs_4_.1, bf16[2,48,2048]{2,1,0:T(8,128)(2,1)S(1)} %get-tuple-element.119.refs_0_, bf16[2,48,1536]{2,1,0:T(8,128)(2,1)S(1)} %get-tuple-element.118.refs_1_), custom_call_target="tpu_custom_call" | custom-call | tf_op jit(solution)/shard_map/fetch/pallas_call | solution.py:296
  71.4 6.6 %down.1.refs_2_.refs_5_ = f32[192,2048]{1,0:T(8,128)S(1)} custom-call(bf16[48,3072]{1,0:T(8,128)(2,1)S(1)} %get-tuple-element.122.refs_0_, bf16[48,3072]{1,0:T(8,128)(2,1)S(1)} %collective-permute-done.26.refs_1_, bf16[48,3072]{1,0:T(8,128)(2,1)S(1)} %collective-permute-done.27.refs_2_, bf16[48,3072]{1,0:T(8,128)(2,1)S(1)} %collective-permute-done.28.refs_3_, ...), custom_call_target="tpu_custom_call" | custom-call | tf_op jit(solution)/shard_map/down/pallas_call | solution.py:267
  79.0 1.6 %collective-permute-start.22 = (bf16[48,1536]{1,0:T(8,128)(2,1)S(1)}, bf16[48,1536]{1,0:T(8,128)(2,1)S(1)}, u32[]{:S(2)}, u32[]{:S(2)}) collective-permute-start(bf16[48,1536]{1,0:T(8,128)(2,1)S(1)} %activate.4.refs_0_), channel_id=1, source_target_pairs={{0,2},{1,3},{2,0},{3,1},{4,6},{5,7},{6,4},{7,5},{8,10},{9,11},{10,... | collective-permute-start | bytes 442376 | tf_op jit(solution)/shard_map/ppermute | solution.py:369
  80.5 5.6 %collective-permute-done.29.refs_1_ = bf16[48,2048]{1,0:T(8,128)(2,1)S(1)} collective-permute-done((bf16[48,2048]{1,0:T(8,128)(2,1)S(1)}, bf16[48,2048]{1,0:T(8,128)(2,1)S(1)}, u32[]{:S(2)}, u32[]{:S(2)}) %collective-permute-start.29) | collective-permute-done | bytes 196640 | tf_op jit(solution)/shard_map/ppermute | solution.py:369
  86.6 1.5 %collective-permute-done.22.refs_1_ = bf16[48,1536]{1,0:T(8,128)(2,1)S(1)} collective-permute-done((bf16[48,1536]{1,0:T(8,128)(2,1)S(1)}, bf16[48,1536]{1,0:T(8,128)(2,1)S(1)}, u32[]{:S(2)}, u32[]{:S(2)}) %collective-permute-start.22) | collective-permute-done | bytes 147488 | tf_op jit(solution)/shard_map/ppermute | solution.py:369
  88.2 1.8 %down_held.2.refs_5_ = f32[192,2048]{1,0:T(8,128)S(1)} custom-call(bf16[48,2048]{1,0:T(8,128)(2,1)S(1)} %activate.5.refs_0_, bf16[48,2048]{1,0:T(8,128)(2,1)S(1)} %collective-permute-done.29.refs_1_, bf16[48,2048]{1,0:T(8,128)(2,1)S(1)} %collective-permute-done.30.refs_2_, bf16[48,2048]{1,0:T(8,128)(2,1)S(1)} %collective-permute-done.31.refs_3_, ...), custom_call_target="tpu_custom_call" | custom-call | tf_op jit(solution)/shard_map/down_held/pallas_call | solution.py:333
  90.0 2.2 %down_held.3 = (bf16[64,2048]{1,0:T(8,128)(2,1)S(1)}, bf16[32,2048]{1,0:T(8,128)(2,1)S(1)}, bf16[32,2048]{1,0:T(8,128)(2,1)S(1)}, bf16[64,2048]{1,0:T(8,128)(2,1)S(1)}, bf16[64,2048]{1,0:T(8,128)(2,1)S(1)}) custom-call(bf16[48,1536]{1,0:T(8,128)(2,1)S(1)} %activate.4.refs_0_, bf16[48,1536]{1,0:T(8,128)(2,1)S(1)} %collective-permute-done.22.refs_1_, ...), custom_call_target="tpu_custom_call" | custom-call | tf_op jit(solution)/shard_map/down_held/pallas_call | solution.py:333
  92.9 3.4 %collective-permute-start.32 = (bf16[64,2048]{1,0:T(8,128)(2,1)S(1)}, bf16[64,2048]{1,0:T(8,128)(2,1)S(1)}, u32[]{:S(2)}, u32[]{:S(2)}) collective-permute-start(bf16[64,2048]{1,0:T(8,128)(2,1)S(1)} %get-tuple-element.127), channel_id=1, source_target_pairs={{0,4},{12,8},{1,5},{13,9},{2,6},{14,10},{3,7},{15,11},{16,20},{28,... | collective-permute-start | bytes 786440 | tf_op jit(solution)/shard_map/ppermute | solution.py:363
  96.3 5.9 %collective-permute-done.32.got_ref = bf16[64,2048]{1,0:T(8,128)(2,1)S(1)} collective-permute-done((bf16[64,2048]{1,0:T(8,128)(2,1)S(1)}, bf16[64,2048]{1,0:T(8,128)(2,1)S(1)}, u32[]{:S(2)}, u32[]{:S(2)}) %collective-permute-start.32) | collective-permute-done | bytes 262176 | tf_op jit(solution)/shard_map/ppermute | solution.py:363
  102.2 3.7 %collective-permute-start.36 = (bf16[64,2048]{1,0:T(8,128)(2,1)S(1)}, bf16[64,2048]{1,0:T(8,128)(2,1)S(1)}, u32[]{:S(2)}, u32[]{:S(2)}) collective-permute-start(bf16[64,2048]{1,0:T(8,128)(2,1)S(1)} %get-tuple-element.132), channel_id=1, source_target_pairs={{0,8},{4,12},{8,0},{12,4},{1,9},{5,13},{9,1},{13,5},{2,10},{6,14},... | collective-permute-start | bytes 786440 | tf_op jit(solution)/shard_map/ppermute | solution.py:363
  105.9 2.0 %collective-permute-start.35 = (bf16[32,2048]{1,0:T(8,128)(2,1)S(1)}, bf16[32,2048]{1,0:T(8,128)(2,1)S(1)}, u32[]{:S(2)}, u32[]{:S(2)}) collective-permute-start(bf16[32,2048]{1,0:T(8,128)(2,1)S(1)} %get-tuple-element.131), channel_id=1, source_target_pairs={{0,4},{4,0},{8,12},{12,8},{1,5},{5,1},{9,13},{13,9},{2,6},{6,2},{1... | collective-permute-start | bytes 393224 | tf_op jit(solution)/shard_map/ppermute | solution.py:363
  108.0 7.4 %collective-permute-done.34 = bf16[32,2048]{1,0:T(8,128)(2,1)S(1)} collective-permute-done((bf16[32,2048]{1,0:T(8,128)(2,1)S(1)}, bf16[32,2048]{1,0:T(8,128)(2,1)S(1)}, u32[]{:S(2)}, u32[]{:S(2)}) %collective-permute-start.34) | collective-permute-done | bytes 131104 | tf_op jit(solution)/shard_map/ppermute | solution.py:363
  115.3 2.5 %collective-permute-done.35 = bf16[32,2048]{1,0:T(8,128)(2,1)S(1)} collective-permute-done((bf16[32,2048]{1,0:T(8,128)(2,1)S(1)}, bf16[32,2048]{1,0:T(8,128)(2,1)S(1)}, u32[]{:S(2)}, u32[]{:S(2)}) %collective-permute-start.35) | collective-permute-done | bytes 131104 | tf_op jit(solution)/shard_map/ppermute | solution.py:363
  (73 shorter events, 16.3 us)
Async XLA Ops:
  0.0 20.9 %collective-permute-start = (bf16[64,2048]{1,0:T(8,128)(2,1)}, bf16[64,2048]{1,0:T(8,128)(2,1)S(1)}, u32[]{:S(2)}, u32[]{:S(2)}) collective-permute-start(bf16[64,2048]{1,0:T(8,128)(2,1)} %tok_ref.1), channel_id=1, source_target_pairs={{0,4},{4,0},{8,12},{12,8},{1,5},{5,1},{9,13},{13,9},{2,6},{6,2},{1... | collective-permute-start | bytes 786440 | tf_op jit(solution)/shard_map/ppermute | solution.py:363
  3.0 17.9 %collective-permute-start.2 = (bf16[64,2048]{1,0:T(8,128)(2,1)}, bf16[64,2048]{1,0:T(8,128)(2,1)S(1)}, u32[]{:S(2)}, u32[]{:S(2)}) collective-permute-start(bf16[64,2048]{1,0:T(8,128)(2,1)} %tok_ref.1), channel_id=1, source_target_pairs={{0,12},{4,8},{8,4},{12,0},{1,13},{5,9},{9,5},{13,1},{2,14},{6,10},... | collective-permute-start | bytes 786440 | tf_op jit(solution)/shard_map/ppermute | solution.py:363
  5.5 23.2 %collective-permute-start.1 = (bf16[64,2048]{1,0:T(8,128)(2,1)}, bf16[64,2048]{1,0:T(8,128)(2,1)S(1)}, u32[]{:S(2)}, u32[]{:S(2)}) collective-permute-start(bf16[64,2048]{1,0:T(8,128)(2,1)} %tok_ref.1), channel_id=1, source_target_pairs={{0,8},{4,12},{8,0},{12,4},{1,9},{5,13},{9,1},{13,5},{2,10},{6,14},... | collective-permute-start | bytes 786440 | tf_op jit(solution)/shard_map/ppermute | solution.py:363
  31.7 3.7 %collective-permute-start.3 = (bf16[48,1536]{1,0:T(8,128)(2,1)S(1)}, bf16[48,1536]{1,0:T(8,128)(2,1)S(1)}, u32[]{:S(2)}, u32[]{:S(2)}) collective-permute-start(bf16[48,1536]{1,0:T(8,128)(2,1)S(1)} %get-tuple-element.76), channel_id=1, source_target_pairs={{0,1},{1,0},{2,3},{3,2},{4,5},{5,4},{6,7},{7,6},{8,9},{9,8},{10,11... | collective-permute-start | bytes 442376 | tf_op jit(solution)/shard_map/ppermute | solution.py:366
  31.8 3.6 %collective-permute-start.4 = (bf16[48,1536]{1,0:T(8,128)(2,1)S(1)}, bf16[48,1536]{1,0:T(8,128)(2,1)S(1)}, u32[]{:S(2)}, u32[]{:S(2)}) collective-permute-start(bf16[48,1536]{1,0:T(8,128)(2,1)S(1)} %get-tuple-element.77), channel_id=1, source_target_pairs={{0,1},{1,0},{2,3},{3,2},{4,5},{5,4},{6,7},{7,6},{8,9},{9,8},{10,11... | collective-permute-start | bytes 442376 | tf_op jit(solution)/shard_map/ppermute | solution.py:366
  36.7 13.1 %collective-permute-start.11 = (bf16[2,48,1536]{2,1,0:T(8,128)(2,1)S(1)}, bf16[2,48,1536]{2,1,0:T(8,128)(2,1)S(1)}, u32[]{:S(2)}, u32[]{:S(2)}) collective-permute-start(bf16[2,48,1536]{2,1,0:T(8,128)(2,1)S(1)} %get-tuple-element.86.refs_0_), channel_id=1, source_target_pairs={{0,2},{1,3},{2,0},{3,1},{4,6},{5,7},{6,4},{7,5},{8,10},{9,11},{10,... | collective-permute-start | bytes 884744 | tf_op jit(solution)/shard_map/ppermute | solution.py:369
  38.3 13.7 %collective-permute-start.12 = (bf16[2,48,1536]{2,1,0:T(8,128)(2,1)S(1)}, bf16[2,48,1536]{2,1,0:T(8,128)(2,1)S(1)}, u32[]{:S(2)}, u32[]{:S(2)}) collective-permute-start(bf16[2,48,1536]{2,1,0:T(8,128)(2,1)S(1)} %get-tuple-element.92.refs_1_), channel_id=1, source_target_pairs={{0,2},{1,3},{2,0},{3,1},{4,6},{5,7},{6,4},{7,5},{8,10},{9,11},{10,... | collective-permute-start | bytes 884744 | tf_op jit(solution)/shard_map/ppermute | solution.py:369
  53.3 9.9 %collective-permute-start.26 = (bf16[48,3072]{1,0:T(8,128)(2,1)S(1)}, bf16[48,3072]{1,0:T(8,128)(2,1)S(1)}, u32[]{:S(2)}, u32[]{:S(2)}) collective-permute-start(bf16[48,3072]{1,0:T(8,128)(2,1)S(1)} %get-tuple-element.122.refs_0_), channel_id=1, source_target_pairs={{0,2},{1,3},{2,0},{3,1},{4,6},{5,7},{6,4},{7,5},{8,10},{9,11},{10,... | collective-permute-start | bytes 884744 | tf_op jit(solution)/shard_map/ppermute | solution.py:369
  55.0 8.2 %collective-permute-start.17 = (bf16[48,1536]{1,0:T(8,128)(2,1)S(1)}, bf16[48,1536]{1,0:T(8,128)(2,1)S(1)}, u32[]{:S(2)}, u32[]{:S(2)}) collective-permute-start(bf16[48,1536]{1,0:T(8,128)(2,1)S(1)} %get-tuple-element.113), channel_id=1, source_target_pairs={{0,1},{1,0},{2,3},{3,2},{4,5},{5,4},{6,7},{7,6},{8,9},{9,8},{10,11... | collective-permute-start | bytes 442376 | tf_op jit(solution)/shard_map/ppermute | solution.py:366
  55.0 8.6 %collective-permute-start.18 = (bf16[48,1536]{1,0:T(8,128)(2,1)S(1)}, bf16[48,1536]{1,0:T(8,128)(2,1)S(1)}, u32[]{:S(2)}, u32[]{:S(2)}) collective-permute-start(bf16[48,1536]{1,0:T(8,128)(2,1)S(1)} %get-tuple-element.114), channel_id=1, source_target_pairs={{0,1},{1,0},{2,3},{3,2},{4,5},{5,4},{6,7},{7,6},{8,9},{9,8},{10,11... | collective-permute-start | bytes 442376 | tf_op jit(solution)/shard_map/ppermute | solution.py:366
  55.5 22.5 %collective-permute-start.25 = (bf16[2,48,2048]{2,1,0:T(8,128)(2,1)S(1)}, bf16[2,48,2048]{2,1,0:T(8,128)(2,1)S(1)}, u32[]{:S(2)}, u32[]{:S(2)}) collective-permute-start(bf16[2,48,2048]{2,1,0:T(8,128)(2,1)S(1)} %get-tuple-element.119.refs_0_), channel_id=1, source_target_pairs={{0,2},{1,3},{2,0},{3,1},{4,6},{5,7},{6,4},{7,5},{8,10},{9,11},{10,... | collective-permute-start | bytes 1179656 | tf_op jit(solution)/shard_map/ppermute | solution.py:369
  56.8 7.0 %collective-permute-start.19 = (bf16[48,1536]{1,0:T(8,128)(2,1)S(1)}, bf16[48,1536]{1,0:T(8,128)(2,1)S(1)}, u32[]{:S(2)}, u32[]{:S(2)}) collective-permute-start(bf16[48,1536]{1,0:T(8,128)(2,1)S(1)} %get-tuple-element.115), channel_id=1, source_target_pairs={{0,1},{1,0},{2,3},{3,2},{4,5},{5,4},{6,7},{7,6},{8,9},{9,8},{10,11... | collective-permute-start | bytes 442376 | tf_op jit(solution)/shard_map/ppermute | solution.py:366
  63.2 8.2 %collective-permute-start.27 = (bf16[48,3072]{1,0:T(8,128)(2,1)S(1)}, bf16[48,3072]{1,0:T(8,128)(2,1)S(1)}, u32[]{:S(2)}, u32[]{:S(2)}) collective-permute-start(bf16[48,3072]{1,0:T(8,128)(2,1)S(1)} %get-tuple-element.122.refs_0_), channel_id=1, source_target_pairs={{0,1},{1,0},{2,3},{3,2},{4,5},{5,4},{6,7},{7,6},{8,9},{9,8},{10,11... | collective-permute-start | bytes 884744 | tf_op jit(solution)/shard_map/ppermute | solution.py:366
  63.7 7.7 %collective-permute-start.28 = (bf16[48,3072]{1,0:T(8,128)(2,1)S(1)}, bf16[48,3072]{1,0:T(8,128)(2,1)S(1)}, u32[]{:S(2)}, u32[]{:S(2)}) collective-permute-start(bf16[48,3072]{1,0:T(8,128)(2,1)S(1)} %collective-permute-done.26.refs_1_), channel_id=1, source_target_pairs={{0,1},{1,0},{2,3},{3,2},{4,5},{5,4},{6,7},{7,6},{8,9},{9,8},{10,11... | collective-permute-start | bytes 884744 | tf_op jit(solution)/shard_map/ppermute | solution.py:366
  64.6 14.2 %collective-permute-start.21 = (bf16[2,48,1536]{2,1,0:T(8,128)(2,1)S(1)}, bf16[2,48,1536]{2,1,0:T(8,128)(2,1)S(1)}, u32[]{:S(2)}, u32[]{:S(2)}) collective-permute-start(bf16[2,48,1536]{2,1,0:T(8,128)(2,1)S(1)} %get-tuple-element.118.refs_1_), channel_id=1, source_target_pairs={{0,2},{1,3},{2,0},{3,1},{4,6},{5,7},{6,4},{7,5},{8,10},{9,11},{10,... | collective-permute-start | bytes 884744 | tf_op jit(solution)/shard_map/ppermute | solution.py:369
  78.3 7.9 %collective-permute-start.29 = (bf16[48,2048]{1,0:T(8,128)(2,1)S(1)}, bf16[48,2048]{1,0:T(8,128)(2,1)S(1)}, u32[]{:S(2)}, u32[]{:S(2)}) collective-permute-start(bf16[48,2048]{1,0:T(8,128)(2,1)S(1)} %activate.5.refs_0_), channel_id=1, source_target_pairs={{0,2},{1,3},{2,0},{3,1},{4,6},{5,7},{6,4},{7,5},{8,10},{9,11},{10,... | collective-permute-start | bytes 589832 | tf_op jit(solution)/shard_map/ppermute | solution.py:369
  79.0 9.2 %collective-permute-start.22 = (bf16[48,1536]{1,0:T(8,128)(2,1)S(1)}, bf16[48,1536]{1,0:T(8,128)(2,1)S(1)}, u32[]{:S(2)}, u32[]{:S(2)}) collective-permute-start(bf16[48,1536]{1,0:T(8,128)(2,1)S(1)} %activate.4.refs_0_), channel_id=1, source_target_pairs={{0,2},{1,3},{2,0},{3,1},{4,6},{5,7},{6,4},{7,5},{8,10},{9,11},{10,... | collective-permute-start | bytes 442376 | tf_op jit(solution)/shard_map/ppermute | solution.py:369
  80.5 7.6 %collective-permute-start.30 = (bf16[48,2048]{1,0:T(8,128)(2,1)S(1)}, bf16[48,2048]{1,0:T(8,128)(2,1)S(1)}, u32[]{:S(2)}, u32[]{:S(2)}) collective-permute-start(bf16[48,2048]{1,0:T(8,128)(2,1)S(1)} %activate.5.refs_0_), channel_id=1, source_target_pairs={{0,1},{1,0},{2,3},{3,2},{4,5},{5,4},{6,7},{7,6},{8,9},{9,8},{10,11... | collective-permute-start | bytes 589832 | tf_op jit(solution)/shard_map/ppermute | solution.py:366
  86.1 3.9 %collective-permute-start.23 = (bf16[48,1536]{1,0:T(8,128)(2,1)S(1)}, bf16[48,1536]{1,0:T(8,128)(2,1)S(1)}, u32[]{:S(2)}, u32[]{:S(2)}) collective-permute-start(bf16[48,1536]{1,0:T(8,128)(2,1)S(1)} %activate.4.refs_0_), channel_id=1, source_target_pairs={{0,1},{1,0},{2,3},{3,2},{4,5},{5,4},{6,7},{7,6},{8,9},{9,8},{10,11... | collective-permute-start | bytes 442376 | tf_op jit(solution)/shard_map/ppermute | solution.py:366
  92.2 4.1 %collective-permute-start.33 = (bf16[64,2048]{1,0:T(8,128)(2,1)S(1)}, bf16[64,2048]{1,0:T(8,128)(2,1)S(1)}, u32[]{:S(2)}, u32[]{:S(2)}) collective-permute-start(bf16[64,2048]{1,0:T(8,128)(2,1)S(1)} %get-tuple-element.127), channel_id=1, source_target_pairs={{4,8},{8,4},{5,9},{9,5},{6,10},{10,6},{7,11},{11,7},{20,24},{24,20... | collective-permute-start | bytes 786440 | tf_op jit(solution)/shard_map/ppermute | solution.py:363
  92.9 9.3 %collective-permute-start.32 = (bf16[64,2048]{1,0:T(8,128)(2,1)S(1)}, bf16[64,2048]{1,0:T(8,128)(2,1)S(1)}, u32[]{:S(2)}, u32[]{:S(2)}) collective-permute-start(bf16[64,2048]{1,0:T(8,128)(2,1)S(1)} %get-tuple-element.127), channel_id=1, source_target_pairs={{0,4},{12,8},{1,5},{13,9},{2,6},{14,10},{3,7},{15,11},{16,20},{28,... | collective-permute-start | bytes 786440 | tf_op jit(solution)/shard_map/ppermute | solution.py:363
  102.2 15.6 %collective-permute-start.36 = (bf16[64,2048]{1,0:T(8,128)(2,1)S(1)}, bf16[64,2048]{1,0:T(8,128)(2,1)S(1)}, u32[]{:S(2)}, u32[]{:S(2)}) collective-permute-start(bf16[64,2048]{1,0:T(8,128)(2,1)S(1)} %get-tuple-element.132), channel_id=1, source_target_pairs={{0,8},{4,12},{8,0},{12,4},{1,9},{5,13},{9,1},{13,5},{2,10},{6,14},... | collective-permute-start | bytes 786440 | tf_op jit(solution)/shard_map/ppermute | solution.py:363
  105.9 9.4 %collective-permute-start.34 = (bf16[32,2048]{1,0:T(8,128)(2,1)S(1)}, bf16[32,2048]{1,0:T(8,128)(2,1)S(1)}, u32[]{:S(2)}, u32[]{:S(2)}) collective-permute-start(bf16[32,2048]{1,0:T(8,128)(2,1)S(1)} %get-tuple-element.130), channel_id=1, source_target_pairs={{0,4},{4,0},{8,12},{12,8},{1,5},{5,1},{9,13},{13,9},{2,6},{6,2},{1... | collective-permute-start | bytes 393224 | tf_op jit(solution)/shard_map/ppermute | solution.py:363
  105.9 11.9 %collective-permute-start.35 = (bf16[32,2048]{1,0:T(8,128)(2,1)S(1)}, bf16[32,2048]{1,0:T(8,128)(2,1)S(1)}, u32[]{:S(2)}, u32[]{:S(2)}) collective-permute-start(bf16[32,2048]{1,0:T(8,128)(2,1)S(1)} %get-tuple-element.131), channel_id=1, source_target_pairs={{0,4},{4,0},{8,12},{12,8},{1,5},{5,1},{9,13},{13,9},{2,6},{6,2},{1... | collective-permute-start | bytes 393224 | tf_op jit(solution)/shard_map/ppermute | solution.py:363
  (15 other events, 31.2 us)

commit v11 on v10

--- a/solution.py
+++ b/solution.py
@@ -97,15 +97,20 @@
     )(pick, *blocks)
 
 
-def send_shapes(half, nx, width):
-    return [jax.ShapeDtypeStruct((half // nx, width), BF16)] * (2 * nx)
+def send_shapes(half, nx, width, split):
+    if split:
+        return [jax.ShapeDtypeStruct((half // nx, width), BF16)] * (2 * nx)
+    return [jax.ShapeDtypeStruct((2, half, width), BF16)]
 
 
 def put_part(i, part, columns, keep_ref, send_refs):
     half = keep_ref.shape[1]
+    keep_ref[i, :, columns] = part[:half]
+    if len(send_refs) == 1:
+        send_refs[0][i, :, columns] = part[half:].astype(BF16)
+        return
     nx = len(send_refs) // 2
     quarter = half // nx
-    keep_ref[i, :, columns] = part[:half]
     for k in range(nx):
         first = half + k * quarter
         send_refs[i * nx + k][:, columns] = part[first:first + quarter].astype(BF16)
@@ -121,14 +126,14 @@
             put_part(i, part, columns, keep_ref, send_refs)
 
 
-def gate_up_held(tok, gate_held, up_held, after, nx, tile):
+def gate_up_held(tok, gate_held, up_held, after, nx, tile, split=False):
     half, width = tok.shape[0] // 2, gate_held.shape[1]
     held, anywhere = pl.BlockSpec(memory_space=pltpu.VMEM), pl.BlockSpec(memory_space=pl.ANY)
     keep, *send = pl.pallas_call(
         functools.partial(gate_up_held_kernel, len(after), tile),
-        out_shape=[jax.ShapeDtypeStruct((2, half, width), F32)] + send_shapes(half, nx, width),
+        out_shape=[jax.ShapeDtypeStruct((2, half, width), F32)] + send_shapes(half, nx, width, split),
         in_specs=[held] * 3 + [anywhere] * len(after),
-        out_specs=[held] * (1 + 2 * nx),
+        out_specs=[held] * (1 + (2 * nx if split else 1)),
         compiler_params=pltpu.CompilerParams(vmem_limit_bytes=6 * MIB),
         cost_estimate=pl.CostEstimate(flops=0, bytes_accessed=0, transcendentals=0),
         name="gate_up_held",
@@ -150,7 +155,7 @@
     weight = pl.BlockSpec((depth, tile), lambda j: (0, start // tile + j))
     keep, *send = pl.pallas_call(
         functools.partial(gate_up_kernel, len(after)),
-        out_shape=[jax.ShapeDtypeStruct((2, half, width), F32)] + send_shapes(half, nx, width),
+        out_shape=[jax.ShapeDtypeStruct((2, half, width), F32)] + send_shapes(half, nx, width, True),
         grid=(width // tile,),
         in_specs=[pl.BlockSpec((live, depth), lambda j: (0, 0)), weight, weight]
         + [pl.BlockSpec(memory_space=pl.ANY)] * len(after),
@@ -163,30 +168,31 @@
     return send, keep
 
 
-def join_kernel(n_unread, nx, keep_ref, *refs):
-    got_refs, out_refs = refs[:2 * nx], refs[2 * nx + n_unread:][:nx]
+def join_kernel(n_got, n_unread, nx, keep_ref, *refs):
+    got_refs, out_refs = refs[:n_got], refs[n_got + n_unread:][:nx]
     quarter = out_refs[0].shape[1]
     for i in range(2):
         for k, out_ref in enumerate(out_refs):
             rows = pl.ds(k * quarter, quarter)
-            out_ref[i] = (keep_ref[i, rows] + got_refs[i * nx + k][...].astype(F32)).astype(out_ref.dtype)
-
-
-def join(keep, got, handed, nx):
+            got = got_refs[0][i, rows] if n_got == 1 else got_refs[i * nx + k][...]
+            out_ref[i] = (keep_ref[i, rows] + got.astype(F32)).astype(out_ref.dtype)
+
+
+def join(keep, got, handed, after, nx):
     two, half, width = keep.shape
     shape = (two, half // nx, width)
     held, anywhere = pl.BlockSpec(memory_space=pltpu.VMEM), pl.BlockSpec(memory_space=pl.ANY)
     out = pl.pallas_call(
-        functools.partial(join_kernel, len(handed), nx),
+        functools.partial(join_kernel, len(got), len(handed) + len(after), nx),
         out_shape=[jax.ShapeDtypeStruct(shape, BF16 if k else F32) for k in range(nx)]
         + [jax.ShapeDtypeStruct(a.shape, a.dtype) for a in handed],
-        in_specs=[held] * (1 + len(got)) + [anywhere] * len(handed),
+        in_specs=[held] * (1 + len(got)) + [anywhere] * (len(handed) + len(after)),
         out_specs=[held] * nx + [anywhere] * len(handed),
         input_output_aliases={1 + len(got) + i: nx + i for i in range(len(handed))},
         compiler_params=pltpu.CompilerParams(vmem_limit_bytes=8 * MIB),
         cost_estimate=pl.CostEstimate(flops=0, bytes_accessed=0, transcendentals=0),
         name="join",
-    )(keep, *got, *handed)
+    )(keep, *got, *handed, *after)
     return out[0], list(out[1:nx]), list(out[nx:])
 
 
@@ -377,31 +383,34 @@
     sends, keeps = [list(a) for a in zip(*made)]
     sums = []
 
-    def exchange(j, handed):
-        mine, blocks, handed = join(keeps[j], [over_core(a) for a in sends[j]], handed, nx)
+    def exchange(j, handed, after):
+        mine, blocks, handed = join(keeps[j], [over_core(a) for a in sends[j]], handed, after, nx)
         sums.append([mine] + [over_x(b, k + 1) for k, b in enumerate(blocks)])
         return blocks, handed
 
     def finish(first, last, handed, after):
         own, handed = activate(sums[first:last], handed, after)
-        h = [own] + [over_x(own, -k) for k in range(1, nx)]
-        return h + [over_core(a) for a in h], handed
-
-    ready, sends[1] = exchange(0, sends[1])
-    ready = ready + exchange(1, [])[0]
-    made = [gate_up_held(tok, *weights[2], ready, nx, tile)]
+        return [own] + [over_x(own, -k) for k in range(1, nx)], handed
+
+    def with_other_core(h):
+        return h + [over_core(a) for a in h]
+
+    ready, sends[1] = exchange(0, sends[1], [])
+    ready = ready + exchange(1, [], [])[0]
+    made = [gate_up_held(tok, *weights[2], ready, nx, tile, True)]
     made.append(gate_up(tok, gate_weight, up_weight, made[0][0][:1], *chunks[3], nx, tile))
-    pieces = len(sends[0])
+    pieces = len(made[0][0])
     hidden, handed = finish(0, 2, made[0][0] + made[1][0], [])
     sends += [handed[:pieces], handed[pieces:]]
     keeps += [keep for _, keep in made]
-    ready, sends[3] = exchange(2, sends[3])
-    ready = ready + exchange(3, [])[0]
+    ready, sends[3] = exchange(2, sends[3], [])
+    ready = ready + exchange(3, [], [])[0]
     rows_held = fetch(down_weight, chunks[2:], ready)
-    total = down(hidden, down_weight, [rows_held[0]], chunks[0][0])
+    total = down(with_other_core(hidden), down_weight, [rows_held[0]], chunks[0][0])
     hidden, _ = finish(2, 3, [], [total])
-    total = down_held(hidden, rows_held[0], total, None, None)
+    total = down_held(with_other_core(hidden), rows_held[0], total, None, None)
     hidden, _ = finish(3, 4, [], [])
+    hidden = with_other_core(hidden)
     out_rows = [tok_dev, part, part, tok_dev, tok_dev] if line else [tok_dev] * n_gx
     spread = down_held(hidden, rows_held[1], total, pick_out, out_rows)
 

time: 119 us -> 117 us (0.983)
    ppermute x22 -> x16, starting transfers between devices: 4.91 us -> 3.37 us  [over_core(): return lax.ppermute(block, 'gy', [(i, i ^ 1) for i in range(n_gy)])]
  transfers between devices with their start and end apart: 37 -> 31, of which waited for: 9 -> 10; matrix products, arithmetic and copies ran while one was open for 0% -> 0% of each run, Pallas kernels for 34% -> 35%
where the time goes in v11:
time: 117 us
  Pallas kernels  46.4 us (40%)
  waiting for transfers between devices  39.8 us (34%)
  starting transfers between devices  28.2 us (24%)
  local copies, waits for them, and re-layouts  1.64 us (1%)
    ppermute x8, waiting for transfers between devices, over_z(): return lax.ppermute(block, 'gx', [(z, z ^ k) for z in among])  23.6 us
    ppermute x8, starting transfers between devices, over_z(): return lax.ppermute(block, 'gx', [(z, z ^ k) for z in among])  15.4 us
    ppermute x7, waiting for transfers between devices, over_x(): lax.ppermute(block, 'gy', [(i, (i + 2 * k) % n_gy) for i in range(n_gy)])  15.2 us
    pallas_call x1, Pallas kernels, prepare(): pl.pallas_call(functools.partial(prepare_kernel, n_gx, nx, chunks), out_s...  13.6 us
    ppermute x7, starting transfers between devices, over_x(): lax.ppermute(block, 'gy', [(i, (i + 2 * k) % n_gy) for i in range(n_gy)])  9.46 us
    pallas_call x3, Pallas kernels, gate_up_held(): pl.pallas_call(functools.partial(gate_up_held_kernel, len(after), tile),...  8.7 us
    pallas_call x1, Pallas kernels, gate_up(): pl.pallas_call(functools.partial(gate_up_kernel, len(after)), out_shape=[...  6.84 us
    pallas_call x1, Pallas kernels, down(): pl.pallas_call(functools.partial(down_kernel, len(hidden)), out_shape=jax...  6.64 us
  transfers between devices with their start and end apart: 31, of which 10 were waited for; matrix products, arithmetic and copies ran while one was open for 0% of the time, Pallas kernels for 35%

profile of v11, /device:TPU:0, one launch (start us, length us, event | category | flops | bytes accessed | tf_op | source)
XLA Modules:
  0.0 117.2 jit_solution(9817808437843001502)
XLA Ops:
  0.0 3.0 %collective-permute-start = (bf16[64,2048]{1,0:T(8,128)(2,1)}, bf16[64,2048]{1,0:T(8,128)(2,1)S(1)}, u32[]{:S(2)}, u32[]{:S(2)}) collective-permute-start(bf16[64,2048]{1,0:T(8,128)(2,1)} %tok_ref.1), channel_id=1, source_target_pairs={{0,4},{4,0},{8,12},{12,8},{1,5},{5,1},{9,13},{13,9},{2,6},{6,2},{1... | collective-permute-start | bytes 786440 | tf_op jit(solution)/shard_map/ppermute | solution.py:369
  3.0 2.5 %collective-permute-start.2 = (bf16[64,2048]{1,0:T(8,128)(2,1)}, bf16[64,2048]{1,0:T(8,128)(2,1)S(1)}, u32[]{:S(2)}, u32[]{:S(2)}) collective-permute-start(bf16[64,2048]{1,0:T(8,128)(2,1)} %tok_ref.1), channel_id=1, source_target_pairs={{0,12},{4,8},{8,4},{12,0},{1,13},{5,9},{9,5},{13,1},{2,14},{6,10},... | collective-permute-start | bytes 786440 | tf_op jit(solution)/shard_map/ppermute | solution.py:369
  7.3 13.6 %prepare.1 = (bf16[192,256]{1,0:T(8,128)(2,1)S(1)}, bf16[256,192]{1,0:T(8,128)(2,1)S(1)}, bf16[64,2048]{1,0:T(8,128)(2,1)S(1)}, bf16[2048,1536]{1,0:T(8,128)(2,1...) custom-call(s32[4]{0:T(128)S(1)} %copy-done.1, ...), custom_call_target="tpu_custom_call" | custom-call | tf_op jit(solution)/shard_map/prepare/pallas_call | solution.py:67
  20.9 7.8 %collective-permute-done.1.refs_2_ = bf16[64,2048]{1,0:T(8,128)(2,1)S(1)} collective-permute-done((bf16[64,2048]{1,0:T(8,128)(2,1)}, bf16[64,2048]{1,0:T(8,128)(2,1)S(1)}, u32[]{:S(2)}, u32[]{:S(2)}) %collective-permute-start.1) | collective-permute-done | bytes 262176 | tf_op jit(solution)/shard_map/ppermute | solution.py:369
  29.1 2.6 %gate_up_held.3 = (f32[2,96,1536]{2,1,0:T(8,128)S(1)}, bf16[2,96,1536]{2,1,0:T(8,128)(2,1)S(1)}) custom-call(bf16[192,2048]{1,0:T(8,128)(2,1)S(1)} %compact.1.tok_ref, bf16[2048,1536]{1,0:T(8,128)(2,1)S(1)} %get-tuple-element.64.gate_ref, bf16[2048,1536]{1,0:T(8,128)(2,1)S(1)} %get-tuple-element.65.up_ref), custom_call_target="tpu_custom_call" | custom-call | tf_op jit(solution)/shard_map/gate_up_held/pallas_call | solution.py:132
  31.8 2.6 %gate_up_held.4 = (f32[2,96,1536]{2,1,0:T(8,128)S(1)}, bf16[2,96,1536]{2,1,0:T(8,128)(2,1)S(1)}) custom-call(bf16[192,2048]{1,0:T(8,128)(2,1)S(1)} %compact.1.tok_ref, bf16[2048,1536]{1,0:T(8,128)(2,1)S(1)} %get-tuple-element.68.gate_ref, bf16[2048,1536]{1,0:T(8,128)(2,1)S(1)} %get-tuple-element.69.up_ref), custom_call_target="tpu_custom_call" | custom-call | tf_op jit(solution)/shard_map/gate_up_held/pallas_call | solution.py:132
  36.8 1.6 %collective-permute-start.6 = (bf16[2,48,1536]{2,1,0:T(8,128)(2,1)S(1)}, bf16[2,48,1536]{2,1,0:T(8,128)(2,1)S(1)}, u32[]{:S(2)}, u32[]{:S(2)}) collective-permute-start(bf16[2,48,1536]{2,1,0:T(8,128)(2,1)S(1)} %get-tuple-element.74.refs_1_), channel_id=1, source_target_pairs={{0,2},{1,3},{2,0},{3,1},{4,6},{5,7},{6,4},{7,5},{8,10},{9,11},{10,... | collective-permute-start | bytes 884744 | tf_op jit(solution)/shard_map/ppermute | solution.py:375
  38.4 3.5 %gate_up_held.5 = (f32[2,96,2048]{2,1,0:T(8,128)S(1)}, bf16[48,2048]{1,0:T(8,128)(2,1)S(1)}, bf16[48,2048]{1,0:T(8,128)(2,1)S(1)}, bf16[48,2048]{1,0:T(8,128)(2,1)S(1)}, bf16[48,2048]{1,0:T(8,128)(2,1)S(1)}) custom-call(bf16[192,2048]{1,0:T(8,128)(2,1)S(1)} %compact.1.tok_ref, bf16[2048,2048]{1,0:T(8,128)(2,1)S(1)} %get-tuple-element.62.gate_ref, ...), custom_call_target="tpu_custom_call" | custom-call | tf_op jit(solution)/shard_map/gate_up_held/pallas_call | solution.py:132
  41.9 6.8 %gate_up.1 = (f32[2,96,1536]{2,1,0:T(8,128)S(1)}, bf16[48,1536]{1,0:T(8,128)(2,1)S(1)}, bf16[48,1536]{1,0:T(8,128)(2,1)S(1)}, bf16[48,1536]{1,0:T(8,128)(2,1)S(1)}, bf16[48,1536]{1,0:T(8,128)(2,1)S(1)}) custom-call(bf16[192,2048]{1,0:T(8,128)(2,1)S(1)} %compact.1.tok_ref, bf16[2048,6656]{1,0:T(8,128)(2,1)} %gate_ref.3, bf16[2048,6656]{1,0:T(8,128)(2,1)} %up_ref.3, ...), custom_call_target="tpu_custom_call" | custom-call | tf_op jit(solution)/shard_map/gate_up/pallas_call | solution.py:156
  48.7 1.7 %collective-permute-done.6.refs_3_ = bf16[2,48,1536]{2,1,0:T(8,128)(2,1)S(1)} collective-permute-done((bf16[2,48,1536]{2,1,0:T(8,128)(2,1)S(1)}, bf16[2,48,1536]{2,1,0:T(8,128)(2,1)S(1)}, u32[]{:S(2)}, u32[]{:S(2)}) %collective-permute-start.6) | collective-permute-done | bytes 294944 | tf_op jit(solution)/shard_map/ppermute | solution.py:375
  55.2 6.4 %collective-permute-done.20.refs_1_ = bf16[48,3072]{1,0:T(8,128)(2,1)S(1)} collective-permute-done((bf16[48,3072]{1,0:T(8,128)(2,1)S(1)}, bf16[48,3072]{1,0:T(8,128)(2,1)S(1)}, u32[]{:S(2)}, u32[]{:S(2)}) %collective-permute-start.20) | collective-permute-done | bytes 294944 | tf_op jit(solution)/shard_map/ppermute | solution.py:375
  63.1 1.5 %collective-permute-start.15 = (bf16[2,48,1536]{2,1,0:T(8,128)(2,1)S(1)}, bf16[2,48,1536]{2,1,0:T(8,128)(2,1)S(1)}, u32[]{:S(2)}, u32[]{:S(2)}) collective-permute-start(bf16[2,48,1536]{2,1,0:T(8,128)(2,1)S(1)} %get-tuple-element.100.refs_1_), channel_id=1, source_target_pairs={{0,2},{1,3},{2,0},{3,1},{4,6},{5,7},{6,4},{7,5},{8,10},{9,11},{10,... | collective-permute-start | bytes 884744 | tf_op jit(solution)/shard_map/ppermute | solution.py:375
  64.6 5.2 %fetch.1 = (bf16[2048,2048]{1,0:T(8,128)(2,1)S(1)}, bf16[1536,2048]{1,0:T(8,128)(2,1)S(1)}) custom-call(bf16[6656,2048]{1,0:T(8,128)(2,1)} %refs_4_.1, bf16[2,48,2048]{2,1,0:T(8,128)(2,1)S(1)} %get-tuple-element.101.refs_0_, bf16[2,48,1536]{2,1,0:T(8,128)(2,1)S(1)} %get-tuple-element.100.refs_1_), custom_call_target="tpu_custom_call" | custom-call | tf_op jit(solution)/shard_map/fetch/pallas_call | solution.py:302
  69.8 6.6 %down.1.refs_2_.refs_5_ = f32[192,2048]{1,0:T(8,128)S(1)} custom-call(bf16[48,3072]{1,0:T(8,128)(2,1)S(1)} %get-tuple-element.104.refs_0_, bf16[48,3072]{1,0:T(8,128)(2,1)S(1)} %collective-permute-done.20.refs_1_, bf16[48,3072]{1,0:T(8,128)(2,1)S(1)} %collective-permute-done.21.refs_2_, bf16[48,3072]{1,0:T(8,128)(2,1)S(1)} %collective-permute-done.22.refs_3_, ...), custom_call_target="tpu_custom_call" | custom-call | tf_op jit(solution)/shard_map/down/pallas_call | solution.py:273
  77.4 1.5 %collective-permute-start.16 = (bf16[48,1536]{1,0:T(8,128)(2,1)S(1)}, bf16[48,1536]{1,0:T(8,128)(2,1)S(1)}, u32[]{:S(2)}, u32[]{:S(2)}) collective-permute-start(bf16[48,1536]{1,0:T(8,128)(2,1)S(1)} %activate.4.refs_0_), channel_id=1, source_target_pairs={{0,2},{1,3},{2,0},{3,1},{4,6},{5,7},{6,4},{7,5},{8,10},{9,11},{10,... | collective-permute-start | bytes 442376 | tf_op jit(solution)/shard_map/ppermute | solution.py:375
  79.0 5.6 %collective-permute-done.23.refs_1_ = bf16[48,2048]{1,0:T(8,128)(2,1)S(1)} collective-permute-done((bf16[48,2048]{1,0:T(8,128)(2,1)S(1)}, bf16[48,2048]{1,0:T(8,128)(2,1)S(1)}, u32[]{:S(2)}, u32[]{:S(2)}) %collective-permute-start.23) | collective-permute-done | bytes 196640 | tf_op jit(solution)/shard_map/ppermute | solution.py:375
  86.6 1.8 %down_held.2.refs_5_ = f32[192,2048]{1,0:T(8,128)S(1)} custom-call(bf16[48,2048]{1,0:T(8,128)(2,1)S(1)} %activate.5.refs_0_, bf16[48,2048]{1,0:T(8,128)(2,1)S(1)} %collective-permute-done.23.refs_1_, bf16[48,2048]{1,0:T(8,128)(2,1)S(1)} %collective-permute-done.24.refs_2_, bf16[48,2048]{1,0:T(8,128)(2,1)S(1)} %collective-permute-done.25.refs_3_, ...), custom_call_target="tpu_custom_call" | custom-call | tf_op jit(solution)/shard_map/down_held/pallas_call | solution.py:339
  88.4 2.2 %down_held.3 = (bf16[64,2048]{1,0:T(8,128)(2,1)S(1)}, bf16[32,2048]{1,0:T(8,128)(2,1)S(1)}, bf16[32,2048]{1,0:T(8,128)(2,1)S(1)}, bf16[64,2048]{1,0:T(8,128)(2,1)S(1)}, bf16[64,2048]{1,0:T(8,128)(2,1)S(1)}) custom-call(bf16[48,1536]{1,0:T(8,128)(2,1)S(1)} %activate.4.refs_0_, bf16[48,1536]{1,0:T(8,128)(2,1)S(1)} %collective-permute-done.16.refs_1_, ...), custom_call_target="tpu_custom_call" | custom-call | tf_op jit(solution)/shard_map/down_held/pallas_call | solution.py:339
  91.3 3.4 %collective-permute-start.26 = (bf16[64,2048]{1,0:T(8,128)(2,1)S(1)}, bf16[64,2048]{1,0:T(8,128)(2,1)S(1)}, u32[]{:S(2)}, u32[]{:S(2)}) collective-permute-start(bf16[64,2048]{1,0:T(8,128)(2,1)S(1)} %get-tuple-element.109), channel_id=1, source_target_pairs={{0,4},{12,8},{1,5},{13,9},{2,6},{14,10},{3,7},{15,11},{16,20},{28,... | collective-permute-start | bytes 786440 | tf_op jit(solution)/shard_map/ppermute | solution.py:369
  94.7 5.9 %collective-permute-done.26.got_ref = bf16[64,2048]{1,0:T(8,128)(2,1)S(1)} collective-permute-done((bf16[64,2048]{1,0:T(8,128)(2,1)S(1)}, bf16[64,2048]{1,0:T(8,128)(2,1)S(1)}, u32[]{:S(2)}, u32[]{:S(2)}) %collective-permute-start.26) | collective-permute-done | bytes 262176 | tf_op jit(solution)/shard_map/ppermute | solution.py:369
  100.7 3.7 %collective-permute-start.30 = (bf16[64,2048]{1,0:T(8,128)(2,1)S(1)}, bf16[64,2048]{1,0:T(8,128)(2,1)S(1)}, u32[]{:S(2)}, u32[]{:S(2)}) collective-permute-start(bf16[64,2048]{1,0:T(8,128)(2,1)S(1)} %get-tuple-element.114), channel_id=1, source_target_pairs={{0,8},{4,12},{8,0},{12,4},{1,9},{5,13},{9,1},{13,5},{2,10},{6,14},... | collective-permute-start | bytes 786440 | tf_op jit(solution)/shard_map/ppermute | solution.py:369
  104.4 2.0 %collective-permute-start.29 = (bf16[32,2048]{1,0:T(8,128)(2,1)S(1)}, bf16[32,2048]{1,0:T(8,128)(2,1)S(1)}, u32[]{:S(2)}, u32[]{:S(2)}) collective-permute-start(bf16[32,2048]{1,0:T(8,128)(2,1)S(1)} %get-tuple-element.113), channel_id=1, source_target_pairs={{0,4},{4,0},{8,12},{12,8},{1,5},{5,1},{9,13},{13,9},{2,6},{6,2},{1... | collective-permute-start | bytes 393224 | tf_op jit(solution)/shard_map/ppermute | solution.py:369
  106.4 7.4 %collective-permute-done.28 = bf16[32,2048]{1,0:T(8,128)(2,1)S(1)} collective-permute-done((bf16[32,2048]{1,0:T(8,128)(2,1)S(1)}, bf16[32,2048]{1,0:T(8,128)(2,1)S(1)}, u32[]{:S(2)}, u32[]{:S(2)}) %collective-permute-start.28) | collective-permute-done | bytes 131104 | tf_op jit(solution)/shard_map/ppermute | solution.py:369
  113.8 2.5 %collective-permute-done.29 = bf16[32,2048]{1,0:T(8,128)(2,1)S(1)} collective-permute-done((bf16[32,2048]{1,0:T(8,128)(2,1)S(1)}, bf16[32,2048]{1,0:T(8,128)(2,1)S(1)}, u32[]{:S(2)}, u32[]{:S(2)}) %collective-permute-start.29) | collective-permute-done | bytes 131104 | tf_op jit(solution)/shard_map/ppermute | solution.py:369
  (61 shorter events, 15.3 us)
Async XLA Ops:
  0.0 20.9 %collective-permute-start = (bf16[64,2048]{1,0:T(8,128)(2,1)}, bf16[64,2048]{1,0:T(8,128)(2,1)S(1)}, u32[]{:S(2)}, u32[]{:S(2)}) collective-permute-start(bf16[64,2048]{1,0:T(8,128)(2,1)} %tok_ref.1), channel_id=1, source_target_pairs={{0,4},{4,0},{8,12},{12,8},{1,5},{5,1},{9,13},{13,9},{2,6},{6,2},{1... | collective-permute-start | bytes 786440 | tf_op jit(solution)/shard_map/ppermute | solution.py:369
  3.0 17.9 %collective-permute-start.2 = (bf16[64,2048]{1,0:T(8,128)(2,1)}, bf16[64,2048]{1,0:T(8,128)(2,1)S(1)}, u32[]{:S(2)}, u32[]{:S(2)}) collective-permute-start(bf16[64,2048]{1,0:T(8,128)(2,1)} %tok_ref.1), channel_id=1, source_target_pairs={{0,12},{4,8},{8,4},{12,0},{1,13},{5,9},{9,5},{13,1},{2,14},{6,10},... | collective-permute-start | bytes 786440 | tf_op jit(solution)/shard_map/ppermute | solution.py:369
  5.5 23.2 %collective-permute-start.1 = (bf16[64,2048]{1,0:T(8,128)(2,1)}, bf16[64,2048]{1,0:T(8,128)(2,1)S(1)}, u32[]{:S(2)}, u32[]{:S(2)}) collective-permute-start(bf16[64,2048]{1,0:T(8,128)(2,1)} %tok_ref.1), channel_id=1, source_target_pairs={{0,8},{4,12},{8,0},{12,4},{1,9},{5,13},{9,1},{13,5},{2,10},{6,14},... | collective-permute-start | bytes 786440 | tf_op jit(solution)/shard_map/ppermute | solution.py:369
  31.7 2.7 %collective-permute-start.3 = (bf16[2,96,1536]{2,1,0:T(8,128)(2,1)S(1)}, bf16[2,96,1536]{2,1,0:T(8,128)(2,1)S(1)}, u32[]{:S(2)}, u32[]{:S(2)}) collective-permute-start(bf16[2,96,1536]{2,1,0:T(8,128)(2,1)S(1)} %get-tuple-element.67), channel_id=1, source_target_pairs={{0,1},{1,0},{2,3},{3,2},{4,5},{5,4},{6,7},{7,6},{8,9},{9,8},{10,11... | collective-permute-start | bytes 1769480 | tf_op jit(solution)/shard_map/ppermute | solution.py:372
  35.1 13.6 %collective-permute-start.5 = (bf16[2,48,1536]{2,1,0:T(8,128)(2,1)S(1)}, bf16[2,48,1536]{2,1,0:T(8,128)(2,1)S(1)}, u32[]{:S(2)}, u32[]{:S(2)}) collective-permute-start(bf16[2,48,1536]{2,1,0:T(8,128)(2,1)S(1)} %get-tuple-element.71.refs_0_), channel_id=1, source_target_pairs={{0,2},{1,3},{2,0},{3,1},{4,6},{5,7},{6,4},{7,5},{8,10},{9,11},{10,... | collective-permute-start | bytes 884744 | tf_op jit(solution)/shard_map/ppermute | solution.py:375
  36.8 13.6 %collective-permute-start.6 = (bf16[2,48,1536]{2,1,0:T(8,128)(2,1)S(1)}, bf16[2,48,1536]{2,1,0:T(8,128)(2,1)S(1)}, u32[]{:S(2)}, u32[]{:S(2)}) collective-permute-start(bf16[2,48,1536]{2,1,0:T(8,128)(2,1)S(1)} %get-tuple-element.74.refs_1_), channel_id=1, source_target_pairs={{0,2},{1,3},{2,0},{3,1},{4,6},{5,7},{6,4},{7,5},{8,10},{9,11},{10,... | collective-permute-start | bytes 884744 | tf_op jit(solution)/shard_map/ppermute | solution.py:375
  50.6 2.6 %collective-permute-start.7 = (bf16[48,2048]{1,0:T(8,128)(2,1)S(1)}, bf16[48,2048]{1,0:T(8,128)(2,1)S(1)}, u32[]{:S(2)}, u32[]{:S(2)}) collective-permute-start(bf16[48,2048]{1,0:T(8,128)(2,1)S(1)} %get-tuple-element.87), channel_id=1, source_target_pairs={{0,1},{1,0},{2,3},{3,2},{4,5},{5,4},{6,7},{7,6},{8,9},{9,8},{10,11... | collective-permute-start | bytes 589832 | tf_op jit(solution)/shard_map/ppermute | solution.py:372
  51.7 9.9 %collective-permute-start.20 = (bf16[48,3072]{1,0:T(8,128)(2,1)S(1)}, bf16[48,3072]{1,0:T(8,128)(2,1)S(1)}, u32[]{:S(2)}, u32[]{:S(2)}) collective-permute-start(bf16[48,3072]{1,0:T(8,128)(2,1)S(1)} %get-tuple-element.104.refs_0_), channel_id=1, source_target_pairs={{0,2},{1,3},{2,0},{3,1},{4,6},{5,7},{6,4},{7,5},{8,10},{9,11},{10,... | collective-permute-start | bytes 884744 | tf_op jit(solution)/shard_map/ppermute | solution.py:375
  53.4 8.2 %collective-permute-start.11 = (bf16[48,1536]{1,0:T(8,128)(2,1)S(1)}, bf16[48,1536]{1,0:T(8,128)(2,1)S(1)}, u32[]{:S(2)}, u32[]{:S(2)}) collective-permute-start(bf16[48,1536]{1,0:T(8,128)(2,1)S(1)} %get-tuple-element.95), channel_id=1, source_target_pairs={{0,1},{1,0},{2,3},{3,2},{4,5},{5,4},{6,7},{7,6},{8,9},{9,8},{10,11... | collective-permute-start | bytes 442376 | tf_op jit(solution)/shard_map/ppermute | solution.py:372
  53.5 8.7 %collective-permute-start.12 = (bf16[48,1536]{1,0:T(8,128)(2,1)S(1)}, bf16[48,1536]{1,0:T(8,128)(2,1)S(1)}, u32[]{:S(2)}, u32[]{:S(2)}) collective-permute-start(bf16[48,1536]{1,0:T(8,128)(2,1)S(1)} %get-tuple-element.96), channel_id=1, source_target_pairs={{0,1},{1,0},{2,3},{3,2},{4,5},{5,4},{6,7},{7,6},{8,9},{9,8},{10,11... | collective-permute-start | bytes 442376 | tf_op jit(solution)/shard_map/ppermute | solution.py:372
  54.0 22.5 %collective-permute-start.19 = (bf16[2,48,2048]{2,1,0:T(8,128)(2,1)S(1)}, bf16[2,48,2048]{2,1,0:T(8,128)(2,1)S(1)}, u32[]{:S(2)}, u32[]{:S(2)}) collective-permute-start(bf16[2,48,2048]{2,1,0:T(8,128)(2,1)S(1)} %get-tuple-element.101.refs_0_), channel_id=1, source_target_pairs={{0,2},{1,3},{2,0},{3,1},{4,6},{5,7},{6,4},{7,5},{8,10},{9,11},{10,... | collective-permute-start | bytes 1179656 | tf_op jit(solution)/shard_map/ppermute | solution.py:375
  55.2 7.0 %collective-permute-start.13 = (bf16[48,1536]{1,0:T(8,128)(2,1)S(1)}, bf16[48,1536]{1,0:T(8,128)(2,1)S(1)}, u32[]{:S(2)}, u32[]{:S(2)}) collective-permute-start(bf16[48,1536]{1,0:T(8,128)(2,1)S(1)} %get-tuple-element.97), channel_id=1, source_target_pairs={{0,1},{1,0},{2,3},{3,2},{4,5},{5,4},{6,7},{7,6},{8,9},{9,8},{10,11... | collective-permute-start | bytes 442376 | tf_op jit(solution)/shard_map/ppermute | solution.py:372
  61.6 8.2 %collective-permute-start.21 = (bf16[48,3072]{1,0:T(8,128)(2,1)S(1)}, bf16[48,3072]{1,0:T(8,128)(2,1)S(1)}, u32[]{:S(2)}, u32[]{:S(2)}) collective-permute-start(bf16[48,3072]{1,0:T(8,128)(2,1)S(1)} %get-tuple-element.104.refs_0_), channel_id=1, source_target_pairs={{0,1},{1,0},{2,3},{3,2},{4,5},{5,4},{6,7},{7,6},{8,9},{9,8},{10,11... | collective-permute-start | bytes 884744 | tf_op jit(solution)/shard_map/ppermute | solution.py:372
  62.1 7.7 %collective-permute-start.22 = (bf16[48,3072]{1,0:T(8,128)(2,1)S(1)}, bf16[48,3072]{1,0:T(8,128)(2,1)S(1)}, u32[]{:S(2)}, u32[]{:S(2)}) collective-permute-start(bf16[48,3072]{1,0:T(8,128)(2,1)S(1)} %collective-permute-done.20.refs_1_), channel_id=1, source_target_pairs={{0,1},{1,0},{2,3},{3,2},{4,5},{5,4},{6,7},{7,6},{8,9},{9,8},{10,11... | collective-permute-start | bytes 884744 | tf_op jit(solution)/shard_map/ppermute | solution.py:372
  63.1 14.2 %collective-permute-start.15 = (bf16[2,48,1536]{2,1,0:T(8,128)(2,1)S(1)}, bf16[2,48,1536]{2,1,0:T(8,128)(2,1)S(1)}, u32[]{:S(2)}, u32[]{:S(2)}) collective-permute-start(bf16[2,48,1536]{2,1,0:T(8,128)(2,1)S(1)} %get-tuple-element.100.refs_1_), channel_id=1, source_target_pairs={{0,2},{1,3},{2,0},{3,1},{4,6},{5,7},{6,4},{7,5},{8,10},{9,11},{10,... | collective-permute-start | bytes 884744 | tf_op jit(solution)/shard_map/ppermute | solution.py:375
  76.7 7.8 %collective-permute-start.23 = (bf16[48,2048]{1,0:T(8,128)(2,1)S(1)}, bf16[48,2048]{1,0:T(8,128)(2,1)S(1)}, u32[]{:S(2)}, u32[]{:S(2)}) collective-permute-start(bf16[48,2048]{1,0:T(8,128)(2,1)S(1)} %activate.5.refs_0_), channel_id=1, source_target_pairs={{0,2},{1,3},{2,0},{3,1},{4,6},{5,7},{6,4},{7,5},{8,10},{9,11},{10,... | collective-permute-start | bytes 589832 | tf_op jit(solution)/shard_map/ppermute | solution.py:375
  77.4 9.2 %collective-permute-start.16 = (bf16[48,1536]{1,0:T(8,128)(2,1)S(1)}, bf16[48,1536]{1,0:T(8,128)(2,1)S(1)}, u32[]{:S(2)}, u32[]{:S(2)}) collective-permute-start(bf16[48,1536]{1,0:T(8,128)(2,1)S(1)} %activate.4.refs_0_), channel_id=1, source_target_pairs={{0,2},{1,3},{2,0},{3,1},{4,6},{5,7},{6,4},{7,5},{8,10},{9,11},{10,... | collective-permute-start | bytes 442376 | tf_op jit(solution)/shard_map/ppermute | solution.py:375
  78.9 7.6 %collective-permute-start.24 = (bf16[48,2048]{1,0:T(8,128)(2,1)S(1)}, bf16[48,2048]{1,0:T(8,128)(2,1)S(1)}, u32[]{:S(2)}, u32[]{:S(2)}) collective-permute-start(bf16[48,2048]{1,0:T(8,128)(2,1)S(1)} %activate.5.refs_0_), channel_id=1, source_target_pairs={{0,1},{1,0},{2,3},{3,2},{4,5},{5,4},{6,7},{7,6},{8,9},{9,8},{10,11... | collective-permute-start | bytes 589832 | tf_op jit(solution)/shard_map/ppermute | solution.py:372
  84.5 3.9 %collective-permute-start.17 = (bf16[48,1536]{1,0:T(8,128)(2,1)S(1)}, bf16[48,1536]{1,0:T(8,128)(2,1)S(1)}, u32[]{:S(2)}, u32[]{:S(2)}) collective-permute-start(bf16[48,1536]{1,0:T(8,128)(2,1)S(1)} %activate.4.refs_0_), channel_id=1, source_target_pairs={{0,1},{1,0},{2,3},{3,2},{4,5},{5,4},{6,7},{7,6},{8,9},{9,8},{10,11... | collective-permute-start | bytes 442376 | tf_op jit(solution)/shard_map/ppermute | solution.py:372
  90.6 4.1 %collective-permute-start.27 = (bf16[64,2048]{1,0:T(8,128)(2,1)S(1)}, bf16[64,2048]{1,0:T(8,128)(2,1)S(1)}, u32[]{:S(2)}, u32[]{:S(2)}) collective-permute-start(bf16[64,2048]{1,0:T(8,128)(2,1)S(1)} %get-tuple-element.109), channel_id=1, source_target_pairs={{4,8},{8,4},{5,9},{9,5},{6,10},{10,6},{7,11},{11,7},{20,24},{24,20... | collective-permute-start | bytes 786440 | tf_op jit(solution)/shard_map/ppermute | solution.py:369
  91.3 9.3 %collective-permute-start.26 = (bf16[64,2048]{1,0:T(8,128)(2,1)S(1)}, bf16[64,2048]{1,0:T(8,128)(2,1)S(1)}, u32[]{:S(2)}, u32[]{:S(2)}) collective-permute-start(bf16[64,2048]{1,0:T(8,128)(2,1)S(1)} %get-tuple-element.109), channel_id=1, source_target_pairs={{0,4},{12,8},{1,5},{13,9},{2,6},{14,10},{3,7},{15,11},{16,20},{28,... | collective-permute-start | bytes 786440 | tf_op jit(solution)/shard_map/ppermute | solution.py:369
  100.7 15.6 %collective-permute-start.30 = (bf16[64,2048]{1,0:T(8,128)(2,1)S(1)}, bf16[64,2048]{1,0:T(8,128)(2,1)S(1)}, u32[]{:S(2)}, u32[]{:S(2)}) collective-permute-start(bf16[64,2048]{1,0:T(8,128)(2,1)S(1)} %get-tuple-element.114), channel_id=1, source_target_pairs={{0,8},{4,12},{8,0},{12,4},{1,9},{5,13},{9,1},{13,5},{2,10},{6,14},... | collective-permute-start | bytes 786440 | tf_op jit(solution)/shard_map/ppermute | solution.py:369
  104.4 9.4 %collective-permute-start.28 = (bf16[32,2048]{1,0:T(8,128)(2,1)S(1)}, bf16[32,2048]{1,0:T(8,128)(2,1)S(1)}, u32[]{:S(2)}, u32[]{:S(2)}) collective-permute-start(bf16[32,2048]{1,0:T(8,128)(2,1)S(1)} %get-tuple-element.112), channel_id=1, source_target_pairs={{0,4},{4,0},{8,12},{12,8},{1,5},{5,1},{9,13},{13,9},{2,6},{6,2},{1... | collective-permute-start | bytes 393224 | tf_op jit(solution)/shard_map/ppermute | solution.py:369
  104.4 11.9 %collective-permute-start.29 = (bf16[32,2048]{1,0:T(8,128)(2,1)S(1)}, bf16[32,2048]{1,0:T(8,128)(2,1)S(1)}, u32[]{:S(2)}, u32[]{:S(2)}) collective-permute-start(bf16[32,2048]{1,0:T(8,128)(2,1)S(1)} %get-tuple-element.113), channel_id=1, source_target_pairs={{0,4},{4,0},{8,12},{12,8},{1,5},{5,1},{9,13},{13,9},{2,6},{6,2},{1... | collective-permute-start | bytes 393224 | tf_op jit(solution)/shard_map/ppermute | solution.py:369
  (9 other events, 15.5 us)

commit v12 on v11

--- a/solution.py
+++ b/solution.py
@@ -227,23 +227,23 @@
     return out[0], out[1:]
 
 
-def relay_kernel(own_ref, got_ref, *refs):
-    out_ref = refs[len(refs) // 2]
+def relay_kernel(n_unread, own_ref, got_ref, *refs):
+    out_ref = refs[n_unread]
     out_ref[...] = (own_ref[...].astype(F32) + got_ref[...].astype(F32)).astype(BF16)
 
 
 def relay(own, got, handed, after):
     held, anywhere = pl.BlockSpec(memory_space=pltpu.VMEM), pl.BlockSpec(memory_space=pl.ANY)
     out = pl.pallas_call(
-        relay_kernel,
+        functools.partial(relay_kernel, len(handed) + len(after)),
         out_shape=[jax.ShapeDtypeStruct(a.shape, a.dtype) for a in (own, *handed)],
-        in_specs=[held, held] + [anywhere] * (1 + len(handed)),
+        in_specs=[held, held] + [anywhere] * (len(handed) + len(after)),
         out_specs=[held] + [anywhere] * len(handed),
         input_output_aliases={2 + i: 1 + i for i in range(len(handed))},
         compiler_params=pltpu.CompilerParams(vmem_limit_bytes=8 * MIB),
         cost_estimate=pl.CostEstimate(flops=0, bytes_accessed=0, transcendentals=0),
         name="relay",
-    )(own, got, *handed, after)
+    )(own, got, *handed, *after)
     return out[0], out[1:]
 
 
@@ -311,7 +311,7 @@
     )(down_weight, *after)
 
 
-def down_held_kernel(n_h, last, tile, *refs):
+def down_held_kernel(n_h, last, out_rows, tile, *refs):
     h_refs, w_ref, total_ref, outs, hidden = refs[:n_h], refs[n_h], refs[n_h + 1], refs[n_h + 2:-1], refs[-1]
     put_rows(h_refs, hidden)
     for j in range(0, total_ref.shape[1], tile):
@@ -321,11 +321,8 @@
             continue
         pick_ref = outs[0]
         spread = jnp.dot(pick_ref[...], total.astype(BF16), preferred_element_type=F32).astype(BF16)
-        row = 0
-        for out_ref in outs[1:]:
-            n = out_ref.shape[0]
-            out_ref[:, j:j + tile] = spread[row:row + n]
-            row += n
+        for row, out_ref in zip(out_rows, outs[1:]):
+            out_ref[:, j:j + tile] = spread[row:row + out_ref.shape[0]]
 
 
 def down_held(hidden, weight_held, total, pick, out_rows):
@@ -333,11 +330,11 @@
     held = pl.BlockSpec(memory_space=pltpu.VMEM)
     last = pick is not None
     if last:
-        out_shape = [jax.ShapeDtypeStruct((n, out_width), BF16) for n in out_rows]
+        out_shape = [jax.ShapeDtypeStruct((n, out_width), BF16) for _, n in out_rows]
     else:
         out_shape = jax.ShapeDtypeStruct((live, out_width), F32)
     return pl.pallas_call(
-        functools.partial(down_held_kernel, len(hidden), last, min(out_width, 512)),
+        functools.partial(down_held_kernel, len(hidden), last, [row for row, _ in out_rows or []], min(out_width, 512)),
         out_shape=out_shape,
         in_specs=[held] * (len(hidden) + (3 if last else 2)),
         out_specs=[held] * len(out_rows) if last else held,
@@ -403,25 +400,29 @@
     hidden, handed = finish(0, 2, made[0][0] + made[1][0], [])
     sends += [handed[:pieces], handed[pieces:]]
     keeps += [keep for _, keep in made]
-    ready, sends[3] = exchange(2, sends[3], [])
-    ready = ready + exchange(3, [], [])[0]
-    rows_held = fetch(down_weight, chunks[2:], ready)
-    total = down(with_other_core(hidden), down_weight, [rows_held[0]], chunks[0][0])
+    rows_held = fetch(down_weight, chunks[2:], hidden[:1])
+    _, sends[3] = exchange(2, sends[3], [rows_held[0]])
+    ready, _ = exchange(3, [], [])
+    total = down(with_other_core(hidden), down_weight, ready, chunks[0][0])
     hidden, _ = finish(2, 3, [], [total])
     total = down_held(with_other_core(hidden), rows_held[0], total, None, None)
     hidden, _ = finish(3, 4, [], [])
     hidden = with_other_core(hidden)
-    out_rows = [tok_dev, part, part, tok_dev, tok_dev] if line else [tok_dev] * n_gx
+    out_rows = [(k * tok_dev, tok_dev) for k in range(n_gx)]
+    if line:
+        halves = [(row, part) for row in range(tok_dev, n_gx * tok_dev, part)]
+        out_rows = out_rows[:1] + out_rows[3:] + halves
     spread = down_held(hidden, rows_held[1], total, pick_out, out_rows)
 
     if line:
-        own, low, high, two, three = spread
-        ends = over_z(three, 1, (0, 3))
+        own, three, *halves = spread
+        ends = [over_z(piece, 1, (0, 3)) for piece in halves[4:]]
         middle = over_z(three, 3, (1, 2))
-        two, near = relay(two, ends, [low, high], middle)
-        far = over_z(two, 2)
-        near = [over_z(a, 1) for a in near]
-        parts = [own, jnp.concatenate(near, axis=0), far, middle]
+        low, _ = relay(halves[2], ends[0], [], [])
+        high, near = relay(halves[3], ends[1], halves[:2], [middle])
+        far = jnp.concatenate([over_z(low, 2), over_z(high, 2)], axis=0)
+        near = jnp.concatenate([over_z(piece, 1) for piece in near], axis=0)
+        parts = [own, near, far, middle]
     else:
         parts = [spread[0]] + [over_z(spread[k], k) for k in range(1, n_gx)]
     return sum(p.astype(F32) for p in parts).astype(BF16)

time: 117 us -> 112 us (0.957)
  waiting for transfers between devices: 39.8 us -> 31.7 us
  starting transfers between devices: 28.2 us -> 30.7 us
    ppermute x8 -> x10, waiting for transfers between devices: 23.6 us -> 16.5 us  [over_z(): return lax.ppermute(block, 'gx', [(z, z ^ k) for z in among])]
    ppermute x8 -> x10, starting transfers between devices: 15.4 us -> 19.5 us  [over_z(): return lax.ppermute(block, 'gx', [(z, z ^ k) for z in among])]
    ppermute x7, starting transfers between devices: 9.46 us -> 7.83 us  [over_x(): lax.ppermute(block, 'gy', [(i, (i + 2 * k) % n_gy) for i in range(n_gy)])]
    pallas_call x3 -> x4, Pallas kernels: 4.08 us -> 4.09 us  [the longest x2 4.02 us: down_held(): pl.pallas_call(functools.partial(down_held_kernel, len(hidden), last, [ro...]
  transfers between devices with their start and end apart: 31 -> 33, of which waited for: 10 -> 13; matrix products, arithmetic and copies ran while one was open for 0% -> 0% of each run, Pallas kernels for 35% -> 37%
where the time goes in v12:
time: 112 us
  Pallas kernels  46.4 us (41%)
  waiting for transfers between devices  31.7 us (28%)
  starting transfers between devices  30.7 us (27%)
  local copies, waits for them, and re-layouts  1.64 us (1%)
    ppermute x10, starting transfers between devices, over_z(): return lax.ppermute(block, 'gx', [(z, z ^ k) for z in among])  19.5 us
    ppermute x10, waiting for transfers between devices, over_z(): return lax.ppermute(block, 'gx', [(z, z ^ k) for z in among])  16.5 us
    ppermute x7, waiting for transfers between devices, over_x(): lax.ppermute(block, 'gy', [(i, (i + 2 * k) % n_gy) for i in range(n_gy)])  14.2 us
    pallas_call x1, Pallas kernels, prepare(): pl.pallas_call(functools.partial(prepare_kernel, n_gx, nx, chunks), out_s...  13.6 us
    pallas_call x3, Pallas kernels, gate_up_held(): pl.pallas_call(functools.partial(gate_up_held_kernel, len(after), tile),...  8.7 us
    ppermute x7, starting transfers between devices, over_x(): lax.ppermute(block, 'gy', [(i, (i + 2 * k) % n_gy) for i in range(n_gy)])  7.83 us
    pallas_call x1, Pallas kernels, gate_up(): pl.pallas_call(functools.partial(gate_up_kernel, len(after)), out_shape=[...  6.84 us
    pallas_call x1, Pallas kernels, down(): pl.pallas_call(functools.partial(down_kernel, len(hidden)), out_shape=jax...  6.63 us
  transfers between devices with their start and end apart: 33, of which 13 were waited for; matrix products, arithmetic and copies ran while one was open for 0% of the time, Pallas kernels for 37%

profile of v12, /device:TPU:0, one launch (start us, length us, event | category | flops | bytes accessed | tf_op | source)
XLA Modules:
  0.0 111.5 jit_solution(12110491422650573919)
XLA Ops:
  0.0 3.0 %collective-permute-start = (bf16[64,2048]{1,0:T(8,128)(2,1)}, bf16[64,2048]{1,0:T(8,128)(2,1)S(1)}, u32[]{:S(2)}, u32[]{:S(2)}) collective-permute-start(bf16[64,2048]{1,0:T(8,128)(2,1)} %tok_ref.1), channel_id=1, source_target_pairs={{0,4},{4,0},{8,12},{12,8},{1,5},{5,1},{9,13},{13,9},{2,6},{6,2},{1... | collective-permute-start | bytes 786440 | tf_op jit(solution)/shard_map/ppermute | solution.py:366
  3.0 2.5 %collective-permute-start.2 = (bf16[64,2048]{1,0:T(8,128)(2,1)}, bf16[64,2048]{1,0:T(8,128)(2,1)S(1)}, u32[]{:S(2)}, u32[]{:S(2)}) collective-permute-start(bf16[64,2048]{1,0:T(8,128)(2,1)} %tok_ref.1), channel_id=1, source_target_pairs={{0,12},{4,8},{8,4},{12,0},{1,13},{5,9},{9,5},{13,1},{2,14},{6,10},... | collective-permute-start | bytes 786440 | tf_op jit(solution)/shard_map/ppermute | solution.py:366
  7.3 13.6 %prepare.1 = (bf16[192,256]{1,0:T(8,128)(2,1)S(1)}, bf16[256,192]{1,0:T(8,128)(2,1)S(1)}, bf16[64,2048]{1,0:T(8,128)(2,1)S(1)}, bf16[2048,1536]{1,0:T(8,128)(2,1...) custom-call(s32[4]{0:T(128)S(1)} %copy-done.1, ...), custom_call_target="tpu_custom_call" | custom-call | tf_op jit(solution)/shard_map/prepare/pallas_call | solution.py:67
  20.9 7.8 %collective-permute-done.1.refs_2_ = bf16[64,2048]{1,0:T(8,128)(2,1)S(1)} collective-permute-done((bf16[64,2048]{1,0:T(8,128)(2,1)}, bf16[64,2048]{1,0:T(8,128)(2,1)S(1)}, u32[]{:S(2)}, u32[]{:S(2)}) %collective-permute-start.1) | collective-permute-done | bytes 262176 | tf_op jit(solution)/shard_map/ppermute | solution.py:366
  29.1 2.6 %gate_up_held.3 = (f32[2,96,1536]{2,1,0:T(8,128)S(1)}, bf16[2,96,1536]{2,1,0:T(8,128)(2,1)S(1)}) custom-call(bf16[192,2048]{1,0:T(8,128)(2,1)S(1)} %compact.1.tok_ref, bf16[2048,1536]{1,0:T(8,128)(2,1)S(1)} %get-tuple-element.67.gate_ref, bf16[2048,1536]{1,0:T(8,128)(2,1)S(1)} %get-tuple-element.68.up_ref), custom_call_target="tpu_custom_call" | custom-call | tf_op jit(solution)/shard_map/gate_up_held/pallas_call | solution.py:132
  31.8 2.6 %gate_up_held.4 = (f32[2,96,1536]{2,1,0:T(8,128)S(1)}, bf16[2,96,1536]{2,1,0:T(8,128)(2,1)S(1)}) custom-call(bf16[192,2048]{1,0:T(8,128)(2,1)S(1)} %compact.1.tok_ref, bf16[2048,1536]{1,0:T(8,128)(2,1)S(1)} %get-tuple-element.71.gate_ref, bf16[2048,1536]{1,0:T(8,128)(2,1)S(1)} %get-tuple-element.72.up_ref), custom_call_target="tpu_custom_call" | custom-call | tf_op jit(solution)/shard_map/gate_up_held/pallas_call | solution.py:132
  36.8 1.6 %collective-permute-start.6 = (bf16[2,48,1536]{2,1,0:T(8,128)(2,1)S(1)}, bf16[2,48,1536]{2,1,0:T(8,128)(2,1)S(1)}, u32[]{:S(2)}, u32[]{:S(2)}) collective-permute-start(bf16[2,48,1536]{2,1,0:T(8,128)(2,1)S(1)} %get-tuple-element.77.refs_1_), channel_id=1, source_target_pairs={{0,2},{1,3},{2,0},{3,1},{4,6},{5,7},{6,4},{7,5},{8,10},{9,11},{10,... | collective-permute-start | bytes 884744 | tf_op jit(solution)/shard_map/ppermute | solution.py:372
  38.4 3.5 %gate_up_held.5 = (f32[2,96,2048]{2,1,0:T(8,128)S(1)}, bf16[48,2048]{1,0:T(8,128)(2,1)S(1)}, bf16[48,2048]{1,0:T(8,128)(2,1)S(1)}, bf16[48,2048]{1,0:T(8,128)(2,1)S(1)}, bf16[48,2048]{1,0:T(8,128)(2,1)S(1)}) custom-call(bf16[192,2048]{1,0:T(8,128)(2,1)S(1)} %compact.1.tok_ref, bf16[2048,2048]{1,0:T(8,128)(2,1)S(1)} %get-tuple-element.65.gate_ref, ...), custom_call_target="tpu_custom_call" | custom-call | tf_op jit(solution)/shard_map/gate_up_held/pallas_call | solution.py:132
  41.9 6.8 %gate_up.1 = (f32[2,96,1536]{2,1,0:T(8,128)S(1)}, bf16[48,1536]{1,0:T(8,128)(2,1)S(1)}, bf16[48,1536]{1,0:T(8,128)(2,1)S(1)}, bf16[48,1536]{1,0:T(8,128)(2,1)S(1)}, bf16[48,1536]{1,0:T(8,128)(2,1)S(1)}) custom-call(bf16[192,2048]{1,0:T(8,128)(2,1)S(1)} %compact.1.tok_ref, bf16[2048,6656]{1,0:T(8,128)(2,1)} %gate_ref.3, bf16[2048,6656]{1,0:T(8,128)(2,1)} %up_ref.3, ...), custom_call_target="tpu_custom_call" | custom-call | tf_op jit(solution)/shard_map/gate_up/pallas_call | solution.py:156
  48.7 1.7 %collective-permute-done.6.refs_3_ = bf16[2,48,1536]{2,1,0:T(8,128)(2,1)S(1)} collective-permute-done((bf16[2,48,1536]{2,1,0:T(8,128)(2,1)S(1)}, bf16[2,48,1536]{2,1,0:T(8,128)(2,1)S(1)}, u32[]{:S(2)}, u32[]{:S(2)}) %collective-permute-start.6) | collective-permute-done | bytes 294944 | tf_op jit(solution)/shard_map/ppermute | solution.py:372
  51.7 1.5 %collective-permute-start.20 = (bf16[48,3072]{1,0:T(8,128)(2,1)S(1)}, bf16[48,3072]{1,0:T(8,128)(2,1)S(1)}, u32[]{:S(2)}, u32[]{:S(2)}) collective-permute-start(bf16[48,3072]{1,0:T(8,128)(2,1)S(1)} %get-tuple-element.98.refs_0_), channel_id=1, source_target_pairs={{0,2},{1,3},{2,0},{3,1},{4,6},{5,7},{6,4},{7,5},{8,10},{9,11},{10,... | collective-permute-start | bytes 884744 | tf_op jit(solution)/shard_map/ppermute | solution.py:372
  53.2 5.2 %fetch.1 = (bf16[2048,2048]{1,0:T(8,128)(2,1)S(1)}, bf16[1536,2048]{1,0:T(8,128)(2,1)S(1)}) custom-call(bf16[6656,2048]{1,0:T(8,128)(2,1)} %refs_4_.1, bf16[48,3072]{1,0:T(8,128)(2,1)S(1)} %get-tuple-element.98.refs_0_), custom_call_target="tpu_custom_call" | custom-call | tf_op jit(solution)/shard_map/fetch/pallas_call | solution.py:302
  62.2 1.5 %collective-permute-start.15 = (bf16[2,48,1536]{2,1,0:T(8,128)(2,1)S(1)}, bf16[2,48,1536]{2,1,0:T(8,128)(2,1)S(1)}, u32[]{:S(2)}, u32[]{:S(2)}) collective-permute-start(bf16[2,48,1536]{2,1,0:T(8,128)(2,1)S(1)} %get-tuple-element.105.refs_5_), channel_id=1, source_target_pairs={{0,2},{1,3},{2,0},{3,1},{4,6},{5,7},{6,4},{7,5},{8,10},{9,11},{10,... | collective-permute-start | bytes 884744 | tf_op jit(solution)/shard_map/ppermute | solution.py:372
  63.8 6.6 %down.1.refs_2_.refs_5_ = f32[192,2048]{1,0:T(8,128)S(1)} custom-call(bf16[48,3072]{1,0:T(8,128)(2,1)S(1)} %get-tuple-element.98.refs_0_, bf16[48,3072]{1,0:T(8,128)(2,1)S(1)} %collective-permute-done.20.refs_1_, bf16[48,3072]{1,0:T(8,128)(2,1)S(1)} %collective-permute-done.21.refs_2_, bf16[48,3072]{1,0:T(8,128)(2,1)S(1)} %collective-permute-done.22.refs_3_, ...), custom_call_target="tpu_custom_call" | custom-call | tf_op jit(solution)/shard_map/down/pallas_call | solution.py:273
  71.9 5.5 %collective-permute-done.15.refs_1_ = bf16[2,48,1536]{2,1,0:T(8,128)(2,1)S(1)} collective-permute-done((bf16[2,48,1536]{2,1,0:T(8,128)(2,1)S(1)}, bf16[2,48,1536]{2,1,0:T(8,128)(2,1)S(1)}, u32[]{:S(2)}, u32[]{:S(2)}) %collective-permute-start.15) | collective-permute-done | bytes 294944 | tf_op jit(solution)/shard_map/ppermute | solution.py:372
  78.2 3.5 %collective-permute-done.23.refs_1_ = bf16[48,2048]{1,0:T(8,128)(2,1)S(1)} collective-permute-done((bf16[48,2048]{1,0:T(8,128)(2,1)S(1)}, bf16[48,2048]{1,0:T(8,128)(2,1)S(1)}, u32[]{:S(2)}, u32[]{:S(2)}) %collective-permute-start.23) | collective-permute-done | bytes 196640 | tf_op jit(solution)/shard_map/ppermute | solution.py:372
  82.2 1.8 %collective-permute-done.16.refs_1_ = bf16[48,1536]{1,0:T(8,128)(2,1)S(1)} collective-permute-done((bf16[48,1536]{1,0:T(8,128)(2,1)S(1)}, bf16[48,1536]{1,0:T(8,128)(2,1)S(1)}, u32[]{:S(2)}, u32[]{:S(2)}) %collective-permute-start.16) | collective-permute-done | bytes 147488 | tf_op jit(solution)/shard_map/ppermute | solution.py:372
  84.0 1.8 %down_held.2.refs_5_ = f32[192,2048]{1,0:T(8,128)S(1)} custom-call(bf16[48,2048]{1,0:T(8,128)(2,1)S(1)} %activate.5.refs_0_, bf16[48,2048]{1,0:T(8,128)(2,1)S(1)} %collective-permute-done.23.refs_1_, bf16[48,2048]{1,0:T(8,128)(2,1)S(1)} %collective-permute-done.24.refs_2_, bf16[48,2048]{1,0:T(8,128)(2,1)S(1)} %collective-permute-done.25.refs_3_, ...), custom_call_target="tpu_custom_call" | custom-call | tf_op jit(solution)/shard_map/down_held/pallas_call | solution.py:336
  85.8 2.2 %down_held.3 = (bf16[64,2048]{1,0:T(8,128)(2,1)S(1)}, bf16[64,2048]{1,0:T(8,128)(2,1)S(1)}, bf16[32,2048]{1,0:T(8,128)(2,1)S(1)}, bf16[32,2048]{1,0:T(8,128)(2,1...) custom-call(bf16[48,1536]{1,0:T(8,128)(2,1)S(1)} %activate.4.refs_0_, ...), custom_call_target="tpu_custom_call" | custom-call | tf_op jit(solution)/shard_map/down_held/pallas_call | solution.py:336
  88.7 3.4 %collective-permute-start.30 = (bf16[32,2048]{1,0:T(8,128)(2,1)S(1)}, bf16[32,2048]{1,0:T(8,128)(2,1)S(1)}, u32[]{:S(2)}, u32[]{:S(2)}) collective-permute-start(bf16[32,2048]{1,0:T(8,128)(2,1)S(1)} %get-tuple-element.119), channel_id=1, source_target_pairs={{0,4},{12,8},{1,5},{13,9},{2,6},{14,10},{3,7},{15,11},{16,20},{28,... | collective-permute-start | bytes 393224 | tf_op jit(solution)/shard_map/ppermute | solution.py:366
  93.4 2.5 %collective-permute-done.30.got_ref = bf16[32,2048]{1,0:T(8,128)(2,1)S(1)} collective-permute-done((bf16[32,2048]{1,0:T(8,128)(2,1)S(1)}, bf16[32,2048]{1,0:T(8,128)(2,1)S(1)}, u32[]{:S(2)}, u32[]{:S(2)}) %collective-permute-start.30) | collective-permute-done | bytes 131104 | tf_op jit(solution)/shard_map/ppermute | solution.py:366
  96.0 3.7 %collective-permute-start.31 = (bf16[32,2048]{1,0:T(8,128)(2,1)S(1)}, bf16[32,2048]{1,0:T(8,128)(2,1)S(1)}, u32[]{:S(2)}, u32[]{:S(2)}) collective-permute-start(bf16[32,2048]{1,0:T(8,128)(2,1)S(1)} %relay.3), channel_id=1, source_target_pairs={{0,8},{4,12},{8,0},{12,4},{1,9},{5,13},{9,1},{13,5},{2,10},{6,14},... | collective-permute-start | bytes 393224 | tf_op jit(solution)/shard_map/ppermute | solution.py:366
  101.8 2.7 %collective-permute-start.32 = (bf16[32,2048]{1,0:T(8,128)(2,1)S(1)}, bf16[32,2048]{1,0:T(8,128)(2,1)S(1)}, u32[]{:S(2)}, u32[]{:S(2)}) collective-permute-start(bf16[32,2048]{1,0:T(8,128)(2,1)S(1)} %get-tuple-element.120), channel_id=1, source_target_pairs={{0,8},{4,12},{8,0},{12,4},{1,9},{5,13},{9,1},{13,5},{2,10},{6,14},... | collective-permute-start | bytes 393224 | tf_op jit(solution)/shard_map/ppermute | solution.py:366
  105.9 3.3 %collective-permute-done.28 = bf16[32,2048]{1,0:T(8,128)(2,1)S(1)} collective-permute-done((bf16[32,2048]{1,0:T(8,128)(2,1)S(1)}, bf16[32,2048]{1,0:T(8,128)(2,1)S(1)}, u32[]{:S(2)}, u32[]{:S(2)}) %collective-permute-start.28) | collective-permute-done | bytes 131104 | tf_op jit(solution)/shard_map/ppermute | solution.py:366
  (66 shorter events, 20.2 us)
Async XLA Ops:
  0.0 20.9 %collective-permute-start = (bf16[64,2048]{1,0:T(8,128)(2,1)}, bf16[64,2048]{1,0:T(8,128)(2,1)S(1)}, u32[]{:S(2)}, u32[]{:S(2)}) collective-permute-start(bf16[64,2048]{1,0:T(8,128)(2,1)} %tok_ref.1), channel_id=1, source_target_pairs={{0,4},{4,0},{8,12},{12,8},{1,5},{5,1},{9,13},{13,9},{2,6},{6,2},{1... | collective-permute-start | bytes 786440 | tf_op jit(solution)/shard_map/ppermute | solution.py:366
  3.0 17.9 %collective-permute-start.2 = (bf16[64,2048]{1,0:T(8,128)(2,1)}, bf16[64,2048]{1,0:T(8,128)(2,1)S(1)}, u32[]{:S(2)}, u32[]{:S(2)}) collective-permute-start(bf16[64,2048]{1,0:T(8,128)(2,1)} %tok_ref.1), channel_id=1, source_target_pairs={{0,12},{4,8},{8,4},{12,0},{1,13},{5,9},{9,5},{13,1},{2,14},{6,10},... | collective-permute-start | bytes 786440 | tf_op jit(solution)/shard_map/ppermute | solution.py:366
  5.5 23.2 %collective-permute-start.1 = (bf16[64,2048]{1,0:T(8,128)(2,1)}, bf16[64,2048]{1,0:T(8,128)(2,1)S(1)}, u32[]{:S(2)}, u32[]{:S(2)}) collective-permute-start(bf16[64,2048]{1,0:T(8,128)(2,1)} %tok_ref.1), channel_id=1, source_target_pairs={{0,8},{4,12},{8,0},{12,4},{1,9},{5,13},{9,1},{13,5},{2,10},{6,14},... | collective-permute-start | bytes 786440 | tf_op jit(solution)/shard_map/ppermute | solution.py:366
  35.1 13.6 %collective-permute-start.5 = (bf16[2,48,1536]{2,1,0:T(8,128)(2,1)S(1)}, bf16[2,48,1536]{2,1,0:T(8,128)(2,1)S(1)}, u32[]{:S(2)}, u32[]{:S(2)}) collective-permute-start(bf16[2,48,1536]{2,1,0:T(8,128)(2,1)S(1)} %get-tuple-element.74.refs_0_), channel_id=1, source_target_pairs={{0,2},{1,3},{2,0},{3,1},{4,6},{5,7},{6,4},{7,5},{8,10},{9,11},{10,... | collective-permute-start | bytes 884744 | tf_op jit(solution)/shard_map/ppermute | solution.py:372
  36.8 13.6 %collective-permute-start.6 = (bf16[2,48,1536]{2,1,0:T(8,128)(2,1)S(1)}, bf16[2,48,1536]{2,1,0:T(8,128)(2,1)S(1)}, u32[]{:S(2)}, u32[]{:S(2)}) collective-permute-start(bf16[2,48,1536]{2,1,0:T(8,128)(2,1)S(1)} %get-tuple-element.77.refs_1_), channel_id=1, source_target_pairs={{0,2},{1,3},{2,0},{3,1},{4,6},{5,7},{6,4},{7,5},{8,10},{9,11},{10,... | collective-permute-start | bytes 884744 | tf_op jit(solution)/shard_map/ppermute | solution.py:372
  50.6 7.8 %collective-permute-start.7 = (bf16[48,2048]{1,0:T(8,128)(2,1)S(1)}, bf16[48,2048]{1,0:T(8,128)(2,1)S(1)}, u32[]{:S(2)}, u32[]{:S(2)}) collective-permute-start(bf16[48,2048]{1,0:T(8,128)(2,1)S(1)} %get-tuple-element.90), channel_id=1, source_target_pairs={{0,1},{1,0},{2,3},{3,2},{4,5},{5,4},{6,7},{7,6},{8,9},{9,8},{10,11... | collective-permute-start | bytes 589832 | tf_op jit(solution)/shard_map/ppermute | solution.py:369
  50.7 7.7 %collective-permute-start.8 = (bf16[48,2048]{1,0:T(8,128)(2,1)S(1)}, bf16[48,2048]{1,0:T(8,128)(2,1)S(1)}, u32[]{:S(2)}, u32[]{:S(2)}) collective-permute-start(bf16[48,2048]{1,0:T(8,128)(2,1)S(1)} %get-tuple-element.91), channel_id=1, source_target_pairs={{0,1},{1,0},{2,3},{3,2},{4,5},{5,4},{6,7},{7,6},{8,9},{9,8},{10,11... | collective-permute-start | bytes 589832 | tf_op jit(solution)/shard_map/ppermute | solution.py:369
  51.2 7.2 %collective-permute-start.9 = (bf16[48,2048]{1,0:T(8,128)(2,1)S(1)}, bf16[48,2048]{1,0:T(8,128)(2,1)S(1)}, u32[]{:S(2)}, u32[]{:S(2)}) collective-permute-start(bf16[48,2048]{1,0:T(8,128)(2,1)S(1)} %get-tuple-element.92), channel_id=1, source_target_pairs={{0,1},{1,0},{2,3},{3,2},{4,5},{5,4},{6,7},{7,6},{8,9},{9,8},{10,11... | collective-permute-start | bytes 589832 | tf_op jit(solution)/shard_map/ppermute | solution.py:369
  51.3 7.1 %collective-permute-start.10 = (bf16[48,2048]{1,0:T(8,128)(2,1)S(1)}, bf16[48,2048]{1,0:T(8,128)(2,1)S(1)}, u32[]{:S(2)}, u32[]{:S(2)}) collective-permute-start(bf16[48,2048]{1,0:T(8,128)(2,1)S(1)} %get-tuple-element.93), channel_id=1, source_target_pairs={{0,1},{1,0},{2,3},{3,2},{4,5},{5,4},{6,7},{7,6},{8,9},{9,8},{10,11... | collective-permute-start | bytes 589832 | tf_op jit(solution)/shard_map/ppermute | solution.py:369
  51.7 9.0 %collective-permute-start.20 = (bf16[48,3072]{1,0:T(8,128)(2,1)S(1)}, bf16[48,3072]{1,0:T(8,128)(2,1)S(1)}, u32[]{:S(2)}, u32[]{:S(2)}) collective-permute-start(bf16[48,3072]{1,0:T(8,128)(2,1)S(1)} %get-tuple-element.98.refs_0_), channel_id=1, source_target_pairs={{0,2},{1,3},{2,0},{3,1},{4,6},{5,7},{6,4},{7,5},{8,10},{9,11},{10,... | collective-permute-start | bytes 884744 | tf_op jit(solution)/shard_map/ppermute | solution.py:372
  59.2 12.0 %collective-permute-start.19 = (bf16[2,48,2048]{2,1,0:T(8,128)(2,1)S(1)}, bf16[2,48,2048]{2,1,0:T(8,128)(2,1)S(1)}, u32[]{:S(2)}, u32[]{:S(2)}) collective-permute-start(bf16[2,48,2048]{2,1,0:T(8,128)(2,1)S(1)} %get-tuple-element.108), channel_id=1, source_target_pairs={{0,2},{1,3},{2,0},{3,1},{4,6},{5,7},{6,4},{7,5},{8,10},{9,11},{10,... | collective-permute-start | bytes 1179656 | tf_op jit(solution)/shard_map/ppermute | solution.py:372
  60.7 3.0 %collective-permute-start.21 = (bf16[48,3072]{1,0:T(8,128)(2,1)S(1)}, bf16[48,3072]{1,0:T(8,128)(2,1)S(1)}, u32[]{:S(2)}, u32[]{:S(2)}) collective-permute-start(bf16[48,3072]{1,0:T(8,128)(2,1)S(1)} %get-tuple-element.98.refs_0_), channel_id=1, source_target_pairs={{0,1},{1,0},{2,3},{3,2},{4,5},{5,4},{6,7},{7,6},{8,9},{9,8},{10,11... | collective-permute-start | bytes 884744 | tf_op jit(solution)/shard_map/ppermute | solution.py:369
  62.2 15.3 %collective-permute-start.15 = (bf16[2,48,1536]{2,1,0:T(8,128)(2,1)S(1)}, bf16[2,48,1536]{2,1,0:T(8,128)(2,1)S(1)}, u32[]{:S(2)}, u32[]{:S(2)}) collective-permute-start(bf16[2,48,1536]{2,1,0:T(8,128)(2,1)S(1)} %get-tuple-element.105.refs_5_), channel_id=1, source_target_pairs={{0,2},{1,3},{2,0},{3,1},{4,6},{5,7},{6,4},{7,5},{8,10},{9,11},{10,... | collective-permute-start | bytes 884744 | tf_op jit(solution)/shard_map/ppermute | solution.py:372
  71.3 10.4 %collective-permute-start.23 = (bf16[48,2048]{1,0:T(8,128)(2,1)S(1)}, bf16[48,2048]{1,0:T(8,128)(2,1)S(1)}, u32[]{:S(2)}, u32[]{:S(2)}) collective-permute-start(bf16[48,2048]{1,0:T(8,128)(2,1)S(1)} %activate.5.refs_0_), channel_id=1, source_target_pairs={{0,2},{1,3},{2,0},{3,1},{4,6},{5,7},{6,4},{7,5},{8,10},{9,11},{10,... | collective-permute-start | bytes 589832 | tf_op jit(solution)/shard_map/ppermute | solution.py:372
  77.6 6.4 %collective-permute-start.16 = (bf16[48,1536]{1,0:T(8,128)(2,1)S(1)}, bf16[48,1536]{1,0:T(8,128)(2,1)S(1)}, u32[]{:S(2)}, u32[]{:S(2)}) collective-permute-start(bf16[48,1536]{1,0:T(8,128)(2,1)S(1)} %activate.4.refs_0_), channel_id=1, source_target_pairs={{0,2},{1,3},{2,0},{3,1},{4,6},{5,7},{6,4},{7,5},{8,10},{9,11},{10,... | collective-permute-start | bytes 442376 | tf_op jit(solution)/shard_map/ppermute | solution.py:372
  78.2 5.8 %collective-permute-start.24 = (bf16[48,2048]{1,0:T(8,128)(2,1)S(1)}, bf16[48,2048]{1,0:T(8,128)(2,1)S(1)}, u32[]{:S(2)}, u32[]{:S(2)}) collective-permute-start(bf16[48,2048]{1,0:T(8,128)(2,1)S(1)} %activate.5.refs_0_), channel_id=1, source_target_pairs={{0,1},{1,0},{2,3},{3,2},{4,5},{5,4},{6,7},{7,6},{8,9},{9,8},{10,11... | collective-permute-start | bytes 589832 | tf_op jit(solution)/shard_map/ppermute | solution.py:369
  81.7 4.1 %collective-permute-start.17 = (bf16[48,1536]{1,0:T(8,128)(2,1)S(1)}, bf16[48,1536]{1,0:T(8,128)(2,1)S(1)}, u32[]{:S(2)}, u32[]{:S(2)}) collective-permute-start(bf16[48,1536]{1,0:T(8,128)(2,1)S(1)} %activate.4.refs_0_), channel_id=1, source_target_pairs={{0,1},{1,0},{2,3},{3,2},{4,5},{5,4},{6,7},{7,6},{8,9},{9,8},{10,11... | collective-permute-start | bytes 442376 | tf_op jit(solution)/shard_map/ppermute | solution.py:369
  88.0 11.6 %collective-permute-start.27 = (bf16[64,2048]{1,0:T(8,128)(2,1)S(1)}, bf16[64,2048]{1,0:T(8,128)(2,1)S(1)}, u32[]{:S(2)}, u32[]{:S(2)}) collective-permute-start(bf16[64,2048]{1,0:T(8,128)(2,1)S(1)} %get-tuple-element.115), channel_id=1, source_target_pairs={{4,8},{8,4},{5,9},{9,5},{6,10},{10,6},{7,11},{11,7},{20,24},{24,20... | collective-permute-start | bytes 786440 | tf_op jit(solution)/shard_map/ppermute | solution.py:366
  88.7 7.2 %collective-permute-start.30 = (bf16[32,2048]{1,0:T(8,128)(2,1)S(1)}, bf16[32,2048]{1,0:T(8,128)(2,1)S(1)}, u32[]{:S(2)}, u32[]{:S(2)}) collective-permute-start(bf16[32,2048]{1,0:T(8,128)(2,1)S(1)} %get-tuple-element.119), channel_id=1, source_target_pairs={{0,4},{12,8},{1,5},{13,9},{2,6},{14,10},{3,7},{15,11},{16,20},{28,... | collective-permute-start | bytes 393224 | tf_op jit(solution)/shard_map/ppermute | solution.py:366
  92.1 7.6 %collective-permute-start.26 = (bf16[32,2048]{1,0:T(8,128)(2,1)S(1)}, bf16[32,2048]{1,0:T(8,128)(2,1)S(1)}, u32[]{:S(2)}, u32[]{:S(2)}) collective-permute-start(bf16[32,2048]{1,0:T(8,128)(2,1)S(1)} %get-tuple-element.112), channel_id=1, source_target_pairs={{0,4},{12,8},{1,5},{13,9},{2,6},{14,10},{3,7},{15,11},{16,20},{28,... | collective-permute-start | bytes 393224 | tf_op jit(solution)/shard_map/ppermute | solution.py:366
  96.0 10.0 %collective-permute-start.31 = (bf16[32,2048]{1,0:T(8,128)(2,1)S(1)}, bf16[32,2048]{1,0:T(8,128)(2,1)S(1)}, u32[]{:S(2)}, u32[]{:S(2)}) collective-permute-start(bf16[32,2048]{1,0:T(8,128)(2,1)S(1)} %relay.3), channel_id=1, source_target_pairs={{0,8},{4,12},{8,0},{12,4},{1,9},{5,13},{9,1},{13,5},{2,10},{6,14},... | collective-permute-start | bytes 393224 | tf_op jit(solution)/shard_map/ppermute | solution.py:366
  99.7 9.6 %collective-permute-start.28 = (bf16[32,2048]{1,0:T(8,128)(2,1)S(1)}, bf16[32,2048]{1,0:T(8,128)(2,1)S(1)}, u32[]{:S(2)}, u32[]{:S(2)}) collective-permute-start(bf16[32,2048]{1,0:T(8,128)(2,1)S(1)} %get-tuple-element.116), channel_id=1, source_target_pairs={{0,4},{4,0},{8,12},{12,8},{1,5},{5,1},{9,13},{13,9},{2,6},{6,2},{1... | collective-permute-start | bytes 393224 | tf_op jit(solution)/shard_map/ppermute | solution.py:366
  100.6 10.1 %collective-permute-start.29 = (bf16[32,2048]{1,0:T(8,128)(2,1)S(1)}, bf16[32,2048]{1,0:T(8,128)(2,1)S(1)}, u32[]{:S(2)}, u32[]{:S(2)}) collective-permute-start(bf16[32,2048]{1,0:T(8,128)(2,1)S(1)} %get-tuple-element.117), channel_id=1, source_target_pairs={{0,4},{4,0},{8,12},{12,8},{1,5},{5,1},{9,13},{13,9},{2,6},{6,2},{1... | collective-permute-start | bytes 393224 | tf_op jit(solution)/shard_map/ppermute | solution.py:366
  101.8 8.9 %collective-permute-start.32 = (bf16[32,2048]{1,0:T(8,128)(2,1)S(1)}, bf16[32,2048]{1,0:T(8,128)(2,1)S(1)}, u32[]{:S(2)}, u32[]{:S(2)}) collective-permute-start(bf16[32,2048]{1,0:T(8,128)(2,1)S(1)} %get-tuple-element.120), channel_id=1, source_target_pairs={{0,8},{4,12},{8,0},{12,4},{1,9},{5,13},{9,1},{13,5},{2,10},{6,14},... | collective-permute-start | bytes 393224 | tf_op jit(solution)/shard_map/ppermute | solution.py:366
  (11 other events, 20.9 us)

commit v13 on v12

--- a/solution.py
+++ b/solution.py
@@ -31,6 +31,10 @@
             owner = lax.rem(x + kx, nx) * 2 + (1 - core if kc else core)
             rows = jnp.where(j >= first, owner * quarter + j - first, rows)
     return rows
+
+
+def gathered_block(k):
+    return k ^ (k >> 1)
 
 
 def prepare_kernel(n_gx, nx, chunks, lengths_ref, tok_ref, gate_ref, up_ref, in_ref, out_ref, held_ref, *refs):
@@ -47,15 +51,17 @@
     live, slots = in_ref.shape
     quarter = live // (2 * nx)
 
-    def slot_of(column):
-        return (z ^ (column // tok_dev)) * tok_dev + column % tok_dev
+    def slot_of(column, block_of):
+        return (z ^ block_of(column // tok_dev)) * tok_dev + column % tok_dev
 
     shape = (live, slots)
     source = row_sources(lengths_ref, local_rows(shape, 0, quarter, nx), n_gx, tok_dev)
-    in_ref[...] = (source == slot_of(lax.broadcasted_iota(jnp.int32, shape, 1))).astype(F32).astype(BF16)
+    slot = slot_of(lax.broadcasted_iota(jnp.int32, shape, 1), gathered_block)
+    in_ref[...] = (source == slot).astype(F32).astype(BF16)
     shape = (slots, live)
     source = row_sources(lengths_ref, local_rows(shape, 1, quarter, nx), n_gx, tok_dev)
-    out_ref[...] = (source == slot_of(lax.broadcasted_iota(jnp.int32, shape, 0))).astype(F32).astype(BF16)
+    slot = slot_of(lax.broadcasted_iota(jnp.int32, shape, 0), lambda k: k)
+    out_ref[...] = (source == slot).astype(F32).astype(BF16)
     for copy in copies:
         copy.wait()
 
@@ -126,14 +132,14 @@
             put_part(i, part, columns, keep_ref, send_refs)
 
 
-def gate_up_held(tok, gate_held, up_held, after, nx, tile, split=False):
+def gate_up_held(tok, gate_held, up_held, after, nx, tile):
     half, width = tok.shape[0] // 2, gate_held.shape[1]
     held, anywhere = pl.BlockSpec(memory_space=pltpu.VMEM), pl.BlockSpec(memory_space=pl.ANY)
     keep, *send = pl.pallas_call(
         functools.partial(gate_up_held_kernel, len(after), tile),
-        out_shape=[jax.ShapeDtypeStruct((2, half, width), F32)] + send_shapes(half, nx, width, split),
+        out_shape=[jax.ShapeDtypeStruct((2, half, width), F32)] + send_shapes(half, nx, width, False),
         in_specs=[held] * 3 + [anywhere] * len(after),
-        out_specs=[held] * (1 + (2 * nx if split else 1)),
+        out_specs=[held] * 2,
         compiler_params=pltpu.CompilerParams(vmem_limit_bytes=6 * MIB),
         cost_estimate=pl.CostEstimate(flops=0, bytes_accessed=0, transcendentals=0),
         name="gate_up_held",
@@ -371,7 +377,7 @@
     def over_x(block, k):
         return lax.ppermute(block, "gy", [(i, (i + 2 * k) % n_gy) for i in range(n_gy)])
 
-    far = [over_z(tokens, k) for k in range(1, n_gx)]
+    far = [over_z(tokens, gathered_block(k)) for k in range(1, n_gx)]
     pick_in, pick_out, held, weights = prepare(lengths, tokens, gate_weight, up_weight, chunks[:3], n_gx, nx, live)
     blocks = [held] + far
     tok = compact(pick_in, blocks)
@@ -394,7 +400,7 @@
 
     ready, sends[1] = exchange(0, sends[1], [])
     ready = ready + exchange(1, [], [])[0]
-    made = [gate_up_held(tok, *weights[2], ready, nx, tile, True)]
+    made = [gate_up_held(tok, *weights[2], ready, nx, tile)]
     made.append(gate_up(tok, gate_weight, up_weight, made[0][0][:1], *chunks[3], nx, tile))
     pieces = len(made[0][0])
     hidden, handed = finish(0, 2, made[0][0] + made[1][0], [])

time: 112 us -> 113 us (level)
  starting transfers between devices: 30.7 us -> 33.7 us
  waiting for transfers between devices: 31.7 us -> 29.8 us
    ppermute x10, starting transfers between devices: 19.5 us -> 23.3 us  [over_z(): return lax.ppermute(block, 'gx', [(z, z ^ k) for z in among])]
    ppermute x10, waiting for transfers between devices: 16.5 us -> 14.6 us  [over_z(): return lax.ppermute(block, 'gx', [(z, z ^ k) for z in among])]
    ppermute x16 -> x13, starting transfers between devices: 3.37 us -> 2.38 us  [over_core(): return lax.ppermute(block, 'gy', [(i, i ^ 1) for i in range(n_gy)])]
  transfers between devices with their start and end apart: 33 -> 30, of which waited for: 13 -> 14; matrix products, arithmetic and copies ran while one was open for 0% -> 0% of each run, Pallas kernels for 37% -> 36%
where the time goes in v13:
time: 113 us
  Pallas kernels  46.4 us (41%)
  starting transfers between devices  33.7 us (30%)
  waiting for transfers between devices  29.8 us (26%)
  local copies, waits for them, and re-layouts  1.67 us (1%)
    ppermute x10, starting transfers between devices, over_z(): return lax.ppermute(block, 'gx', [(z, z ^ k) for z in among])  23.3 us
    ppermute x10, waiting for transfers between devices, over_z(): return lax.ppermute(block, 'gx', [(z, z ^ k) for z in among])  14.6 us
    ppermute x7, waiting for transfers between devices, over_x(): lax.ppermute(block, 'gy', [(i, (i + 2 * k) % n_gy) for i in range(n_gy)])  14.3 us
    pallas_call x1, Pallas kernels, prepare(): pl.pallas_call(functools.partial(prepare_kernel, n_gx, nx, chunks), out_s...  13.6 us
    pallas_call x3, Pallas kernels, gate_up_held(): pl.pallas_call(functools.partial(gate_up_held_kernel, len(after), tile),...  8.73 us
    ppermute x7, starting transfers between devices, over_x(): lax.ppermute(block, 'gy', [(i, (i + 2 * k) % n_gy) for i in range(n_gy)])  8 us
    pallas_call x1, Pallas kernels, gate_up(): pl.pallas_call(functools.partial(gate_up_kernel, len(after)), out_shape=[...  6.84 us
    pallas_call x1, Pallas kernels, down(): pl.pallas_call(functools.partial(down_kernel, len(hidden)), out_shape=jax...  6.63 us
  transfers between devices with their start and end apart: 30, of which 14 were waited for; matrix products, arithmetic and copies ran while one was open for 0% of the time, Pallas kernels for 36%

profile of v13, /device:TPU:0, one launch (start us, length us, event | category | flops | bytes accessed | tf_op | source)
XLA Modules:
  0.0 112.6 jit_solution(16668452241717207422)
XLA Ops:
  0.0 3.0 %collective-permute-start = (bf16[64,2048]{1,0:T(8,128)(2,1)}, bf16[64,2048]{1,0:T(8,128)(2,1)S(1)}, u32[]{:S(2)}, u32[]{:S(2)}) collective-permute-start(bf16[64,2048]{1,0:T(8,128)(2,1)} %tok_ref.1), channel_id=1, source_target_pairs={{0,4},{4,0},{8,12},{12,8},{1,5},{5,1},{9,13},{13,9},{2,6},{6,2},{1... | collective-permute-start | bytes 786440 | tf_op jit(solution)/shard_map/ppermute | solution.py:372
  3.0 2.6 %collective-permute-start.2 = (bf16[64,2048]{1,0:T(8,128)(2,1)}, bf16[64,2048]{1,0:T(8,128)(2,1)S(1)}, u32[]{:S(2)}, u32[]{:S(2)}) collective-permute-start(bf16[64,2048]{1,0:T(8,128)(2,1)} %tok_ref.1), channel_id=1, source_target_pairs={{0,8},{4,12},{8,0},{12,4},{1,9},{5,13},{9,1},{13,5},{2,10},{6,14},... | collective-permute-start | bytes 786440 | tf_op jit(solution)/shard_map/ppermute | solution.py:372
  7.3 13.6 %prepare.1 = (bf16[192,256]{1,0:T(8,128)(2,1)S(1)}, bf16[256,192]{1,0:T(8,128)(2,1)S(1)}, bf16[64,2048]{1,0:T(8,128)(2,1)S(1)}, bf16[2048,1536]{1,0:T(8,128)(2,1...) custom-call(s32[4]{0:T(128)S(1)} %copy-done.1, ...), custom_call_target="tpu_custom_call" | custom-call | tf_op jit(solution)/shard_map/prepare/pallas_call | solution.py:73
  20.9 3.7 %collective-permute-done.2.refs_3_ = bf16[64,2048]{1,0:T(8,128)(2,1)S(1)} collective-permute-done((bf16[64,2048]{1,0:T(8,128)(2,1)}, bf16[64,2048]{1,0:T(8,128)(2,1)S(1)}, u32[]{:S(2)}, u32[]{:S(2)}) %collective-permute-start.2) | collective-permute-done | bytes 262176 | tf_op jit(solution)/shard_map/ppermute | solution.py:372
  25.0 2.6 %gate_up_held.3 = (f32[2,96,1536]{2,1,0:T(8,128)S(1)}, bf16[2,96,1536]{2,1,0:T(8,128)(2,1)S(1)}) custom-call(bf16[192,2048]{1,0:T(8,128)(2,1)S(1)} %compact.1.tok_ref, bf16[2048,1536]{1,0:T(8,128)(2,1)S(1)} %get-tuple-element.61.gate_ref, bf16[2048,1536]{1,0:T(8,128)(2,1)S(1)} %get-tuple-element.62.up_ref), custom_call_target="tpu_custom_call" | custom-call | tf_op jit(solution)/shard_map/gate_up_held/pallas_call | solution.py:138
  27.7 2.6 %gate_up_held.4 = (f32[2,96,1536]{2,1,0:T(8,128)S(1)}, bf16[2,96,1536]{2,1,0:T(8,128)(2,1)S(1)}) custom-call(bf16[192,2048]{1,0:T(8,128)(2,1)S(1)} %compact.1.tok_ref, bf16[2048,1536]{1,0:T(8,128)(2,1)S(1)} %get-tuple-element.65.gate_ref, bf16[2048,1536]{1,0:T(8,128)(2,1)S(1)} %get-tuple-element.66.up_ref), custom_call_target="tpu_custom_call" | custom-call | tf_op jit(solution)/shard_map/gate_up_held/pallas_call | solution.py:138
  32.7 1.6 %collective-permute-start.6 = (bf16[2,48,1536]{2,1,0:T(8,128)(2,1)S(1)}, bf16[2,48,1536]{2,1,0:T(8,128)(2,1)S(1)}, u32[]{:S(2)}, u32[]{:S(2)}) collective-permute-start(bf16[2,48,1536]{2,1,0:T(8,128)(2,1)S(1)} %get-tuple-element.71.refs_1_), channel_id=1, source_target_pairs={{0,2},{1,3},{2,0},{3,1},{4,6},{5,7},{6,4},{7,5},{8,10},{9,11},{10,... | collective-permute-start | bytes 884744 | tf_op jit(solution)/shard_map/ppermute | solution.py:378
  34.3 3.5 %gate_up_held.5 = (f32[2,96,2048]{2,1,0:T(8,128)S(1)}, bf16[2,96,2048]{2,1,0:T(8,128)(2,1)S(1)}) custom-call(bf16[192,2048]{1,0:T(8,128)(2,1)S(1)} %compact.1.tok_ref, bf16[2048,2048]{1,0:T(8,128)(2,1)S(1)} %get-tuple-element.59.gate_ref, bf16[2048,2048]{1,0:T(8,128)(2,1)S(1)} %get-tuple-element.60.up_ref, ...), custom_call_target="tpu_custom_call" | custom-call | tf_op jit(solution)/shard_map/gate_up_held/pallas_call | solution.py:138
  37.8 6.8 %gate_up.1 = (f32[2,96,1536]{2,1,0:T(8,128)S(1)}, bf16[48,1536]{1,0:T(8,128)(2,1)S(1)}, bf16[48,1536]{1,0:T(8,128)(2,1)S(1)}, bf16[48,1536]{1,0:T(8,128)(2,1)S(1)}, bf16[48,1536]{1,0:T(8,128)(2,1)S(1)}) custom-call(bf16[192,2048]{1,0:T(8,128)(2,1)S(1)} %compact.1.tok_ref, bf16[2048,6656]{1,0:T(8,128)(2,1)} %gate_ref.3, bf16[2048,6656]{1,0:T(8,128)(2,1)} %up_ref.3, ...), custom_call_target="tpu_custom_call" | custom-call | tf_op jit(solution)/shard_map/gate_up/pallas_call | solution.py:162
  44.7 1.7 %collective-permute-done.6.refs_3_ = bf16[2,48,1536]{2,1,0:T(8,128)(2,1)S(1)} collective-permute-done((bf16[2,48,1536]{2,1,0:T(8,128)(2,1)S(1)}, bf16[2,48,1536]{2,1,0:T(8,128)(2,1)S(1)}, u32[]{:S(2)}, u32[]{:S(2)}) %collective-permute-start.6) | collective-permute-done | bytes 294944 | tf_op jit(solution)/shard_map/ppermute | solution.py:378
  48.2 5.2 %fetch.1 = (bf16[2048,2048]{1,0:T(8,128)(2,1)S(1)}, bf16[1536,2048]{1,0:T(8,128)(2,1)S(1)}) custom-call(bf16[6656,2048]{1,0:T(8,128)(2,1)} %refs_4_.1, bf16[48,3072]{1,0:T(8,128)(2,1)S(1)} %get-tuple-element.86.refs_0_), custom_call_target="tpu_custom_call" | custom-call | tf_op jit(solution)/shard_map/fetch/pallas_call | solution.py:308
  57.5 1.6 %collective-permute-start.12 = (bf16[2,48,1536]{2,1,0:T(8,128)(2,1)S(1)}, bf16[2,48,1536]{2,1,0:T(8,128)(2,1)S(1)}, u32[]{:S(2)}, u32[]{:S(2)}) collective-permute-start(bf16[2,48,1536]{2,1,0:T(8,128)(2,1)S(1)} %get-tuple-element.93.refs_5_), channel_id=1, source_target_pairs={{0,2},{1,3},{2,0},{3,1},{4,6},{5,7},{6,4},{7,5},{8,10},{9,11},{10,... | collective-permute-start | bytes 884744 | tf_op jit(solution)/shard_map/ppermute | solution.py:378
  59.2 6.6 %down.1.refs_2_.refs_5_ = f32[192,2048]{1,0:T(8,128)S(1)} custom-call(bf16[48,3072]{1,0:T(8,128)(2,1)S(1)} %get-tuple-element.86.refs_0_, bf16[48,3072]{1,0:T(8,128)(2,1)S(1)} %collective-permute-done.17.refs_1_, bf16[48,3072]{1,0:T(8,128)(2,1)S(1)} %collective-permute-done.18.refs_2_, bf16[48,3072]{1,0:T(8,128)(2,1)S(1)} %collective-permute-done.19.refs_3_, ...), custom_call_target="tpu_custom_call" | custom-call | tf_op jit(solution)/shard_map/down/pallas_call | solution.py:279
  66.8 5.6 %collective-permute-done.12.refs_1_ = bf16[2,48,1536]{2,1,0:T(8,128)(2,1)S(1)} collective-permute-done((bf16[2,48,1536]{2,1,0:T(8,128)(2,1)S(1)}, bf16[2,48,1536]{2,1,0:T(8,128)(2,1)S(1)}, u32[]{:S(2)}, u32[]{:S(2)}) %collective-permute-start.12) | collective-permute-done | bytes 294944 | tf_op jit(solution)/shard_map/ppermute | solution.py:378
  73.1 3.5 %collective-permute-done.20.refs_1_ = bf16[48,2048]{1,0:T(8,128)(2,1)S(1)} collective-permute-done((bf16[48,2048]{1,0:T(8,128)(2,1)S(1)}, bf16[48,2048]{1,0:T(8,128)(2,1)S(1)}, u32[]{:S(2)}, u32[]{:S(2)}) %collective-permute-start.20) | collective-permute-done | bytes 196640 | tf_op jit(solution)/shard_map/ppermute | solution.py:378
  77.1 1.9 %collective-permute-done.13.refs_1_ = bf16[48,1536]{1,0:T(8,128)(2,1)S(1)} collective-permute-done((bf16[48,1536]{1,0:T(8,128)(2,1)S(1)}, bf16[48,1536]{1,0:T(8,128)(2,1)S(1)}, u32[]{:S(2)}, u32[]{:S(2)}) %collective-permute-start.13) | collective-permute-done | bytes 147488 | tf_op jit(solution)/shard_map/ppermute | solution.py:378
  79.0 1.8 %down_held.2.refs_5_ = f32[192,2048]{1,0:T(8,128)S(1)} custom-call(bf16[48,2048]{1,0:T(8,128)(2,1)S(1)} %activate.5.refs_0_, bf16[48,2048]{1,0:T(8,128)(2,1)S(1)} %collective-permute-done.20.refs_1_, bf16[48,2048]{1,0:T(8,128)(2,1)S(1)} %collective-permute-done.21.refs_2_, bf16[48,2048]{1,0:T(8,128)(2,1)S(1)} %collective-permute-done.22.refs_3_, ...), custom_call_target="tpu_custom_call" | custom-call | tf_op jit(solution)/shard_map/down_held/pallas_call | solution.py:342
  80.9 2.2 %down_held.3 = (bf16[64,2048]{1,0:T(8,128)(2,1)S(1)}, bf16[64,2048]{1,0:T(8,128)(2,1)S(1)}, bf16[32,2048]{1,0:T(8,128)(2,1)S(1)}, bf16[32,2048]{1,0:T(8,128)(2,1...) custom-call(bf16[48,1536]{1,0:T(8,128)(2,1)S(1)} %activate.4.refs_0_, ...), custom_call_target="tpu_custom_call" | custom-call | tf_op jit(solution)/shard_map/down_held/pallas_call | solution.py:342
  83.8 9.5 %collective-permute-start.27 = (bf16[32,2048]{1,0:T(8,128)(2,1)S(1)}, bf16[32,2048]{1,0:T(8,128)(2,1)S(1)}, u32[]{:S(2)}, u32[]{:S(2)}) collective-permute-start(bf16[32,2048]{1,0:T(8,128)(2,1)S(1)} %get-tuple-element.107), channel_id=1, source_target_pairs={{0,4},{12,8},{1,5},{13,9},{2,6},{14,10},{3,7},{15,11},{16,20},{28,... | collective-permute-start | bytes 393224 | tf_op jit(solution)/shard_map/ppermute | solution.py:372
  94.5 2.5 %collective-permute-done.27.got_ref = bf16[32,2048]{1,0:T(8,128)(2,1)S(1)} collective-permute-done((bf16[32,2048]{1,0:T(8,128)(2,1)S(1)}, bf16[32,2048]{1,0:T(8,128)(2,1)S(1)}, u32[]{:S(2)}, u32[]{:S(2)}) %collective-permute-start.27) | collective-permute-done | bytes 131104 | tf_op jit(solution)/shard_map/ppermute | solution.py:372
  97.1 2.4 %collective-permute-start.28 = (bf16[32,2048]{1,0:T(8,128)(2,1)S(1)}, bf16[32,2048]{1,0:T(8,128)(2,1)S(1)}, u32[]{:S(2)}, u32[]{:S(2)}) collective-permute-start(bf16[32,2048]{1,0:T(8,128)(2,1)S(1)} %relay.3), channel_id=1, source_target_pairs={{0,8},{4,12},{8,0},{12,4},{1,9},{5,13},{9,1},{13,5},{2,10},{6,14},... | collective-permute-start | bytes 393224 | tf_op jit(solution)/shard_map/ppermute | solution.py:372
  99.9 2.5 %collective-permute-start.25 = (bf16[32,2048]{1,0:T(8,128)(2,1)S(1)}, bf16[32,2048]{1,0:T(8,128)(2,1)S(1)}, u32[]{:S(2)}, u32[]{:S(2)}) collective-permute-start(bf16[32,2048]{1,0:T(8,128)(2,1)S(1)} %get-tuple-element.104), channel_id=1, source_target_pairs={{0,4},{4,0},{8,12},{12,8},{1,5},{5,1},{9,13},{13,9},{2,6},{6,2},{1... | collective-permute-start | bytes 393224 | tf_op jit(solution)/shard_map/ppermute | solution.py:372
  104.8 5.2 %collective-permute-done.25 = bf16[32,2048]{1,0:T(8,128)(2,1)S(1)} collective-permute-done((bf16[32,2048]{1,0:T(8,128)(2,1)S(1)}, bf16[32,2048]{1,0:T(8,128)(2,1)S(1)}, u32[]{:S(2)}, u32[]{:S(2)}) %collective-permute-start.25) | collective-permute-done | bytes 131104 | tf_op jit(solution)/shard_map/ppermute | solution.py:372
  110.0 1.8 %collective-permute-done.26 = bf16[32,2048]{1,0:T(8,128)(2,1)S(1)} collective-permute-done((bf16[32,2048]{1,0:T(8,128)(2,1)S(1)}, bf16[32,2048]{1,0:T(8,128)(2,1)S(1)}, u32[]{:S(2)}, u32[]{:S(2)}) %collective-permute-start.26) | collective-permute-done | bytes 131104 | tf_op jit(solution)/shard_map/ppermute | solution.py:372
  (60 shorter events, 18.3 us)
Async XLA Ops:
  0.0 20.9 %collective-permute-start = (bf16[64,2048]{1,0:T(8,128)(2,1)}, bf16[64,2048]{1,0:T(8,128)(2,1)S(1)}, u32[]{:S(2)}, u32[]{:S(2)}) collective-permute-start(bf16[64,2048]{1,0:T(8,128)(2,1)} %tok_ref.1), channel_id=1, source_target_pairs={{0,4},{4,0},{8,12},{12,8},{1,5},{5,1},{9,13},{13,9},{2,6},{6,2},{1... | collective-permute-start | bytes 786440 | tf_op jit(solution)/shard_map/ppermute | solution.py:372
  3.0 21.6 %collective-permute-start.2 = (bf16[64,2048]{1,0:T(8,128)(2,1)}, bf16[64,2048]{1,0:T(8,128)(2,1)S(1)}, u32[]{:S(2)}, u32[]{:S(2)}) collective-permute-start(bf16[64,2048]{1,0:T(8,128)(2,1)} %tok_ref.1), channel_id=1, source_target_pairs={{0,8},{4,12},{8,0},{12,4},{1,9},{5,13},{9,1},{13,5},{2,10},{6,14},... | collective-permute-start | bytes 786440 | tf_op jit(solution)/shard_map/ppermute | solution.py:372
  5.6 19.0 %collective-permute-start.1 = (bf16[64,2048]{1,0:T(8,128)(2,1)}, bf16[64,2048]{1,0:T(8,128)(2,1)S(1)}, u32[]{:S(2)}, u32[]{:S(2)}) collective-permute-start(bf16[64,2048]{1,0:T(8,128)(2,1)} %tok_ref.1), channel_id=1, source_target_pairs={{0,12},{4,8},{8,4},{12,0},{1,13},{5,9},{9,5},{13,1},{2,14},{6,10},... | collective-permute-start | bytes 786440 | tf_op jit(solution)/shard_map/ppermute | solution.py:372
  27.6 2.7 %collective-permute-start.3 = (bf16[2,96,1536]{2,1,0:T(8,128)(2,1)S(1)}, bf16[2,96,1536]{2,1,0:T(8,128)(2,1)S(1)}, u32[]{:S(2)}, u32[]{:S(2)}) collective-permute-start(bf16[2,96,1536]{2,1,0:T(8,128)(2,1)S(1)} %get-tuple-element.64), channel_id=1, source_target_pairs={{0,1},{1,0},{2,3},{3,2},{4,5},{5,4},{6,7},{7,6},{8,9},{9,8},{10,11... | collective-permute-start | bytes 1769480 | tf_op jit(solution)/shard_map/ppermute | solution.py:375
  31.0 13.6 %collective-permute-start.5 = (bf16[2,48,1536]{2,1,0:T(8,128)(2,1)S(1)}, bf16[2,48,1536]{2,1,0:T(8,128)(2,1)S(1)}, u32[]{:S(2)}, u32[]{:S(2)}) collective-permute-start(bf16[2,48,1536]{2,1,0:T(8,128)(2,1)S(1)} %get-tuple-element.68.refs_0_), channel_id=1, source_target_pairs={{0,2},{1,3},{2,0},{3,1},{4,6},{5,7},{6,4},{7,5},{8,10},{9,11},{10,... | collective-permute-start | bytes 884744 | tf_op jit(solution)/shard_map/ppermute | solution.py:378
  32.7 13.6 %collective-permute-start.6 = (bf16[2,48,1536]{2,1,0:T(8,128)(2,1)S(1)}, bf16[2,48,1536]{2,1,0:T(8,128)(2,1)S(1)}, u32[]{:S(2)}, u32[]{:S(2)}) collective-permute-start(bf16[2,48,1536]{2,1,0:T(8,128)(2,1)S(1)} %get-tuple-element.71.refs_1_), channel_id=1, source_target_pairs={{0,2},{1,3},{2,0},{3,1},{4,6},{5,7},{6,4},{7,5},{8,10},{9,11},{10,... | collective-permute-start | bytes 884744 | tf_op jit(solution)/shard_map/ppermute | solution.py:378
  46.6 6.8 %collective-permute-start.7 = (bf16[2,96,2048]{2,1,0:T(8,128)(2,1)S(1)}, bf16[2,96,2048]{2,1,0:T(8,128)(2,1)S(1)}, u32[]{:S(2)}, u32[]{:S(2)}) collective-permute-start(bf16[2,96,2048]{2,1,0:T(8,128)(2,1)S(1)} %get-tuple-element.81), channel_id=1, source_target_pairs={{0,1},{1,0},{2,3},{3,2},{4,5},{5,4},{6,7},{7,6},{8,9},{9,8},{10,11... | collective-permute-start | bytes 2359304 | tf_op jit(solution)/shard_map/ppermute | solution.py:375
  46.6 9.4 %collective-permute-start.17 = (bf16[48,3072]{1,0:T(8,128)(2,1)S(1)}, bf16[48,3072]{1,0:T(8,128)(2,1)S(1)}, u32[]{:S(2)}, u32[]{:S(2)}) collective-permute-start(bf16[48,3072]{1,0:T(8,128)(2,1)S(1)} %get-tuple-element.86.refs_0_), channel_id=1, source_target_pairs={{0,2},{1,3},{2,0},{3,1},{4,6},{5,7},{6,4},{7,5},{8,10},{9,11},{10,... | collective-permute-start | bytes 884744 | tf_op jit(solution)/shard_map/ppermute | solution.py:378
  53.8 2.8 %collective-permute-start.9 = (bf16[48,1536]{1,0:T(8,128)(2,1)S(1)}, bf16[48,1536]{1,0:T(8,128)(2,1)S(1)}, u32[]{:S(2)}, u32[]{:S(2)}) collective-permute-start(bf16[48,1536]{1,0:T(8,128)(2,1)S(1)} %get-tuple-element.89), channel_id=1, source_target_pairs={{0,1},{1,0},{2,3},{3,2},{4,5},{5,4},{6,7},{7,6},{8,9},{9,8},{10,11... | collective-permute-start | bytes 442376 | tf_op jit(solution)/shard_map/ppermute | solution.py:375
  54.1 12.0 %collective-permute-start.16 = (bf16[2,48,2048]{2,1,0:T(8,128)(2,1)S(1)}, bf16[2,48,2048]{2,1,0:T(8,128)(2,1)S(1)}, u32[]{:S(2)}, u32[]{:S(2)}) collective-permute-start(bf16[2,48,2048]{2,1,0:T(8,128)(2,1)S(1)} %get-tuple-element.96), channel_id=1, source_target_pairs={{0,2},{1,3},{2,0},{3,1},{4,6},{5,7},{6,4},{7,5},{8,10},{9,11},{10,... | collective-permute-start | bytes 1179656 | tf_op jit(solution)/shard_map/ppermute | solution.py:378
  56.1 3.1 %collective-permute-start.18 = (bf16[48,3072]{1,0:T(8,128)(2,1)S(1)}, bf16[48,3072]{1,0:T(8,128)(2,1)S(1)}, u32[]{:S(2)}, u32[]{:S(2)}) collective-permute-start(bf16[48,3072]{1,0:T(8,128)(2,1)S(1)} %get-tuple-element.86.refs_0_), channel_id=1, source_target_pairs={{0,1},{1,0},{2,3},{3,2},{4,5},{5,4},{6,7},{7,6},{8,9},{9,8},{10,11... | collective-permute-start | bytes 884744 | tf_op jit(solution)/shard_map/ppermute | solution.py:375
  56.6 2.6 %collective-permute-start.19 = (bf16[48,3072]{1,0:T(8,128)(2,1)S(1)}, bf16[48,3072]{1,0:T(8,128)(2,1)S(1)}, u32[]{:S(2)}, u32[]{:S(2)}) collective-permute-start(bf16[48,3072]{1,0:T(8,128)(2,1)S(1)} %collective-permute-done.17.refs_1_), channel_id=1, source_target_pairs={{0,1},{1,0},{2,3},{3,2},{4,5},{5,4},{6,7},{7,6},{8,9},{9,8},{10,11... | collective-permute-start | bytes 884744 | tf_op jit(solution)/shard_map/ppermute | solution.py:375
  57.5 14.9 %collective-permute-start.12 = (bf16[2,48,1536]{2,1,0:T(8,128)(2,1)S(1)}, bf16[2,48,1536]{2,1,0:T(8,128)(2,1)S(1)}, u32[]{:S(2)}, u32[]{:S(2)}) collective-permute-start(bf16[2,48,1536]{2,1,0:T(8,128)(2,1)S(1)} %get-tuple-element.93.refs_5_), channel_id=1, source_target_pairs={{0,2},{1,3},{2,0},{3,1},{4,6},{5,7},{6,4},{7,5},{8,10},{9,11},{10,... | collective-permute-start | bytes 884744 | tf_op jit(solution)/shard_map/ppermute | solution.py:378
  66.2 10.4 %collective-permute-start.20 = (bf16[48,2048]{1,0:T(8,128)(2,1)S(1)}, bf16[48,2048]{1,0:T(8,128)(2,1)S(1)}, u32[]{:S(2)}, u32[]{:S(2)}) collective-permute-start(bf16[48,2048]{1,0:T(8,128)(2,1)S(1)} %activate.5.refs_0_), channel_id=1, source_target_pairs={{0,2},{1,3},{2,0},{3,1},{4,6},{5,7},{6,4},{7,5},{8,10},{9,11},{10,... | collective-permute-start | bytes 589832 | tf_op jit(solution)/shard_map/ppermute | solution.py:378
  72.5 6.5 %collective-permute-start.13 = (bf16[48,1536]{1,0:T(8,128)(2,1)S(1)}, bf16[48,1536]{1,0:T(8,128)(2,1)S(1)}, u32[]{:S(2)}, u32[]{:S(2)}) collective-permute-start(bf16[48,1536]{1,0:T(8,128)(2,1)S(1)} %activate.4.refs_0_), channel_id=1, source_target_pairs={{0,2},{1,3},{2,0},{3,1},{4,6},{5,7},{6,4},{7,5},{8,10},{9,11},{10,... | collective-permute-start | bytes 442376 | tf_op jit(solution)/shard_map/ppermute | solution.py:378
  73.1 5.9 %collective-permute-start.21 = (bf16[48,2048]{1,0:T(8,128)(2,1)S(1)}, bf16[48,2048]{1,0:T(8,128)(2,1)S(1)}, u32[]{:S(2)}, u32[]{:S(2)}) collective-permute-start(bf16[48,2048]{1,0:T(8,128)(2,1)S(1)} %activate.5.refs_0_), channel_id=1, source_target_pairs={{0,1},{1,0},{2,3},{3,2},{4,5},{5,4},{6,7},{7,6},{8,9},{9,8},{10,11... | collective-permute-start | bytes 589832 | tf_op jit(solution)/shard_map/ppermute | solution.py:375
  76.6 4.2 %collective-permute-start.14 = (bf16[48,1536]{1,0:T(8,128)(2,1)S(1)}, bf16[48,1536]{1,0:T(8,128)(2,1)S(1)}, u32[]{:S(2)}, u32[]{:S(2)}) collective-permute-start(bf16[48,1536]{1,0:T(8,128)(2,1)S(1)} %activate.4.refs_0_), channel_id=1, source_target_pairs={{0,1},{1,0},{2,3},{3,2},{4,5},{5,4},{6,7},{7,6},{8,9},{9,8},{10,11... | collective-permute-start | bytes 442376 | tf_op jit(solution)/shard_map/ppermute | solution.py:375
  83.1 16.8 %collective-permute-start.24 = (bf16[64,2048]{1,0:T(8,128)(2,1)S(1)}, bf16[64,2048]{1,0:T(8,128)(2,1)S(1)}, u32[]{:S(2)}, u32[]{:S(2)}) collective-permute-start(bf16[64,2048]{1,0:T(8,128)(2,1)S(1)} %get-tuple-element.103), channel_id=1, source_target_pairs={{4,8},{8,4},{5,9},{9,5},{6,10},{10,6},{7,11},{11,7},{20,24},{24,20... | collective-permute-start | bytes 786440 | tf_op jit(solution)/shard_map/ppermute | solution.py:372
  83.8 13.3 %collective-permute-start.27 = (bf16[32,2048]{1,0:T(8,128)(2,1)S(1)}, bf16[32,2048]{1,0:T(8,128)(2,1)S(1)}, u32[]{:S(2)}, u32[]{:S(2)}) collective-permute-start(bf16[32,2048]{1,0:T(8,128)(2,1)S(1)} %get-tuple-element.107), channel_id=1, source_target_pairs={{0,4},{12,8},{1,5},{13,9},{2,6},{14,10},{3,7},{15,11},{16,20},{28,... | collective-permute-start | bytes 393224 | tf_op jit(solution)/shard_map/ppermute | solution.py:372
  93.2 6.6 %collective-permute-start.23 = (bf16[32,2048]{1,0:T(8,128)(2,1)S(1)}, bf16[32,2048]{1,0:T(8,128)(2,1)S(1)}, u32[]{:S(2)}, u32[]{:S(2)}) collective-permute-start(bf16[32,2048]{1,0:T(8,128)(2,1)S(1)} %get-tuple-element.100), channel_id=1, source_target_pairs={{0,4},{12,8},{1,5},{13,9},{2,6},{14,10},{3,7},{15,11},{16,20},{28,... | collective-permute-start | bytes 393224 | tf_op jit(solution)/shard_map/ppermute | solution.py:372
  97.1 7.7 %collective-permute-start.28 = (bf16[32,2048]{1,0:T(8,128)(2,1)S(1)}, bf16[32,2048]{1,0:T(8,128)(2,1)S(1)}, u32[]{:S(2)}, u32[]{:S(2)}) collective-permute-start(bf16[32,2048]{1,0:T(8,128)(2,1)S(1)} %relay.3), channel_id=1, source_target_pairs={{0,8},{4,12},{8,0},{12,4},{1,9},{5,13},{9,1},{13,5},{2,10},{6,14},... | collective-permute-start | bytes 393224 | tf_op jit(solution)/shard_map/ppermute | solution.py:372
  99.9 10.1 %collective-permute-start.25 = (bf16[32,2048]{1,0:T(8,128)(2,1)S(1)}, bf16[32,2048]{1,0:T(8,128)(2,1)S(1)}, u32[]{:S(2)}, u32[]{:S(2)}) collective-permute-start(bf16[32,2048]{1,0:T(8,128)(2,1)S(1)} %get-tuple-element.104), channel_id=1, source_target_pairs={{0,4},{4,0},{8,12},{12,8},{1,5},{5,1},{9,13},{13,9},{2,6},{6,2},{1... | collective-permute-start | bytes 393224 | tf_op jit(solution)/shard_map/ppermute | solution.py:372
  102.5 9.3 %collective-permute-start.26 = (bf16[32,2048]{1,0:T(8,128)(2,1)S(1)}, bf16[32,2048]{1,0:T(8,128)(2,1)S(1)}, u32[]{:S(2)}, u32[]{:S(2)}) collective-permute-start(bf16[32,2048]{1,0:T(8,128)(2,1)S(1)} %get-tuple-element.105), channel_id=1, source_target_pairs={{0,4},{4,0},{8,12},{12,8},{1,5},{5,1},{9,13},{13,9},{2,6},{6,2},{1... | collective-permute-start | bytes 393224 | tf_op jit(solution)/shard_map/ppermute | solution.py:372
  102.5 9.3 %collective-permute-start.29 = (bf16[32,2048]{1,0:T(8,128)(2,1)S(1)}, bf16[32,2048]{1,0:T(8,128)(2,1)S(1)}, u32[]{:S(2)}, u32[]{:S(2)}) collective-permute-start(bf16[32,2048]{1,0:T(8,128)(2,1)S(1)} %get-tuple-element.108), channel_id=1, source_target_pairs={{0,8},{4,12},{8,0},{12,4},{1,9},{5,13},{9,1},{13,5},{2,10},{6,14},... | collective-permute-start | bytes 393224 | tf_op jit(solution)/shard_map/ppermute | solution.py:372
  (8 other events, 14.0 us)

commit v14 on v12

--- a/solution.py
+++ b/solution.py
@@ -33,14 +33,51 @@
     return rows
 
 
-def prepare_kernel(n_gx, nx, chunks, lengths_ref, tok_ref, gate_ref, up_ref, in_ref, out_ref, held_ref, *refs):
-    outs, sems = refs[:-1], refs[-1]
+def start_copies(chunks, gate_ref, up_ref, outs, sems):
     copies = []
     for i, (start, width) in enumerate(chunks):
         for k, src in enumerate((gate_ref, up_ref)):
             copies.append(pltpu.make_async_copy(src.at[:, pl.ds(start, width)], outs[2 * i + k], sems.at[2 * i + k]))
     for copy in copies:
         copy.start()
+    return copies
+
+
+def fetch_columns_kernel(n_after, chunk, gate_ref, up_ref, *refs):
+    for copy in start_copies([chunk], gate_ref, up_ref, refs[n_after:-1], refs[-1]):
+        copy.wait()
+
+
+def fetch_columns(gate_weight, up_weight, chunk, after):
+    held, anywhere = pl.BlockSpec(memory_space=pltpu.VMEM), pl.BlockSpec(memory_space=pl.ANY)
+    return pl.pallas_call(
+        functools.partial(fetch_columns_kernel, len(after), chunk),
+        out_shape=[jax.ShapeDtypeStruct((gate_weight.shape[0], chunk[1]), BF16)] * 2,
+        in_specs=[anywhere] * (2 + len(after)),
+        out_specs=[held] * 2,
+        scratch_shapes=[pltpu.SemaphoreType.DMA((2,))],
+        cost_estimate=pl.CostEstimate(flops=0, bytes_accessed=0, transcendentals=0),
+        compiler_params=pltpu.CompilerParams(vmem_limit_bytes=6 * MIB),
+        name="fetch_columns",
+    )(gate_weight, up_weight, *after)
+
+
+def follow(handed, after):
+    anywhere = pl.BlockSpec(memory_space=pl.ANY)
+    return pl.pallas_call(
+        lambda *refs: None,
+        out_shape=jax.ShapeDtypeStruct(handed.shape, handed.dtype),
+        in_specs=[anywhere] * (1 + len(after)),
+        out_specs=anywhere,
+        input_output_aliases={0: 0},
+        compiler_params=pltpu.CompilerParams(vmem_limit_bytes=4 * MIB),
+        cost_estimate=pl.CostEstimate(flops=0, bytes_accessed=0, transcendentals=0),
+        name="follow",
+    )(handed, *after)
+
+
+def prepare_kernel(n_gx, nx, chunks, lengths_ref, tok_ref, gate_ref, up_ref, in_ref, out_ref, held_ref, *refs):
+    copies = start_copies(chunks, gate_ref, up_ref, refs[:-1], refs[-1])
     held_ref[...] = tok_ref[...]
     tok_dev = tok_ref.shape[0]
     z = lax.axis_index("gx")
@@ -82,19 +119,30 @@
     return out[0], out[1], out[2], [out[3 + 2 * i:5 + 2 * i] for i in range(len(chunks))]
 
 
-def compact_kernel(pick_ref, *refs):
-    rows = jnp.concatenate([r[...] for r in refs[:-1]], axis=0)
+def compact_kernel(sizes, pick_ref, *refs):
+    refs = list(refs)
+    blocks = []
+    for n in sizes:
+        block = refs.pop(0)[...]
+        for _ in range(n - 1):
+            block = block + refs.pop(0)[...]
+        blocks.append(block)
+    rows = jnp.concatenate(blocks, axis=0)
     refs[-1][...] = jnp.dot(pick_ref[...], rows, preferred_element_type=F32).astype(BF16)
 
 
-def compact(pick, blocks):
-    return pl.pallas_call(
-        compact_kernel,
-        out_shape=jax.ShapeDtypeStruct((pick.shape[0], blocks[0].shape[1]), BF16),
+def compact(pick, blocks, after):
+    held, anywhere = pl.BlockSpec(memory_space=pltpu.VMEM), pl.BlockSpec(memory_space=pl.ANY)
+    flat = [b for block in blocks for b in block]
+    return pl.pallas_call(
+        functools.partial(compact_kernel, [len(block) for block in blocks]),
+        out_shape=jax.ShapeDtypeStruct((pick.shape[0], flat[0].shape[1]), BF16),
+        in_specs=[held] * (1 + len(flat)) + [anywhere] * len(after),
+        out_specs=held,
         compiler_params=pltpu.CompilerParams(vmem_limit_bytes=5 * MIB),
         cost_estimate=pl.CostEstimate(flops=0, bytes_accessed=0, transcendentals=0),
         name="compact",
-    )(pick, *blocks)
+    )(pick, *flat, *after)
 
 
 def send_shapes(half, nx, width, split):
@@ -126,14 +174,14 @@
             put_part(i, part, columns, keep_ref, send_refs)
 
 
-def gate_up_held(tok, gate_held, up_held, after, nx, tile, split=False):
+def gate_up_held(tok, gate_held, up_held, after, nx, tile):
     half, width = tok.shape[0] // 2, gate_held.shape[1]
     held, anywhere = pl.BlockSpec(memory_space=pltpu.VMEM), pl.BlockSpec(memory_space=pl.ANY)
     keep, *send = pl.pallas_call(
         functools.partial(gate_up_held_kernel, len(after), tile),
-        out_shape=[jax.ShapeDtypeStruct((2, half, width), F32)] + send_shapes(half, nx, width, split),
+        out_shape=[jax.ShapeDtypeStruct((2, half, width), F32)] + send_shapes(half, nx, width, False),
         in_specs=[held] * 3 + [anywhere] * len(after),
-        out_specs=[held] * (1 + (2 * nx if split else 1)),
+        out_specs=[held] * 2,
         compiler_params=pltpu.CompilerParams(vmem_limit_bytes=6 * MIB),
         cost_estimate=pl.CostEstimate(flops=0, bytes_accessed=0, transcendentals=0),
         name="gate_up_held",
@@ -371,10 +419,19 @@
     def over_x(block, k):
         return lax.ppermute(block, "gy", [(i, (i + 2 * k) % n_gy) for i in range(n_gy)])
 
-    far = [over_z(tokens, k) for k in range(1, n_gx)]
-    pick_in, pick_out, held, weights = prepare(lengths, tokens, gate_weight, up_weight, chunks[:3], n_gx, nx, live)
-    blocks = [held] + far
-    tok = compact(pick_in, blocks)
+    pick_in, pick_out, held, weights = prepare(lengths, tokens, gate_weight, up_weight, chunks[:2], n_gx, nx, live)
+    if line:
+        two = over_z(tokens, 2)
+        one = over_z(tokens, 1)
+        middle = over_z(tokens, 3, (1, 2))
+        two = follow(two, [pick_in])
+        blocks = [[held], [one], [two], [middle, over_z(two, 1, (1, 2))]]
+        ready = [two]
+    else:
+        blocks = [[held]] + [[over_z(tokens, k)] for k in range(1, n_gx)]
+        ready = [pick_in]
+    weights.append(fetch_columns(gate_weight, up_weight, chunks[2], ready))
+    tok = compact(pick_in, blocks, weights[2][:1])
 
     made = [gate_up_held(tok, *weights[i], [], nx, tile) for i in range(2)]
     sends, keeps = [list(a) for a in zip(*made)]
@@ -394,7 +451,7 @@
 
     ready, sends[1] = exchange(0, sends[1], [])
     ready = ready + exchange(1, [], [])[0]
-    made = [gate_up_held(tok, *weights[2], ready, nx, tile, True)]
+    made = [gate_up_held(tok, *weights[2], ready, nx, tile)]
     made.append(gate_up(tok, gate_weight, up_weight, made[0][0][:1], *chunks[3], nx, tile))
     pieces = len(made[0][0])
     hidden, handed = finish(0, 2, made[0][0] + made[1][0], [])

time: 112 us -> 129 us (1.15)
  local copies, waits for them, and re-layouts: 1.64 us -> 21.5 us
  waiting for transfers between devices: 31.7 us -> 25.2 us
  starting transfers between devices: 30.7 us -> 34 us
    unnamed x4 -> x18, local copies, waits for them, and re-layouts: 1.64 us -> 21.5 us
    ppermute x10 -> x11, waiting for transfers between devices: 16.5 us -> 10.1 us  [over_z(): return lax.ppermute(block, 'gx', [(z, z ^ k) for z in among])]
    pallas_call x1 -> x3, Pallas kernels: 0.38 us -> 5.15 us  [the longest x1 4.76 us: fetch_columns(): pl.pallas_call(functools.partial(fetch_columns_kernel, len(after), chunk)...]
    pallas_call x1, Pallas kernels: 13.6 us -> 8.94 us  [prepare(): pl.pallas_call(functools.partial(prepare_kernel, n_gx, nx, chunks), out_s...]
    ppermute x10 -> x11, starting transfers between devices: 19.5 us -> 23.5 us  [over_z(): return lax.ppermute(block, 'gx', [(z, z ^ k) for z in among])]
    ppermute x16 -> x13, starting transfers between devices: 3.37 us -> 2.37 us  [over_core(): return lax.ppermute(block, 'gy', [(i, i ^ 1) for i in range(n_gy)])]
  transfers between devices with their start and end apart: 33 -> 31, of which waited for: 13 -> 12; matrix products, arithmetic and copies ran while one was open for 0% -> 0% of each run, Pallas kernels for 37% -> 32%
where the time goes in v14:
time: 129 us; the launch traced here: 128 us
  Pallas kernels  46.4 us (36%)
  starting transfers between devices  34 us (26%)
  waiting for transfers between devices  25.2 us (20%)
  local copies, waits for them, and re-layouts  21.5 us (17%)
    ppermute x11, starting transfers between devices, over_z(): return lax.ppermute(block, 'gx', [(z, z ^ k) for z in among])  23.5 us
    unnamed x18, local copies, waits for them, and re-layouts  21.5 us
    ppermute x7, waiting for transfers between devices, over_x(): lax.ppermute(block, 'gy', [(i, (i + 2 * k) % n_gy) for i in range(n_gy)])  14.2 us
    ppermute x11, waiting for transfers between devices, over_z(): return lax.ppermute(block, 'gx', [(z, z ^ k) for z in among])  10.1 us
    pallas_call x1, Pallas kernels, prepare(): pl.pallas_call(functools.partial(prepare_kernel, n_gx, nx, chunks), out_s...  8.94 us
    pallas_call x3, Pallas kernels, gate_up_held(): pl.pallas_call(functools.partial(gate_up_held_kernel, len(after), tile),...  8.64 us
    ppermute x7, starting transfers between devices, over_x(): lax.ppermute(block, 'gy', [(i, (i + 2 * k) % n_gy) for i in range(n_gy)])  8.06 us
    pallas_call x1, Pallas kernels, down(): pl.pallas_call(functools.partial(down_kernel, len(hidden)), out_shape=jax...  6.81 us
  transfers between devices with their start and end apart: 31, of which 12 were waited for; matrix products, arithmetic and copies ran while one was open for 0% of the time, Pallas kernels for 32%

profile of v14, /device:TPU:0, one launch (start us, length us, event | category | flops | bytes accessed | tf_op | source)
XLA Modules:
  0.0 128.3 jit_solution(8831081387812464554)
XLA Ops:
  0.0 4.0 %collective-permute-start.1 = (bf16[64,2048]{1,0:T(8,128)(2,1)}, bf16[64,2048]{1,0:T(8,128)(2,1)S(1)}, u32[]{:S(2)}, u32[]{:S(2)}) collective-permute-start(bf16[64,2048]{1,0:T(8,128)(2,1)} %tok_ref.1), channel_id=1, source_target_pairs={{0,8},{4,12},{8,0},{12,4},{1,9},{5,13},{9,1},{13,5},{2,10},{6,14},... | collective-permute-start | bytes 786440 | tf_op jit(solution)/shard_map/ppermute | solution.py:414
  7.9 8.9 %prepare.1 = (bf16[192,256]{1,0:T(8,128)(2,1)S(1)}, bf16[256,192]{1,0:T(8,128)(2,1)S(1)}, bf16[64,2048]{1,0:T(8,128)(2,1)S(1)}, bf16[2048,1536]{1,0:T(8,128)(2,1...) custom-call(s32[4]{0:T(128)S(1)} %copy-done.8, ...), custom_call_target="tpu_custom_call" | custom-call | tf_op jit(solution)/shard_map/prepare/pallas_call | solution.py:104
  16.9 2.7 %copy-done.1 = bf16[2048,1536]{1,0:T(8,128)(2,1)} copy-done((bf16[2048,1536]{1,0:T(8,128)(2,1)}, bf16[2048,1536]{1,0:T(8,128)(2,1)S(1)}, u32[]{:S(2)}) %copy-start.1) | copy-done | bytes 6291480
  19.5 2.7 %copy-done.3 = bf16[2048,1536]{1,0:T(8,128)(2,1)} copy-done((bf16[2048,1536]{1,0:T(8,128)(2,1)}, bf16[2048,1536]{1,0:T(8,128)(2,1)S(1)}, u32[]{:S(2)}) %copy-start.3) | copy-done | bytes 6291480
  24.2 8.7 %copy-done = bf16[2048,6656]{1,0:T(8,128)(2,1)S(1)} copy-done((bf16[2048,6656]{1,0:T(8,128)(2,1)S(1)}, bf16[2048,6656]{1,0:T(8,128)(2,1)}, u32[]{:S(2)}) %copy-start) | copy-done | bytes 27263000
  32.9 4.8 %fetch_columns.1 = (bf16[2048,2048]{1,0:T(8,128)(2,1)S(1)}, bf16[2048,2048]{1,0:T(8,128)(2,1)S(1)}) custom-call(bf16[2048,6656]{1,0:T(8,128)(2,1)S(1)} %copy-done, bf16[2048,6656]{1,0:T(8,128)(2,1)} %up_ref.5, bf16[64,2048]{1,0:T(8,128)(2,1)S(1)} %follow.1.refs_0_.refs_2_), custom_call_target="tpu_custom_call" | custom-call | tf_op jit(solution)/shard_map/fetch_columns/pallas_call | solution.py:53
  38.1 2.4 %copy-done.2 = bf16[2048,1536]{1,0:T(8,128)(2,1)S(1)} copy-done((bf16[2048,1536]{1,0:T(8,128)(2,1)S(1)}, bf16[2048,1536]{1,0:T(8,128)(2,1)}, u32[]{:S(2)}) %copy-start.2) | copy-done | bytes 6291480
  40.5 2.8 %copy-done.4 = bf16[2048,1536]{1,0:T(8,128)(2,1)S(1)} copy-done((bf16[2048,1536]{1,0:T(8,128)(2,1)S(1)}, bf16[2048,1536]{1,0:T(8,128)(2,1)}, u32[]{:S(2)}) %copy-start.4) | copy-done | bytes 6291480
  43.3 2.6 %gate_up_held.3 = (f32[2,96,1536]{2,1,0:T(8,128)S(1)}, bf16[2,96,1536]{2,1,0:T(8,128)(2,1)S(1)}) custom-call(bf16[192,2048]{1,0:T(8,128)(2,1)S(1)} %compact.1.tok_ref, bf16[2048,1536]{1,0:T(8,128)(2,1)S(1)} %copy-done.2, bf16[2048,1536]{1,0:T(8,128)(2,1)S(1)} %copy-done.4), custom_call_target="tpu_custom_call" | custom-call | tf_op jit(solution)/shard_map/gate_up_held/pallas_call | solution.py:180
  46.0 2.6 %gate_up_held.4 = (f32[2,96,1536]{2,1,0:T(8,128)S(1)}, bf16[2,96,1536]{2,1,0:T(8,128)(2,1)S(1)}) custom-call(bf16[192,2048]{1,0:T(8,128)(2,1)S(1)} %compact.1.tok_ref, bf16[2048,1536]{1,0:T(8,128)(2,1)S(1)} %get-tuple-element.65.gate_ref, bf16[2048,1536]{1,0:T(8,128)(2,1)S(1)} %get-tuple-element.66.up_ref), custom_call_target="tpu_custom_call" | custom-call | tf_op jit(solution)/shard_map/gate_up_held/pallas_call | solution.py:180
  52.5 3.4 %gate_up_held.5 = (f32[2,96,2048]{2,1,0:T(8,128)S(1)}, bf16[2,96,2048]{2,1,0:T(8,128)(2,1)S(1)}) custom-call(bf16[192,2048]{1,0:T(8,128)(2,1)S(1)} %compact.1.tok_ref, bf16[2048,2048]{1,0:T(8,128)(2,1)S(1)} %get-tuple-element.59.refs_5_.gate_ref, bf16[2048,2048]{1,0:T(8,128)(2,1)S(1)} %get-tuple-element.60.up_ref, ...), custom_call_target="tpu_custom_call" | custom-call | tf_op jit(solution)/shard_map/gate_up_held/pallas_call | solution.py:180
  56.0 6.7 %gate_up.1 = (f32[2,96,1536]{2,1,0:T(8,128)S(1)}, bf16[48,1536]{1,0:T(8,128)(2,1)S(1)}, bf16[48,1536]{1,0:T(8,128)(2,1)S(1)}, bf16[48,1536]{1,0:T(8,128)(2,1)S(1)}, bf16[48,1536]{1,0:T(8,128)(2,1)S(1)}) custom-call(bf16[192,2048]{1,0:T(8,128)(2,1)S(1)} %compact.1.tok_ref, bf16[2048,6656]{1,0:T(8,128)(2,1)} %gate_ref.5, bf16[2048,6656]{1,0:T(8,128)(2,1)} %up_ref.5, ...), custom_call_target="tpu_custom_call" | custom-call | tf_op jit(solution)/shard_map/gate_up/pallas_call | solution.py:204
  62.7 1.9 %collective-permute-done.7.refs_3_ = bf16[2,48,1536]{2,1,0:T(8,128)(2,1)S(1)} collective-permute-done((bf16[2,48,1536]{2,1,0:T(8,128)(2,1)S(1)}, bf16[2,48,1536]{2,1,0:T(8,128)(2,1)S(1)}, u32[]{:S(2)}, u32[]{:S(2)}) %collective-permute-start.7) | collective-permute-done | bytes 294944 | tf_op jit(solution)/shard_map/ppermute | solution.py:420
  66.4 5.2 %fetch.1 = (bf16[2048,2048]{1,0:T(8,128)(2,1)S(1)}, bf16[1536,2048]{1,0:T(8,128)(2,1)S(1)}) custom-call(bf16[6656,2048]{1,0:T(8,128)(2,1)} %refs_4_.1, bf16[48,3072]{1,0:T(8,128)(2,1)S(1)} %get-tuple-element.86.refs_0_), custom_call_target="tpu_custom_call" | custom-call | tf_op jit(solution)/shard_map/fetch/pallas_call | solution.py:350
  77.4 6.8 %down.1.refs_2_.refs_5_ = f32[192,2048]{1,0:T(8,128)S(1)} custom-call(bf16[48,3072]{1,0:T(8,128)(2,1)S(1)} %get-tuple-element.86.refs_0_, bf16[48,3072]{1,0:T(8,128)(2,1)S(1)} %collective-permute-done.18.refs_1_, bf16[48,3072]{1,0:T(8,128)(2,1)S(1)} %collective-permute-done.19.refs_2_, bf16[48,3072]{1,0:T(8,128)(2,1)S(1)} %collective-permute-done.20.refs_3_, ...), custom_call_target="tpu_custom_call" | custom-call | tf_op jit(solution)/shard_map/down/pallas_call | solution.py:321
  85.1 5.5 %collective-permute-done.13.refs_1_ = bf16[2,48,1536]{2,1,0:T(8,128)(2,1)S(1)} collective-permute-done((bf16[2,48,1536]{2,1,0:T(8,128)(2,1)S(1)}, bf16[2,48,1536]{2,1,0:T(8,128)(2,1)S(1)}, u32[]{:S(2)}, u32[]{:S(2)}) %collective-permute-start.13) | collective-permute-done | bytes 294944 | tf_op jit(solution)/shard_map/ppermute | solution.py:420
  91.4 3.5 %collective-permute-done.21.refs_1_ = bf16[48,2048]{1,0:T(8,128)(2,1)S(1)} collective-permute-done((bf16[48,2048]{1,0:T(8,128)(2,1)S(1)}, bf16[48,2048]{1,0:T(8,128)(2,1)S(1)}, u32[]{:S(2)}, u32[]{:S(2)}) %collective-permute-start.21) | collective-permute-done | bytes 196640 | tf_op jit(solution)/shard_map/ppermute | solution.py:420
  99.1 2.2 %down_held.3 = (bf16[64,2048]{1,0:T(8,128)(2,1)S(1)}, bf16[64,2048]{1,0:T(8,128)(2,1)S(1)}, bf16[32,2048]{1,0:T(8,128)(2,1)S(1)}, bf16[32,2048]{1,0:T(8,128)(2,1...) custom-call(bf16[48,1536]{1,0:T(8,128)(2,1)S(1)} %activate.4.refs_0_, ...), custom_call_target="tpu_custom_call" | custom-call | tf_op jit(solution)/shard_map/down_held/pallas_call | solution.py:384
  102.0 6.9 %collective-permute-start.28 = (bf16[32,2048]{1,0:T(8,128)(2,1)S(1)}, bf16[32,2048]{1,0:T(8,128)(2,1)S(1)}, u32[]{:S(2)}, u32[]{:S(2)}) collective-permute-start(bf16[32,2048]{1,0:T(8,128)(2,1)S(1)} %get-tuple-element.107), channel_id=1, source_target_pairs={{0,4},{12,8},{1,5},{13,9},{2,6},{14,10},{3,7},{15,11},{16,20},{28,... | collective-permute-start | bytes 393224 | tf_op jit(solution)/shard_map/ppermute | solution.py:414
  110.2 2.5 %collective-permute-done.28.got_ref = bf16[32,2048]{1,0:T(8,128)(2,1)S(1)} collective-permute-done((bf16[32,2048]{1,0:T(8,128)(2,1)S(1)}, bf16[32,2048]{1,0:T(8,128)(2,1)S(1)}, u32[]{:S(2)}, u32[]{:S(2)}) %collective-permute-start.28) | collective-permute-done | bytes 131104 | tf_op jit(solution)/shard_map/ppermute | solution.py:414
  112.7 2.9 %collective-permute-start.29 = (bf16[32,2048]{1,0:T(8,128)(2,1)S(1)}, bf16[32,2048]{1,0:T(8,128)(2,1)S(1)}, u32[]{:S(2)}, u32[]{:S(2)}) collective-permute-start(bf16[32,2048]{1,0:T(8,128)(2,1)S(1)} %relay.3), channel_id=1, source_target_pairs={{0,8},{4,12},{8,0},{12,4},{1,9},{5,13},{9,1},{13,5},{2,10},{6,14},... | collective-permute-start | bytes 393224 | tf_op jit(solution)/shard_map/ppermute | solution.py:414
  115.7 2.0 %collective-permute-start.26 = (bf16[32,2048]{1,0:T(8,128)(2,1)S(1)}, bf16[32,2048]{1,0:T(8,128)(2,1)S(1)}, u32[]{:S(2)}, u32[]{:S(2)}) collective-permute-start(bf16[32,2048]{1,0:T(8,128)(2,1)S(1)} %get-tuple-element.104), channel_id=1, source_target_pairs={{0,4},{4,0},{8,12},{12,8},{1,5},{5,1},{9,13},{13,9},{2,6},{6,2},{1... | collective-permute-start | bytes 393224 | tf_op jit(solution)/shard_map/ppermute | solution.py:414
  117.8 2.1 %collective-permute-start.30 = (bf16[32,2048]{1,0:T(8,128)(2,1)S(1)}, bf16[32,2048]{1,0:T(8,128)(2,1)S(1)}, u32[]{:S(2)}, u32[]{:S(2)}) collective-permute-start(bf16[32,2048]{1,0:T(8,128)(2,1)S(1)} %get-tuple-element.108), channel_id=1, source_target_pairs={{0,8},{4,12},{8,0},{12,4},{1,9},{5,13},{9,1},{13,5},{2,10},{6,14},... | collective-permute-start | bytes 393224 | tf_op jit(solution)/shard_map/ppermute | solution.py:414
  121.1 4.6 %collective-permute-done.26 = bf16[32,2048]{1,0:T(8,128)(2,1)S(1)} collective-permute-done((bf16[32,2048]{1,0:T(8,128)(2,1)S(1)}, bf16[32,2048]{1,0:T(8,128)(2,1)S(1)}, u32[]{:S(2)}, u32[]{:S(2)}) %collective-permute-start.26) | collective-permute-done | bytes 131104 | tf_op jit(solution)/shard_map/ppermute | solution.py:414
  (78 shorter events, 29.6 us)
Async XLA Ops:
  0.0 22.2 %collective-permute-start.1 = (bf16[64,2048]{1,0:T(8,128)(2,1)}, bf16[64,2048]{1,0:T(8,128)(2,1)S(1)}, u32[]{:S(2)}, u32[]{:S(2)}) collective-permute-start(bf16[64,2048]{1,0:T(8,128)(2,1)} %tok_ref.1), channel_id=1, source_target_pairs={{0,8},{4,12},{8,0},{12,4},{1,9},{5,13},{9,1},{13,5},{2,10},{6,14},... | collective-permute-start | bytes 786440 | tf_op jit(solution)/shard_map/ppermute | solution.py:414
  4.0 33.7 %collective-permute-start = (bf16[64,2048]{1,0:T(8,128)(2,1)}, bf16[64,2048]{1,0:T(8,128)(2,1)S(1)}, u32[]{:S(2)}, u32[]{:S(2)}) collective-permute-start(bf16[64,2048]{1,0:T(8,128)(2,1)} %tok_ref.1), channel_id=1, source_target_pairs={{0,4},{4,0},{8,12},{12,8},{1,5},{5,1},{9,13},{13,9},{2,6},{6,2},{1... | collective-permute-start | bytes 786440 | tf_op jit(solution)/shard_map/ppermute | solution.py:414
  5.6 32.1 %collective-permute-start.2 = (bf16[64,2048]{1,0:T(8,128)(2,1)}, bf16[64,2048]{1,0:T(8,128)(2,1)S(1)}, u32[]{:S(2)}, u32[]{:S(2)}) collective-permute-start(bf16[64,2048]{1,0:T(8,128)(2,1)} %tok_ref.1), channel_id=1, source_target_pairs={{4,8},{8,4},{5,9},{9,5},{6,10},{10,6},{7,11},{11,7},{20,24},{24,20... | collective-permute-start | bytes 786440 | tf_op jit(solution)/shard_map/ppermute | solution.py:414
  22.9 14.9 %collective-permute-start.3 = (bf16[64,2048]{1,0:T(8,128)(2,1)S(1)}, bf16[64,2048]{1,0:T(8,128)(2,1)S(1)}, u32[]{:S(2)}, u32[]{:S(2)}) collective-permute-start(bf16[64,2048]{1,0:T(8,128)(2,1)S(1)} %follow.1.refs_0_.refs_2_), channel_id=1, source_target_pairs={{4,0},{8,12},{5,1},{9,13},{6,2},{10,14},{7,3},{11,15},{20,16},{24,... | collective-permute-start | bytes 786440 | tf_op jit(solution)/shard_map/ppermute | solution.py:414
  45.9 2.7 %collective-permute-start.4 = (bf16[2,96,1536]{2,1,0:T(8,128)(2,1)S(1)}, bf16[2,96,1536]{2,1,0:T(8,128)(2,1)S(1)}, u32[]{:S(2)}, u32[]{:S(2)}) collective-permute-start(bf16[2,96,1536]{2,1,0:T(8,128)(2,1)S(1)} %get-tuple-element.64), channel_id=1, source_target_pairs={{0,1},{1,0},{2,3},{3,2},{4,5},{5,4},{6,7},{7,6},{8,9},{9,8},{10,11... | collective-permute-start | bytes 1769480 | tf_op jit(solution)/shard_map/ppermute | solution.py:417
  49.2 13.4 %collective-permute-start.6 = (bf16[2,48,1536]{2,1,0:T(8,128)(2,1)S(1)}, bf16[2,48,1536]{2,1,0:T(8,128)(2,1)S(1)}, u32[]{:S(2)}, u32[]{:S(2)}) collective-permute-start(bf16[2,48,1536]{2,1,0:T(8,128)(2,1)S(1)} %get-tuple-element.68.refs_0_), channel_id=1, source_target_pairs={{0,2},{1,3},{2,0},{3,1},{4,6},{5,7},{6,4},{7,5},{8,10},{9,11},{10,... | collective-permute-start | bytes 884744 | tf_op jit(solution)/shard_map/ppermute | solution.py:420
  51.0 13.6 %collective-permute-start.7 = (bf16[2,48,1536]{2,1,0:T(8,128)(2,1)S(1)}, bf16[2,48,1536]{2,1,0:T(8,128)(2,1)S(1)}, u32[]{:S(2)}, u32[]{:S(2)}) collective-permute-start(bf16[2,48,1536]{2,1,0:T(8,128)(2,1)S(1)} %get-tuple-element.71.refs_1_), channel_id=1, source_target_pairs={{0,2},{1,3},{2,0},{3,1},{4,6},{5,7},{6,4},{7,5},{8,10},{9,11},{10,... | collective-permute-start | bytes 884744 | tf_op jit(solution)/shard_map/ppermute | solution.py:420
  64.8 6.8 %collective-permute-start.8 = (bf16[2,96,2048]{2,1,0:T(8,128)(2,1)S(1)}, bf16[2,96,2048]{2,1,0:T(8,128)(2,1)S(1)}, u32[]{:S(2)}, u32[]{:S(2)}) collective-permute-start(bf16[2,96,2048]{2,1,0:T(8,128)(2,1)S(1)} %get-tuple-element.81), channel_id=1, source_target_pairs={{0,1},{1,0},{2,3},{3,2},{4,5},{5,4},{6,7},{7,6},{8,9},{9,8},{10,11... | collective-permute-start | bytes 2359304 | tf_op jit(solution)/shard_map/ppermute | solution.py:417
  64.9 9.4 %collective-permute-start.18 = (bf16[48,3072]{1,0:T(8,128)(2,1)S(1)}, bf16[48,3072]{1,0:T(8,128)(2,1)S(1)}, u32[]{:S(2)}, u32[]{:S(2)}) collective-permute-start(bf16[48,3072]{1,0:T(8,128)(2,1)S(1)} %get-tuple-element.86.refs_0_), channel_id=1, source_target_pairs={{0,2},{1,3},{2,0},{3,1},{4,6},{5,7},{6,4},{7,5},{8,10},{9,11},{10,... | collective-permute-start | bytes 884744 | tf_op jit(solution)/shard_map/ppermute | solution.py:420
  72.0 2.8 %collective-permute-start.10 = (bf16[48,1536]{1,0:T(8,128)(2,1)S(1)}, bf16[48,1536]{1,0:T(8,128)(2,1)S(1)}, u32[]{:S(2)}, u32[]{:S(2)}) collective-permute-start(bf16[48,1536]{1,0:T(8,128)(2,1)S(1)} %get-tuple-element.89), channel_id=1, source_target_pairs={{0,1},{1,0},{2,3},{3,2},{4,5},{5,4},{6,7},{7,6},{8,9},{9,8},{10,11... | collective-permute-start | bytes 442376 | tf_op jit(solution)/shard_map/ppermute | solution.py:417
  72.4 12.0 %collective-permute-start.17 = (bf16[2,48,2048]{2,1,0:T(8,128)(2,1)S(1)}, bf16[2,48,2048]{2,1,0:T(8,128)(2,1)S(1)}, u32[]{:S(2)}, u32[]{:S(2)}) collective-permute-start(bf16[2,48,2048]{2,1,0:T(8,128)(2,1)S(1)} %get-tuple-element.96), channel_id=1, source_target_pairs={{0,2},{1,3},{2,0},{3,1},{4,6},{5,7},{6,4},{7,5},{8,10},{9,11},{10,... | collective-permute-start | bytes 1179656 | tf_op jit(solution)/shard_map/ppermute | solution.py:420
  74.3 3.1 %collective-permute-start.19 = (bf16[48,3072]{1,0:T(8,128)(2,1)S(1)}, bf16[48,3072]{1,0:T(8,128)(2,1)S(1)}, u32[]{:S(2)}, u32[]{:S(2)}) collective-permute-start(bf16[48,3072]{1,0:T(8,128)(2,1)S(1)} %get-tuple-element.86.refs_0_), channel_id=1, source_target_pairs={{0,1},{1,0},{2,3},{3,2},{4,5},{5,4},{6,7},{7,6},{8,9},{9,8},{10,11... | collective-permute-start | bytes 884744 | tf_op jit(solution)/shard_map/ppermute | solution.py:417
  75.8 14.9 %collective-permute-start.13 = (bf16[2,48,1536]{2,1,0:T(8,128)(2,1)S(1)}, bf16[2,48,1536]{2,1,0:T(8,128)(2,1)S(1)}, u32[]{:S(2)}, u32[]{:S(2)}) collective-permute-start(bf16[2,48,1536]{2,1,0:T(8,128)(2,1)S(1)} %get-tuple-element.93.refs_5_), channel_id=1, source_target_pairs={{0,2},{1,3},{2,0},{3,1},{4,6},{5,7},{6,4},{7,5},{8,10},{9,11},{10,... | collective-permute-start | bytes 884744 | tf_op jit(solution)/shard_map/ppermute | solution.py:420
  84.5 10.4 %collective-permute-start.21 = (bf16[48,2048]{1,0:T(8,128)(2,1)S(1)}, bf16[48,2048]{1,0:T(8,128)(2,1)S(1)}, u32[]{:S(2)}, u32[]{:S(2)}) collective-permute-start(bf16[48,2048]{1,0:T(8,128)(2,1)S(1)} %activate.5.refs_0_), channel_id=1, source_target_pairs={{0,2},{1,3},{2,0},{3,1},{4,6},{5,7},{6,4},{7,5},{8,10},{9,11},{10,... | collective-permute-start | bytes 589832 | tf_op jit(solution)/shard_map/ppermute | solution.py:420
  90.8 6.5 %collective-permute-start.14 = (bf16[48,1536]{1,0:T(8,128)(2,1)S(1)}, bf16[48,1536]{1,0:T(8,128)(2,1)S(1)}, u32[]{:S(2)}, u32[]{:S(2)}) collective-permute-start(bf16[48,1536]{1,0:T(8,128)(2,1)S(1)} %activate.4.refs_0_), channel_id=1, source_target_pairs={{0,2},{1,3},{2,0},{3,1},{4,6},{5,7},{6,4},{7,5},{8,10},{9,11},{10,... | collective-permute-start | bytes 442376 | tf_op jit(solution)/shard_map/ppermute | solution.py:420
  91.4 5.9 %collective-permute-start.22 = (bf16[48,2048]{1,0:T(8,128)(2,1)S(1)}, bf16[48,2048]{1,0:T(8,128)(2,1)S(1)}, u32[]{:S(2)}, u32[]{:S(2)}) collective-permute-start(bf16[48,2048]{1,0:T(8,128)(2,1)S(1)} %activate.5.refs_0_), channel_id=1, source_target_pairs={{0,1},{1,0},{2,3},{3,2},{4,5},{5,4},{6,7},{7,6},{8,9},{9,8},{10,11... | collective-permute-start | bytes 589832 | tf_op jit(solution)/shard_map/ppermute | solution.py:417
  94.8 4.2 %collective-permute-start.15 = (bf16[48,1536]{1,0:T(8,128)(2,1)S(1)}, bf16[48,1536]{1,0:T(8,128)(2,1)S(1)}, u32[]{:S(2)}, u32[]{:S(2)}) collective-permute-start(bf16[48,1536]{1,0:T(8,128)(2,1)S(1)} %activate.4.refs_0_), channel_id=1, source_target_pairs={{0,1},{1,0},{2,3},{3,2},{4,5},{5,4},{6,7},{7,6},{8,9},{9,8},{10,11... | collective-permute-start | bytes 442376 | tf_op jit(solution)/shard_map/ppermute | solution.py:417
  101.3 14.4 %collective-permute-start.25 = (bf16[64,2048]{1,0:T(8,128)(2,1)S(1)}, bf16[64,2048]{1,0:T(8,128)(2,1)S(1)}, u32[]{:S(2)}, u32[]{:S(2)}) collective-permute-start(bf16[64,2048]{1,0:T(8,128)(2,1)S(1)} %get-tuple-element.103), channel_id=1, source_target_pairs={{4,8},{8,4},{5,9},{9,5},{6,10},{10,6},{7,11},{11,7},{20,24},{24,20... | collective-permute-start | bytes 786440 | tf_op jit(solution)/shard_map/ppermute | solution.py:414
  102.0 10.7 %collective-permute-start.28 = (bf16[32,2048]{1,0:T(8,128)(2,1)S(1)}, bf16[32,2048]{1,0:T(8,128)(2,1)S(1)}, u32[]{:S(2)}, u32[]{:S(2)}) collective-permute-start(bf16[32,2048]{1,0:T(8,128)(2,1)S(1)} %get-tuple-element.107), channel_id=1, source_target_pairs={{0,4},{12,8},{1,5},{13,9},{2,6},{14,10},{3,7},{15,11},{16,20},{28,... | collective-permute-start | bytes 393224 | tf_op jit(solution)/shard_map/ppermute | solution.py:414
  108.9 6.8 %collective-permute-start.24 = (bf16[32,2048]{1,0:T(8,128)(2,1)S(1)}, bf16[32,2048]{1,0:T(8,128)(2,1)S(1)}, u32[]{:S(2)}, u32[]{:S(2)}) collective-permute-start(bf16[32,2048]{1,0:T(8,128)(2,1)S(1)} %get-tuple-element.100), channel_id=1, source_target_pairs={{0,4},{12,8},{1,5},{13,9},{2,6},{14,10},{3,7},{15,11},{16,20},{28,... | collective-permute-start | bytes 393224 | tf_op jit(solution)/shard_map/ppermute | solution.py:414
  112.7 8.3 %collective-permute-start.29 = (bf16[32,2048]{1,0:T(8,128)(2,1)S(1)}, bf16[32,2048]{1,0:T(8,128)(2,1)S(1)}, u32[]{:S(2)}, u32[]{:S(2)}) collective-permute-start(bf16[32,2048]{1,0:T(8,128)(2,1)S(1)} %relay.3), channel_id=1, source_target_pairs={{0,8},{4,12},{8,0},{12,4},{1,9},{5,13},{9,1},{13,5},{2,10},{6,14},... | collective-permute-start | bytes 393224 | tf_op jit(solution)/shard_map/ppermute | solution.py:414
  115.7 10.0 %collective-permute-start.26 = (bf16[32,2048]{1,0:T(8,128)(2,1)S(1)}, bf16[32,2048]{1,0:T(8,128)(2,1)S(1)}, u32[]{:S(2)}, u32[]{:S(2)}) collective-permute-start(bf16[32,2048]{1,0:T(8,128)(2,1)S(1)} %get-tuple-element.104), channel_id=1, source_target_pairs={{0,4},{4,0},{8,12},{12,8},{1,5},{5,1},{9,13},{13,9},{2,6},{6,2},{1... | collective-permute-start | bytes 393224 | tf_op jit(solution)/shard_map/ppermute | solution.py:414
  117.7 9.8 %collective-permute-start.27 = (bf16[32,2048]{1,0:T(8,128)(2,1)S(1)}, bf16[32,2048]{1,0:T(8,128)(2,1)S(1)}, u32[]{:S(2)}, u32[]{:S(2)}) collective-permute-start(bf16[32,2048]{1,0:T(8,128)(2,1)S(1)} %get-tuple-element.105), channel_id=1, source_target_pairs={{0,4},{4,0},{8,12},{12,8},{1,5},{5,1},{9,13},{13,9},{2,6},{6,2},{1... | collective-permute-start | bytes 393224 | tf_op jit(solution)/shard_map/ppermute | solution.py:414
  117.8 9.7 %collective-permute-start.30 = (bf16[32,2048]{1,0:T(8,128)(2,1)S(1)}, bf16[32,2048]{1,0:T(8,128)(2,1)S(1)}, u32[]{:S(2)}, u32[]{:S(2)}) collective-permute-start(bf16[32,2048]{1,0:T(8,128)(2,1)S(1)} %get-tuple-element.108), channel_id=1, source_target_pairs={{0,8},{4,12},{8,0},{12,4},{1,9},{5,13},{9,1},{13,5},{2,10},{6,14},... | collective-permute-start | bytes 393224 | tf_op jit(solution)/shard_map/ppermute | solution.py:414
  (16 other events, 45.2 us)

commit v15 on v14

--- a/solution.py
+++ b/solution.py
@@ -57,7 +57,7 @@
         out_specs=[held] * 2,
         scratch_shapes=[pltpu.SemaphoreType.DMA((2,))],
         cost_estimate=pl.CostEstimate(flops=0, bytes_accessed=0, transcendentals=0),
-        compiler_params=pltpu.CompilerParams(vmem_limit_bytes=6 * MIB),
+        compiler_params=pltpu.CompilerParams(vmem_limit_bytes=12 * MIB),
         name="fetch_columns",
     )(gate_weight, up_weight, *after)
 

time: 129 us -> 111 us (0.86)
  local copies, waits for them, and re-layouts: 21.5 us -> 1.61 us
  waiting for transfers between devices: 25.2 us -> 28.4 us
  starting transfers between devices: 34 us -> 31.8 us
    unnamed x18 -> x8, local copies, waits for them, and re-layouts: 21.5 us -> 1.61 us
    ppermute x11, waiting for transfers between devices: 10.1 us -> 13.2 us  [over_z(): return lax.ppermute(block, 'gx', [(z, z ^ k) for z in among])]
    ppermute x11, starting transfers between devices: 23.5 us -> 21.4 us  [over_z(): return lax.ppermute(block, 'gx', [(z, z ^ k) for z in among])]
  transfers between devices with their start and end apart: 31 -> 31, of which waited for: 12 -> 15; matrix products, arithmetic and copies ran while one was open for 0% -> 0% of each run, Pallas kernels for 32% -> 38%
where the time goes in v15:
time: 111 us; the launch traced here: 110 us
  Pallas kernels  47.4 us (43%)
  starting transfers between devices  31.8 us (29%)
  waiting for transfers between devices  28.4 us (26%)
  local copies, waits for them, and re-layouts  1.61 us (1%)
    ppermute x11, starting transfers between devices, over_z(): return lax.ppermute(block, 'gx', [(z, z ^ k) for z in among])  21.4 us
    ppermute x7, waiting for transfers between devices, over_x(): lax.ppermute(block, 'gy', [(i, (i + 2 * k) % n_gy) for i in range(n_gy)])  14.3 us
    ppermute x11, waiting for transfers between devices, over_z(): return lax.ppermute(block, 'gx', [(z, z ^ k) for z in among])  13.2 us
    pallas_call x1, Pallas kernels, prepare(): pl.pallas_call(functools.partial(prepare_kernel, n_gx, nx, chunks), out_s...  8.94 us
    pallas_call x3, Pallas kernels, gate_up_held(): pl.pallas_call(functools.partial(gate_up_held_kernel, len(after), tile),...  8.63 us
    ppermute x7, starting transfers between devices, over_x(): lax.ppermute(block, 'gy', [(i, (i + 2 * k) % n_gy) for i in range(n_gy)])  7.97 us
    pallas_call x1, Pallas kernels, gate_up(): pl.pallas_call(functools.partial(gate_up_kernel, len(after)), out_shape=[...  6.84 us
    pallas_call x1, Pallas kernels, down(): pl.pallas_call(functools.partial(down_kernel, len(hidden)), out_shape=jax...  6.63 us
  transfers between devices with their start and end apart: 31, of which 15 were waited for; matrix products, arithmetic and copies ran while one was open for 0% of the time, Pallas kernels for 38%

profile of v15, /device:TPU:0, one launch (start us, length us, event | category | flops | bytes accessed | tf_op | source)
XLA Modules:
  0.0 110.4 jit_solution(16478141574612851071)
XLA Ops:
  0.0 4.0 %collective-permute-start.1 = (bf16[64,2048]{1,0:T(8,128)(2,1)}, bf16[64,2048]{1,0:T(8,128)(2,1)S(1)}, u32[]{:S(2)}, u32[]{:S(2)}) collective-permute-start(bf16[64,2048]{1,0:T(8,128)(2,1)} %tok_ref.1), channel_id=1, source_target_pairs={{0,8},{4,12},{8,0},{12,4},{1,9},{5,13},{9,1},{13,5},{2,10},{6,14},... | collective-permute-start | bytes 786440 | tf_op jit(solution)/shard_map/ppermute | solution.py:414
  4.0 1.6 %collective-permute-start = (bf16[64,2048]{1,0:T(8,128)(2,1)}, bf16[64,2048]{1,0:T(8,128)(2,1)S(1)}, u32[]{:S(2)}, u32[]{:S(2)}) collective-permute-start(bf16[64,2048]{1,0:T(8,128)(2,1)} %tok_ref.1), channel_id=1, source_target_pairs={{0,4},{4,0},{8,12},{12,8},{1,5},{5,1},{9,13},{13,9},{2,6},{6,2},{1... | collective-permute-start | bytes 786440 | tf_op jit(solution)/shard_map/ppermute | solution.py:414
  7.9 8.9 %prepare.1 = (bf16[192,256]{1,0:T(8,128)(2,1)S(1)}, bf16[256,192]{1,0:T(8,128)(2,1)S(1)}, bf16[64,2048]{1,0:T(8,128)(2,1)S(1)}, bf16[2048,1536]{1,0:T(8,128)(2,1...) custom-call(s32[4]{0:T(128)S(1)} %copy-done.3, ...), custom_call_target="tpu_custom_call" | custom-call | tf_op jit(solution)/shard_map/prepare/pallas_call | solution.py:104
  18.3 5.8 %fetch_columns.1 = (bf16[2048,2048]{1,0:T(8,128)(2,1)S(1)}, bf16[2048,2048]{1,0:T(8,128)(2,1)S(1)}) custom-call(bf16[2048,6656]{1,0:T(8,128)(2,1)} %gate_ref.5, bf16[2048,6656]{1,0:T(8,128)(2,1)} %up_ref.5, bf16[64,2048]{1,0:T(8,128)(2,1)S(1)} %follow.1.refs_0_.refs_2_), custom_call_target="tpu_custom_call" | custom-call | tf_op jit(solution)/shard_map/fetch_columns/pallas_call | solution.py:53
  24.2 2.1 %collective-permute-done.3.refs_4_ = bf16[64,2048]{1,0:T(8,128)(2,1)S(1)} collective-permute-done((bf16[64,2048]{1,0:T(8,128)(2,1)S(1)}, bf16[64,2048]{1,0:T(8,128)(2,1)S(1)}, u32[]{:S(2)}, u32[]{:S(2)}) %collective-permute-start.3) | collective-permute-done | bytes 262176 | tf_op jit(solution)/shard_map/ppermute | solution.py:414
  26.6 2.6 %gate_up_held.3 = (f32[2,96,1536]{2,1,0:T(8,128)S(1)}, bf16[2,96,1536]{2,1,0:T(8,128)(2,1)S(1)}) custom-call(bf16[192,2048]{1,0:T(8,128)(2,1)S(1)} %compact.1.tok_ref, bf16[2048,1536]{1,0:T(8,128)(2,1)S(1)} %get-tuple-element.61.gate_ref, bf16[2048,1536]{1,0:T(8,128)(2,1)S(1)} %get-tuple-element.62.up_ref), custom_call_target="tpu_custom_call" | custom-call | tf_op jit(solution)/shard_map/gate_up_held/pallas_call | solution.py:180
  29.3 2.6 %gate_up_held.4 = (f32[2,96,1536]{2,1,0:T(8,128)S(1)}, bf16[2,96,1536]{2,1,0:T(8,128)(2,1)S(1)}) custom-call(bf16[192,2048]{1,0:T(8,128)(2,1)S(1)} %compact.1.tok_ref, bf16[2048,1536]{1,0:T(8,128)(2,1)S(1)} %get-tuple-element.65.gate_ref, bf16[2048,1536]{1,0:T(8,128)(2,1)S(1)} %get-tuple-element.66.up_ref), custom_call_target="tpu_custom_call" | custom-call | tf_op jit(solution)/shard_map/gate_up_held/pallas_call | solution.py:180
  35.9 3.4 %gate_up_held.5 = (f32[2,96,2048]{2,1,0:T(8,128)S(1)}, bf16[2,96,2048]{2,1,0:T(8,128)(2,1)S(1)}) custom-call(bf16[192,2048]{1,0:T(8,128)(2,1)S(1)} %compact.1.tok_ref, bf16[2048,2048]{1,0:T(8,128)(2,1)S(1)} %get-tuple-element.59.refs_5_.gate_ref, bf16[2048,2048]{1,0:T(8,128)(2,1)S(1)} %get-tuple-element.60.up_ref, ...), custom_call_target="tpu_custom_call" | custom-call | tf_op jit(solution)/shard_map/gate_up_held/pallas_call | solution.py:180
  39.3 6.8 %gate_up.1 = (f32[2,96,1536]{2,1,0:T(8,128)S(1)}, bf16[48,1536]{1,0:T(8,128)(2,1)S(1)}, bf16[48,1536]{1,0:T(8,128)(2,1)S(1)}, bf16[48,1536]{1,0:T(8,128)(2,1)S(1)}, bf16[48,1536]{1,0:T(8,128)(2,1)S(1)}) custom-call(bf16[192,2048]{1,0:T(8,128)(2,1)S(1)} %compact.1.tok_ref, bf16[2048,6656]{1,0:T(8,128)(2,1)} %gate_ref.5, bf16[2048,6656]{1,0:T(8,128)(2,1)} %up_ref.5, ...), custom_call_target="tpu_custom_call" | custom-call | tf_op jit(solution)/shard_map/gate_up/pallas_call | solution.py:204
  46.2 1.7 %collective-permute-done.7.refs_3_ = bf16[2,48,1536]{2,1,0:T(8,128)(2,1)S(1)} collective-permute-done((bf16[2,48,1536]{2,1,0:T(8,128)(2,1)S(1)}, bf16[2,48,1536]{2,1,0:T(8,128)(2,1)S(1)}, u32[]{:S(2)}, u32[]{:S(2)}) %collective-permute-start.7) | collective-permute-done | bytes 294944 | tf_op jit(solution)/shard_map/ppermute | solution.py:420
  49.8 5.2 %fetch.1 = (bf16[2048,2048]{1,0:T(8,128)(2,1)S(1)}, bf16[1536,2048]{1,0:T(8,128)(2,1)S(1)}) custom-call(bf16[6656,2048]{1,0:T(8,128)(2,1)} %refs_4_.1, bf16[48,3072]{1,0:T(8,128)(2,1)S(1)} %get-tuple-element.86.refs_0_), custom_call_target="tpu_custom_call" | custom-call | tf_op jit(solution)/shard_map/fetch/pallas_call | solution.py:350
  59.2 1.6 %collective-permute-start.13 = (bf16[2,48,1536]{2,1,0:T(8,128)(2,1)S(1)}, bf16[2,48,1536]{2,1,0:T(8,128)(2,1)S(1)}, u32[]{:S(2)}, u32[]{:S(2)}) collective-permute-start(bf16[2,48,1536]{2,1,0:T(8,128)(2,1)S(1)} %get-tuple-element.93.refs_5_), channel_id=1, source_target_pairs={{0,2},{1,3},{2,0},{3,1},{4,6},{5,7},{6,4},{7,5},{8,10},{9,11},{10,... | collective-permute-start | bytes 884744 | tf_op jit(solution)/shard_map/ppermute | solution.py:420
  60.8 6.6 %down.1.refs_2_.refs_5_ = f32[192,2048]{1,0:T(8,128)S(1)} custom-call(bf16[48,3072]{1,0:T(8,128)(2,1)S(1)} %get-tuple-element.86.refs_0_, bf16[48,3072]{1,0:T(8,128)(2,1)S(1)} %collective-permute-done.18.refs_1_, bf16[48,3072]{1,0:T(8,128)(2,1)S(1)} %collective-permute-done.19.refs_2_, bf16[48,3072]{1,0:T(8,128)(2,1)S(1)} %collective-permute-done.20.refs_3_, ...), custom_call_target="tpu_custom_call" | custom-call | tf_op jit(solution)/shard_map/down/pallas_call | solution.py:321
  68.5 5.5 %collective-permute-done.13.refs_1_ = bf16[2,48,1536]{2,1,0:T(8,128)(2,1)S(1)} collective-permute-done((bf16[2,48,1536]{2,1,0:T(8,128)(2,1)S(1)}, bf16[2,48,1536]{2,1,0:T(8,128)(2,1)S(1)}, u32[]{:S(2)}, u32[]{:S(2)}) %collective-permute-start.13) | collective-permute-done | bytes 294944 | tf_op jit(solution)/shard_map/ppermute | solution.py:420
  74.8 3.5 %collective-permute-done.21.refs_1_ = bf16[48,2048]{1,0:T(8,128)(2,1)S(1)} collective-permute-done((bf16[48,2048]{1,0:T(8,128)(2,1)S(1)}, bf16[48,2048]{1,0:T(8,128)(2,1)S(1)}, u32[]{:S(2)}, u32[]{:S(2)}) %collective-permute-start.21) | collective-permute-done | bytes 196640 | tf_op jit(solution)/shard_map/ppermute | solution.py:420
  78.7 1.9 %collective-permute-done.14.refs_1_ = bf16[48,1536]{1,0:T(8,128)(2,1)S(1)} collective-permute-done((bf16[48,1536]{1,0:T(8,128)(2,1)S(1)}, bf16[48,1536]{1,0:T(8,128)(2,1)S(1)}, u32[]{:S(2)}, u32[]{:S(2)}) %collective-permute-start.14) | collective-permute-done | bytes 147488 | tf_op jit(solution)/shard_map/ppermute | solution.py:420
  80.6 1.8 %down_held.2.refs_5_ = f32[192,2048]{1,0:T(8,128)S(1)} custom-call(bf16[48,2048]{1,0:T(8,128)(2,1)S(1)} %activate.5.refs_0_, bf16[48,2048]{1,0:T(8,128)(2,1)S(1)} %collective-permute-done.21.refs_1_, bf16[48,2048]{1,0:T(8,128)(2,1)S(1)} %collective-permute-done.22.refs_2_, bf16[48,2048]{1,0:T(8,128)(2,1)S(1)} %collective-permute-done.23.refs_3_, ...), custom_call_target="tpu_custom_call" | custom-call | tf_op jit(solution)/shard_map/down_held/pallas_call | solution.py:384
  82.5 2.2 %down_held.3 = (bf16[64,2048]{1,0:T(8,128)(2,1)S(1)}, bf16[64,2048]{1,0:T(8,128)(2,1)S(1)}, bf16[32,2048]{1,0:T(8,128)(2,1)S(1)}, bf16[32,2048]{1,0:T(8,128)(2,1...) custom-call(bf16[48,1536]{1,0:T(8,128)(2,1)S(1)} %activate.4.refs_0_, ...), custom_call_target="tpu_custom_call" | custom-call | tf_op jit(solution)/shard_map/down_held/pallas_call | solution.py:384
  85.4 5.6 %collective-permute-start.28 = (bf16[32,2048]{1,0:T(8,128)(2,1)S(1)}, bf16[32,2048]{1,0:T(8,128)(2,1)S(1)}, u32[]{:S(2)}, u32[]{:S(2)}) collective-permute-start(bf16[32,2048]{1,0:T(8,128)(2,1)S(1)} %get-tuple-element.107), channel_id=1, source_target_pairs={{0,4},{12,8},{1,5},{13,9},{2,6},{14,10},{3,7},{15,11},{16,20},{28,... | collective-permute-start | bytes 393224 | tf_op jit(solution)/shard_map/ppermute | solution.py:414
  92.3 2.5 %collective-permute-done.28.got_ref = bf16[32,2048]{1,0:T(8,128)(2,1)S(1)} collective-permute-done((bf16[32,2048]{1,0:T(8,128)(2,1)S(1)}, bf16[32,2048]{1,0:T(8,128)(2,1)S(1)}, u32[]{:S(2)}, u32[]{:S(2)}) %collective-permute-start.28) | collective-permute-done | bytes 131104 | tf_op jit(solution)/shard_map/ppermute | solution.py:414
  94.8 2.5 %collective-permute-start.29 = (bf16[32,2048]{1,0:T(8,128)(2,1)S(1)}, bf16[32,2048]{1,0:T(8,128)(2,1)S(1)}, u32[]{:S(2)}, u32[]{:S(2)}) collective-permute-start(bf16[32,2048]{1,0:T(8,128)(2,1)S(1)} %relay.3), channel_id=1, source_target_pairs={{0,8},{4,12},{8,0},{12,4},{1,9},{5,13},{9,1},{13,5},{2,10},{6,14},... | collective-permute-start | bytes 393224 | tf_op jit(solution)/shard_map/ppermute | solution.py:414
  97.6 2.5 %collective-permute-start.26 = (bf16[32,2048]{1,0:T(8,128)(2,1)S(1)}, bf16[32,2048]{1,0:T(8,128)(2,1)S(1)}, u32[]{:S(2)}, u32[]{:S(2)}) collective-permute-start(bf16[32,2048]{1,0:T(8,128)(2,1)S(1)} %get-tuple-element.104), channel_id=1, source_target_pairs={{0,4},{4,0},{8,12},{12,8},{1,5},{5,1},{9,13},{13,9},{2,6},{6,2},{1... | collective-permute-start | bytes 393224 | tf_op jit(solution)/shard_map/ppermute | solution.py:414
  102.5 5.2 %collective-permute-done.26 = bf16[32,2048]{1,0:T(8,128)(2,1)S(1)} collective-permute-done((bf16[32,2048]{1,0:T(8,128)(2,1)S(1)}, bf16[32,2048]{1,0:T(8,128)(2,1)S(1)}, u32[]{:S(2)}, u32[]{:S(2)}) %collective-permute-start.26) | collective-permute-done | bytes 131104 | tf_op jit(solution)/shard_map/ppermute | solution.py:414
  107.8 1.8 %collective-permute-done.27 = bf16[32,2048]{1,0:T(8,128)(2,1)S(1)} collective-permute-done((bf16[32,2048]{1,0:T(8,128)(2,1)S(1)}, bf16[32,2048]{1,0:T(8,128)(2,1)S(1)}, u32[]{:S(2)}, u32[]{:S(2)}) %collective-permute-start.27) | collective-permute-done | bytes 131104 | tf_op jit(solution)/shard_map/ppermute | solution.py:414
  (68 shorter events, 22.0 us)
Async XLA Ops:
  0.0 17.0 %collective-permute-start.1 = (bf16[64,2048]{1,0:T(8,128)(2,1)}, bf16[64,2048]{1,0:T(8,128)(2,1)S(1)}, u32[]{:S(2)}, u32[]{:S(2)}) collective-permute-start(bf16[64,2048]{1,0:T(8,128)(2,1)} %tok_ref.1), channel_id=1, source_target_pairs={{0,8},{4,12},{8,0},{12,4},{1,9},{5,13},{9,1},{13,5},{2,10},{6,14},... | collective-permute-start | bytes 786440 | tf_op jit(solution)/shard_map/ppermute | solution.py:414
  4.0 20.1 %collective-permute-start = (bf16[64,2048]{1,0:T(8,128)(2,1)}, bf16[64,2048]{1,0:T(8,128)(2,1)S(1)}, u32[]{:S(2)}, u32[]{:S(2)}) collective-permute-start(bf16[64,2048]{1,0:T(8,128)(2,1)} %tok_ref.1), channel_id=1, source_target_pairs={{0,4},{4,0},{8,12},{12,8},{1,5},{5,1},{9,13},{13,9},{2,6},{6,2},{1... | collective-permute-start | bytes 786440 | tf_op jit(solution)/shard_map/ppermute | solution.py:414
  5.6 18.6 %collective-permute-start.2 = (bf16[64,2048]{1,0:T(8,128)(2,1)}, bf16[64,2048]{1,0:T(8,128)(2,1)S(1)}, u32[]{:S(2)}, u32[]{:S(2)}) collective-permute-start(bf16[64,2048]{1,0:T(8,128)(2,1)} %tok_ref.1), channel_id=1, source_target_pairs={{4,8},{8,4},{5,9},{9,5},{6,10},{10,6},{7,11},{11,7},{20,24},{24,20... | collective-permute-start | bytes 786440 | tf_op jit(solution)/shard_map/ppermute | solution.py:414
  17.0 9.2 %collective-permute-start.3 = (bf16[64,2048]{1,0:T(8,128)(2,1)S(1)}, bf16[64,2048]{1,0:T(8,128)(2,1)S(1)}, u32[]{:S(2)}, u32[]{:S(2)}) collective-permute-start(bf16[64,2048]{1,0:T(8,128)(2,1)S(1)} %follow.1.refs_0_.refs_2_), channel_id=1, source_target_pairs={{4,0},{8,12},{5,1},{9,13},{6,2},{10,14},{7,3},{11,15},{20,16},{24,... | collective-permute-start | bytes 786440 | tf_op jit(solution)/shard_map/ppermute | solution.py:414
  29.3 2.7 %collective-permute-start.4 = (bf16[2,96,1536]{2,1,0:T(8,128)(2,1)S(1)}, bf16[2,96,1536]{2,1,0:T(8,128)(2,1)S(1)}, u32[]{:S(2)}, u32[]{:S(2)}) collective-permute-start(bf16[2,96,1536]{2,1,0:T(8,128)(2,1)S(1)} %get-tuple-element.64), channel_id=1, source_target_pairs={{0,1},{1,0},{2,3},{3,2},{4,5},{5,4},{6,7},{7,6},{8,9},{9,8},{10,11... | collective-permute-start | bytes 1769480 | tf_op jit(solution)/shard_map/ppermute | solution.py:417
  32.6 13.6 %collective-permute-start.6 = (bf16[2,48,1536]{2,1,0:T(8,128)(2,1)S(1)}, bf16[2,48,1536]{2,1,0:T(8,128)(2,1)S(1)}, u32[]{:S(2)}, u32[]{:S(2)}) collective-permute-start(bf16[2,48,1536]{2,1,0:T(8,128)(2,1)S(1)} %get-tuple-element.68.refs_0_), channel_id=1, source_target_pairs={{0,2},{1,3},{2,0},{3,1},{4,6},{5,7},{6,4},{7,5},{8,10},{9,11},{10,... | collective-permute-start | bytes 884744 | tf_op jit(solution)/shard_map/ppermute | solution.py:420
  34.4 13.6 %collective-permute-start.7 = (bf16[2,48,1536]{2,1,0:T(8,128)(2,1)S(1)}, bf16[2,48,1536]{2,1,0:T(8,128)(2,1)S(1)}, u32[]{:S(2)}, u32[]{:S(2)}) collective-permute-start(bf16[2,48,1536]{2,1,0:T(8,128)(2,1)S(1)} %get-tuple-element.71.refs_1_), channel_id=1, source_target_pairs={{0,2},{1,3},{2,0},{3,1},{4,6},{5,7},{6,4},{7,5},{8,10},{9,11},{10,... | collective-permute-start | bytes 884744 | tf_op jit(solution)/shard_map/ppermute | solution.py:420
  48.2 6.8 %collective-permute-start.8 = (bf16[2,96,2048]{2,1,0:T(8,128)(2,1)S(1)}, bf16[2,96,2048]{2,1,0:T(8,128)(2,1)S(1)}, u32[]{:S(2)}, u32[]{:S(2)}) collective-permute-start(bf16[2,96,2048]{2,1,0:T(8,128)(2,1)S(1)} %get-tuple-element.81), channel_id=1, source_target_pairs={{0,1},{1,0},{2,3},{3,2},{4,5},{5,4},{6,7},{7,6},{8,9},{9,8},{10,11... | collective-permute-start | bytes 2359304 | tf_op jit(solution)/shard_map/ppermute | solution.py:417
  48.3 9.4 %collective-permute-start.18 = (bf16[48,3072]{1,0:T(8,128)(2,1)S(1)}, bf16[48,3072]{1,0:T(8,128)(2,1)S(1)}, u32[]{:S(2)}, u32[]{:S(2)}) collective-permute-start(bf16[48,3072]{1,0:T(8,128)(2,1)S(1)} %get-tuple-element.86.refs_0_), channel_id=1, source_target_pairs={{0,2},{1,3},{2,0},{3,1},{4,6},{5,7},{6,4},{7,5},{8,10},{9,11},{10,... | collective-permute-start | bytes 884744 | tf_op jit(solution)/shard_map/ppermute | solution.py:420
  55.4 2.8 %collective-permute-start.10 = (bf16[48,1536]{1,0:T(8,128)(2,1)S(1)}, bf16[48,1536]{1,0:T(8,128)(2,1)S(1)}, u32[]{:S(2)}, u32[]{:S(2)}) collective-permute-start(bf16[48,1536]{1,0:T(8,128)(2,1)S(1)} %get-tuple-element.89), channel_id=1, source_target_pairs={{0,1},{1,0},{2,3},{3,2},{4,5},{5,4},{6,7},{7,6},{8,9},{9,8},{10,11... | collective-permute-start | bytes 442376 | tf_op jit(solution)/shard_map/ppermute | solution.py:417
  55.7 12.0 %collective-permute-start.17 = (bf16[2,48,2048]{2,1,0:T(8,128)(2,1)S(1)}, bf16[2,48,2048]{2,1,0:T(8,128)(2,1)S(1)}, u32[]{:S(2)}, u32[]{:S(2)}) collective-permute-start(bf16[2,48,2048]{2,1,0:T(8,128)(2,1)S(1)} %get-tuple-element.96), channel_id=1, source_target_pairs={{0,2},{1,3},{2,0},{3,1},{4,6},{5,7},{6,4},{7,5},{8,10},{9,11},{10,... | collective-permute-start | bytes 1179656 | tf_op jit(solution)/shard_map/ppermute | solution.py:420
  57.7 3.1 %collective-permute-start.19 = (bf16[48,3072]{1,0:T(8,128)(2,1)S(1)}, bf16[48,3072]{1,0:T(8,128)(2,1)S(1)}, u32[]{:S(2)}, u32[]{:S(2)}) collective-permute-start(bf16[48,3072]{1,0:T(8,128)(2,1)S(1)} %get-tuple-element.86.refs_0_), channel_id=1, source_target_pairs={{0,1},{1,0},{2,3},{3,2},{4,5},{5,4},{6,7},{7,6},{8,9},{9,8},{10,11... | collective-permute-start | bytes 884744 | tf_op jit(solution)/shard_map/ppermute | solution.py:417
  59.2 14.9 %collective-permute-start.13 = (bf16[2,48,1536]{2,1,0:T(8,128)(2,1)S(1)}, bf16[2,48,1536]{2,1,0:T(8,128)(2,1)S(1)}, u32[]{:S(2)}, u32[]{:S(2)}) collective-permute-start(bf16[2,48,1536]{2,1,0:T(8,128)(2,1)S(1)} %get-tuple-element.93.refs_5_), channel_id=1, source_target_pairs={{0,2},{1,3},{2,0},{3,1},{4,6},{5,7},{6,4},{7,5},{8,10},{9,11},{10,... | collective-permute-start | bytes 884744 | tf_op jit(solution)/shard_map/ppermute | solution.py:420
  67.8 10.4 %collective-permute-start.21 = (bf16[48,2048]{1,0:T(8,128)(2,1)S(1)}, bf16[48,2048]{1,0:T(8,128)(2,1)S(1)}, u32[]{:S(2)}, u32[]{:S(2)}) collective-permute-start(bf16[48,2048]{1,0:T(8,128)(2,1)S(1)} %activate.5.refs_0_), channel_id=1, source_target_pairs={{0,2},{1,3},{2,0},{3,1},{4,6},{5,7},{6,4},{7,5},{8,10},{9,11},{10,... | collective-permute-start | bytes 589832 | tf_op jit(solution)/shard_map/ppermute | solution.py:420
  74.1 6.5 %collective-permute-start.14 = (bf16[48,1536]{1,0:T(8,128)(2,1)S(1)}, bf16[48,1536]{1,0:T(8,128)(2,1)S(1)}, u32[]{:S(2)}, u32[]{:S(2)}) collective-permute-start(bf16[48,1536]{1,0:T(8,128)(2,1)S(1)} %activate.4.refs_0_), channel_id=1, source_target_pairs={{0,2},{1,3},{2,0},{3,1},{4,6},{5,7},{6,4},{7,5},{8,10},{9,11},{10,... | collective-permute-start | bytes 442376 | tf_op jit(solution)/shard_map/ppermute | solution.py:420
  74.8 5.9 %collective-permute-start.22 = (bf16[48,2048]{1,0:T(8,128)(2,1)S(1)}, bf16[48,2048]{1,0:T(8,128)(2,1)S(1)}, u32[]{:S(2)}, u32[]{:S(2)}) collective-permute-start(bf16[48,2048]{1,0:T(8,128)(2,1)S(1)} %activate.5.refs_0_), channel_id=1, source_target_pairs={{0,1},{1,0},{2,3},{3,2},{4,5},{5,4},{6,7},{7,6},{8,9},{9,8},{10,11... | collective-permute-start | bytes 589832 | tf_op jit(solution)/shard_map/ppermute | solution.py:417
  78.2 4.2 %collective-permute-start.15 = (bf16[48,1536]{1,0:T(8,128)(2,1)S(1)}, bf16[48,1536]{1,0:T(8,128)(2,1)S(1)}, u32[]{:S(2)}, u32[]{:S(2)}) collective-permute-start(bf16[48,1536]{1,0:T(8,128)(2,1)S(1)} %activate.4.refs_0_), channel_id=1, source_target_pairs={{0,1},{1,0},{2,3},{3,2},{4,5},{5,4},{6,7},{7,6},{8,9},{9,8},{10,11... | collective-permute-start | bytes 442376 | tf_op jit(solution)/shard_map/ppermute | solution.py:417
  84.7 12.9 %collective-permute-start.25 = (bf16[64,2048]{1,0:T(8,128)(2,1)S(1)}, bf16[64,2048]{1,0:T(8,128)(2,1)S(1)}, u32[]{:S(2)}, u32[]{:S(2)}) collective-permute-start(bf16[64,2048]{1,0:T(8,128)(2,1)S(1)} %get-tuple-element.103), channel_id=1, source_target_pairs={{4,8},{8,4},{5,9},{9,5},{6,10},{10,6},{7,11},{11,7},{20,24},{24,20... | collective-permute-start | bytes 786440 | tf_op jit(solution)/shard_map/ppermute | solution.py:414
  85.4 9.4 %collective-permute-start.28 = (bf16[32,2048]{1,0:T(8,128)(2,1)S(1)}, bf16[32,2048]{1,0:T(8,128)(2,1)S(1)}, u32[]{:S(2)}, u32[]{:S(2)}) collective-permute-start(bf16[32,2048]{1,0:T(8,128)(2,1)S(1)} %get-tuple-element.107), channel_id=1, source_target_pairs={{0,4},{12,8},{1,5},{13,9},{2,6},{14,10},{3,7},{15,11},{16,20},{28,... | collective-permute-start | bytes 393224 | tf_op jit(solution)/shard_map/ppermute | solution.py:414
  91.0 6.6 %collective-permute-start.24 = (bf16[32,2048]{1,0:T(8,128)(2,1)S(1)}, bf16[32,2048]{1,0:T(8,128)(2,1)S(1)}, u32[]{:S(2)}, u32[]{:S(2)}) collective-permute-start(bf16[32,2048]{1,0:T(8,128)(2,1)S(1)} %get-tuple-element.100), channel_id=1, source_target_pairs={{0,4},{12,8},{1,5},{13,9},{2,6},{14,10},{3,7},{15,11},{16,20},{28,... | collective-permute-start | bytes 393224 | tf_op jit(solution)/shard_map/ppermute | solution.py:414
  94.8 7.7 %collective-permute-start.29 = (bf16[32,2048]{1,0:T(8,128)(2,1)S(1)}, bf16[32,2048]{1,0:T(8,128)(2,1)S(1)}, u32[]{:S(2)}, u32[]{:S(2)}) collective-permute-start(bf16[32,2048]{1,0:T(8,128)(2,1)S(1)} %relay.3), channel_id=1, source_target_pairs={{0,8},{4,12},{8,0},{12,4},{1,9},{5,13},{9,1},{13,5},{2,10},{6,14},... | collective-permute-start | bytes 393224 | tf_op jit(solution)/shard_map/ppermute | solution.py:414
  97.6 10.1 %collective-permute-start.26 = (bf16[32,2048]{1,0:T(8,128)(2,1)S(1)}, bf16[32,2048]{1,0:T(8,128)(2,1)S(1)}, u32[]{:S(2)}, u32[]{:S(2)}) collective-permute-start(bf16[32,2048]{1,0:T(8,128)(2,1)S(1)} %get-tuple-element.104), channel_id=1, source_target_pairs={{0,4},{4,0},{8,12},{12,8},{1,5},{5,1},{9,13},{13,9},{2,6},{6,2},{1... | collective-permute-start | bytes 393224 | tf_op jit(solution)/shard_map/ppermute | solution.py:414
  100.2 9.3 %collective-permute-start.27 = (bf16[32,2048]{1,0:T(8,128)(2,1)S(1)}, bf16[32,2048]{1,0:T(8,128)(2,1)S(1)}, u32[]{:S(2)}, u32[]{:S(2)}) collective-permute-start(bf16[32,2048]{1,0:T(8,128)(2,1)S(1)} %get-tuple-element.105), channel_id=1, source_target_pairs={{0,4},{4,0},{8,12},{12,8},{1,5},{5,1},{9,13},{13,9},{2,6},{6,2},{1... | collective-permute-start | bytes 393224 | tf_op jit(solution)/shard_map/ppermute | solution.py:414
  100.3 9.3 %collective-permute-start.30 = (bf16[32,2048]{1,0:T(8,128)(2,1)S(1)}, bf16[32,2048]{1,0:T(8,128)(2,1)S(1)}, u32[]{:S(2)}, u32[]{:S(2)}) collective-permute-start(bf16[32,2048]{1,0:T(8,128)(2,1)S(1)} %get-tuple-element.108), channel_id=1, source_target_pairs={{0,8},{4,12},{8,0},{12,4},{1,9},{5,13},{9,1},{13,5},{2,10},{6,14},... | collective-permute-start | bytes 393224 | tf_op jit(solution)/shard_map/ppermute | solution.py:414
  (11 other events, 32.1 us)

commit v16 on v15

--- a/solution.py
+++ b/solution.py
@@ -468,18 +468,18 @@
     out_rows = [(k * tok_dev, tok_dev) for k in range(n_gx)]
     if line:
         halves = [(row, part) for row in range(tok_dev, n_gx * tok_dev, part)]
-        out_rows = out_rows[:1] + out_rows[3:] + halves
+        out_rows = out_rows[:1] + halves
     spread = down_held(hidden, rows_held[1], total, pick_out, out_rows)
 
     if line:
-        own, three, *halves = spread
+        own, *halves = spread
         ends = [over_z(piece, 1, (0, 3)) for piece in halves[4:]]
-        middle = over_z(three, 3, (1, 2))
+        middle = [over_z(piece, 3, (1, 2)) for piece in halves[4:]]
         low, _ = relay(halves[2], ends[0], [], [])
-        high, near = relay(halves[3], ends[1], halves[:2], [middle])
+        high, near = relay(halves[3], ends[1], halves[:2], middle)
         far = jnp.concatenate([over_z(low, 2), over_z(high, 2)], axis=0)
         near = jnp.concatenate([over_z(piece, 1) for piece in near], axis=0)
-        parts = [own, near, far, middle]
+        parts = [own, near, far, jnp.concatenate(middle, axis=0)]
     else:
         parts = [spread[0]] + [over_z(spread[k], k) for k in range(1, n_gx)]
     return sum(p.astype(F32) for p in parts).astype(BF16)

time: 111 us -> 114 us (1.027)
  starting transfers between devices: 31.8 us -> 37.5 us
  waiting for transfers between devices: 28.4 us -> 25.8 us
    ppermute x11 -> x12, starting transfers between devices: 21.4 us -> 27.2 us  [over_z(): return lax.ppermute(block, 'gx', [(z, z ^ k) for z in among])]
    ppermute x11 -> x12, waiting for transfers between devices: 13.2 us -> 10.5 us  [over_z(): return lax.ppermute(block, 'gx', [(z, z ^ k) for z in among])]
  transfers between devices with their start and end apart: 31 -> 32, of which waited for: 15 -> 13; matrix products, arithmetic and copies ran while one was open for 0% -> 0% of each run, Pallas kernels for 38% -> 37%
where the time goes in v16:
time: 114 us; the launch traced here: 113 us
  Pallas kernels  47.4 us (42%)
  starting transfers between devices  37.5 us (33%)
  waiting for transfers between devices  25.8 us (23%)
  local copies, waits for them, and re-layouts  1.61 us (1%)
    ppermute x12, starting transfers between devices, over_z(): return lax.ppermute(block, 'gx', [(z, z ^ k) for z in among])  27.2 us
    ppermute x7, waiting for transfers between devices, over_x(): lax.ppermute(block, 'gy', [(i, (i + 2 * k) % n_gy) for i in range(n_gy)])  14.3 us
    ppermute x12, waiting for transfers between devices, over_z(): return lax.ppermute(block, 'gx', [(z, z ^ k) for z in among])  10.5 us
    pallas_call x1, Pallas kernels, prepare(): pl.pallas_call(functools.partial(prepare_kernel, n_gx, nx, chunks), out_s...  8.94 us
    pallas_call x3, Pallas kernels, gate_up_held(): pl.pallas_call(functools.partial(gate_up_held_kernel, len(after), tile),...  8.63 us
    ppermute x7, starting transfers between devices, over_x(): lax.ppermute(block, 'gy', [(i, (i + 2 * k) % n_gy) for i in range(n_gy)])  7.97 us
    pallas_call x1, Pallas kernels, gate_up(): pl.pallas_call(functools.partial(gate_up_kernel, len(after)), out_shape=[...  6.84 us
    pallas_call x1, Pallas kernels, down(): pl.pallas_call(functools.partial(down_kernel, len(hidden)), out_shape=jax...  6.63 us
  transfers between devices with their start and end apart: 32, of which 13 were waited for; matrix products, arithmetic and copies ran while one was open for 0% of the time, Pallas kernels for 37%

profile of v16, /device:TPU:0, one launch (start us, length us, event | category | flops | bytes accessed | tf_op | source)
XLA Modules:
  0.0 113.5 jit_solution(10958731961531475848)
XLA Ops:
  0.0 4.0 %collective-permute-start.1 = (bf16[64,2048]{1,0:T(8,128)(2,1)}, bf16[64,2048]{1,0:T(8,128)(2,1)S(1)}, u32[]{:S(2)}, u32[]{:S(2)}) collective-permute-start(bf16[64,2048]{1,0:T(8,128)(2,1)} %tok_ref.1), channel_id=1, source_target_pairs={{0,8},{4,12},{8,0},{12,4},{1,9},{5,13},{9,1},{13,5},{2,10},{6,14},... | collective-permute-start | bytes 786440 | tf_op jit(solution)/shard_map/ppermute | solution.py:414
  7.9 8.9 %prepare.1 = (bf16[192,256]{1,0:T(8,128)(2,1)S(1)}, bf16[256,192]{1,0:T(8,128)(2,1)S(1)}, bf16[64,2048]{1,0:T(8,128)(2,1)S(1)}, bf16[2048,1536]{1,0:T(8,128)(2,1...) custom-call(s32[4]{0:T(128)S(1)} %copy-done.3, ...), custom_call_target="tpu_custom_call" | custom-call | tf_op jit(solution)/shard_map/prepare/pallas_call | solution.py:104
  18.3 5.8 %fetch_columns.1 = (bf16[2048,2048]{1,0:T(8,128)(2,1)S(1)}, bf16[2048,2048]{1,0:T(8,128)(2,1)S(1)}) custom-call(bf16[2048,6656]{1,0:T(8,128)(2,1)} %gate_ref.5, bf16[2048,6656]{1,0:T(8,128)(2,1)} %up_ref.5, bf16[64,2048]{1,0:T(8,128)(2,1)S(1)} %follow.1.refs_0_.refs_2_), custom_call_target="tpu_custom_call" | custom-call | tf_op jit(solution)/shard_map/fetch_columns/pallas_call | solution.py:53
  24.2 2.1 %collective-permute-done.3.refs_4_ = bf16[64,2048]{1,0:T(8,128)(2,1)S(1)} collective-permute-done((bf16[64,2048]{1,0:T(8,128)(2,1)S(1)}, bf16[64,2048]{1,0:T(8,128)(2,1)S(1)}, u32[]{:S(2)}, u32[]{:S(2)}) %collective-permute-start.3) | collective-permute-done | bytes 262176 | tf_op jit(solution)/shard_map/ppermute | solution.py:414
  26.6 2.6 %gate_up_held.3 = (f32[2,96,1536]{2,1,0:T(8,128)S(1)}, bf16[2,96,1536]{2,1,0:T(8,128)(2,1)S(1)}) custom-call(bf16[192,2048]{1,0:T(8,128)(2,1)S(1)} %compact.1.tok_ref, bf16[2048,1536]{1,0:T(8,128)(2,1)S(1)} %get-tuple-element.60.gate_ref, bf16[2048,1536]{1,0:T(8,128)(2,1)S(1)} %get-tuple-element.61.up_ref), custom_call_target="tpu_custom_call" | custom-call | tf_op jit(solution)/shard_map/gate_up_held/pallas_call | solution.py:180
  29.3 2.6 %gate_up_held.4 = (f32[2,96,1536]{2,1,0:T(8,128)S(1)}, bf16[2,96,1536]{2,1,0:T(8,128)(2,1)S(1)}) custom-call(bf16[192,2048]{1,0:T(8,128)(2,1)S(1)} %compact.1.tok_ref, bf16[2048,1536]{1,0:T(8,128)(2,1)S(1)} %get-tuple-element.64.gate_ref, bf16[2048,1536]{1,0:T(8,128)(2,1)S(1)} %get-tuple-element.65.up_ref), custom_call_target="tpu_custom_call" | custom-call | tf_op jit(solution)/shard_map/gate_up_held/pallas_call | solution.py:180
  35.9 3.4 %gate_up_held.5 = (f32[2,96,2048]{2,1,0:T(8,128)S(1)}, bf16[2,96,2048]{2,1,0:T(8,128)(2,1)S(1)}) custom-call(bf16[192,2048]{1,0:T(8,128)(2,1)S(1)} %compact.1.tok_ref, bf16[2048,2048]{1,0:T(8,128)(2,1)S(1)} %get-tuple-element.58.refs_5_.gate_ref, bf16[2048,2048]{1,0:T(8,128)(2,1)S(1)} %get-tuple-element.59.up_ref, ...), custom_call_target="tpu_custom_call" | custom-call | tf_op jit(solution)/shard_map/gate_up_held/pallas_call | solution.py:180
  39.3 6.8 %gate_up.1 = (f32[2,96,1536]{2,1,0:T(8,128)S(1)}, bf16[48,1536]{1,0:T(8,128)(2,1)S(1)}, bf16[48,1536]{1,0:T(8,128)(2,1)S(1)}, bf16[48,1536]{1,0:T(8,128)(2,1)S(1)}, bf16[48,1536]{1,0:T(8,128)(2,1)S(1)}) custom-call(bf16[192,2048]{1,0:T(8,128)(2,1)S(1)} %compact.1.tok_ref, bf16[2048,6656]{1,0:T(8,128)(2,1)} %gate_ref.5, bf16[2048,6656]{1,0:T(8,128)(2,1)} %up_ref.5, ...), custom_call_target="tpu_custom_call" | custom-call | tf_op jit(solution)/shard_map/gate_up/pallas_call | solution.py:204
  46.2 1.7 %collective-permute-done.7.refs_3_ = bf16[2,48,1536]{2,1,0:T(8,128)(2,1)S(1)} collective-permute-done((bf16[2,48,1536]{2,1,0:T(8,128)(2,1)S(1)}, bf16[2,48,1536]{2,1,0:T(8,128)(2,1)S(1)}, u32[]{:S(2)}, u32[]{:S(2)}) %collective-permute-start.7) | collective-permute-done | bytes 294944 | tf_op jit(solution)/shard_map/ppermute | solution.py:420
  49.8 5.2 %fetch.1 = (bf16[2048,2048]{1,0:T(8,128)(2,1)S(1)}, bf16[1536,2048]{1,0:T(8,128)(2,1)S(1)}) custom-call(bf16[6656,2048]{1,0:T(8,128)(2,1)} %refs_4_.1, bf16[48,3072]{1,0:T(8,128)(2,1)S(1)} %get-tuple-element.85.refs_0_), custom_call_target="tpu_custom_call" | custom-call | tf_op jit(solution)/shard_map/fetch/pallas_call | solution.py:350
  59.2 1.6 %collective-permute-start.13 = (bf16[2,48,1536]{2,1,0:T(8,128)(2,1)S(1)}, bf16[2,48,1536]{2,1,0:T(8,128)(2,1)S(1)}, u32[]{:S(2)}, u32[]{:S(2)}) collective-permute-start(bf16[2,48,1536]{2,1,0:T(8,128)(2,1)S(1)} %get-tuple-element.92.refs_5_), channel_id=1, source_target_pairs={{0,2},{1,3},{2,0},{3,1},{4,6},{5,7},{6,4},{7,5},{8,10},{9,11},{10,... | collective-permute-start | bytes 884744 | tf_op jit(solution)/shard_map/ppermute | solution.py:420
  60.8 6.6 %down.1.refs_2_.refs_5_ = f32[192,2048]{1,0:T(8,128)S(1)} custom-call(bf16[48,3072]{1,0:T(8,128)(2,1)S(1)} %get-tuple-element.85.refs_0_, bf16[48,3072]{1,0:T(8,128)(2,1)S(1)} %collective-permute-done.18.refs_1_, bf16[48,3072]{1,0:T(8,128)(2,1)S(1)} %collective-permute-done.19.refs_2_, bf16[48,3072]{1,0:T(8,128)(2,1)S(1)} %collective-permute-done.20.refs_3_, ...), custom_call_target="tpu_custom_call" | custom-call | tf_op jit(solution)/shard_map/down/pallas_call | solution.py:321
  68.5 5.5 %collective-permute-done.13.refs_1_ = bf16[2,48,1536]{2,1,0:T(8,128)(2,1)S(1)} collective-permute-done((bf16[2,48,1536]{2,1,0:T(8,128)(2,1)S(1)}, bf16[2,48,1536]{2,1,0:T(8,128)(2,1)S(1)}, u32[]{:S(2)}, u32[]{:S(2)}) %collective-permute-start.13) | collective-permute-done | bytes 294944 | tf_op jit(solution)/shard_map/ppermute | solution.py:420
  74.8 3.5 %collective-permute-done.21.refs_1_ = bf16[48,2048]{1,0:T(8,128)(2,1)S(1)} collective-permute-done((bf16[48,2048]{1,0:T(8,128)(2,1)S(1)}, bf16[48,2048]{1,0:T(8,128)(2,1)S(1)}, u32[]{:S(2)}, u32[]{:S(2)}) %collective-permute-start.21) | collective-permute-done | bytes 196640 | tf_op jit(solution)/shard_map/ppermute | solution.py:420
  78.7 1.9 %collective-permute-done.14.refs_1_ = bf16[48,1536]{1,0:T(8,128)(2,1)S(1)} collective-permute-done((bf16[48,1536]{1,0:T(8,128)(2,1)S(1)}, bf16[48,1536]{1,0:T(8,128)(2,1)S(1)}, u32[]{:S(2)}, u32[]{:S(2)}) %collective-permute-start.14) | collective-permute-done | bytes 147488 | tf_op jit(solution)/shard_map/ppermute | solution.py:420
  80.6 1.8 %down_held.2.refs_5_ = f32[192,2048]{1,0:T(8,128)S(1)} custom-call(bf16[48,2048]{1,0:T(8,128)(2,1)S(1)} %activate.5.refs_0_, bf16[48,2048]{1,0:T(8,128)(2,1)S(1)} %collective-permute-done.21.refs_1_, bf16[48,2048]{1,0:T(8,128)(2,1)S(1)} %collective-permute-done.22.refs_2_, bf16[48,2048]{1,0:T(8,128)(2,1)S(1)} %collective-permute-done.23.refs_3_, ...), custom_call_target="tpu_custom_call" | custom-call | tf_op jit(solution)/shard_map/down_held/pallas_call | solution.py:384
  82.5 2.2 %down_held.3 = (bf16[64,2048]{1,0:T(8,128)(2,1)S(1)}, bf16[32,2048]{1,0:T(8,128)(2,1)S(1)}, bf16[32,2048]{1,0:T(8,128)(2,1)S(1)}, bf16[32,2048]{1,0:T(8,128)(2,1...) custom-call(bf16[48,1536]{1,0:T(8,128)(2,1)S(1)} %activate.4.refs_0_, ...), custom_call_target="tpu_custom_call" | custom-call | tf_op jit(solution)/shard_map/down_held/pallas_call | solution.py:384
  84.7 2.8 %collective-permute-start.29 = (bf16[32,2048]{1,0:T(8,128)(2,1)S(1)}, bf16[32,2048]{1,0:T(8,128)(2,1)S(1)}, u32[]{:S(2)}, u32[]{:S(2)}) collective-permute-start(bf16[32,2048]{1,0:T(8,128)(2,1)S(1)} %get-tuple-element.102), channel_id=1, source_target_pairs={{0,4},{12,8},{1,5},{13,9},{2,6},{14,10},{3,7},{15,11},{16,20},{28,... | collective-permute-start | bytes 393224 | tf_op jit(solution)/shard_map/ppermute | solution.py:414
  88.2 4.0 %collective-permute-start.24 = (bf16[32,2048]{1,0:T(8,128)(2,1)S(1)}, bf16[32,2048]{1,0:T(8,128)(2,1)S(1)}, u32[]{:S(2)}, u32[]{:S(2)}) collective-permute-start(bf16[32,2048]{1,0:T(8,128)(2,1)S(1)} %get-tuple-element.99), channel_id=1, source_target_pairs={{0,4},{12,8},{1,5},{13,9},{2,6},{14,10},{3,7},{15,11},{16,20},{28,... | collective-permute-start | bytes 393224 | tf_op jit(solution)/shard_map/ppermute | solution.py:414
  93.0 2.1 %collective-permute-start.30 = (bf16[32,2048]{1,0:T(8,128)(2,1)S(1)}, bf16[32,2048]{1,0:T(8,128)(2,1)S(1)}, u32[]{:S(2)}, u32[]{:S(2)}) collective-permute-start(bf16[32,2048]{1,0:T(8,128)(2,1)S(1)} %relay.3), channel_id=1, source_target_pairs={{0,8},{4,12},{8,0},{12,4},{1,9},{5,13},{9,1},{13,5},{2,10},{6,14},... | collective-permute-start | bytes 393224 | tf_op jit(solution)/shard_map/ppermute | solution.py:414
  95.5 7.2 %collective-permute-start.27 = (bf16[32,2048]{1,0:T(8,128)(2,1)S(1)}, bf16[32,2048]{1,0:T(8,128)(2,1)S(1)}, u32[]{:S(2)}, u32[]{:S(2)}) collective-permute-start(bf16[32,2048]{1,0:T(8,128)(2,1)S(1)} %get-tuple-element.103), channel_id=1, source_target_pairs={{0,4},{4,0},{8,12},{12,8},{1,5},{5,1},{9,13},{13,9},{2,6},{6,2},{1... | collective-permute-start | bytes 393224 | tf_op jit(solution)/shard_map/ppermute | solution.py:414
  102.9 1.9 %collective-permute-start.31 = (bf16[32,2048]{1,0:T(8,128)(2,1)S(1)}, bf16[32,2048]{1,0:T(8,128)(2,1)S(1)}, u32[]{:S(2)}, u32[]{:S(2)}) collective-permute-start(bf16[32,2048]{1,0:T(8,128)(2,1)S(1)} %get-tuple-element.106), channel_id=1, source_target_pairs={{0,8},{4,12},{8,0},{12,4},{1,9},{5,13},{9,1},{13,5},{2,10},{6,14},... | collective-permute-start | bytes 393224 | tf_op jit(solution)/shard_map/ppermute | solution.py:414
  104.8 5.2 %collective-permute-done.27 = bf16[32,2048]{1,0:T(8,128)(2,1)S(1)} collective-permute-done((bf16[32,2048]{1,0:T(8,128)(2,1)S(1)}, bf16[32,2048]{1,0:T(8,128)(2,1)S(1)}, u32[]{:S(2)}, u32[]{:S(2)}) %collective-permute-start.27) | collective-permute-done | bytes 131104 | tf_op jit(solution)/shard_map/ppermute | solution.py:414
  109.9 2.7 %collective-permute-done.28 = bf16[32,2048]{1,0:T(8,128)(2,1)S(1)} collective-permute-done((bf16[32,2048]{1,0:T(8,128)(2,1)S(1)}, bf16[32,2048]{1,0:T(8,128)(2,1)S(1)}, u32[]{:S(2)}, u32[]{:S(2)}) %collective-permute-start.28) | collective-permute-done | bytes 131104 | tf_op jit(solution)/shard_map/ppermute | solution.py:414
  (70 shorter events, 20.7 us)
Async XLA Ops:
  0.0 17.0 %collective-permute-start.1 = (bf16[64,2048]{1,0:T(8,128)(2,1)}, bf16[64,2048]{1,0:T(8,128)(2,1)S(1)}, u32[]{:S(2)}, u32[]{:S(2)}) collective-permute-start(bf16[64,2048]{1,0:T(8,128)(2,1)} %tok_ref.1), channel_id=1, source_target_pairs={{0,8},{4,12},{8,0},{12,4},{1,9},{5,13},{9,1},{13,5},{2,10},{6,14},... | collective-permute-start | bytes 786440 | tf_op jit(solution)/shard_map/ppermute | solution.py:414
  4.0 20.1 %collective-permute-start = (bf16[64,2048]{1,0:T(8,128)(2,1)}, bf16[64,2048]{1,0:T(8,128)(2,1)S(1)}, u32[]{:S(2)}, u32[]{:S(2)}) collective-permute-start(bf16[64,2048]{1,0:T(8,128)(2,1)} %tok_ref.1), channel_id=1, source_target_pairs={{0,4},{4,0},{8,12},{12,8},{1,5},{5,1},{9,13},{13,9},{2,6},{6,2},{1... | collective-permute-start | bytes 786440 | tf_op jit(solution)/shard_map/ppermute | solution.py:414
  5.6 18.6 %collective-permute-start.2 = (bf16[64,2048]{1,0:T(8,128)(2,1)}, bf16[64,2048]{1,0:T(8,128)(2,1)S(1)}, u32[]{:S(2)}, u32[]{:S(2)}) collective-permute-start(bf16[64,2048]{1,0:T(8,128)(2,1)} %tok_ref.1), channel_id=1, source_target_pairs={{4,8},{8,4},{5,9},{9,5},{6,10},{10,6},{7,11},{11,7},{20,24},{24,20... | collective-permute-start | bytes 786440 | tf_op jit(solution)/shard_map/ppermute | solution.py:414
  17.0 9.2 %collective-permute-start.3 = (bf16[64,2048]{1,0:T(8,128)(2,1)S(1)}, bf16[64,2048]{1,0:T(8,128)(2,1)S(1)}, u32[]{:S(2)}, u32[]{:S(2)}) collective-permute-start(bf16[64,2048]{1,0:T(8,128)(2,1)S(1)} %follow.1.refs_0_.refs_2_), channel_id=1, source_target_pairs={{4,0},{8,12},{5,1},{9,13},{6,2},{10,14},{7,3},{11,15},{20,16},{24,... | collective-permute-start | bytes 786440 | tf_op jit(solution)/shard_map/ppermute | solution.py:414
  32.6 13.6 %collective-permute-start.6 = (bf16[2,48,1536]{2,1,0:T(8,128)(2,1)S(1)}, bf16[2,48,1536]{2,1,0:T(8,128)(2,1)S(1)}, u32[]{:S(2)}, u32[]{:S(2)}) collective-permute-start(bf16[2,48,1536]{2,1,0:T(8,128)(2,1)S(1)} %get-tuple-element.67.refs_0_), channel_id=1, source_target_pairs={{0,2},{1,3},{2,0},{3,1},{4,6},{5,7},{6,4},{7,5},{8,10},{9,11},{10,... | collective-permute-start | bytes 884744 | tf_op jit(solution)/shard_map/ppermute | solution.py:420
  34.4 13.6 %collective-permute-start.7 = (bf16[2,48,1536]{2,1,0:T(8,128)(2,1)S(1)}, bf16[2,48,1536]{2,1,0:T(8,128)(2,1)S(1)}, u32[]{:S(2)}, u32[]{:S(2)}) collective-permute-start(bf16[2,48,1536]{2,1,0:T(8,128)(2,1)S(1)} %get-tuple-element.70.refs_1_), channel_id=1, source_target_pairs={{0,2},{1,3},{2,0},{3,1},{4,6},{5,7},{6,4},{7,5},{8,10},{9,11},{10,... | collective-permute-start | bytes 884744 | tf_op jit(solution)/shard_map/ppermute | solution.py:420
  48.2 6.8 %collective-permute-start.8 = (bf16[2,96,2048]{2,1,0:T(8,128)(2,1)S(1)}, bf16[2,96,2048]{2,1,0:T(8,128)(2,1)S(1)}, u32[]{:S(2)}, u32[]{:S(2)}) collective-permute-start(bf16[2,96,2048]{2,1,0:T(8,128)(2,1)S(1)} %get-tuple-element.80), channel_id=1, source_target_pairs={{0,1},{1,0},{2,3},{3,2},{4,5},{5,4},{6,7},{7,6},{8,9},{9,8},{10,11... | collective-permute-start | bytes 2359304 | tf_op jit(solution)/shard_map/ppermute | solution.py:417
  48.3 9.4 %collective-permute-start.18 = (bf16[48,3072]{1,0:T(8,128)(2,1)S(1)}, bf16[48,3072]{1,0:T(8,128)(2,1)S(1)}, u32[]{:S(2)}, u32[]{:S(2)}) collective-permute-start(bf16[48,3072]{1,0:T(8,128)(2,1)S(1)} %get-tuple-element.85.refs_0_), channel_id=1, source_target_pairs={{0,2},{1,3},{2,0},{3,1},{4,6},{5,7},{6,4},{7,5},{8,10},{9,11},{10,... | collective-permute-start | bytes 884744 | tf_op jit(solution)/shard_map/ppermute | solution.py:420
  55.4 2.8 %collective-permute-start.10 = (bf16[48,1536]{1,0:T(8,128)(2,1)S(1)}, bf16[48,1536]{1,0:T(8,128)(2,1)S(1)}, u32[]{:S(2)}, u32[]{:S(2)}) collective-permute-start(bf16[48,1536]{1,0:T(8,128)(2,1)S(1)} %get-tuple-element.88), channel_id=1, source_target_pairs={{0,1},{1,0},{2,3},{3,2},{4,5},{5,4},{6,7},{7,6},{8,9},{9,8},{10,11... | collective-permute-start | bytes 442376 | tf_op jit(solution)/shard_map/ppermute | solution.py:417
  55.7 12.0 %collective-permute-start.17 = (bf16[2,48,2048]{2,1,0:T(8,128)(2,1)S(1)}, bf16[2,48,2048]{2,1,0:T(8,128)(2,1)S(1)}, u32[]{:S(2)}, u32[]{:S(2)}) collective-permute-start(bf16[2,48,2048]{2,1,0:T(8,128)(2,1)S(1)} %get-tuple-element.95), channel_id=1, source_target_pairs={{0,2},{1,3},{2,0},{3,1},{4,6},{5,7},{6,4},{7,5},{8,10},{9,11},{10,... | collective-permute-start | bytes 1179656 | tf_op jit(solution)/shard_map/ppermute | solution.py:420
  57.7 3.1 %collective-permute-start.19 = (bf16[48,3072]{1,0:T(8,128)(2,1)S(1)}, bf16[48,3072]{1,0:T(8,128)(2,1)S(1)}, u32[]{:S(2)}, u32[]{:S(2)}) collective-permute-start(bf16[48,3072]{1,0:T(8,128)(2,1)S(1)} %get-tuple-element.85.refs_0_), channel_id=1, source_target_pairs={{0,1},{1,0},{2,3},{3,2},{4,5},{5,4},{6,7},{7,6},{8,9},{9,8},{10,11... | collective-permute-start | bytes 884744 | tf_op jit(solution)/shard_map/ppermute | solution.py:417
  59.2 14.9 %collective-permute-start.13 = (bf16[2,48,1536]{2,1,0:T(8,128)(2,1)S(1)}, bf16[2,48,1536]{2,1,0:T(8,128)(2,1)S(1)}, u32[]{:S(2)}, u32[]{:S(2)}) collective-permute-start(bf16[2,48,1536]{2,1,0:T(8,128)(2,1)S(1)} %get-tuple-element.92.refs_5_), channel_id=1, source_target_pairs={{0,2},{1,3},{2,0},{3,1},{4,6},{5,7},{6,4},{7,5},{8,10},{9,11},{10,... | collective-permute-start | bytes 884744 | tf_op jit(solution)/shard_map/ppermute | solution.py:420
  67.8 10.4 %collective-permute-start.21 = (bf16[48,2048]{1,0:T(8,128)(2,1)S(1)}, bf16[48,2048]{1,0:T(8,128)(2,1)S(1)}, u32[]{:S(2)}, u32[]{:S(2)}) collective-permute-start(bf16[48,2048]{1,0:T(8,128)(2,1)S(1)} %activate.5.refs_0_), channel_id=1, source_target_pairs={{0,2},{1,3},{2,0},{3,1},{4,6},{5,7},{6,4},{7,5},{8,10},{9,11},{10,... | collective-permute-start | bytes 589832 | tf_op jit(solution)/shard_map/ppermute | solution.py:420
  74.1 6.5 %collective-permute-start.14 = (bf16[48,1536]{1,0:T(8,128)(2,1)S(1)}, bf16[48,1536]{1,0:T(8,128)(2,1)S(1)}, u32[]{:S(2)}, u32[]{:S(2)}) collective-permute-start(bf16[48,1536]{1,0:T(8,128)(2,1)S(1)} %activate.4.refs_0_), channel_id=1, source_target_pairs={{0,2},{1,3},{2,0},{3,1},{4,6},{5,7},{6,4},{7,5},{8,10},{9,11},{10,... | collective-permute-start | bytes 442376 | tf_op jit(solution)/shard_map/ppermute | solution.py:420
  74.8 5.9 %collective-permute-start.22 = (bf16[48,2048]{1,0:T(8,128)(2,1)S(1)}, bf16[48,2048]{1,0:T(8,128)(2,1)S(1)}, u32[]{:S(2)}, u32[]{:S(2)}) collective-permute-start(bf16[48,2048]{1,0:T(8,128)(2,1)S(1)} %activate.5.refs_0_), channel_id=1, source_target_pairs={{0,1},{1,0},{2,3},{3,2},{4,5},{5,4},{6,7},{7,6},{8,9},{9,8},{10,11... | collective-permute-start | bytes 589832 | tf_op jit(solution)/shard_map/ppermute | solution.py:417
  78.2 4.2 %collective-permute-start.15 = (bf16[48,1536]{1,0:T(8,128)(2,1)S(1)}, bf16[48,1536]{1,0:T(8,128)(2,1)S(1)}, u32[]{:S(2)}, u32[]{:S(2)}) collective-permute-start(bf16[48,1536]{1,0:T(8,128)(2,1)S(1)} %activate.4.refs_0_), channel_id=1, source_target_pairs={{0,1},{1,0},{2,3},{3,2},{4,5},{5,4},{6,7},{7,6},{8,9},{9,8},{10,11... | collective-permute-start | bytes 442376 | tf_op jit(solution)/shard_map/ppermute | solution.py:417
  84.7 8.3 %collective-permute-start.29 = (bf16[32,2048]{1,0:T(8,128)(2,1)S(1)}, bf16[32,2048]{1,0:T(8,128)(2,1)S(1)}, u32[]{:S(2)}, u32[]{:S(2)}) collective-permute-start(bf16[32,2048]{1,0:T(8,128)(2,1)S(1)} %get-tuple-element.102), channel_id=1, source_target_pairs={{0,4},{12,8},{1,5},{13,9},{2,6},{14,10},{3,7},{15,11},{16,20},{28,... | collective-permute-start | bytes 393224 | tf_op jit(solution)/shard_map/ppermute | solution.py:414
  87.5 7.6 %collective-permute-start.26 = (bf16[32,2048]{1,0:T(8,128)(2,1)S(1)}, bf16[32,2048]{1,0:T(8,128)(2,1)S(1)}, u32[]{:S(2)}, u32[]{:S(2)}) collective-permute-start(bf16[32,2048]{1,0:T(8,128)(2,1)S(1)} %get-tuple-element.99), channel_id=1, source_target_pairs={{4,8},{8,4},{5,9},{9,5},{6,10},{10,6},{7,11},{11,7},{20,24},{24,20... | collective-permute-start | bytes 393224 | tf_op jit(solution)/shard_map/ppermute | solution.py:414
  88.2 7.3 %collective-permute-start.24 = (bf16[32,2048]{1,0:T(8,128)(2,1)S(1)}, bf16[32,2048]{1,0:T(8,128)(2,1)S(1)}, u32[]{:S(2)}, u32[]{:S(2)}) collective-permute-start(bf16[32,2048]{1,0:T(8,128)(2,1)S(1)} %get-tuple-element.99), channel_id=1, source_target_pairs={{0,4},{12,8},{1,5},{13,9},{2,6},{14,10},{3,7},{15,11},{16,20},{28,... | collective-permute-start | bytes 393224 | tf_op jit(solution)/shard_map/ppermute | solution.py:414
  92.3 3.2 %collective-permute-start.25 = (bf16[32,2048]{1,0:T(8,128)(2,1)S(1)}, bf16[32,2048]{1,0:T(8,128)(2,1)S(1)}, u32[]{:S(2)}, u32[]{:S(2)}) collective-permute-start(bf16[32,2048]{1,0:T(8,128)(2,1)S(1)} %get-tuple-element.102), channel_id=1, source_target_pairs={{4,8},{8,4},{5,9},{9,5},{6,10},{10,6},{7,11},{11,7},{20,24},{24,20... | collective-permute-start | bytes 393224 | tf_op jit(solution)/shard_map/ppermute | solution.py:414
  93.0 11.8 %collective-permute-start.30 = (bf16[32,2048]{1,0:T(8,128)(2,1)S(1)}, bf16[32,2048]{1,0:T(8,128)(2,1)S(1)}, u32[]{:S(2)}, u32[]{:S(2)}) collective-permute-start(bf16[32,2048]{1,0:T(8,128)(2,1)S(1)} %relay.3), channel_id=1, source_target_pairs={{0,8},{4,12},{8,0},{12,4},{1,9},{5,13},{9,1},{13,5},{2,10},{6,14},... | collective-permute-start | bytes 393224 | tf_op jit(solution)/shard_map/ppermute | solution.py:414
  95.5 14.4 %collective-permute-start.27 = (bf16[32,2048]{1,0:T(8,128)(2,1)S(1)}, bf16[32,2048]{1,0:T(8,128)(2,1)S(1)}, u32[]{:S(2)}, u32[]{:S(2)}) collective-permute-start(bf16[32,2048]{1,0:T(8,128)(2,1)S(1)} %get-tuple-element.103), channel_id=1, source_target_pairs={{0,4},{4,0},{8,12},{12,8},{1,5},{5,1},{9,13},{13,9},{2,6},{6,2},{1... | collective-permute-start | bytes 393224 | tf_op jit(solution)/shard_map/ppermute | solution.py:414
  102.8 9.9 %collective-permute-start.28 = (bf16[32,2048]{1,0:T(8,128)(2,1)S(1)}, bf16[32,2048]{1,0:T(8,128)(2,1)S(1)}, u32[]{:S(2)}, u32[]{:S(2)}) collective-permute-start(bf16[32,2048]{1,0:T(8,128)(2,1)S(1)} %get-tuple-element.104), channel_id=1, source_target_pairs={{0,4},{4,0},{8,12},{12,8},{1,5},{5,1},{9,13},{13,9},{2,6},{6,2},{1... | collective-permute-start | bytes 393224 | tf_op jit(solution)/shard_map/ppermute | solution.py:414
  102.9 9.8 %collective-permute-start.31 = (bf16[32,2048]{1,0:T(8,128)(2,1)S(1)}, bf16[32,2048]{1,0:T(8,128)(2,1)S(1)}, u32[]{:S(2)}, u32[]{:S(2)}) collective-permute-start(bf16[32,2048]{1,0:T(8,128)(2,1)S(1)} %get-tuple-element.106), channel_id=1, source_target_pairs={{0,8},{4,12},{8,0},{12,4},{1,9},{5,13},{9,1},{13,5},{2,10},{6,14},... | collective-permute-start | bytes 393224 | tf_op jit(solution)/shard_map/ppermute | solution.py:414
  (12 other events, 34.8 us)

commit v17 on v16

--- a/solution.py
+++ b/solution.py
@@ -476,10 +476,10 @@
         ends = [over_z(piece, 1, (0, 3)) for piece in halves[4:]]
         middle = [over_z(piece, 3, (1, 2)) for piece in halves[4:]]
         low, _ = relay(halves[2], ends[0], [], [])
-        high, near = relay(halves[3], ends[1], halves[:2], middle)
+        high, near = relay(halves[3], ends[1], halves[:2], [low])
         far = jnp.concatenate([over_z(low, 2), over_z(high, 2)], axis=0)
         near = jnp.concatenate([over_z(piece, 1) for piece in near], axis=0)
-        parts = [own, near, far, jnp.concatenate(middle, axis=0)]
+        parts = [own, far, near, jnp.concatenate(middle, axis=0)]
     else:
         parts = [spread[0]] + [over_z(spread[k], k) for k in range(1, n_gx)]
     return sum(p.astype(F32) for p in parts).astype(BF16)

time: 114 us -> 112 us (0.982)
  starting transfers between devices: 37.5 us -> 31.3 us
  waiting for transfers between devices: 25.8 us -> 29.9 us
    ppermute x12, starting transfers between devices: 27.2 us -> 20.9 us  [over_z(): return lax.ppermute(block, 'gx', [(z, z ^ k) for z in among])]
    ppermute x12, waiting for transfers between devices: 10.5 us -> 14.6 us  [over_z(): return lax.ppermute(block, 'gx', [(z, z ^ k) for z in among])]
  transfers between devices with their start and end apart: 32 -> 32, of which waited for: 13 -> 14; matrix products, arithmetic and copies ran while one was open for 0% -> 0% of each run, Pallas kernels for 37% -> 38%
where the time goes in v17:
time: 112 us; the launch traced here: 111 us
  Pallas kernels  47.4 us (42%)
  starting transfers between devices  31.3 us (28%)
  waiting for transfers between devices  29.9 us (27%)
  local copies, waits for them, and re-layouts  1.61 us (1%)
    ppermute x12, starting transfers between devices, over_z(): return lax.ppermute(block, 'gx', [(z, z ^ k) for z in among])  20.9 us
    ppermute x12, waiting for transfers between devices, over_z(): return lax.ppermute(block, 'gx', [(z, z ^ k) for z in among])  14.6 us
    ppermute x7, waiting for transfers between devices, over_x(): lax.ppermute(block, 'gy', [(i, (i + 2 * k) % n_gy) for i in range(n_gy)])  14.3 us
    pallas_call x1, Pallas kernels, prepare(): pl.pallas_call(functools.partial(prepare_kernel, n_gx, nx, chunks), out_s...  8.94 us
    pallas_call x3, Pallas kernels, gate_up_held(): pl.pallas_call(functools.partial(gate_up_held_kernel, len(after), tile),...  8.63 us
    ppermute x7, starting transfers between devices, over_x(): lax.ppermute(block, 'gy', [(i, (i + 2 * k) % n_gy) for i in range(n_gy)])  7.97 us
    pallas_call x1, Pallas kernels, gate_up(): pl.pallas_call(functools.partial(gate_up_kernel, len(after)), out_shape=[...  6.84 us
    pallas_call x1, Pallas kernels, down(): pl.pallas_call(functools.partial(down_kernel, len(hidden)), out_shape=jax...  6.63 us
  transfers between devices with their start and end apart: 32, of which 14 were waited for; matrix products, arithmetic and copies ran while one was open for 0% of the time, Pallas kernels for 38%

profile of v17, /device:TPU:0, one launch (start us, length us, event | category | flops | bytes accessed | tf_op | source)
XLA Modules:
  0.0 111.4 jit_solution(14146963178740164183)
XLA Ops:
  0.0 4.0 %collective-permute-start.1 = (bf16[64,2048]{1,0:T(8,128)(2,1)}, bf16[64,2048]{1,0:T(8,128)(2,1)S(1)}, u32[]{:S(2)}, u32[]{:S(2)}) collective-permute-start(bf16[64,2048]{1,0:T(8,128)(2,1)} %tok_ref.1), channel_id=1, source_target_pairs={{0,8},{4,12},{8,0},{12,4},{1,9},{5,13},{9,1},{13,5},{2,10},{6,14},... | collective-permute-start | bytes 786440 | tf_op jit(solution)/shard_map/ppermute | solution.py:414
  4.0 1.6 %collective-permute-start = (bf16[64,2048]{1,0:T(8,128)(2,1)}, bf16[64,2048]{1,0:T(8,128)(2,1)S(1)}, u32[]{:S(2)}, u32[]{:S(2)}) collective-permute-start(bf16[64,2048]{1,0:T(8,128)(2,1)} %tok_ref.1), channel_id=1, source_target_pairs={{0,4},{4,0},{8,12},{12,8},{1,5},{5,1},{9,13},{13,9},{2,6},{6,2},{1... | collective-permute-start | bytes 786440 | tf_op jit(solution)/shard_map/ppermute | solution.py:414
  7.9 8.9 %prepare.1 = (bf16[192,256]{1,0:T(8,128)(2,1)S(1)}, bf16[256,192]{1,0:T(8,128)(2,1)S(1)}, bf16[64,2048]{1,0:T(8,128)(2,1)S(1)}, bf16[2048,1536]{1,0:T(8,128)(2,1...) custom-call(s32[4]{0:T(128)S(1)} %copy-done.3, ...), custom_call_target="tpu_custom_call" | custom-call | tf_op jit(solution)/shard_map/prepare/pallas_call | solution.py:104
  18.3 5.8 %fetch_columns.1 = (bf16[2048,2048]{1,0:T(8,128)(2,1)S(1)}, bf16[2048,2048]{1,0:T(8,128)(2,1)S(1)}) custom-call(bf16[2048,6656]{1,0:T(8,128)(2,1)} %gate_ref.5, bf16[2048,6656]{1,0:T(8,128)(2,1)} %up_ref.5, bf16[64,2048]{1,0:T(8,128)(2,1)S(1)} %follow.1.refs_0_.refs_2_), custom_call_target="tpu_custom_call" | custom-call | tf_op jit(solution)/shard_map/fetch_columns/pallas_call | solution.py:53
  24.2 2.1 %collective-permute-done.3.refs_4_ = bf16[64,2048]{1,0:T(8,128)(2,1)S(1)} collective-permute-done((bf16[64,2048]{1,0:T(8,128)(2,1)S(1)}, bf16[64,2048]{1,0:T(8,128)(2,1)S(1)}, u32[]{:S(2)}, u32[]{:S(2)}) %collective-permute-start.3) | collective-permute-done | bytes 262176 | tf_op jit(solution)/shard_map/ppermute | solution.py:414
  26.6 2.6 %gate_up_held.3 = (f32[2,96,1536]{2,1,0:T(8,128)S(1)}, bf16[2,96,1536]{2,1,0:T(8,128)(2,1)S(1)}) custom-call(bf16[192,2048]{1,0:T(8,128)(2,1)S(1)} %compact.1.tok_ref, bf16[2048,1536]{1,0:T(8,128)(2,1)S(1)} %get-tuple-element.60.gate_ref, bf16[2048,1536]{1,0:T(8,128)(2,1)S(1)} %get-tuple-element.61.up_ref), custom_call_target="tpu_custom_call" | custom-call | tf_op jit(solution)/shard_map/gate_up_held/pallas_call | solution.py:180
  29.3 2.6 %gate_up_held.4 = (f32[2,96,1536]{2,1,0:T(8,128)S(1)}, bf16[2,96,1536]{2,1,0:T(8,128)(2,1)S(1)}) custom-call(bf16[192,2048]{1,0:T(8,128)(2,1)S(1)} %compact.1.tok_ref, bf16[2048,1536]{1,0:T(8,128)(2,1)S(1)} %get-tuple-element.64.gate_ref, bf16[2048,1536]{1,0:T(8,128)(2,1)S(1)} %get-tuple-element.65.up_ref), custom_call_target="tpu_custom_call" | custom-call | tf_op jit(solution)/shard_map/gate_up_held/pallas_call | solution.py:180
  35.9 3.4 %gate_up_held.5 = (f32[2,96,2048]{2,1,0:T(8,128)S(1)}, bf16[2,96,2048]{2,1,0:T(8,128)(2,1)S(1)}) custom-call(bf16[192,2048]{1,0:T(8,128)(2,1)S(1)} %compact.1.tok_ref, bf16[2048,2048]{1,0:T(8,128)(2,1)S(1)} %get-tuple-element.58.refs_5_.gate_ref, bf16[2048,2048]{1,0:T(8,128)(2,1)S(1)} %get-tuple-element.59.up_ref, ...), custom_call_target="tpu_custom_call" | custom-call | tf_op jit(solution)/shard_map/gate_up_held/pallas_call | solution.py:180
  39.3 6.8 %gate_up.1 = (f32[2,96,1536]{2,1,0:T(8,128)S(1)}, bf16[48,1536]{1,0:T(8,128)(2,1)S(1)}, bf16[48,1536]{1,0:T(8,128)(2,1)S(1)}, bf16[48,1536]{1,0:T(8,128)(2,1)S(1)}, bf16[48,1536]{1,0:T(8,128)(2,1)S(1)}) custom-call(bf16[192,2048]{1,0:T(8,128)(2,1)S(1)} %compact.1.tok_ref, bf16[2048,6656]{1,0:T(8,128)(2,1)} %gate_ref.5, bf16[2048,6656]{1,0:T(8,128)(2,1)} %up_ref.5, ...), custom_call_target="tpu_custom_call" | custom-call | tf_op jit(solution)/shard_map/gate_up/pallas_call | solution.py:204
  46.2 1.7 %collective-permute-done.7.refs_3_ = bf16[2,48,1536]{2,1,0:T(8,128)(2,1)S(1)} collective-permute-done((bf16[2,48,1536]{2,1,0:T(8,128)(2,1)S(1)}, bf16[2,48,1536]{2,1,0:T(8,128)(2,1)S(1)}, u32[]{:S(2)}, u32[]{:S(2)}) %collective-permute-start.7) | collective-permute-done | bytes 294944 | tf_op jit(solution)/shard_map/ppermute | solution.py:420
  49.8 5.2 %fetch.1 = (bf16[2048,2048]{1,0:T(8,128)(2,1)S(1)}, bf16[1536,2048]{1,0:T(8,128)(2,1)S(1)}) custom-call(bf16[6656,2048]{1,0:T(8,128)(2,1)} %refs_4_.1, bf16[48,3072]{1,0:T(8,128)(2,1)S(1)} %get-tuple-element.85.refs_0_), custom_call_target="tpu_custom_call" | custom-call | tf_op jit(solution)/shard_map/fetch/pallas_call | solution.py:350
  59.2 1.6 %collective-permute-start.13 = (bf16[2,48,1536]{2,1,0:T(8,128)(2,1)S(1)}, bf16[2,48,1536]{2,1,0:T(8,128)(2,1)S(1)}, u32[]{:S(2)}, u32[]{:S(2)}) collective-permute-start(bf16[2,48,1536]{2,1,0:T(8,128)(2,1)S(1)} %get-tuple-element.92.refs_5_), channel_id=1, source_target_pairs={{0,2},{1,3},{2,0},{3,1},{4,6},{5,7},{6,4},{7,5},{8,10},{9,11},{10,... | collective-permute-start | bytes 884744 | tf_op jit(solution)/shard_map/ppermute | solution.py:420
  60.8 6.6 %down.1.refs_2_.refs_5_ = f32[192,2048]{1,0:T(8,128)S(1)} custom-call(bf16[48,3072]{1,0:T(8,128)(2,1)S(1)} %get-tuple-element.85.refs_0_, bf16[48,3072]{1,0:T(8,128)(2,1)S(1)} %collective-permute-done.18.refs_1_, bf16[48,3072]{1,0:T(8,128)(2,1)S(1)} %collective-permute-done.19.refs_2_, bf16[48,3072]{1,0:T(8,128)(2,1)S(1)} %collective-permute-done.20.refs_3_, ...), custom_call_target="tpu_custom_call" | custom-call | tf_op jit(solution)/shard_map/down/pallas_call | solution.py:321
  68.5 5.5 %collective-permute-done.13.refs_1_ = bf16[2,48,1536]{2,1,0:T(8,128)(2,1)S(1)} collective-permute-done((bf16[2,48,1536]{2,1,0:T(8,128)(2,1)S(1)}, bf16[2,48,1536]{2,1,0:T(8,128)(2,1)S(1)}, u32[]{:S(2)}, u32[]{:S(2)}) %collective-permute-start.13) | collective-permute-done | bytes 294944 | tf_op jit(solution)/shard_map/ppermute | solution.py:420
  74.8 3.5 %collective-permute-done.21.refs_1_ = bf16[48,2048]{1,0:T(8,128)(2,1)S(1)} collective-permute-done((bf16[48,2048]{1,0:T(8,128)(2,1)S(1)}, bf16[48,2048]{1,0:T(8,128)(2,1)S(1)}, u32[]{:S(2)}, u32[]{:S(2)}) %collective-permute-start.21) | collective-permute-done | bytes 196640 | tf_op jit(solution)/shard_map/ppermute | solution.py:420
  78.7 1.9 %collective-permute-done.14.refs_1_ = bf16[48,1536]{1,0:T(8,128)(2,1)S(1)} collective-permute-done((bf16[48,1536]{1,0:T(8,128)(2,1)S(1)}, bf16[48,1536]{1,0:T(8,128)(2,1)S(1)}, u32[]{:S(2)}, u32[]{:S(2)}) %collective-permute-start.14) | collective-permute-done | bytes 147488 | tf_op jit(solution)/shard_map/ppermute | solution.py:420
  80.6 1.8 %down_held.2.refs_5_ = f32[192,2048]{1,0:T(8,128)S(1)} custom-call(bf16[48,2048]{1,0:T(8,128)(2,1)S(1)} %activate.5.refs_0_, bf16[48,2048]{1,0:T(8,128)(2,1)S(1)} %collective-permute-done.21.refs_1_, bf16[48,2048]{1,0:T(8,128)(2,1)S(1)} %collective-permute-done.22.refs_2_, bf16[48,2048]{1,0:T(8,128)(2,1)S(1)} %collective-permute-done.23.refs_3_, ...), custom_call_target="tpu_custom_call" | custom-call | tf_op jit(solution)/shard_map/down_held/pallas_call | solution.py:384
  82.5 2.2 %down_held.3 = (bf16[64,2048]{1,0:T(8,128)(2,1)S(1)}, bf16[32,2048]{1,0:T(8,128)(2,1)S(1)}, bf16[32,2048]{1,0:T(8,128)(2,1)S(1)}, bf16[32,2048]{1,0:T(8,128)(2,1...) custom-call(bf16[48,1536]{1,0:T(8,128)(2,1)S(1)} %activate.4.refs_0_, ...), custom_call_target="tpu_custom_call" | custom-call | tf_op jit(solution)/shard_map/down_held/pallas_call | solution.py:384
  84.7 2.8 %collective-permute-start.24 = (bf16[32,2048]{1,0:T(8,128)(2,1)S(1)}, bf16[32,2048]{1,0:T(8,128)(2,1)S(1)}, u32[]{:S(2)}, u32[]{:S(2)}) collective-permute-start(bf16[32,2048]{1,0:T(8,128)(2,1)S(1)} %get-tuple-element.99), channel_id=1, source_target_pairs={{0,4},{12,8},{1,5},{13,9},{2,6},{14,10},{3,7},{15,11},{16,20},{28,... | collective-permute-start | bytes 393224 | tf_op jit(solution)/shard_map/ppermute | solution.py:414
  91.4 3.8 %collective-permute-start.25 = (bf16[32,2048]{1,0:T(8,128)(2,1)S(1)}, bf16[32,2048]{1,0:T(8,128)(2,1)S(1)}, u32[]{:S(2)}, u32[]{:S(2)}) collective-permute-start(bf16[32,2048]{1,0:T(8,128)(2,1)S(1)} %relay.2.refs_2_), channel_id=1, source_target_pairs={{0,8},{4,12},{8,0},{12,4},{1,9},{5,13},{9,1},{13,5},{2,10},{6,14},... | collective-permute-start | bytes 393224 | tf_op jit(solution)/shard_map/ppermute | solution.py:414
  95.2 2.1 %collective-permute-start.27 = (bf16[32,2048]{1,0:T(8,128)(2,1)S(1)}, bf16[32,2048]{1,0:T(8,128)(2,1)S(1)}, u32[]{:S(2)}, u32[]{:S(2)}) collective-permute-start(bf16[32,2048]{1,0:T(8,128)(2,1)S(1)} %get-tuple-element.104), channel_id=1, source_target_pairs={{0,8},{4,12},{8,0},{12,4},{1,9},{5,13},{9,1},{13,5},{2,10},{6,14},... | collective-permute-start | bytes 393224 | tf_op jit(solution)/shard_map/ppermute | solution.py:414
  97.3 2.0 %collective-permute-start.29 = (bf16[32,2048]{1,0:T(8,128)(2,1)S(1)}, bf16[32,2048]{1,0:T(8,128)(2,1)S(1)}, u32[]{:S(2)}, u32[]{:S(2)}) collective-permute-start(bf16[32,2048]{1,0:T(8,128)(2,1)S(1)} %get-tuple-element.106), channel_id=1, source_target_pairs={{0,4},{4,0},{8,12},{12,8},{1,5},{5,1},{9,13},{13,9},{2,6},{6,2},{1... | collective-permute-start | bytes 393224 | tf_op jit(solution)/shard_map/ppermute | solution.py:414
  99.3 8.5 %collective-permute-done.25 = bf16[32,2048]{1,0:T(8,128)(2,1)S(1)} collective-permute-done((bf16[32,2048]{1,0:T(8,128)(2,1)S(1)}, bf16[32,2048]{1,0:T(8,128)(2,1)S(1)}, u32[]{:S(2)}, u32[]{:S(2)}) %collective-permute-start.25) | collective-permute-done | bytes 131104 | tf_op jit(solution)/shard_map/ppermute | solution.py:414
  107.8 2.1 %collective-permute-done.27 = bf16[32,2048]{1,0:T(8,128)(2,1)S(1)} collective-permute-done((bf16[32,2048]{1,0:T(8,128)(2,1)S(1)}, bf16[32,2048]{1,0:T(8,128)(2,1)S(1)}, u32[]{:S(2)}, u32[]{:S(2)}) %collective-permute-start.27) | collective-permute-done | bytes 131104 | tf_op jit(solution)/shard_map/ppermute | solution.py:414
  (70 shorter events, 21.7 us)
Async XLA Ops:
  0.0 17.0 %collective-permute-start.1 = (bf16[64,2048]{1,0:T(8,128)(2,1)}, bf16[64,2048]{1,0:T(8,128)(2,1)S(1)}, u32[]{:S(2)}, u32[]{:S(2)}) collective-permute-start(bf16[64,2048]{1,0:T(8,128)(2,1)} %tok_ref.1), channel_id=1, source_target_pairs={{0,8},{4,12},{8,0},{12,4},{1,9},{5,13},{9,1},{13,5},{2,10},{6,14},... | collective-permute-start | bytes 786440 | tf_op jit(solution)/shard_map/ppermute | solution.py:414
  4.0 20.1 %collective-permute-start = (bf16[64,2048]{1,0:T(8,128)(2,1)}, bf16[64,2048]{1,0:T(8,128)(2,1)S(1)}, u32[]{:S(2)}, u32[]{:S(2)}) collective-permute-start(bf16[64,2048]{1,0:T(8,128)(2,1)} %tok_ref.1), channel_id=1, source_target_pairs={{0,4},{4,0},{8,12},{12,8},{1,5},{5,1},{9,13},{13,9},{2,6},{6,2},{1... | collective-permute-start | bytes 786440 | tf_op jit(solution)/shard_map/ppermute | solution.py:414
  5.6 18.6 %collective-permute-start.2 = (bf16[64,2048]{1,0:T(8,128)(2,1)}, bf16[64,2048]{1,0:T(8,128)(2,1)S(1)}, u32[]{:S(2)}, u32[]{:S(2)}) collective-permute-start(bf16[64,2048]{1,0:T(8,128)(2,1)} %tok_ref.1), channel_id=1, source_target_pairs={{4,8},{8,4},{5,9},{9,5},{6,10},{10,6},{7,11},{11,7},{20,24},{24,20... | collective-permute-start | bytes 786440 | tf_op jit(solution)/shard_map/ppermute | solution.py:414
  17.0 9.2 %collective-permute-start.3 = (bf16[64,2048]{1,0:T(8,128)(2,1)S(1)}, bf16[64,2048]{1,0:T(8,128)(2,1)S(1)}, u32[]{:S(2)}, u32[]{:S(2)}) collective-permute-start(bf16[64,2048]{1,0:T(8,128)(2,1)S(1)} %follow.1.refs_0_.refs_2_), channel_id=1, source_target_pairs={{4,0},{8,12},{5,1},{9,13},{6,2},{10,14},{7,3},{11,15},{20,16},{24,... | collective-permute-start | bytes 786440 | tf_op jit(solution)/shard_map/ppermute | solution.py:414
  32.6 13.6 %collective-permute-start.6 = (bf16[2,48,1536]{2,1,0:T(8,128)(2,1)S(1)}, bf16[2,48,1536]{2,1,0:T(8,128)(2,1)S(1)}, u32[]{:S(2)}, u32[]{:S(2)}) collective-permute-start(bf16[2,48,1536]{2,1,0:T(8,128)(2,1)S(1)} %get-tuple-element.67.refs_0_), channel_id=1, source_target_pairs={{0,2},{1,3},{2,0},{3,1},{4,6},{5,7},{6,4},{7,5},{8,10},{9,11},{10,... | collective-permute-start | bytes 884744 | tf_op jit(solution)/shard_map/ppermute | solution.py:420
  34.4 13.6 %collective-permute-start.7 = (bf16[2,48,1536]{2,1,0:T(8,128)(2,1)S(1)}, bf16[2,48,1536]{2,1,0:T(8,128)(2,1)S(1)}, u32[]{:S(2)}, u32[]{:S(2)}) collective-permute-start(bf16[2,48,1536]{2,1,0:T(8,128)(2,1)S(1)} %get-tuple-element.70.refs_1_), channel_id=1, source_target_pairs={{0,2},{1,3},{2,0},{3,1},{4,6},{5,7},{6,4},{7,5},{8,10},{9,11},{10,... | collective-permute-start | bytes 884744 | tf_op jit(solution)/shard_map/ppermute | solution.py:420
  48.2 6.8 %collective-permute-start.8 = (bf16[2,96,2048]{2,1,0:T(8,128)(2,1)S(1)}, bf16[2,96,2048]{2,1,0:T(8,128)(2,1)S(1)}, u32[]{:S(2)}, u32[]{:S(2)}) collective-permute-start(bf16[2,96,2048]{2,1,0:T(8,128)(2,1)S(1)} %get-tuple-element.80), channel_id=1, source_target_pairs={{0,1},{1,0},{2,3},{3,2},{4,5},{5,4},{6,7},{7,6},{8,9},{9,8},{10,11... | collective-permute-start | bytes 2359304 | tf_op jit(solution)/shard_map/ppermute | solution.py:417
  48.3 9.4 %collective-permute-start.18 = (bf16[48,3072]{1,0:T(8,128)(2,1)S(1)}, bf16[48,3072]{1,0:T(8,128)(2,1)S(1)}, u32[]{:S(2)}, u32[]{:S(2)}) collective-permute-start(bf16[48,3072]{1,0:T(8,128)(2,1)S(1)} %get-tuple-element.85.refs_0_), channel_id=1, source_target_pairs={{0,2},{1,3},{2,0},{3,1},{4,6},{5,7},{6,4},{7,5},{8,10},{9,11},{10,... | collective-permute-start | bytes 884744 | tf_op jit(solution)/shard_map/ppermute | solution.py:420
  55.4 2.8 %collective-permute-start.10 = (bf16[48,1536]{1,0:T(8,128)(2,1)S(1)}, bf16[48,1536]{1,0:T(8,128)(2,1)S(1)}, u32[]{:S(2)}, u32[]{:S(2)}) collective-permute-start(bf16[48,1536]{1,0:T(8,128)(2,1)S(1)} %get-tuple-element.88), channel_id=1, source_target_pairs={{0,1},{1,0},{2,3},{3,2},{4,5},{5,4},{6,7},{7,6},{8,9},{9,8},{10,11... | collective-permute-start | bytes 442376 | tf_op jit(solution)/shard_map/ppermute | solution.py:417
  55.7 12.0 %collective-permute-start.17 = (bf16[2,48,2048]{2,1,0:T(8,128)(2,1)S(1)}, bf16[2,48,2048]{2,1,0:T(8,128)(2,1)S(1)}, u32[]{:S(2)}, u32[]{:S(2)}) collective-permute-start(bf16[2,48,2048]{2,1,0:T(8,128)(2,1)S(1)} %get-tuple-element.95), channel_id=1, source_target_pairs={{0,2},{1,3},{2,0},{3,1},{4,6},{5,7},{6,4},{7,5},{8,10},{9,11},{10,... | collective-permute-start | bytes 1179656 | tf_op jit(solution)/shard_map/ppermute | solution.py:420
  57.7 3.1 %collective-permute-start.19 = (bf16[48,3072]{1,0:T(8,128)(2,1)S(1)}, bf16[48,3072]{1,0:T(8,128)(2,1)S(1)}, u32[]{:S(2)}, u32[]{:S(2)}) collective-permute-start(bf16[48,3072]{1,0:T(8,128)(2,1)S(1)} %get-tuple-element.85.refs_0_), channel_id=1, source_target_pairs={{0,1},{1,0},{2,3},{3,2},{4,5},{5,4},{6,7},{7,6},{8,9},{9,8},{10,11... | collective-permute-start | bytes 884744 | tf_op jit(solution)/shard_map/ppermute | solution.py:417
  59.2 14.9 %collective-permute-start.13 = (bf16[2,48,1536]{2,1,0:T(8,128)(2,1)S(1)}, bf16[2,48,1536]{2,1,0:T(8,128)(2,1)S(1)}, u32[]{:S(2)}, u32[]{:S(2)}) collective-permute-start(bf16[2,48,1536]{2,1,0:T(8,128)(2,1)S(1)} %get-tuple-element.92.refs_5_), channel_id=1, source_target_pairs={{0,2},{1,3},{2,0},{3,1},{4,6},{5,7},{6,4},{7,5},{8,10},{9,11},{10,... | collective-permute-start | bytes 884744 | tf_op jit(solution)/shard_map/ppermute | solution.py:420
  67.8 10.4 %collective-permute-start.21 = (bf16[48,2048]{1,0:T(8,128)(2,1)S(1)}, bf16[48,2048]{1,0:T(8,128)(2,1)S(1)}, u32[]{:S(2)}, u32[]{:S(2)}) collective-permute-start(bf16[48,2048]{1,0:T(8,128)(2,1)S(1)} %activate.5.refs_0_), channel_id=1, source_target_pairs={{0,2},{1,3},{2,0},{3,1},{4,6},{5,7},{6,4},{7,5},{8,10},{9,11},{10,... | collective-permute-start | bytes 589832 | tf_op jit(solution)/shard_map/ppermute | solution.py:420
  74.1 6.5 %collective-permute-start.14 = (bf16[48,1536]{1,0:T(8,128)(2,1)S(1)}, bf16[48,1536]{1,0:T(8,128)(2,1)S(1)}, u32[]{:S(2)}, u32[]{:S(2)}) collective-permute-start(bf16[48,1536]{1,0:T(8,128)(2,1)S(1)} %activate.4.refs_0_), channel_id=1, source_target_pairs={{0,2},{1,3},{2,0},{3,1},{4,6},{5,7},{6,4},{7,5},{8,10},{9,11},{10,... | collective-permute-start | bytes 442376 | tf_op jit(solution)/shard_map/ppermute | solution.py:420
  74.8 5.9 %collective-permute-start.22 = (bf16[48,2048]{1,0:T(8,128)(2,1)S(1)}, bf16[48,2048]{1,0:T(8,128)(2,1)S(1)}, u32[]{:S(2)}, u32[]{:S(2)}) collective-permute-start(bf16[48,2048]{1,0:T(8,128)(2,1)S(1)} %activate.5.refs_0_), channel_id=1, source_target_pairs={{0,1},{1,0},{2,3},{3,2},{4,5},{5,4},{6,7},{7,6},{8,9},{9,8},{10,11... | collective-permute-start | bytes 589832 | tf_op jit(solution)/shard_map/ppermute | solution.py:417
  78.2 4.2 %collective-permute-start.15 = (bf16[48,1536]{1,0:T(8,128)(2,1)S(1)}, bf16[48,1536]{1,0:T(8,128)(2,1)S(1)}, u32[]{:S(2)}, u32[]{:S(2)}) collective-permute-start(bf16[48,1536]{1,0:T(8,128)(2,1)S(1)} %activate.4.refs_0_), channel_id=1, source_target_pairs={{0,1},{1,0},{2,3},{3,2},{4,5},{5,4},{6,7},{7,6},{8,9},{9,8},{10,11... | collective-permute-start | bytes 442376 | tf_op jit(solution)/shard_map/ppermute | solution.py:417
  84.7 6.6 %collective-permute-start.24 = (bf16[32,2048]{1,0:T(8,128)(2,1)S(1)}, bf16[32,2048]{1,0:T(8,128)(2,1)S(1)}, u32[]{:S(2)}, u32[]{:S(2)}) collective-permute-start(bf16[32,2048]{1,0:T(8,128)(2,1)S(1)} %get-tuple-element.99), channel_id=1, source_target_pairs={{0,4},{12,8},{1,5},{13,9},{2,6},{14,10},{3,7},{15,11},{16,20},{28,... | collective-permute-start | bytes 393224 | tf_op jit(solution)/shard_map/ppermute | solution.py:414
  87.5 7.6 %collective-permute-start.26 = (bf16[32,2048]{1,0:T(8,128)(2,1)S(1)}, bf16[32,2048]{1,0:T(8,128)(2,1)S(1)}, u32[]{:S(2)}, u32[]{:S(2)}) collective-permute-start(bf16[32,2048]{1,0:T(8,128)(2,1)S(1)} %get-tuple-element.101), channel_id=1, source_target_pairs={{0,4},{12,8},{1,5},{13,9},{2,6},{14,10},{3,7},{15,11},{16,20},{28,... | collective-permute-start | bytes 393224 | tf_op jit(solution)/shard_map/ppermute | solution.py:414
  88.8 8.4 %collective-permute-start.30 = (bf16[32,2048]{1,0:T(8,128)(2,1)S(1)}, bf16[32,2048]{1,0:T(8,128)(2,1)S(1)}, u32[]{:S(2)}, u32[]{:S(2)}) collective-permute-start(bf16[32,2048]{1,0:T(8,128)(2,1)S(1)} %get-tuple-element.99), channel_id=1, source_target_pairs={{4,8},{8,4},{5,9},{9,5},{6,10},{10,6},{7,11},{11,7},{20,24},{24,20... | collective-permute-start | bytes 393224 | tf_op jit(solution)/shard_map/ppermute | solution.py:414
  89.5 9.8 %collective-permute-start.31 = (bf16[32,2048]{1,0:T(8,128)(2,1)S(1)}, bf16[32,2048]{1,0:T(8,128)(2,1)S(1)}, u32[]{:S(2)}, u32[]{:S(2)}) collective-permute-start(bf16[32,2048]{1,0:T(8,128)(2,1)S(1)} %get-tuple-element.101), channel_id=1, source_target_pairs={{4,8},{8,4},{5,9},{9,5},{6,10},{10,6},{7,11},{11,7},{20,24},{24,20... | collective-permute-start | bytes 393224 | tf_op jit(solution)/shard_map/ppermute | solution.py:414
  91.4 16.5 %collective-permute-start.25 = (bf16[32,2048]{1,0:T(8,128)(2,1)S(1)}, bf16[32,2048]{1,0:T(8,128)(2,1)S(1)}, u32[]{:S(2)}, u32[]{:S(2)}) collective-permute-start(bf16[32,2048]{1,0:T(8,128)(2,1)S(1)} %relay.2.refs_2_), channel_id=1, source_target_pairs={{0,8},{4,12},{8,0},{12,4},{1,9},{5,13},{9,1},{13,5},{2,10},{6,14},... | collective-permute-start | bytes 393224 | tf_op jit(solution)/shard_map/ppermute | solution.py:414
  95.2 14.8 %collective-permute-start.27 = (bf16[32,2048]{1,0:T(8,128)(2,1)S(1)}, bf16[32,2048]{1,0:T(8,128)(2,1)S(1)}, u32[]{:S(2)}, u32[]{:S(2)}) collective-permute-start(bf16[32,2048]{1,0:T(8,128)(2,1)S(1)} %get-tuple-element.104), channel_id=1, source_target_pairs={{0,8},{4,12},{8,0},{12,4},{1,9},{5,13},{9,1},{13,5},{2,10},{6,14},... | collective-permute-start | bytes 393224 | tf_op jit(solution)/shard_map/ppermute | solution.py:414
  97.3 12.7 %collective-permute-start.28 = (bf16[32,2048]{1,0:T(8,128)(2,1)S(1)}, bf16[32,2048]{1,0:T(8,128)(2,1)S(1)}, u32[]{:S(2)}, u32[]{:S(2)}) collective-permute-start(bf16[32,2048]{1,0:T(8,128)(2,1)S(1)} %get-tuple-element.105), channel_id=1, source_target_pairs={{0,4},{4,0},{8,12},{12,8},{1,5},{5,1},{9,13},{13,9},{2,6},{6,2},{1... | collective-permute-start | bytes 393224 | tf_op jit(solution)/shard_map/ppermute | solution.py:414
  97.3 13.3 %collective-permute-start.29 = (bf16[32,2048]{1,0:T(8,128)(2,1)S(1)}, bf16[32,2048]{1,0:T(8,128)(2,1)S(1)}, u32[]{:S(2)}, u32[]{:S(2)}) collective-permute-start(bf16[32,2048]{1,0:T(8,128)(2,1)S(1)} %get-tuple-element.106), channel_id=1, source_target_pairs={{0,4},{4,0},{8,12},{12,8},{1,5},{5,1},{9,13},{13,9},{2,6},{6,2},{1... | collective-permute-start | bytes 393224 | tf_op jit(solution)/shard_map/ppermute | solution.py:414
  (12 other events, 34.8 us)

commit v18 on v15

--- a/solution.py
+++ b/solution.py
@@ -475,11 +475,11 @@
         own, three, *halves = spread
         ends = [over_z(piece, 1, (0, 3)) for piece in halves[4:]]
         middle = over_z(three, 3, (1, 2))
-        low, _ = relay(halves[2], ends[0], [], [])
-        high, near = relay(halves[3], ends[1], halves[:2], [middle])
+        low, near = relay(halves[2], ends[0], halves[:2], [])
+        high, _ = relay(halves[3], ends[1], [], [middle])
         far = jnp.concatenate([over_z(low, 2), over_z(high, 2)], axis=0)
         near = jnp.concatenate([over_z(piece, 1) for piece in near], axis=0)
-        parts = [own, near, far, middle]
+        parts = [own, far, near, middle]
     else:
         parts = [spread[0]] + [over_z(spread[k], k) for k in range(1, n_gx)]
     return sum(p.astype(F32) for p in parts).astype(BF16)

time: 111 us -> 109 us (0.982)
  transfers between devices with their start and end apart: 31 -> 31, of which waited for: 15 -> 14; matrix products, arithmetic and copies ran while one was open for 0% -> 0% of each run, Pallas kernels for 38% -> 38%
where the time goes in v18:
time: 109 us
  Pallas kernels  47.4 us (43%)
  starting transfers between devices  31 us (28%)
  waiting for transfers between devices  27.9 us (26%)
  local copies, waits for them, and re-layouts  1.61 us (1%)
    ppermute x11, starting transfers between devices, over_z(): return lax.ppermute(block, 'gx', [(z, z ^ k) for z in among])  20.7 us
    ppermute x7, waiting for transfers between devices, over_x(): lax.ppermute(block, 'gy', [(i, (i + 2 * k) % n_gy) for i in range(n_gy)])  14.3 us
    ppermute x11, waiting for transfers between devices, over_z(): return lax.ppermute(block, 'gx', [(z, z ^ k) for z in among])  12.7 us
    pallas_call x1, Pallas kernels, prepare(): pl.pallas_call(functools.partial(prepare_kernel, n_gx, nx, chunks), out_s...  8.94 us
    pallas_call x3, Pallas kernels, gate_up_held(): pl.pallas_call(functools.partial(gate_up_held_kernel, len(after), tile),...  8.63 us
    ppermute x7, starting transfers between devices, over_x(): lax.ppermute(block, 'gy', [(i, (i + 2 * k) % n_gy) for i in range(n_gy)])  7.97 us
    pallas_call x1, Pallas kernels, gate_up(): pl.pallas_call(functools.partial(gate_up_kernel, len(after)), out_shape=[...  6.84 us
    pallas_call x1, Pallas kernels, down(): pl.pallas_call(functools.partial(down_kernel, len(hidden)), out_shape=jax...  6.63 us
  transfers between devices with their start and end apart: 31, of which 14 were waited for; matrix products, arithmetic and copies ran while one was open for 0% of the time, Pallas kernels for 38%

profile of v18, /device:TPU:0, one launch (start us, length us, event | category | flops | bytes accessed | tf_op | source)
XLA Modules:
  0.0 109.2 jit_solution(3733117257183120417)
XLA Ops:
  0.0 4.0 %collective-permute-start.1 = (bf16[64,2048]{1,0:T(8,128)(2,1)}, bf16[64,2048]{1,0:T(8,128)(2,1)S(1)}, u32[]{:S(2)}, u32[]{:S(2)}) collective-permute-start(bf16[64,2048]{1,0:T(8,128)(2,1)} %tok_ref.1), channel_id=1, source_target_pairs={{0,8},{4,12},{8,0},{12,4},{1,9},{5,13},{9,1},{13,5},{2,10},{6,14},... | collective-permute-start | bytes 786440 | tf_op jit(solution)/shard_map/ppermute | solution.py:414
  4.0 1.6 %collective-permute-start = (bf16[64,2048]{1,0:T(8,128)(2,1)}, bf16[64,2048]{1,0:T(8,128)(2,1)S(1)}, u32[]{:S(2)}, u32[]{:S(2)}) collective-permute-start(bf16[64,2048]{1,0:T(8,128)(2,1)} %tok_ref.1), channel_id=1, source_target_pairs={{0,4},{4,0},{8,12},{12,8},{1,5},{5,1},{9,13},{13,9},{2,6},{6,2},{1... | collective-permute-start | bytes 786440 | tf_op jit(solution)/shard_map/ppermute | solution.py:414
  7.9 8.9 %prepare.1 = (bf16[192,256]{1,0:T(8,128)(2,1)S(1)}, bf16[256,192]{1,0:T(8,128)(2,1)S(1)}, bf16[64,2048]{1,0:T(8,128)(2,1)S(1)}, bf16[2048,1536]{1,0:T(8,128)(2,1...) custom-call(s32[4]{0:T(128)S(1)} %copy-done.3, ...), custom_call_target="tpu_custom_call" | custom-call | tf_op jit(solution)/shard_map/prepare/pallas_call | solution.py:104
  18.3 5.8 %fetch_columns.1 = (bf16[2048,2048]{1,0:T(8,128)(2,1)S(1)}, bf16[2048,2048]{1,0:T(8,128)(2,1)S(1)}) custom-call(bf16[2048,6656]{1,0:T(8,128)(2,1)} %gate_ref.5, bf16[2048,6656]{1,0:T(8,128)(2,1)} %up_ref.5, bf16[64,2048]{1,0:T(8,128)(2,1)S(1)} %follow.1.refs_0_.refs_2_), custom_call_target="tpu_custom_call" | custom-call | tf_op jit(solution)/shard_map/fetch_columns/pallas_call | solution.py:53
  24.2 2.1 %collective-permute-done.3.refs_4_ = bf16[64,2048]{1,0:T(8,128)(2,1)S(1)} collective-permute-done((bf16[64,2048]{1,0:T(8,128)(2,1)S(1)}, bf16[64,2048]{1,0:T(8,128)(2,1)S(1)}, u32[]{:S(2)}, u32[]{:S(2)}) %collective-permute-start.3) | collective-permute-done | bytes 262176 | tf_op jit(solution)/shard_map/ppermute | solution.py:414
  26.6 2.6 %gate_up_held.3 = (f32[2,96,1536]{2,1,0:T(8,128)S(1)}, bf16[2,96,1536]{2,1,0:T(8,128)(2,1)S(1)}) custom-call(bf16[192,2048]{1,0:T(8,128)(2,1)S(1)} %compact.1.tok_ref, bf16[2048,1536]{1,0:T(8,128)(2,1)S(1)} %get-tuple-element.61.gate_ref, bf16[2048,1536]{1,0:T(8,128)(2,1)S(1)} %get-tuple-element.62.up_ref), custom_call_target="tpu_custom_call" | custom-call | tf_op jit(solution)/shard_map/gate_up_held/pallas_call | solution.py:180
  29.3 2.6 %gate_up_held.4 = (f32[2,96,1536]{2,1,0:T(8,128)S(1)}, bf16[2,96,1536]{2,1,0:T(8,128)(2,1)S(1)}) custom-call(bf16[192,2048]{1,0:T(8,128)(2,1)S(1)} %compact.1.tok_ref, bf16[2048,1536]{1,0:T(8,128)(2,1)S(1)} %get-tuple-element.65.gate_ref, bf16[2048,1536]{1,0:T(8,128)(2,1)S(1)} %get-tuple-element.66.up_ref), custom_call_target="tpu_custom_call" | custom-call | tf_op jit(solution)/shard_map/gate_up_held/pallas_call | solution.py:180
  35.9 3.4 %gate_up_held.5 = (f32[2,96,2048]{2,1,0:T(8,128)S(1)}, bf16[2,96,2048]{2,1,0:T(8,128)(2,1)S(1)}) custom-call(bf16[192,2048]{1,0:T(8,128)(2,1)S(1)} %compact.1.tok_ref, bf16[2048,2048]{1,0:T(8,128)(2,1)S(1)} %get-tuple-element.59.refs_5_.gate_ref, bf16[2048,2048]{1,0:T(8,128)(2,1)S(1)} %get-tuple-element.60.up_ref, ...), custom_call_target="tpu_custom_call" | custom-call | tf_op jit(solution)/shard_map/gate_up_held/pallas_call | solution.py:180
  39.3 6.8 %gate_up.1 = (f32[2,96,1536]{2,1,0:T(8,128)S(1)}, bf16[48,1536]{1,0:T(8,128)(2,1)S(1)}, bf16[48,1536]{1,0:T(8,128)(2,1)S(1)}, bf16[48,1536]{1,0:T(8,128)(2,1)S(1)}, bf16[48,1536]{1,0:T(8,128)(2,1)S(1)}) custom-call(bf16[192,2048]{1,0:T(8,128)(2,1)S(1)} %compact.1.tok_ref, bf16[2048,6656]{1,0:T(8,128)(2,1)} %gate_ref.5, bf16[2048,6656]{1,0:T(8,128)(2,1)} %up_ref.5, ...), custom_call_target="tpu_custom_call" | custom-call | tf_op jit(solution)/shard_map/gate_up/pallas_call | solution.py:204
  46.2 1.7 %collective-permute-done.7.refs_3_ = bf16[2,48,1536]{2,1,0:T(8,128)(2,1)S(1)} collective-permute-done((bf16[2,48,1536]{2,1,0:T(8,128)(2,1)S(1)}, bf16[2,48,1536]{2,1,0:T(8,128)(2,1)S(1)}, u32[]{:S(2)}, u32[]{:S(2)}) %collective-permute-start.7) | collective-permute-done | bytes 294944 | tf_op jit(solution)/shard_map/ppermute | solution.py:420
  49.8 5.2 %fetch.1 = (bf16[2048,2048]{1,0:T(8,128)(2,1)S(1)}, bf16[1536,2048]{1,0:T(8,128)(2,1)S(1)}) custom-call(bf16[6656,2048]{1,0:T(8,128)(2,1)} %refs_4_.1, bf16[48,3072]{1,0:T(8,128)(2,1)S(1)} %get-tuple-element.86.refs_0_), custom_call_target="tpu_custom_call" | custom-call | tf_op jit(solution)/shard_map/fetch/pallas_call | solution.py:350
  59.2 1.6 %collective-permute-start.13 = (bf16[2,48,1536]{2,1,0:T(8,128)(2,1)S(1)}, bf16[2,48,1536]{2,1,0:T(8,128)(2,1)S(1)}, u32[]{:S(2)}, u32[]{:S(2)}) collective-permute-start(bf16[2,48,1536]{2,1,0:T(8,128)(2,1)S(1)} %get-tuple-element.93.refs_5_), channel_id=1, source_target_pairs={{0,2},{1,3},{2,0},{3,1},{4,6},{5,7},{6,4},{7,5},{8,10},{9,11},{10,... | collective-permute-start | bytes 884744 | tf_op jit(solution)/shard_map/ppermute | solution.py:420
  60.8 6.6 %down.1.refs_2_.refs_5_ = f32[192,2048]{1,0:T(8,128)S(1)} custom-call(bf16[48,3072]{1,0:T(8,128)(2,1)S(1)} %get-tuple-element.86.refs_0_, bf16[48,3072]{1,0:T(8,128)(2,1)S(1)} %collective-permute-done.18.refs_1_, bf16[48,3072]{1,0:T(8,128)(2,1)S(1)} %collective-permute-done.19.refs_2_, bf16[48,3072]{1,0:T(8,128)(2,1)S(1)} %collective-permute-done.20.refs_3_, ...), custom_call_target="tpu_custom_call" | custom-call | tf_op jit(solution)/shard_map/down/pallas_call | solution.py:321
  68.5 5.5 %collective-permute-done.13.refs_1_ = bf16[2,48,1536]{2,1,0:T(8,128)(2,1)S(1)} collective-permute-done((bf16[2,48,1536]{2,1,0:T(8,128)(2,1)S(1)}, bf16[2,48,1536]{2,1,0:T(8,128)(2,1)S(1)}, u32[]{:S(2)}, u32[]{:S(2)}) %collective-permute-start.13) | collective-permute-done | bytes 294944 | tf_op jit(solution)/shard_map/ppermute | solution.py:420
  74.8 3.5 %collective-permute-done.21.refs_1_ = bf16[48,2048]{1,0:T(8,128)(2,1)S(1)} collective-permute-done((bf16[48,2048]{1,0:T(8,128)(2,1)S(1)}, bf16[48,2048]{1,0:T(8,128)(2,1)S(1)}, u32[]{:S(2)}, u32[]{:S(2)}) %collective-permute-start.21) | collective-permute-done | bytes 196640 | tf_op jit(solution)/shard_map/ppermute | solution.py:420
  78.7 1.9 %collective-permute-done.14.refs_1_ = bf16[48,1536]{1,0:T(8,128)(2,1)S(1)} collective-permute-done((bf16[48,1536]{1,0:T(8,128)(2,1)S(1)}, bf16[48,1536]{1,0:T(8,128)(2,1)S(1)}, u32[]{:S(2)}, u32[]{:S(2)}) %collective-permute-start.14) | collective-permute-done | bytes 147488 | tf_op jit(solution)/shard_map/ppermute | solution.py:420
  80.6 1.8 %down_held.2.refs_5_ = f32[192,2048]{1,0:T(8,128)S(1)} custom-call(bf16[48,2048]{1,0:T(8,128)(2,1)S(1)} %activate.5.refs_0_, bf16[48,2048]{1,0:T(8,128)(2,1)S(1)} %collective-permute-done.21.refs_1_, bf16[48,2048]{1,0:T(8,128)(2,1)S(1)} %collective-permute-done.22.refs_2_, bf16[48,2048]{1,0:T(8,128)(2,1)S(1)} %collective-permute-done.23.refs_3_, ...), custom_call_target="tpu_custom_call" | custom-call | tf_op jit(solution)/shard_map/down_held/pallas_call | solution.py:384
  82.5 2.2 %down_held.3 = (bf16[64,2048]{1,0:T(8,128)(2,1)S(1)}, bf16[64,2048]{1,0:T(8,128)(2,1)S(1)}, bf16[32,2048]{1,0:T(8,128)(2,1)S(1)}, bf16[32,2048]{1,0:T(8,128)(2,1...) custom-call(bf16[48,1536]{1,0:T(8,128)(2,1)S(1)} %activate.4.refs_0_, ...), custom_call_target="tpu_custom_call" | custom-call | tf_op jit(solution)/shard_map/down_held/pallas_call | solution.py:384
  85.4 5.6 %collective-permute-start.24 = (bf16[32,2048]{1,0:T(8,128)(2,1)S(1)}, bf16[32,2048]{1,0:T(8,128)(2,1)S(1)}, u32[]{:S(2)}, u32[]{:S(2)}) collective-permute-start(bf16[32,2048]{1,0:T(8,128)(2,1)S(1)} %get-tuple-element.100), channel_id=1, source_target_pairs={{0,4},{12,8},{1,5},{13,9},{2,6},{14,10},{3,7},{15,11},{16,20},{28,... | collective-permute-start | bytes 393224 | tf_op jit(solution)/shard_map/ppermute | solution.py:414
  92.3 2.5 %collective-permute-done.24.got_ref = bf16[32,2048]{1,0:T(8,128)(2,1)S(1)} collective-permute-done((bf16[32,2048]{1,0:T(8,128)(2,1)S(1)}, bf16[32,2048]{1,0:T(8,128)(2,1)S(1)}, u32[]{:S(2)}, u32[]{:S(2)}) %collective-permute-start.24) | collective-permute-done | bytes 131104 | tf_op jit(solution)/shard_map/ppermute | solution.py:414
  94.8 2.5 %collective-permute-start.25 = (bf16[32,2048]{1,0:T(8,128)(2,1)S(1)}, bf16[32,2048]{1,0:T(8,128)(2,1)S(1)}, u32[]{:S(2)}, u32[]{:S(2)}) collective-permute-start(bf16[32,2048]{1,0:T(8,128)(2,1)S(1)} %get-tuple-element.103), channel_id=1, source_target_pairs={{0,8},{4,12},{8,0},{12,4},{1,9},{5,13},{9,1},{13,5},{2,10},{6,14},... | collective-permute-start | bytes 393224 | tf_op jit(solution)/shard_map/ppermute | solution.py:414
  97.5 1.9 %collective-permute-start.30 = (bf16[32,2048]{1,0:T(8,128)(2,1)S(1)}, bf16[32,2048]{1,0:T(8,128)(2,1)S(1)}, u32[]{:S(2)}, u32[]{:S(2)}) collective-permute-start(bf16[32,2048]{1,0:T(8,128)(2,1)S(1)} %get-tuple-element.108), channel_id=1, source_target_pairs={{0,4},{4,0},{8,12},{12,8},{1,5},{5,1},{9,13},{13,9},{2,6},{6,2},{1... | collective-permute-start | bytes 393224 | tf_op jit(solution)/shard_map/ppermute | solution.py:414
  100.4 3.7 %collective-permute-done.25 = bf16[32,2048]{1,0:T(8,128)(2,1)S(1)} collective-permute-done((bf16[32,2048]{1,0:T(8,128)(2,1)S(1)}, bf16[32,2048]{1,0:T(8,128)(2,1)S(1)}, u32[]{:S(2)}, u32[]{:S(2)}) %collective-permute-start.25) | collective-permute-done | bytes 131104 | tf_op jit(solution)/shard_map/ppermute | solution.py:414
  104.1 2.7 %collective-permute-done.29 = bf16[32,2048]{1,0:T(8,128)(2,1)S(1)} collective-permute-done((bf16[32,2048]{1,0:T(8,128)(2,1)S(1)}, bf16[32,2048]{1,0:T(8,128)(2,1)S(1)}, u32[]{:S(2)}, u32[]{:S(2)}) %collective-permute-start.29) | collective-permute-done | bytes 131104 | tf_op jit(solution)/shard_map/ppermute | solution.py:414
  (68 shorter events, 22.0 us)
Async XLA Ops:
  0.0 17.0 %collective-permute-start.1 = (bf16[64,2048]{1,0:T(8,128)(2,1)}, bf16[64,2048]{1,0:T(8,128)(2,1)S(1)}, u32[]{:S(2)}, u32[]{:S(2)}) collective-permute-start(bf16[64,2048]{1,0:T(8,128)(2,1)} %tok_ref.1), channel_id=1, source_target_pairs={{0,8},{4,12},{8,0},{12,4},{1,9},{5,13},{9,1},{13,5},{2,10},{6,14},... | collective-permute-start | bytes 786440 | tf_op jit(solution)/shard_map/ppermute | solution.py:414
  4.0 20.1 %collective-permute-start = (bf16[64,2048]{1,0:T(8,128)(2,1)}, bf16[64,2048]{1,0:T(8,128)(2,1)S(1)}, u32[]{:S(2)}, u32[]{:S(2)}) collective-permute-start(bf16[64,2048]{1,0:T(8,128)(2,1)} %tok_ref.1), channel_id=1, source_target_pairs={{0,4},{4,0},{8,12},{12,8},{1,5},{5,1},{9,13},{13,9},{2,6},{6,2},{1... | collective-permute-start | bytes 786440 | tf_op jit(solution)/shard_map/ppermute | solution.py:414
  5.6 18.6 %collective-permute-start.2 = (bf16[64,2048]{1,0:T(8,128)(2,1)}, bf16[64,2048]{1,0:T(8,128)(2,1)S(1)}, u32[]{:S(2)}, u32[]{:S(2)}) collective-permute-start(bf16[64,2048]{1,0:T(8,128)(2,1)} %tok_ref.1), channel_id=1, source_target_pairs={{4,8},{8,4},{5,9},{9,5},{6,10},{10,6},{7,11},{11,7},{20,24},{24,20... | collective-permute-start | bytes 786440 | tf_op jit(solution)/shard_map/ppermute | solution.py:414
  17.0 9.2 %collective-permute-start.3 = (bf16[64,2048]{1,0:T(8,128)(2,1)S(1)}, bf16[64,2048]{1,0:T(8,128)(2,1)S(1)}, u32[]{:S(2)}, u32[]{:S(2)}) collective-permute-start(bf16[64,2048]{1,0:T(8,128)(2,1)S(1)} %follow.1.refs_0_.refs_2_), channel_id=1, source_target_pairs={{4,0},{8,12},{5,1},{9,13},{6,2},{10,14},{7,3},{11,15},{20,16},{24,... | collective-permute-start | bytes 786440 | tf_op jit(solution)/shard_map/ppermute | solution.py:414
  29.3 2.7 %collective-permute-start.4 = (bf16[2,96,1536]{2,1,0:T(8,128)(2,1)S(1)}, bf16[2,96,1536]{2,1,0:T(8,128)(2,1)S(1)}, u32[]{:S(2)}, u32[]{:S(2)}) collective-permute-start(bf16[2,96,1536]{2,1,0:T(8,128)(2,1)S(1)} %get-tuple-element.64), channel_id=1, source_target_pairs={{0,1},{1,0},{2,3},{3,2},{4,5},{5,4},{6,7},{7,6},{8,9},{9,8},{10,11... | collective-permute-start | bytes 1769480 | tf_op jit(solution)/shard_map/ppermute | solution.py:417
  32.6 13.6 %collective-permute-start.6 = (bf16[2,48,1536]{2,1,0:T(8,128)(2,1)S(1)}, bf16[2,48,1536]{2,1,0:T(8,128)(2,1)S(1)}, u32[]{:S(2)}, u32[]{:S(2)}) collective-permute-start(bf16[2,48,1536]{2,1,0:T(8,128)(2,1)S(1)} %get-tuple-element.68.refs_0_), channel_id=1, source_target_pairs={{0,2},{1,3},{2,0},{3,1},{4,6},{5,7},{6,4},{7,5},{8,10},{9,11},{10,... | collective-permute-start | bytes 884744 | tf_op jit(solution)/shard_map/ppermute | solution.py:420
  34.4 13.6 %collective-permute-start.7 = (bf16[2,48,1536]{2,1,0:T(8,128)(2,1)S(1)}, bf16[2,48,1536]{2,1,0:T(8,128)(2,1)S(1)}, u32[]{:S(2)}, u32[]{:S(2)}) collective-permute-start(bf16[2,48,1536]{2,1,0:T(8,128)(2,1)S(1)} %get-tuple-element.71.refs_1_), channel_id=1, source_target_pairs={{0,2},{1,3},{2,0},{3,1},{4,6},{5,7},{6,4},{7,5},{8,10},{9,11},{10,... | collective-permute-start | bytes 884744 | tf_op jit(solution)/shard_map/ppermute | solution.py:420
  48.2 6.8 %collective-permute-start.8 = (bf16[2,96,2048]{2,1,0:T(8,128)(2,1)S(1)}, bf16[2,96,2048]{2,1,0:T(8,128)(2,1)S(1)}, u32[]{:S(2)}, u32[]{:S(2)}) collective-permute-start(bf16[2,96,2048]{2,1,0:T(8,128)(2,1)S(1)} %get-tuple-element.81), channel_id=1, source_target_pairs={{0,1},{1,0},{2,3},{3,2},{4,5},{5,4},{6,7},{7,6},{8,9},{9,8},{10,11... | collective-permute-start | bytes 2359304 | tf_op jit(solution)/shard_map/ppermute | solution.py:417
  48.3 9.4 %collective-permute-start.18 = (bf16[48,3072]{1,0:T(8,128)(2,1)S(1)}, bf16[48,3072]{1,0:T(8,128)(2,1)S(1)}, u32[]{:S(2)}, u32[]{:S(2)}) collective-permute-start(bf16[48,3072]{1,0:T(8,128)(2,1)S(1)} %get-tuple-element.86.refs_0_), channel_id=1, source_target_pairs={{0,2},{1,3},{2,0},{3,1},{4,6},{5,7},{6,4},{7,5},{8,10},{9,11},{10,... | collective-permute-start | bytes 884744 | tf_op jit(solution)/shard_map/ppermute | solution.py:420
  55.4 2.8 %collective-permute-start.10 = (bf16[48,1536]{1,0:T(8,128)(2,1)S(1)}, bf16[48,1536]{1,0:T(8,128)(2,1)S(1)}, u32[]{:S(2)}, u32[]{:S(2)}) collective-permute-start(bf16[48,1536]{1,0:T(8,128)(2,1)S(1)} %get-tuple-element.89), channel_id=1, source_target_pairs={{0,1},{1,0},{2,3},{3,2},{4,5},{5,4},{6,7},{7,6},{8,9},{9,8},{10,11... | collective-permute-start | bytes 442376 | tf_op jit(solution)/shard_map/ppermute | solution.py:417
  55.7 12.0 %collective-permute-start.17 = (bf16[2,48,2048]{2,1,0:T(8,128)(2,1)S(1)}, bf16[2,48,2048]{2,1,0:T(8,128)(2,1)S(1)}, u32[]{:S(2)}, u32[]{:S(2)}) collective-permute-start(bf16[2,48,2048]{2,1,0:T(8,128)(2,1)S(1)} %get-tuple-element.96), channel_id=1, source_target_pairs={{0,2},{1,3},{2,0},{3,1},{4,6},{5,7},{6,4},{7,5},{8,10},{9,11},{10,... | collective-permute-start | bytes 1179656 | tf_op jit(solution)/shard_map/ppermute | solution.py:420
  57.7 3.1 %collective-permute-start.19 = (bf16[48,3072]{1,0:T(8,128)(2,1)S(1)}, bf16[48,3072]{1,0:T(8,128)(2,1)S(1)}, u32[]{:S(2)}, u32[]{:S(2)}) collective-permute-start(bf16[48,3072]{1,0:T(8,128)(2,1)S(1)} %get-tuple-element.86.refs_0_), channel_id=1, source_target_pairs={{0,1},{1,0},{2,3},{3,2},{4,5},{5,4},{6,7},{7,6},{8,9},{9,8},{10,11... | collective-permute-start | bytes 884744 | tf_op jit(solution)/shard_map/ppermute | solution.py:417
  59.2 14.9 %collective-permute-start.13 = (bf16[2,48,1536]{2,1,0:T(8,128)(2,1)S(1)}, bf16[2,48,1536]{2,1,0:T(8,128)(2,1)S(1)}, u32[]{:S(2)}, u32[]{:S(2)}) collective-permute-start(bf16[2,48,1536]{2,1,0:T(8,128)(2,1)S(1)} %get-tuple-element.93.refs_5_), channel_id=1, source_target_pairs={{0,2},{1,3},{2,0},{3,1},{4,6},{5,7},{6,4},{7,5},{8,10},{9,11},{10,... | collective-permute-start | bytes 884744 | tf_op jit(solution)/shard_map/ppermute | solution.py:420
  67.8 10.4 %collective-permute-start.21 = (bf16[48,2048]{1,0:T(8,128)(2,1)S(1)}, bf16[48,2048]{1,0:T(8,128)(2,1)S(1)}, u32[]{:S(2)}, u32[]{:S(2)}) collective-permute-start(bf16[48,2048]{1,0:T(8,128)(2,1)S(1)} %activate.5.refs_0_), channel_id=1, source_target_pairs={{0,2},{1,3},{2,0},{3,1},{4,6},{5,7},{6,4},{7,5},{8,10},{9,11},{10,... | collective-permute-start | bytes 589832 | tf_op jit(solution)/shard_map/ppermute | solution.py:420
  74.1 6.5 %collective-permute-start.14 = (bf16[48,1536]{1,0:T(8,128)(2,1)S(1)}, bf16[48,1536]{1,0:T(8,128)(2,1)S(1)}, u32[]{:S(2)}, u32[]{:S(2)}) collective-permute-start(bf16[48,1536]{1,0:T(8,128)(2,1)S(1)} %activate.4.refs_0_), channel_id=1, source_target_pairs={{0,2},{1,3},{2,0},{3,1},{4,6},{5,7},{6,4},{7,5},{8,10},{9,11},{10,... | collective-permute-start | bytes 442376 | tf_op jit(solution)/shard_map/ppermute | solution.py:420
  74.8 5.9 %collective-permute-start.22 = (bf16[48,2048]{1,0:T(8,128)(2,1)S(1)}, bf16[48,2048]{1,0:T(8,128)(2,1)S(1)}, u32[]{:S(2)}, u32[]{:S(2)}) collective-permute-start(bf16[48,2048]{1,0:T(8,128)(2,1)S(1)} %activate.5.refs_0_), channel_id=1, source_target_pairs={{0,1},{1,0},{2,3},{3,2},{4,5},{5,4},{6,7},{7,6},{8,9},{9,8},{10,11... | collective-permute-start | bytes 589832 | tf_op jit(solution)/shard_map/ppermute | solution.py:417
  78.2 4.2 %collective-permute-start.15 = (bf16[48,1536]{1,0:T(8,128)(2,1)S(1)}, bf16[48,1536]{1,0:T(8,128)(2,1)S(1)}, u32[]{:S(2)}, u32[]{:S(2)}) collective-permute-start(bf16[48,1536]{1,0:T(8,128)(2,1)S(1)} %activate.4.refs_0_), channel_id=1, source_target_pairs={{0,1},{1,0},{2,3},{3,2},{4,5},{5,4},{6,7},{7,6},{8,9},{9,8},{10,11... | collective-permute-start | bytes 442376 | tf_op jit(solution)/shard_map/ppermute | solution.py:417
  84.7 14.7 %collective-permute-start.27 = (bf16[64,2048]{1,0:T(8,128)(2,1)S(1)}, bf16[64,2048]{1,0:T(8,128)(2,1)S(1)}, u32[]{:S(2)}, u32[]{:S(2)}) collective-permute-start(bf16[64,2048]{1,0:T(8,128)(2,1)S(1)} %get-tuple-element.106), channel_id=1, source_target_pairs={{4,8},{8,4},{5,9},{9,5},{6,10},{10,6},{7,11},{11,7},{20,24},{24,20... | collective-permute-start | bytes 786440 | tf_op jit(solution)/shard_map/ppermute | solution.py:414
  85.4 9.4 %collective-permute-start.24 = (bf16[32,2048]{1,0:T(8,128)(2,1)S(1)}, bf16[32,2048]{1,0:T(8,128)(2,1)S(1)}, u32[]{:S(2)}, u32[]{:S(2)}) collective-permute-start(bf16[32,2048]{1,0:T(8,128)(2,1)S(1)} %get-tuple-element.100), channel_id=1, source_target_pairs={{0,4},{12,8},{1,5},{13,9},{2,6},{14,10},{3,7},{15,11},{16,20},{28,... | collective-permute-start | bytes 393224 | tf_op jit(solution)/shard_map/ppermute | solution.py:414
  91.0 8.4 %collective-permute-start.26 = (bf16[32,2048]{1,0:T(8,128)(2,1)S(1)}, bf16[32,2048]{1,0:T(8,128)(2,1)S(1)}, u32[]{:S(2)}, u32[]{:S(2)}) collective-permute-start(bf16[32,2048]{1,0:T(8,128)(2,1)S(1)} %get-tuple-element.105), channel_id=1, source_target_pairs={{0,4},{12,8},{1,5},{13,9},{2,6},{14,10},{3,7},{15,11},{16,20},{28,... | collective-permute-start | bytes 393224 | tf_op jit(solution)/shard_map/ppermute | solution.py:414
  94.8 9.3 %collective-permute-start.25 = (bf16[32,2048]{1,0:T(8,128)(2,1)S(1)}, bf16[32,2048]{1,0:T(8,128)(2,1)S(1)}, u32[]{:S(2)}, u32[]{:S(2)}) collective-permute-start(bf16[32,2048]{1,0:T(8,128)(2,1)S(1)} %get-tuple-element.103), channel_id=1, source_target_pairs={{0,8},{4,12},{8,0},{12,4},{1,9},{5,13},{9,1},{13,5},{2,10},{6,14},... | collective-permute-start | bytes 393224 | tf_op jit(solution)/shard_map/ppermute | solution.py:414
  97.3 9.5 %collective-permute-start.29 = (bf16[32,2048]{1,0:T(8,128)(2,1)S(1)}, bf16[32,2048]{1,0:T(8,128)(2,1)S(1)}, u32[]{:S(2)}, u32[]{:S(2)}) collective-permute-start(bf16[32,2048]{1,0:T(8,128)(2,1)S(1)} %get-tuple-element.107), channel_id=1, source_target_pairs={{0,4},{4,0},{8,12},{12,8},{1,5},{5,1},{9,13},{13,9},{2,6},{6,2},{1... | collective-permute-start | bytes 393224 | tf_op jit(solution)/shard_map/ppermute | solution.py:414
  97.5 10.9 %collective-permute-start.30 = (bf16[32,2048]{1,0:T(8,128)(2,1)S(1)}, bf16[32,2048]{1,0:T(8,128)(2,1)S(1)}, u32[]{:S(2)}, u32[]{:S(2)}) collective-permute-start(bf16[32,2048]{1,0:T(8,128)(2,1)S(1)} %get-tuple-element.108), channel_id=1, source_target_pairs={{0,4},{4,0},{8,12},{12,8},{1,5},{5,1},{9,13},{13,9},{2,6},{6,2},{1... | collective-permute-start | bytes 393224 | tf_op jit(solution)/shard_map/ppermute | solution.py:414
  99.4 8.9 %collective-permute-start.28 = (bf16[32,2048]{1,0:T(8,128)(2,1)S(1)}, bf16[32,2048]{1,0:T(8,128)(2,1)S(1)}, u32[]{:S(2)}, u32[]{:S(2)}) collective-permute-start(bf16[32,2048]{1,0:T(8,128)(2,1)S(1)} %relay.3), channel_id=1, source_target_pairs={{0,8},{4,12},{8,0},{12,4},{1,9},{5,13},{9,1},{13,5},{2,10},{6,14},... | collective-permute-start | bytes 393224 | tf_op jit(solution)/shard_map/ppermute | solution.py:414
  (11 other events, 32.1 us)
